TPU v7x, 512 devices: a whole 4x8x8 slice. The times are simulated.
512 devices in a mesh: row: 16 (over z_lo, x), col: 8 (over y), fiber: 4 (over z_hi, core).
Axes of the slice: x: 4, y: 8, z: 8 (z_hi: 2, z_lo: 4; z = z_hi * 4 + z_lo), core: 2. Of those that a mesh axis runs over, the one named last changes fastest.
Arguments:
- values: float32 [12288, 12288], P('row', ('col', 'fiber')), may hold values from -6 to 6
- tile_mask: int32 [96, 96], P('row', ('col', 'fiber')), may hold values from 0 to 1, as said below
- keep_mask: int32 [96, 96], P('row', ('col', 'fiber')), may hold values 0 or 1
Outputs:
- flows: float32 [12288, 12288], P('row', ('col', 'fiber'))
Inputs may be any that keep to these rules, and one draw needn't show every extreme that they name: `tile_mask`: 1 marks a tile that holds entries; every diagonal tile is 1, and tiles with low indices are denser.
All inputs are finite; a program needn't handle non-finite values. No bound on the sum of `keep_mask` on one device may be relied on, other than what follows from the above.
Results may differ from a plain program's by a relative error of at most 0.017.
Values may be sent and summed in bfloat16 or wider, within the bound.
No kernel may reach another device: no remote copies, remote signals or barrier semaphores. Data moves between devices by JAX's collectives and lax.ppermute only.
A program may use at most 64 MiB of HBM per device.

v0:
```python
import jax
import jax.numpy as jnp
from jax import lax
from jax.sharding import PartitionSpec as P


def cut_along(shard, dim, peers):
    lengths = shard.shape
    parts = shard.reshape(*lengths[:dim], peers, lengths[dim] // peers, *lengths[dim + 1 :])
    return jnp.moveaxis(parts, dim, 0)


def sum_at_owner(shard, axis, dim):
    parts = cut_along(shard, dim, lax.axis_size(axis))
    arrived = lax.all_to_all(parts, axis, split_axis=0, concat_axis=0, tiled=True)
    return arrived.astype(jnp.float32).sum(axis=0)


def sent_to_all(shard, axis):
    copies = jnp.broadcast_to(shard, (lax.axis_size(axis), *shard.shape))
    return lax.all_to_all(copies, axis, split_axis=0, concat_axis=0, tiled=True)


def taken_together(shard, axis):
    return sent_to_all(shard, axis).sum(axis=0)


def spread_tiles(mask, tile_size):
    count_rows, count_cols = mask.shape
    wide = jnp.broadcast_to(
        mask.astype(jnp.float32)[:, None, :, None], (count_rows, tile_size, count_cols, tile_size)
    )
    return wide.reshape(count_rows * tile_size, count_cols * tile_size)


def local(values, tile_mask, keep_mask):
    n_row = lax.axis_size("row")
    n_fib = lax.axis_size("fiber")
    tile_size = values.shape[1] // tile_mask.shape[1]
    weighted = (values * spread_tiles(tile_mask, tile_size)).astype(jnp.bfloat16)
    rows_dev, unit_width = weighted.shape
    sub_width = unit_width // n_fib
    unit_count = rows_dev // unit_width
    left_stack = weighted.reshape(rows_dev, n_fib, sub_width)
    right_stack = weighted.reshape(unit_count, n_fib, sub_width, unit_width)
    left_recv, right_recv = (
        lax.all_to_all(left_stack, "fiber", split_axis=1, concat_axis=1, tiled=True),
        lax.all_to_all(right_stack, "fiber", split_axis=1, concat_axis=1, tiled=True),
    )
    left_local = left_recv.reshape(rows_dev, unit_width)
    right_local = jnp.transpose(right_recv, (0, 2, 1, 3)).reshape(
        unit_count * sub_width, n_fib * unit_width
    )
    left_all = lax.all_gather(left_local, "col", axis=1, tiled=True)
    partial_product = jnp.dot(
        left_all,
        lax.all_gather(right_local, "row", axis=0, tiled=True),
        preferred_element_type=jnp.float32,
    )
    expanded = sum_at_owner(partial_product.astype(jnp.bfloat16), "fiber", 1)
    squared = expanded * expanded
    col_total = taken_together(jnp.sum(squared, axis=0), "row")
    col_scale = col_total / (rows_dev * n_row) + 1e-06
    return spread_tiles(keep_mask, tile_size) * squared / col_scale[None, :]


def solution(mesh):
    return jax.shard_map(
        local,
        mesh=mesh,
        in_specs=(
            P("row", ("col", "fiber")),
            P("row", ("col", "fiber")),
            P("row", ("col", "fiber")),
        ),
        out_specs=P("row", ("col", "fiber")),
        check_vma=False,
    )
```

profile of v0, /device:TPU:1, one launch (start us, length us, event | category | flops | bytes accessed | tf_op | source)
XLA Modules:
  0.0 310.3 jit_solution(8198016643156649648)
XLA Ops:
  6.5 0.0 all-gather.3.cloned.1.call-start
  6.5 0.7 convert_element_type.16
  7.2 1.6 copy.27
  8.9 0.2 broadcast_in_dim.7
  9.0 0.4 fusion
  9.4 24.5 %all_to_all.21 = bf16[768,4,96]{0,2,1:T(8,128)(2,1)} all-to-all(bf16[768,4,96]{0,2,1:T(8,128)(2,1)S(1)} %bitcast.34), channel_id=1, replica_groups=mesh['row'=16,'col'=8,'fiber'=4] {'fiber'}, dimensions={1} | all-to-all | bytes 1179648 | tf_op jit(solution)/shard_map/all_to_all | solution.py:47
  33.9 0.0 all-gather.3.cloned.1.call-update
  34.0 0.0 all-gather.5.cloned.1.call-start
  34.0 0.3 copy.28
  34.3 0.1 copy.29
  34.4 22.1 %all_to_all.22 = bf16[2,4,96,384]{3,2,0,1:T(8,128)(2,1)S(1)} all-to-all(bf16[2,4,96,384]{3,2,0,1:T(8,128)(2,1)S(1)} %copy.29), channel_id=1, replica_groups=mesh['row'=16,'col'=8,'fiber'=4] {'fiber'}, dimensions={1} | all-to-all | bytes 1179648 | tf_op jit(solution)/shard_map/all_to_all | solution.py:48
  56.5 0.5 copy.30
  57.0 0.9 copy.40
  57.9 0.0 all-gather.5.cloned.1.call-update
  57.9 42.4 %all-gather.3.cloned.1.call-done = bf16[768,3072]{0,1:T(8,128)(2,1)} async-done(((bf16[768,384]{0,1:T(8,128)(2,1)}), bf16[768,3072]{0,1:T(8,128)(2,1)}) %all-gather.3.cloned.1.call-update) | async-done | bytes 4718608 | tf_op jit(solution)/shard_map/all_gather | solution.py:54
  100.3 117.2 %all-gather.5.cloned.1.call-done = bf16[3072,1536]{1,0:T(8,128)(2,1)} async-done(((bf16[192,1536]{1,0:T(8,128)(2,1)}), bf16[3072,1536]{1,0:T(8,128)(2,1)}) %all-gather.5.cloned.1.call-update) | async-done | bytes 9437200 | tf_op jit(solution)/shard_map/all_gather | solution.py:57
  217.5 11.6 %convolution_convert_fusion = bf16[768,1536]{1,0:T(8,128)(2,1)S(1)} fusion(bf16[768,3072]{0,1:T(8,128)(2,1)} %all-gather.3.cloned.1.call-done, bf16[3072,1536]{1,0:T(8,128)(2,1)} %all-gather.5.cloned.1.call-done), kind=kOutput, calls=%fused_computation.1 | convolution fusion | flops 7248936960 | bytes 16515072 | tf_op jit(solution)/shard_map/dot_general | solution.py:55
  229.1 0.2 copy.44
  229.4 46.7 %all_to_all.23 = bf16[4,768,384]{2,1,0:T(8,128)(2,1)S(1)} all-to-all(bf16[4,768,384]{2,1,0:T(8,128)(2,1)S(1)} %bitcast.31), channel_id=1, replica_groups=mesh['row'=16,'col'=8,'fiber'=4] {'fiber'}, dimensions={0} | all-to-all | bytes 4718592 | tf_op jit(solution)/shard_map/all_to_all | solution.py:15
  276.0 0.0 copy-start
  276.1 0.4 convert_reduce_fusion
  276.4 0.1 multiply_reduce_fusion
  276.6 0.6 broadcast_in_dim.8
  277.2 17.4 %all-to-all-start.3 = ((f32[16,1,384]{2,1,0:T(1,128)}), f32[16,1,384]{2,1,0:T(1,128)}, u32[]{:S(2)}, u32[]{:S(2)}) async-start(f32[16,1,384]{2,1,0:T(1,128)} %broadcast_in_dim.8), calls=%async_computation.3 | async-start | bytes 49152 | tf_op jit(solution)/shard_map/all_to_all | solution.py:21
  294.6 0.0 copy-done
  294.6 0.2 broadcast_in_dim.6
  294.8 0.3 copy.45
  295.0 0.4 copy.33
  295.4 6.2 %all-to-all-done.3 = f32[16,1,384]{2,1,0:T(1,128)} async-done(((f32[16,1,384]{2,1,0:T(1,128)}), f32[16,1,384]{2,1,0:T(1,128)}, u32[]{:S(2)}, u32[]{:S(2)}) %all-to-all-start.3) | async-done | bytes 24608 | tf_op jit(solution)/shard_map/all_to_all | solution.py:21
  301.5 0.8 reduce_sum.29
  302.3 1.1 multiply_divide_fusion
  (2 shorter events, 0.0 us)
Async XLA Ops:
  6.5 93.8 %all-gather.3.cloned.1.call-start = ((), (), s32[]{:S(2)}) async-start(), calls=%async_computation.4 | async-start | bytes 5308416 | tf_op jit(solution)/shard_map/all_gather | solution.py:54
  34.0 183.6 %all-gather.5.cloned.1.call-start = ((), (), s32[]{:S(2)}) async-start(), calls=%async_computation.5 | async-start | bytes 10027008 | tf_op jit(solution)/shard_map/all_gather | solution.py:57
  276.0 18.5 %copy-start = (s32[6,3]{0,1:T(4,128)S(1)}, s32[6,3]{0,1:T(4,128)}, u32[]{:S(2)}) copy-start(s32[6,3]{0,1:T(4,128)} %param.5) | copy-start | bytes 220
  277.2 24.4 %all-to-all-start.3 = ((f32[16,1,384]{2,1,0:T(1,128)}), f32[16,1,384]{2,1,0:T(1,128)}, u32[]{:S(2)}, u32[]{:S(2)}) async-start(f32[16,1,384]{2,1,0:T(1,128)} %broadcast_in_dim.8), calls=%async_computation.3 | async-start | bytes 49152 | tf_op jit(solution)/shard_map/all_to_all | solution.py:21
Sparse Core Ops, SparseCore 0:
  34.1 66.2 all-gather.2
  102.4 115.0 all-gather.4
where the time goes:
time: 312 us; the launch traced here: 310 us
  waiting for transfers between devices  166 us (53%)
  blocking collectives  93.3 us (30%)
  starting transfers between devices  17.4 us (6%)
  between operations  13.5 us (4%)
  matrix products  11.6 us (4%)
  local copies, waits for them, and re-layouts  5.17 us (2%)
  other arithmetic  3.47 us (1%)
    all_gather x1, waiting for transfers between devices, local(): lax.all_gather(right_local, 'row', axis=0, tiled=True)  117 us
    all_to_all x1, blocking collectives, sum_at_owner(): lax.all_to_all(parts, axis, split_axis=0, concat_axis=0, tiled=True)  46.7 us
    all_gather x1, waiting for transfers between devices, local(): left_all = lax.all_gather(left_local, 'col', axis=1, tiled=True)  42.4 us
    all_to_all x1, blocking collectives, local(): lax.all_to_all(left_stack, 'fiber', split_axis=1, concat_axis=1, tiled=True)  24.5 us
    all_to_all x1, blocking collectives, local(): lax.all_to_all(right_stack, 'fiber', split_axis=1, concat_axis=1, tiled=T...  22.1 us
    all_to_all x1, starting transfers between devices, sent_to_all(): return lax.all_to_all(copies, axis, split_axis=0, concat_axis=0, tiled=True)  17.4 us
    dot_general x1, matrix products, local(): jnp.dot(left_all, lax.all_gather(right_local, 'row', axis=0, tiled=True),...  11.6 us
  transfers between devices with their start and end apart: 3, of which 3 were waited for; matrix products, arithmetic and copies ran while one was open for 1% of the time, Pallas kernels for 0%

commit v1 on v0

v1 whole, which is shorter than its diff:
```python
import jax
import jax.numpy as jnp
from jax import lax
from jax.sharding import Mesh
from jax.sharding import PartitionSpec as P

Z_LO, X, Y, Z_HI, CORE = 4, 4, 8, 2, 2
Z = Z_LO * Z_HI


def spread_tiles(mask, tile_size):
    count_rows, count_cols = mask.shape
    wide = jnp.broadcast_to(
        mask.astype(jnp.float32)[:, None, :, None], (count_rows, tile_size, count_cols, tile_size)
    )
    return wide.reshape(count_rows * tile_size, count_cols * tile_size)


def z_index(z):
    return (z % Z_LO) * Z_HI + z // Z_LO


def shift_z(shard, step):
    pairs = [(z_index(z), z_index((z + step) % Z)) for z in range(Z)]
    return lax.ppermute(shard, ("zlo", "zhi"), pairs)


def shift_x(shard, step):
    return lax.ppermute(shard, "x", [(i, (i + step) % X) for i in range(X)])


def swap(shard, axis):
    return lax.ppermute(shard, axis, [(0, 1), (1, 0)])


def pick(stack, index):
    return lax.dynamic_index_in_dim(stack, index, 0, keepdims=False)


def ring(shard):
    half = shard.shape[0] // 2
    arrived = [(0, shard)]
    up = down = shard
    for d in range(1, Z // 2):
        up, down = shift_z(up, 1), shift_z(down, -1)
        arrived += [(d, up), (-d, down)]
    far = jnp.concatenate([shift_z(up[:half], 1), shift_z(down[half:], -1)], 0)
    return arrived + [(Z // 2, far)]


def local(values, tile_mask, keep_mask):
    rows, unit = values.shape
    tile_size = unit // tile_mask.shape[1]
    sub = unit // (X * CORE)
    half = rows // 2
    x, core, zhi, zlo = (lax.axis_index(a) for a in ("x", "core", "zhi", "zlo"))
    z = zhi * Z_LO + zlo
    weighted = (values * spread_tiles(tile_mask, tile_size)).astype(jnp.bfloat16)

    left = weighted.T.reshape(X * CORE, sub, 2, half).transpose(0, 2, 1, 3)
    right = weighted.reshape(CORE, X * CORE, sub, unit).transpose(1, 0, 2, 3)
    both = jnp.concatenate([left, right], 1)
    both = lax.all_to_all(both, ("x", "core"), split_axis=0, concat_axis=0, tiled=True)
    both = both.reshape(X, CORE, 4, sub, unit)

    left = both[:, :, :2].transpose(2, 1, 3, 0, 4).reshape(2, CORE * sub, X * half)
    left_near = pick(left, zhi)
    left_far = swap(pick(left, 1 - zhi), "zhi")
    left_near = lax.all_gather(left_near, "y", axis=0, tiled=True)
    left_far = lax.all_gather(left_far, "y", axis=0, tiled=True)

    right = both[:, :, 2:].reshape(2, 2, CORE, CORE, sub, unit).transpose(2, 1, 0, 3, 4, 5)
    right = right.reshape(CORE, 2, 4 * sub, unit)

    def panel(shard):
        whole = jnp.zeros((2, 2, Z_LO, 4 * sub, unit), jnp.bfloat16)
        for d, part in ring(shard):
            origin = (z - d) % Z
            hi, lo = origin // Z_LO, origin % Z_LO
            for k_hi in range(2):
                whole = lax.dynamic_update_slice(
                    whole, part[k_hi][None, None, None], (hi, (k_hi + zhi) % 2, lo, 0, 0)
                )
        whole = whole.reshape(2, 2, Z_LO * 4 * sub, unit)
        return jnp.concatenate([whole[0], whole[1]], -1)

    def product(panel_of):
        return lax.dot_general(
            left_near, panel_of[0], (((0,), (0,)), ((), ())), preferred_element_type=jnp.float32
        ) + lax.dot_general(
            left_far, panel_of[1], (((0,), (0,)), ((), ())), preferred_element_type=jnp.float32
        )

    theirs = panel(pick(right, 1 - core))
    ours = panel(pick(right, core))
    sent = swap(product(theirs).astype(jnp.bfloat16), "core")
    total = product(ours) + sent.astype(jnp.float32)
    total = total.reshape(X, half, 2 * unit)
    rounded = total.astype(jnp.bfloat16)
    partial = pick(total, x)
    for step in range(1, X):
        partial = partial + shift_x(pick(rounded, (x + step) % X), step).astype(jnp.float32)

    squares = jnp.sum(partial * partial, axis=0)
    partial = partial.reshape(half, 2, unit).transpose(1, 0, 2)
    other = swap(pick(partial, 1 - zhi).astype(jnp.bfloat16), "zhi").astype(jnp.float32)
    mine = pick(partial, zhi)
    peers = Z_LO * X * Z_HI
    sums = jnp.broadcast_to(squares, (peers, 1, 2 * unit))
    sums = lax.all_to_all(sums, ("zlo", "x", "zhi"), split_axis=0, concat_axis=0, tiled=True)
    col_total = pick(sums.sum(axis=(0, 1)).reshape(2, unit), zhi)
    col_scale = col_total / (rows * Z_LO * X) + 1e-06
    expanded = jnp.concatenate(
        [jnp.where(zhi == 0, mine, other), jnp.where(zhi == 0, other, mine)], 0
    )
    return spread_tiles(keep_mask, tile_size) * (expanded * expanded) / col_scale[None, :]


def solution(mesh):
    physical = Mesh(
        mesh.devices.reshape(Z_LO, X, Y, Z_HI, CORE), ("zlo", "x", "y", "zhi", "core")
    )
    spec = P(("zlo", "x"), ("y", "zhi", "core"))
    return jax.shard_map(
        local, mesh=physical, in_specs=(spec, spec, spec), out_specs=spec, check_vma=False
    )
```

time: 312 us -> 227 us (0.73)
  waiting for transfers between devices: 166 us -> 53.2 us
  blocking collectives: 93.3 us -> 0 us
  starting transfers between devices: 17.4 us -> 93.7 us
  local copies, waits for them, and re-layouts: 5.17 us -> 41.7 us
  matrix products: 11.6 us -> 16.7 us
    all_gather x2, waiting for transfers between devices: 160 us -> 0.01 us  [the longest x1 0.01 us: local(): left_near = lax.all_gather(left_near, 'y', axis=0, tiled=True)]
    all_to_all x3 -> x0, blocking collectives: 93.3 us -> none  [the longest x1 46.7 us: sum_at_owner(): lax.all_to_all(parts, axis, split_axis=0, concat_axis=0, tiled=True)]
    ppermute x0 -> x22, starting transfers between devices: none -> 77.9 us  [the longest x16 53.6 us: shift_z(): return lax.ppermute(shard, ('zlo', 'zhi'), pairs)]
    ppermute x0 -> x22, waiting for transfers between devices: none -> 23.8 us  [the longest x3 23.8 us: shift_x(): return lax.ppermute(shard, 'x', [(i, (i + step) % X) for i in range(X)])]
    all_to_all x1 -> x2, waiting for transfers between devices: 6.15 us -> 29.4 us  [the longest x1 16.5 us: local(): lax.all_to_all(both, ('x', 'core'), split_axis=0, concat_axis=0, tiled=True)]
    dynamic_update_slice x0 -> x30, local copies, waits for them, and re-layouts: none -> 20.5 us  [panel(): lax.dynamic_update_slice(whole, part[k_hi][None, None, None], (hi, (k_hi...]
    dot_general x1 -> x4, matrix products: 11.6 us -> 16.7 us  [the longest x2 8.59 us: product(): lax.dot_general(left_far, panel_of[1], (((0,), (0,)), ((), ())), preferre...]
    dynamic_slice x0 -> x6, local copies, waits for them, and re-layouts: none -> 5.07 us  [pick(): return lax.dynamic_index_in_dim(stack, index, 0, keepdims=False)]
  transfers between devices with their start and end apart: 3 -> 26, of which waited for: 3 -> 5; matrix products, arithmetic and copies ran while one was open for 1% -> 18% of each run, Pallas kernels for 0% -> 0%
where the time goes in v1:
time: 227 us; the launch traced here: 225 us
  starting transfers between devices  93.7 us (41%)
  waiting for transfers between devices  53.2 us (23%)
  local copies, waits for them, and re-layouts  41.7 us (18%)
  matrix products  16.7 us (7%)
  between operations  14.5 us (6%)
  other arithmetic  5.63 us (2%)
    ppermute x16, starting transfers between devices, shift_z(): return lax.ppermute(shard, ('zlo', 'zhi'), pairs)  53.6 us
    ppermute x3, waiting for transfers between devices, shift_x(): return lax.ppermute(shard, 'x', [(i, (i + step) % X) for i in range(X)])  23.8 us
    dynamic_update_slice x30, local copies, waits for them, and re-layouts, panel(): lax.dynamic_update_slice(whole, part[k_hi][None, None, None], (hi, (k_hi...  20.5 us
    all_to_all x1, waiting for transfers between devices, local(): lax.all_to_all(both, ('x', 'core'), split_axis=0, concat_axis=0, tiled=True)  16.5 us
    ppermute x3, starting transfers between devices, swap(): return lax.ppermute(shard, axis, [(0, 1), (1, 0)])  16.5 us
    all_to_all x1, waiting for transfers between devices, local(): lax.all_to_all(sums, ('zlo', 'x', 'zhi'), split_axis=0, concat_axis=0, ti...  12.8 us
    all_to_all x1, starting transfers between devices, local(): lax.all_to_all(both, ('x', 'core'), split_axis=0, concat_axis=0, tiled=True)  10.3 us
    dot_general x2, matrix products, product(): lax.dot_general(left_far, panel_of[1], (((0,), (0,)), ((), ())), preferre...  8.59 us
  transfers between devices with their start and end apart: 26, of which 5 were waited for; matrix products, arithmetic and copies ran while one was open for 18% of the time, Pallas kernels for 0%

profile of v1, /device:TPU:1, one launch (start us, length us, event | category | flops | bytes accessed | tf_op | source)
XLA Modules:
  0.0 225.4 jit_solution(2731812150046637035)
XLA Ops:
  9.8 2.2 pad_maximum_fusion.2
  12.1 10.3 %all-to-all-start = ((bf16[8,4,48,384]{3,1,2,0:T(4,128)(2,1)}), bf16[8,4,48,384]{3,1,2,0:T(4,128)(2,1)S(1)}, u32[]{:S(2)}, u32[]{:S(2)}) async-start(bf16[8,4,48,384]{3,1,2,0:T(4,128)(2,1)} %pad_maximum_fusion.2), calls=%async_computation | async-start | bytes 2359296 | tf_op jit(solution)/shard_map/all_to_all | solution.py:63
  22.4 16.5 %all-to-all-done = bf16[8,4,48,384]{3,1,2,0:T(4,128)(2,1)S(1)} async-done(((bf16[8,4,48,384]{3,1,2,0:T(4,128)(2,1)}), bf16[8,4,48,384]{3,1,2,0:T(4,128)(2,1)S(1)}, u32[]{:S(2)}, u32[]{:S(2)}) %all-to-all-start) | async-done | bytes 1179680 | tf_op jit(solution)/shard_map/all_to_all | solution.py:63
  42.0 1.9 collective-permute-start.9
  44.0 6.1 %collective-permute-start.10 = (bf16[2,192,384]{2,1,0:T(8,128)(2,1)S(1)}, bf16[2,192,384]{2,1,0:T(8,128)(2,1)}, u32[]{:S(2)}, u32[]{:S(2)}) collective-permute-start(bf16[2,192,384]{2,1,0:T(8,128)(2,1)S(1)} %get-tuple-element.19), channel_id=1, source_target_pairs={{0,386},{128,0},{256,128},{384,256},{2,384},{130,2},{258,130},{386... | collective-permute-start | bytes 884744 | tf_op jit(solution)/shard_map/ppermute | solution.py:25
  50.1 1.9 collective-permute-start
  52.0 4.6 %collective-permute-start.1 = (bf16[2,192,384]{2,1,0:T(8,128)(2,1)S(1)}, bf16[2,192,384]{2,1,0:T(8,128)(2,1)S(1)}, u32[]{:S(2)}, u32[]{:S(2)}) collective-permute-start(bf16[2,192,384]{2,1,0:T(8,128)(2,1)S(1)} %get-tuple-element.18), channel_id=1, source_target_pairs={{0,386},{128,0},{256,128},{384,256},{2,384},{130,2},{258,130},{386... | collective-permute-start | bytes 884744 | tf_op jit(solution)/shard_map/ppermute | solution.py:25
  56.6 4.5 %collective-permute-start.8 = (bf16[96,1536]{1,0:T(8,128)(2,1)}, bf16[96,1536]{1,0:T(8,128)(2,1)S(1)}, u32[]{:S(2)}, u32[]{:S(2)}) collective-permute-start(bf16[96,1536]{1,0:T(8,128)(2,1)} %get-tuple-element.22), channel_id=1, source_target_pairs={{0,2},{2,0},{1,3},{3,1},{4,6},{6,4},{5,7},{7,5},{8,10},{10,8},{9,1... | collective-permute-start | bytes 884744 | tf_op jit(solution)/shard_map/ppermute | solution.py:33
  66.6 4.6 %collective-permute-start.12 = (bf16[2,192,384]{2,1,0:T(8,128)(2,1)}, bf16[2,192,384]{2,1,0:T(8,128)(2,1)}, u32[]{:S(2)}, u32[]{:S(2)}) collective-permute-start(bf16[2,192,384]{2,1,0:T(8,128)(2,1)} %collective-permute-done.10), channel_id=1, source_target_pairs={{0,386},{128,0},{256,128},{384,256},{2,384},{130,2},{258,130},{386... | collective-permute-start | bytes 884744 | tf_op jit(solution)/shard_map/ppermute | solution.py:25
  71.1 1.9 collective-permute-start.2
  78.2 4.6 %collective-permute-start.3 = (bf16[2,192,384]{2,1,0:T(8,128)(2,1)S(1)}, bf16[2,192,384]{2,1,0:T(8,128)(2,1)}, u32[]{:S(2)}, u32[]{:S(2)}) collective-permute-start(bf16[2,192,384]{2,1,0:T(8,128)(2,1)S(1)} %collective-permute-done.1), channel_id=1, source_target_pairs={{0,386},{128,0},{256,128},{384,256},{2,384},{130,2},{258,130},{386... | collective-permute-start | bytes 884744 | tf_op jit(solution)/shard_map/ppermute | solution.py:25
  88.8 4.6 %collective-permute-start.14 = (bf16[2,192,384]{2,1,0:T(8,128)(2,1)}, bf16[2,192,384]{2,1,0:T(8,128)(2,1)S(1)}, u32[]{:S(2)}, u32[]{:S(2)}) collective-permute-start(bf16[2,192,384]{2,1,0:T(8,128)(2,1)} %collective-permute-done.12), channel_id=1, source_target_pairs={{0,386},{128,0},{256,128},{384,256},{2,384},{130,2},{258,130},{386... | collective-permute-start | bytes 884744 | tf_op jit(solution)/shard_map/ppermute | solution.py:25
  95.2 1.9 collective-permute-start.4
  97.8 4.6 %collective-permute-start.5 = (bf16[2,192,384]{2,1,0:T(8,128)(2,1)}, bf16[2,192,384]{2,1,0:T(8,128)(2,1)S(1)}, u32[]{:S(2)}, u32[]{:S(2)}) collective-permute-start(bf16[2,192,384]{2,1,0:T(8,128)(2,1)} %collective-permute-done.3), channel_id=1, source_target_pairs={{0,386},{128,0},{256,128},{384,256},{2,384},{130,2},{258,130},{386... | collective-permute-start | bytes 884744 | tf_op jit(solution)/shard_map/ppermute | solution.py:25
  106.3 1.9 collective-permute-start.15
  108.3 4.6 %collective-permute-start.16 = (bf16[1,192,384]{2,1,0:T(8,128)(2,1)S(1)}, bf16[1,192,384]{2,1,0:T(8,128)(2,1)S(1)}, u32[]{:S(2)}, u32[]{:S(2)}) collective-permute-start(bf16[1,192,384]{2,1,0:T(8,128)(2,1)S(1)} %slice.193), channel_id=1, source_target_pairs={{0,386},{128,0},{256,128},{384,256},{2,384},{130,2},{258,130},{386... | collective-permute-start | bytes 442376 | tf_op jit(solution)/shard_map/ppermute | solution.py:25
  112.9 1.9 collective-permute-start.6
  114.8 4.8 %collective-permute-start.7 = (bf16[1,192,384]{2,1,0:T(8,128)(2,1)S(1)}, bf16[1,192,384]{2,1,0:T(8,128)(2,1)S(1)}, u32[]{:S(2)}, u32[]{:S(2)}) collective-permute-start(bf16[1,192,384]{2,1,0:T(8,128)(2,1)S(1)} %slice.177), channel_id=1, source_target_pairs={{0,386},{128,0},{256,128},{384,256},{2,384},{130,2},{258,130},{386... | collective-permute-start | bytes 442376 | tf_op jit(solution)/shard_map/ppermute | solution.py:25
  125.2 6.1 %fusion = f32[1536,768]{1,0:T(8,128)} fusion(bf16[1,768,1536]{2,1,0:T(8,128)(2,1)} %all-gather.6.cloned.1.call-done, bf16[2,768,384]{2,1,0:T(8,128)(2,1)} %bitcast.207, bf16[2,768,384]{2,1,0:T(8,128)(2,1)S(1)} %bitcast.205), kind=kOutput, calls=%fused_computation.6 | convolution fusion | flops 1814298624 | bytes 9437184 | tf_op jit(solution)/shard_map/dot_general | solution.py:88
  131.3 6.5 %add_convert_fusion = bf16[1536,768]{1,0:T(8,128)(2,1)} fusion(f32[1536,768]{1,0:T(8,128)} %fusion, bf16[768,1536]{1,0:T(8,128)(2,1)} %all-gather.4.cloned.1.call-done, bf16[2,768,384]{2,1,0:T(8,128)(2,1)S(1)} %bitcast.206, bf16[2,768,384]{2,1,0:T(8,128)(2,1)S(1)} %bitcast.208), kind=kOutput, calls=%fused_computation.1 | convolution fusion | flops 1816657920 | bytes 11796480 | tf_op jit(solution)/shard_map/dot_general | solution.py:90
  137.7 7.5 %collective-permute-start.17 = (bf16[1536,768]{1,0:T(8,128)(2,1)}, bf16[1536,768]{1,0:T(8,128)(2,1)S(1)}, u32[]{:S(2)}, u32[]{:S(2)}) collective-permute-start(bf16[1536,768]{1,0:T(8,128)(2,1)} %add_convert_fusion), channel_id=1, source_target_pairs={{0,1},{1,0},{2,3},{3,2},{4,5},{5,4},{6,7},{7,6},{8,9},{9,8},{10,11... | collective-permute-start | bytes 7077896 | tf_op jit(solution)/shard_map/ppermute | solution.py:33
  145.3 2.0 fusion.54
  147.7 2.1 fusion.2
  149.8 2.1 fusion.16
  156.1 2.8 %collective-permute-start.20 = (bf16[384,768]{0,1:T(8,128)(2,1)}, bf16[384,768]{0,1:T(8,128)(2,1)S(1)}, u32[]{:S(2)}, u32[]{:S(2)}) collective-permute-start(bf16[384,768]{0,1:T(8,128)(2,1)} %bitcast.57), channel_id=1, source_target_pairs={{0,96},{32,0},{64,32},{96,64},{1,97},{33,1},{65,33},{97,65},{2,98}... | collective-permute-start | bytes 1769480 | tf_op jit(solution)/shard_map/ppermute | solution.py:29
  160.0 3.1 %collective-permute-start.19 = (bf16[384,768]{0,1:T(8,128)(2,1)}, bf16[384,768]{0,1:T(8,128)(2,1)S(1)}, u32[]{:S(2)}, u32[]{:S(2)}) collective-permute-start(bf16[384,768]{0,1:T(8,128)(2,1)} %bitcast.56), channel_id=1, source_target_pairs={{0,64},{32,96},{64,0},{96,32},{1,65},{33,97},{65,1},{97,33},{2,66}... | collective-permute-start | bytes 1769480 | tf_op jit(solution)/shard_map/ppermute | solution.py:29
  167.9 5.3 %collective-permute-done.20 = bf16[384,768]{0,1:T(8,128)(2,1)S(1)} collective-permute-done((bf16[384,768]{0,1:T(8,128)(2,1)}, bf16[384,768]{0,1:T(8,128)(2,1)S(1)}, u32[]{:S(2)}, u32[]{:S(2)}) %collective-permute-start.20) | collective-permute-done | bytes 589856 | tf_op jit(solution)/shard_map/ppermute | solution.py:29
  173.2 5.1 %collective-permute-done.19 = bf16[384,768]{0,1:T(8,128)(2,1)S(1)} collective-permute-done((bf16[384,768]{0,1:T(8,128)(2,1)}, bf16[384,768]{0,1:T(8,128)(2,1)S(1)}, u32[]{:S(2)}, u32[]{:S(2)}) %collective-permute-start.19) | collective-permute-done | bytes 589856 | tf_op jit(solution)/shard_map/ppermute | solution.py:29
  178.3 13.3 %collective-permute-done.18 = bf16[384,768]{0,1:T(8,128)(2,1)} collective-permute-done((bf16[384,768]{0,1:T(8,128)(2,1)}, bf16[384,768]{0,1:T(8,128)(2,1)}, u32[]{:S(2)}, u32[]{:S(2)}) %collective-permute-start.18) | collective-permute-done | bytes 589856 | tf_op jit(solution)/shard_map/ppermute | solution.py:29
  193.1 4.4 %collective-permute-start.21 = (bf16[384,384]{0,1:T(8,128)(2,1)S(1)}, bf16[384,384]{0,1:T(8,128)(2,1)S(1)}, u32[]{:S(2)}, u32[]{:S(2)}) collective-permute-start(bf16[384,384]{0,1:T(8,128)(2,1)S(1)} %fusion.21), channel_id=1, source_target_pairs={{0,2},{2,0},{1,3},{3,1},{4,6},{6,4},{5,7},{7,5},{8,10},{10,8},{9,1... | collective-permute-start | bytes 884744 | tf_op jit(solution)/shard_map/ppermute | solution.py:33
  198.2 5.4 %all-to-all-start.1 = ((f32[32,1,768]{2,1,0:T(1,128)}), f32[32,1,768]{2,1,0:T(1,128)S(1)}, u32[]{:S(2)}, u32[]{:S(2)}) async-start(f32[32,1,768]{2,1,0:T(1,128)} %broadcast_in_dim.8), calls=%async_computation.1 | async-start | bytes 196608 | tf_op jit(solution)/shard_map/all_to_all | solution.py:110
  203.7 12.8 %all-to-all-done.1 = f32[32,1,768]{2,1,0:T(1,128)S(1)} async-done(((f32[32,1,768]{2,1,0:T(1,128)}), f32[32,1,768]{2,1,0:T(1,128)S(1)}, u32[]{:S(2)}, u32[]{:S(2)}) %all-to-all-start.1) | async-done | bytes 98336 | tf_op jit(solution)/shard_map/all_to_all | solution.py:110
  (112 shorter events, 48.9 us)
Async XLA Ops:
  6.5 1.7 copy-start.3
  12.1 26.9 %all-to-all-start = ((bf16[8,4,48,384]{3,1,2,0:T(4,128)(2,1)}), bf16[8,4,48,384]{3,1,2,0:T(4,128)(2,1)S(1)}, u32[]{:S(2)}, u32[]{:S(2)}) async-start(bf16[8,4,48,384]{3,1,2,0:T(4,128)(2,1)} %pad_maximum_fusion.2), calls=%async_computation | async-start | bytes 2359296 | tf_op jit(solution)/shard_map/all_to_all | solution.py:63
  22.4 102.8 %all-gather.6.cloned.1.call-start = ((), (), s32[]{:S(2)}) async-start(), calls=%async_computation.3 | async-start | bytes 2654208 | tf_op jit(solution)/shard_map/all_gather | solution.py:69
  41.3 89.9 %all-gather.4.cloned.1.call-start = ((), (), s32[]{:S(2)}) async-start(), calls=%async_computation.2 | async-start | bytes 2654208 | tf_op jit(solution)/shard_map/all_gather | solution.py:70
  42.0 22.6 %collective-permute-start.9 = (bf16[2,192,384]{2,1,0:T(8,128)(2,1)S(1)}, bf16[2,192,384]{2,1,0:T(8,128)(2,1)}, u32[]{:S(2)}, u32[]{:S(2)}) collective-permute-start(bf16[2,192,384]{2,1,0:T(8,128)(2,1)S(1)} %get-tuple-element.19), channel_id=1, source_target_pairs={{0,128},{128,256},{256,384},{384,2},{2,130},{130,258},{258,386},{3... | collective-permute-start | bytes 884744 | tf_op jit(solution)/shard_map/ppermute | solution.py:25
  44.0 22.6 %collective-permute-start.10 = (bf16[2,192,384]{2,1,0:T(8,128)(2,1)S(1)}, bf16[2,192,384]{2,1,0:T(8,128)(2,1)}, u32[]{:S(2)}, u32[]{:S(2)}) collective-permute-start(bf16[2,192,384]{2,1,0:T(8,128)(2,1)S(1)} %get-tuple-element.19), channel_id=1, source_target_pairs={{0,386},{128,0},{256,128},{384,256},{2,384},{130,2},{258,130},{386... | collective-permute-start | bytes 884744 | tf_op jit(solution)/shard_map/ppermute | solution.py:25
  50.1 21.0 %collective-permute-start = (bf16[2,192,384]{2,1,0:T(8,128)(2,1)S(1)}, bf16[2,192,384]{2,1,0:T(8,128)(2,1)S(1)}, u32[]{:S(2)}, u32[]{:S(2)}) collective-permute-start(bf16[2,192,384]{2,1,0:T(8,128)(2,1)S(1)} %get-tuple-element.18), channel_id=1, source_target_pairs={{0,128},{128,256},{256,384},{384,2},{2,130},{130,258},{258,386},{3... | collective-permute-start | bytes 884744 | tf_op jit(solution)/shard_map/ppermute | solution.py:25
  52.0 26.2 %collective-permute-start.1 = (bf16[2,192,384]{2,1,0:T(8,128)(2,1)S(1)}, bf16[2,192,384]{2,1,0:T(8,128)(2,1)S(1)}, u32[]{:S(2)}, u32[]{:S(2)}) collective-permute-start(bf16[2,192,384]{2,1,0:T(8,128)(2,1)S(1)} %get-tuple-element.18), channel_id=1, source_target_pairs={{0,386},{128,0},{256,128},{384,256},{2,384},{130,2},{258,130},{386... | collective-permute-start | bytes 884744 | tf_op jit(solution)/shard_map/ppermute | solution.py:25
  56.6 26.9 %collective-permute-start.8 = (bf16[96,1536]{1,0:T(8,128)(2,1)}, bf16[96,1536]{1,0:T(8,128)(2,1)S(1)}, u32[]{:S(2)}, u32[]{:S(2)}) collective-permute-start(bf16[96,1536]{1,0:T(8,128)(2,1)} %get-tuple-element.22), channel_id=1, source_target_pairs={{0,2},{2,0},{1,3},{3,1},{4,6},{6,4},{5,7},{7,5},{8,10},{10,8},{9,1... | collective-permute-start | bytes 884744 | tf_op jit(solution)/shard_map/ppermute | solution.py:33
  64.6 20.3 %collective-permute-start.11 = (bf16[2,192,384]{2,1,0:T(8,128)(2,1)}, bf16[2,192,384]{2,1,0:T(8,128)(2,1)}, u32[]{:S(2)}, u32[]{:S(2)}) collective-permute-start(bf16[2,192,384]{2,1,0:T(8,128)(2,1)} %collective-permute-done.9), channel_id=1, source_target_pairs={{0,128},{128,256},{256,384},{384,2},{2,130},{130,258},{258,386},{3... | collective-permute-start | bytes 884744 | tf_op jit(solution)/shard_map/ppermute | solution.py:25
  66.6 22.2 %collective-permute-start.12 = (bf16[2,192,384]{2,1,0:T(8,128)(2,1)}, bf16[2,192,384]{2,1,0:T(8,128)(2,1)}, u32[]{:S(2)}, u32[]{:S(2)}) collective-permute-start(bf16[2,192,384]{2,1,0:T(8,128)(2,1)} %collective-permute-done.10), channel_id=1, source_target_pairs={{0,386},{128,0},{256,128},{384,256},{2,384},{130,2},{258,130},{386... | collective-permute-start | bytes 884744 | tf_op jit(solution)/shard_map/ppermute | solution.py:25
  71.1 24.1 %collective-permute-start.2 = (bf16[2,192,384]{2,1,0:T(8,128)(2,1)S(1)}, bf16[2,192,384]{2,1,0:T(8,128)(2,1)S(1)}, u32[]{:S(2)}, u32[]{:S(2)}) collective-permute-start(bf16[2,192,384]{2,1,0:T(8,128)(2,1)S(1)} %collective-permute-done), channel_id=1, source_target_pairs={{0,128},{128,256},{256,384},{384,2},{2,130},{130,258},{258,386},{3... | collective-permute-start | bytes 884744 | tf_op jit(solution)/shard_map/ppermute | solution.py:25
  78.2 19.6 %collective-permute-start.3 = (bf16[2,192,384]{2,1,0:T(8,128)(2,1)S(1)}, bf16[2,192,384]{2,1,0:T(8,128)(2,1)}, u32[]{:S(2)}, u32[]{:S(2)}) collective-permute-start(bf16[2,192,384]{2,1,0:T(8,128)(2,1)S(1)} %collective-permute-done.1), channel_id=1, source_target_pairs={{0,386},{128,0},{256,128},{384,256},{2,384},{130,2},{258,130},{386... | collective-permute-start | bytes 884744 | tf_op jit(solution)/shard_map/ppermute | solution.py:25
  84.9 21.4 %collective-permute-start.13 = (bf16[2,192,384]{2,1,0:T(8,128)(2,1)}, bf16[2,192,384]{2,1,0:T(8,128)(2,1)S(1)}, u32[]{:S(2)}, u32[]{:S(2)}) collective-permute-start(bf16[2,192,384]{2,1,0:T(8,128)(2,1)} %collective-permute-done.11), channel_id=1, source_target_pairs={{0,128},{128,256},{256,384},{384,2},{2,130},{130,258},{258,386},{3... | collective-permute-start | bytes 884744 | tf_op jit(solution)/shard_map/ppermute | solution.py:25
  88.8 19.5 %collective-permute-start.14 = (bf16[2,192,384]{2,1,0:T(8,128)(2,1)}, bf16[2,192,384]{2,1,0:T(8,128)(2,1)S(1)}, u32[]{:S(2)}, u32[]{:S(2)}) collective-permute-start(bf16[2,192,384]{2,1,0:T(8,128)(2,1)} %collective-permute-done.12), channel_id=1, source_target_pairs={{0,386},{128,0},{256,128},{384,256},{2,384},{130,2},{258,130},{386... | collective-permute-start | bytes 884744 | tf_op jit(solution)/shard_map/ppermute | solution.py:25
  95.2 17.6 %collective-permute-start.4 = (bf16[2,192,384]{2,1,0:T(8,128)(2,1)S(1)}, bf16[2,192,384]{2,1,0:T(8,128)(2,1)S(1)}, u32[]{:S(2)}, u32[]{:S(2)}) collective-permute-start(bf16[2,192,384]{2,1,0:T(8,128)(2,1)S(1)} %collective-permute-done.2), channel_id=1, source_target_pairs={{0,128},{128,256},{256,384},{384,2},{2,130},{130,258},{258,386},{3... | collective-permute-start | bytes 884744 | tf_op jit(solution)/shard_map/ppermute | solution.py:25
  97.8 17.0 %collective-permute-start.5 = (bf16[2,192,384]{2,1,0:T(8,128)(2,1)}, bf16[2,192,384]{2,1,0:T(8,128)(2,1)S(1)}, u32[]{:S(2)}, u32[]{:S(2)}) collective-permute-start(bf16[2,192,384]{2,1,0:T(8,128)(2,1)} %collective-permute-done.3), channel_id=1, source_target_pairs={{0,386},{128,0},{256,128},{384,256},{2,384},{130,2},{258,130},{386... | collective-permute-start | bytes 884744 | tf_op jit(solution)/shard_map/ppermute | solution.py:25
  106.3 16.2 %collective-permute-start.15 = (bf16[1,192,384]{2,1,0:T(8,128)(2,1)S(1)}, bf16[1,192,384]{2,1,0:T(8,128)(2,1)S(1)}, u32[]{:S(2)}, u32[]{:S(2)}) collective-permute-start(bf16[1,192,384]{2,1,0:T(8,128)(2,1)S(1)} %slice.190), channel_id=1, source_target_pairs={{0,128},{128,256},{256,384},{384,2},{2,130},{130,258},{258,386},{3... | collective-permute-start | bytes 442376 | tf_op jit(solution)/shard_map/ppermute | solution.py:25
  108.3 14.9 %collective-permute-start.16 = (bf16[1,192,384]{2,1,0:T(8,128)(2,1)S(1)}, bf16[1,192,384]{2,1,0:T(8,128)(2,1)S(1)}, u32[]{:S(2)}, u32[]{:S(2)}) collective-permute-start(bf16[1,192,384]{2,1,0:T(8,128)(2,1)S(1)} %slice.193), channel_id=1, source_target_pairs={{0,386},{128,0},{256,128},{384,256},{2,384},{130,2},{258,130},{386... | collective-permute-start | bytes 442376 | tf_op jit(solution)/shard_map/ppermute | solution.py:25
  112.9 9.6 %collective-permute-start.6 = (bf16[1,192,384]{2,1,0:T(8,128)(2,1)S(1)}, bf16[1,192,384]{2,1,0:T(8,128)(2,1)S(1)}, u32[]{:S(2)}, u32[]{:S(2)}) collective-permute-start(bf16[1,192,384]{2,1,0:T(8,128)(2,1)S(1)} %slice.174), channel_id=1, source_target_pairs={{0,128},{128,256},{256,384},{384,2},{2,130},{130,258},{258,386},{3... | collective-permute-start | bytes 442376 | tf_op jit(solution)/shard_map/ppermute | solution.py:25
  114.8 8.4 %collective-permute-start.7 = (bf16[1,192,384]{2,1,0:T(8,128)(2,1)S(1)}, bf16[1,192,384]{2,1,0:T(8,128)(2,1)S(1)}, u32[]{:S(2)}, u32[]{:S(2)}) collective-permute-start(bf16[1,192,384]{2,1,0:T(8,128)(2,1)S(1)} %slice.177), channel_id=1, source_target_pairs={{0,386},{128,0},{256,128},{384,256},{2,384},{130,2},{258,130},{386... | collective-permute-start | bytes 442376 | tf_op jit(solution)/shard_map/ppermute | solution.py:25
  125.2 6.1 %copy-start.1 = (bf16[1,2,4,192,384]{4,3,2,1,0:T(8,128)(2,1)S(1)}, bf16[1,2,4,192,384]{4,3,2,1,0:T(8,128)(2,1)}, u32[]{:S(2)}) copy-start(bf16[1,2,4,192,384]{4,3,2,1,0:T(8,128)(2,1)} %get-tuple-element.13) | copy-start | bytes 3538948
  137.7 14.2 %collective-permute-start.17 = (bf16[1536,768]{1,0:T(8,128)(2,1)}, bf16[1536,768]{1,0:T(8,128)(2,1)S(1)}, u32[]{:S(2)}, u32[]{:S(2)}) collective-permute-start(bf16[1536,768]{1,0:T(8,128)(2,1)} %add_convert_fusion), channel_id=1, source_target_pairs={{0,1},{1,0},{2,3},{3,2},{4,5},{5,4},{6,7},{7,6},{8,9},{9,8},{10,11... | collective-permute-start | bytes 7077896 | tf_op jit(solution)/shard_map/ppermute | solution.py:33
  145.3 2.4 %copy-start.5 = (bf16[1,768,1536]{2,1,0:T(8,128)(2,1)S(1)}, bf16[1,768,1536]{2,1,0:T(8,128)(2,1)}, u32[]{:S(2)}) copy-start(bf16[1,768,1536]{2,1,0:T(8,128)(2,1)} %all-gather.6.cloned.1.call-done) | copy-start | bytes 7077892
  147.7 2.1 copy-start.6
  152.8 2.1 copy-start
  156.1 17.0 %collective-permute-start.20 = (bf16[384,768]{0,1:T(8,128)(2,1)}, bf16[384,768]{0,1:T(8,128)(2,1)S(1)}, u32[]{:S(2)}, u32[]{:S(2)}) collective-permute-start(bf16[384,768]{0,1:T(8,128)(2,1)} %bitcast.57), channel_id=1, source_target_pairs={{0,96},{32,0},{64,32},{96,64},{1,97},{33,1},{65,33},{97,65},{2,98}... | collective-permute-start | bytes 1769480 | tf_op jit(solution)/shard_map/ppermute | solution.py:29
  160.0 18.3 %collective-permute-start.19 = (bf16[384,768]{0,1:T(8,128)(2,1)}, bf16[384,768]{0,1:T(8,128)(2,1)S(1)}, u32[]{:S(2)}, u32[]{:S(2)}) collective-permute-start(bf16[384,768]{0,1:T(8,128)(2,1)} %bitcast.56), channel_id=1, source_target_pairs={{0,64},{32,96},{64,0},{96,32},{1,65},{33,97},{65,1},{97,33},{2,66}... | collective-permute-start | bytes 1769480 | tf_op jit(solution)/shard_map/ppermute | solution.py:29
  164.2 27.4 %collective-permute-start.18 = (bf16[384,768]{0,1:T(8,128)(2,1)}, bf16[384,768]{0,1:T(8,128)(2,1)}, u32[]{:S(2)}, u32[]{:S(2)}) collective-permute-start(bf16[384,768]{0,1:T(8,128)(2,1)} %bitcast.55), channel_id=1, source_target_pairs={{0,32},{32,64},{64,96},{96,0},{1,33},{33,65},{65,97},{97,1},{2,34}... | collective-permute-start | bytes 1769480 | tf_op jit(solution)/shard_map/ppermute | solution.py:29
  167.8 35.8 %copy-start.4 = (s32[6,3]{0,1:T(4,128)S(1)}, s32[6,3]{0,1:T(4,128)}, u32[]{:S(2)}) copy-start(s32[6,3]{0,1:T(4,128)} %param.5) | copy-start | bytes 220
  193.1 23.5 %collective-permute-start.21 = (bf16[384,384]{0,1:T(8,128)(2,1)S(1)}, bf16[384,384]{0,1:T(8,128)(2,1)S(1)}, u32[]{:S(2)}, u32[]{:S(2)}) collective-permute-start(bf16[384,384]{0,1:T(8,128)(2,1)S(1)} %fusion.21), channel_id=1, source_target_pairs={{0,2},{2,0},{1,3},{3,1},{4,6},{6,4},{5,7},{7,5},{8,10},{10,8},{9,1... | collective-permute-start | bytes 884744 | tf_op jit(solution)/shard_map/ppermute | solution.py:33
  198.2 18.3 %all-to-all-start.1 = ((f32[32,1,768]{2,1,0:T(1,128)}), f32[32,1,768]{2,1,0:T(1,128)S(1)}, u32[]{:S(2)}, u32[]{:S(2)}) async-start(f32[32,1,768]{2,1,0:T(1,128)} %broadcast_in_dim.8), calls=%async_computation.1 | async-start | bytes 196608 | tf_op jit(solution)/shard_map/all_to_all | solution.py:110
  (1 other events, 0.7 us)
Sparse Core Ops, SparseCore 0:
  41.5 39.5 all-gather.5
  84.4 41.9 all-gather.3

commit v2 on v1

v2 whole, which is shorter than its diff:
```python
import jax
import jax.numpy as jnp
from jax import lax
from jax.sharding import Mesh
from jax.sharding import PartitionSpec as P

Z_LO, X, Y, Z_HI, CORE = 4, 4, 8, 2, 2


def spread_tiles(mask, tile_size):
    count_rows, count_cols = mask.shape
    wide = jnp.broadcast_to(
        mask.astype(jnp.float32)[:, None, :, None], (count_rows, tile_size, count_cols, tile_size)
    )
    return wide.reshape(count_rows * tile_size, count_cols * tile_size)


def shift_y(shard, step):
    return lax.ppermute(shard, "y", [(i, (i + step) % Y) for i in range(Y)])


def shift_x(shard, step):
    return lax.ppermute(shard, "x", [(i, (i + step) % X) for i in range(X)])


def swap(shard, axis):
    return lax.ppermute(shard, axis, [(0, 1), (1, 0)])


def pick(stack, index):
    return lax.dynamic_index_in_dim(stack, index, 0, keepdims=False)


def in_order(first, second):
    return lax.optimization_barrier((first, second))


def rings(near, far, shift, size):
    arrived = ([(0, near)], [])
    ends = [[near, near], [far, far]]
    for d in range(1, size // 2):
        for which in (0, 1):
            up, down = ends[which]
            up, down = shift(up, 1), shift(down, -1)
            if d == 1 and which == 0:
                up, far = in_order(up, far)
                ends[1] = [far, far]
                arrived[1].append((0, far))
            ends[which] = [up, down]
            arrived[which].extend([(d, up), (-d, down)])
    half = near.shape[0] // 2
    for which in (0, 1):
        up, down = ends[which]
        last = jnp.concatenate([shift(up[:half], 1), shift(down[half:], -1)], 0)
        arrived[which].append((size // 2, last))
    return arrived


def local(values, tile_mask, keep_mask):
    rows, unit = values.shape
    tile_size = unit // tile_mask.shape[1]
    sub = unit // (X * CORE)
    half = rows // 2
    x, y, core, zhi = (lax.axis_index(a) for a in ("x", "y", "core", "zhi"))
    weighted = (values * spread_tiles(tile_mask, tile_size)).astype(jnp.bfloat16)

    left = weighted.T.reshape(X * CORE, sub, 2, half).transpose(0, 2, 1, 3)
    right = weighted.reshape(CORE, X * CORE, sub, unit).transpose(1, 0, 2, 3)
    both = jnp.concatenate([left, right], 1)
    both = lax.all_to_all(both, ("x", "core"), split_axis=0, concat_axis=0, tiled=True)
    both = both.reshape(X, CORE, 4, sub, unit)

    right = both[:, :, 2:].reshape(2, 2, CORE, CORE, sub, unit).transpose(1, 0, 3, 4, 2, 5)
    right = jnp.where(core == 0, right, right[..., ::-1, :]).reshape(1, 8 * sub, CORE * unit)
    right = lax.all_gather(right, ("zhi", "zlo"), axis=0, tiled=True)
    right = right.reshape(Z_HI, Z_LO * 8 * sub, CORE * unit)

    left = both[:, :, :2].transpose(2, 1, 3, 0, 4).reshape(2, CORE * sub, X * half)
    far = swap(pick(left, 1 - zhi), "zhi")
    whole = jnp.zeros((Y // 2, Z_HI, 2, CORE * sub, X * half), jnp.bfloat16)
    for arrived, hi in zip(rings(pick(left, zhi), far, shift_y, Y), (zhi, 1 - zhi)):
        for d, shard in arrived:
            origin = (y - d) % Y
            whole = lax.dynamic_update_slice(
                whole, shard[None, None, None], (origin // 2, hi, origin % 2, 0, 0)
            )
    left = whole.reshape(Y * Z_HI * CORE * sub, X * half)

    def columns(which):
        product = lax.dot_general(
            left, pick(right, which), (((0,), (0,)), ((), ())), preferred_element_type=jnp.float32
        )
        sent = swap(product[:, unit:].astype(jnp.bfloat16), "core")
        total = product[:, :unit] + sent.astype(jnp.float32)
        total = total.reshape(X, half, unit)
        rounded = total.astype(jnp.bfloat16)
        partial = pick(total, x)
        for step in range(1, X):
            partial = partial + shift_x(pick(rounded, (x + step) % X), step).astype(jnp.float32)
        return partial

    other = columns(1 - zhi)
    sums = swap(jnp.sum(other * other, axis=0)[None], "zhi")
    other = swap(other.astype(jnp.bfloat16), "zhi").astype(jnp.float32)
    mine = columns(zhi)
    sums = sums + jnp.sum(mine * mine, axis=0)[None]
    sums = jnp.broadcast_to(sums, (Z_LO * X, 1, unit))
    sums = lax.all_to_all(sums, ("zlo", "x"), split_axis=0, concat_axis=0, tiled=True)
    col_scale = sums.sum(axis=(0, 1)) / (rows * Z_LO * X) + 1e-06
    expanded = jnp.concatenate(
        [jnp.where(zhi == 0, mine, other), jnp.where(zhi == 0, other, mine)], 0
    )
    return spread_tiles(keep_mask, tile_size) * (expanded * expanded) / col_scale[None, :]


def solution(mesh):
    physical = Mesh(
        mesh.devices.reshape(Z_LO, X, Y, Z_HI, CORE), ("zlo", "x", "y", "zhi", "core")
    )
    spec = P(("zlo", "x"), ("y", "zhi", "core"))
    return jax.shard_map(
        local, mesh=physical, in_specs=(spec, spec, spec), out_specs=spec, check_vma=False
    )
```

time: 227 us -> 235 us (1.035)
  starting transfers between devices: 93.7 us -> 120 us
  waiting for transfers between devices: 53.2 us -> 34.1 us
  other arithmetic: 5.63 us -> 12.7 us
  matrix products: 16.7 us -> 13 us
  local copies, waits for them, and re-layouts: 41.7 us -> 38.1 us
    ppermute x3 -> x6, waiting for transfers between devices: 23.8 us -> 0.02 us  [shift_x(): return lax.ppermute(shard, 'x', [(i, (i + step) % X) for i in range(X)])]
    ppermute x3 -> x5, starting transfers between devices: 16.5 us -> 30.3 us  [swap(): return lax.ppermute(shard, axis, [(0, 1), (1, 0)])]
    ppermute x3 -> x6, starting transfers between devices: 7.78 us -> 18.6 us  [shift_x(): return lax.ppermute(shard, 'x', [(i, (i + step) % X) for i in range(X)])]
    dynamic_update_slice x30 -> x14, local copies, waits for them, and re-layouts: 20.5 us -> 10.3 us  [local(): lax.dynamic_update_slice(whole, shard[None, None, None], (origin // 2, hi...]
    ppermute x16, waiting for transfers between devices: 0.04 us -> 5.57 us  [shift_y(): return lax.ppermute(shard, 'y', [(i, (i + step) % Y) for i in range(Y)])]
    dynamic_slice x6 -> x11, local copies, waits for them, and re-layouts: 5.07 us -> 9.89 us  [pick(): return lax.dynamic_index_in_dim(stack, index, 0, keepdims=False)]
    dot_general x4 -> x2, matrix products: 16.7 us -> 13 us  [columns(): lax.dot_general(left, pick(right, which), (((0,), (0,)), ((), ())), prefe...]
    add x2 -> x4, other arithmetic: 0.93 us -> 4.38 us  [the longest x2 4.36 us: columns(): total = product[:, :unit] + sent.astype(jnp.float32)]
  transfers between devices with their start and end apart: 26 -> 30, of which waited for: 5 -> 6; matrix products, arithmetic and copies ran while one was open for 18% -> 15% of each run, Pallas kernels for 0% -> 0%
where the time goes in v2:
time: 235 us; the launch traced here: 233 us
  starting transfers between devices  120 us (51%)
  local copies, waits for them, and re-layouts  38.1 us (16%)
  waiting for transfers between devices  34.1 us (15%)
  between operations  14.4 us (6%)
  matrix products  13 us (6%)
  other arithmetic  12.7 us (5%)
    ppermute x16, starting transfers between devices, shift_y(): return lax.ppermute(shard, 'y', [(i, (i + step) % Y) for i in range(Y)])  54.2 us
    ppermute x5, starting transfers between devices, swap(): return lax.ppermute(shard, axis, [(0, 1), (1, 0)])  30.3 us
    ppermute x6, starting transfers between devices, shift_x(): return lax.ppermute(shard, 'x', [(i, (i + step) % X) for i in range(X)])  18.6 us
    all_to_all x1, waiting for transfers between devices, local(): lax.all_to_all(both, ('x', 'core'), split_axis=0, concat_axis=0, tiled=True)  16.5 us
    dot_general x2, matrix products, columns(): lax.dot_general(left, pick(right, which), (((0,), (0,)), ((), ())), prefe...  13 us
    all_to_all x1, waiting for transfers between devices, local(): lax.all_to_all(sums, ('zlo', 'x'), split_axis=0, concat_axis=0, tiled=True)  11.1 us
    all_to_all x1, starting transfers between devices, local(): lax.all_to_all(both, ('x', 'core'), split_axis=0, concat_axis=0, tiled=True)  10.3 us
    dynamic_update_slice x14, local copies, waits for them, and re-layouts, local(): lax.dynamic_update_slice(whole, shard[None, None, None], (origin // 2, hi...  10.3 us
  transfers between devices with their start and end apart: 30, of which 6 were waited for; matrix products, arithmetic and copies ran while one was open for 15% of the time, Pallas kernels for 0%

profile of v2, /device:TPU:1, one launch (start us, length us, event | category | flops | bytes accessed | tf_op | source)
XLA Modules:
  0.0 232.7 jit_solution(12749369882359695973)
XLA Ops:
  10.5 2.2 pad_maximum_fusion
  12.7 10.3 %all-to-all-start = ((bf16[8,4,48,384]{3,1,2,0:T(4,128)(2,1)}), bf16[8,4,48,384]{3,1,2,0:T(4,128)(2,1)S(1)}, u32[]{:S(2)}, u32[]{:S(2)}) async-start(bf16[8,4,48,384]{3,1,2,0:T(4,128)(2,1)} %pad_maximum_fusion), calls=%async_computation | async-start | bytes 2359296 | tf_op jit(solution)/shard_map/all_to_all | solution.py:70
  23.0 16.5 %all-to-all-done = bf16[8,4,48,384]{3,1,2,0:T(4,128)(2,1)S(1)} async-done(((bf16[8,4,48,384]{3,1,2,0:T(4,128)(2,1)}), bf16[8,4,48,384]{3,1,2,0:T(4,128)(2,1)S(1)}, u32[]{:S(2)}, u32[]{:S(2)}) %all-to-all-start) | async-done | bytes 1179680 | tf_op jit(solution)/shard_map/all_to_all | solution.py:70
  45.0 7.4 %collective-permute-start.1 = (bf16[96,1536]{1,0:T(8,128)(2,1)S(1)}, bf16[96,1536]{1,0:T(8,128)(2,1)S(1)}, u32[]{:S(2)}, u32[]{:S(2)}) collective-permute-start(bf16[96,1536]{1,0:T(8,128)(2,1)S(1)} %get-tuple-element.23), channel_id=1, source_target_pairs={{0,2},{2,0},{1,3},{3,1},{4,6},{6,4},{5,7},{7,5},{8,10},{10,8},{9,1... | collective-permute-start | bytes 884744 | tf_op jit(solution)/shard_map/ppermute | solution.py:27
  52.3 3.8 %collective-permute-start.2 = (bf16[96,1536]{1,0:T(8,128)(2,1)S(1)}, bf16[96,1536]{1,0:T(8,128)(2,1)S(1)}, u32[]{:S(2)}, u32[]{:S(2)}) collective-permute-start(bf16[96,1536]{1,0:T(8,128)(2,1)S(1)} %get-tuple-element.24), channel_id=1, source_target_pairs={{0,28},{4,0},{8,4},{12,8},{16,12},{20,16},{24,20},{28,24},{1,29},{... | collective-permute-start | bytes 884744 | tf_op jit(solution)/shard_map/ppermute | solution.py:19
  56.6 2.7 %broadcast_in_dim.74 = bf16[4,2,2,96,1536]{4,3,2,1,0:T(8,128)(2,1)} broadcast(bf16[]{:T(256)} %constant.268.clone.1), dimensions={} | broadcast | bytes 4718594 | tf_op jit(solution)/shard_map/broadcast_in_dim | solution.py:80
  60.0 3.7 %collective-permute-start.9 = (bf16[96,1536]{1,0:T(8,128)(2,1)S(1)}, bf16[96,1536]{1,0:T(8,128)(2,1)S(1)}, u32[]{:S(2)}, u32[]{:S(2)}) collective-permute-start(bf16[96,1536]{1,0:T(8,128)(2,1)S(1)} %collective-permute-done.1), channel_id=1, source_target_pairs={{0,4},{4,8},{8,12},{12,16},{16,20},{20,24},{24,28},{28,0},{1,5},{5... | collective-permute-start | bytes 884744 | tf_op jit(solution)/shard_map/ppermute | solution.py:19
  63.7 5.3 %collective-permute-start.10 = (bf16[96,1536]{1,0:T(8,128)(2,1)S(1)}, bf16[96,1536]{1,0:T(8,128)(2,1)S(1)}, u32[]{:S(2)}, u32[]{:S(2)}) collective-permute-start(bf16[96,1536]{1,0:T(8,128)(2,1)S(1)} %collective-permute-done.1), channel_id=1, source_target_pairs={{0,28},{4,0},{8,4},{12,8},{16,12},{20,16},{24,20},{28,24},{1,29},{... | collective-permute-start | bytes 884744 | tf_op jit(solution)/shard_map/ppermute | solution.py:19
  70.9 4.6 %collective-permute-start.4 = (bf16[96,1536]{1,0:T(8,128)(2,1)S(1)}, bf16[96,1536]{1,0:T(8,128)(2,1)S(1)}, u32[]{:S(2)}, u32[]{:S(2)}) collective-permute-start(bf16[96,1536]{1,0:T(8,128)(2,1)S(1)} %collective-permute-done.2), channel_id=1, source_target_pairs={{0,28},{4,0},{8,4},{12,8},{16,12},{20,16},{24,20},{28,24},{1,29},{... | collective-permute-start | bytes 884744 | tf_op jit(solution)/shard_map/ppermute | solution.py:19
  76.9 2.5 %collective-permute-done.3 = bf16[96,1536]{1,0:T(8,128)(2,1)S(1)} collective-permute-done((bf16[96,1536]{1,0:T(8,128)(2,1)S(1)}, bf16[96,1536]{1,0:T(8,128)(2,1)S(1)}, u32[]{:S(2)}, u32[]{:S(2)}) %collective-permute-start.3) | collective-permute-done | bytes 294944 | tf_op jit(solution)/shard_map/ppermute | solution.py:19
  79.4 5.2 %collective-permute-start.5 = (bf16[96,1536]{1,0:T(8,128)(2,1)S(1)}, bf16[96,1536]{1,0:T(8,128)(2,1)S(1)}, u32[]{:S(2)}, u32[]{:S(2)}) collective-permute-start(bf16[96,1536]{1,0:T(8,128)(2,1)S(1)} %collective-permute-done.3), channel_id=1, source_target_pairs={{0,4},{4,8},{8,12},{12,16},{16,20},{20,24},{24,28},{28,0},{1,5},{5... | collective-permute-start | bytes 884744 | tf_op jit(solution)/shard_map/ppermute | solution.py:19
  87.7 4.4 %collective-permute-start.11 = (bf16[96,1536]{1,0:T(8,128)(2,1)S(1)}, bf16[96,1536]{1,0:T(8,128)(2,1)S(1)}, u32[]{:S(2)}, u32[]{:S(2)}) collective-permute-start(bf16[96,1536]{1,0:T(8,128)(2,1)S(1)} %collective-permute-done.9), channel_id=1, source_target_pairs={{0,4},{4,8},{8,12},{12,16},{16,20},{20,24},{24,28},{28,0},{1,5},{5... | collective-permute-start | bytes 884744 | tf_op jit(solution)/shard_map/ppermute | solution.py:19
  95.7 3.1 %collective-permute-start.7 = (bf16[48,1536]{1,0:T(8,128)(2,1)S(1)}, bf16[48,1536]{1,0:T(8,128)(2,1)S(1)}, u32[]{:S(2)}, u32[]{:S(2)}) collective-permute-start(bf16[48,1536]{1,0:T(8,128)(2,1)S(1)} %slice.43), channel_id=1, source_target_pairs={{0,4},{4,8},{8,12},{12,16},{16,20},{20,24},{24,28},{28,0},{1,5},{5... | collective-permute-start | bytes 442376 | tf_op jit(solution)/shard_map/ppermute | solution.py:19
  98.9 3.4 %collective-permute-start.8 = (bf16[48,1536]{1,0:T(8,128)(2,1)S(1)}, bf16[48,1536]{1,0:T(8,128)(2,1)S(1)}, u32[]{:S(2)}, u32[]{:S(2)}) collective-permute-start(bf16[48,1536]{1,0:T(8,128)(2,1)S(1)} %slice.44), channel_id=1, source_target_pairs={{0,28},{4,0},{8,4},{12,8},{16,12},{20,16},{24,20},{28,24},{1,29},{... | collective-permute-start | bytes 442376 | tf_op jit(solution)/shard_map/ppermute | solution.py:19
  102.3 2.7 %collective-permute-start.13 = (bf16[96,1536]{1,0:T(8,128)(2,1)S(1)}, bf16[96,1536]{1,0:T(8,128)(2,1)S(1)}, u32[]{:S(2)}, u32[]{:S(2)}) collective-permute-start(bf16[96,1536]{1,0:T(8,128)(2,1)S(1)} %collective-permute-done.11), channel_id=1, source_target_pairs={{0,4},{4,8},{8,12},{12,16},{16,20},{20,24},{24,28},{28,0},{1,5},{5... | collective-permute-start | bytes 884744 | tf_op jit(solution)/shard_map/ppermute | solution.py:19
  105.0 3.8 %collective-permute-start.14 = (bf16[96,1536]{1,0:T(8,128)(2,1)S(1)}, bf16[96,1536]{1,0:T(8,128)(2,1)S(1)}, u32[]{:S(2)}, u32[]{:S(2)}) collective-permute-start(bf16[96,1536]{1,0:T(8,128)(2,1)S(1)} %collective-permute-done.12), channel_id=1, source_target_pairs={{0,28},{4,0},{8,4},{12,8},{16,12},{20,16},{24,20},{28,24},{1,29},{... | collective-permute-start | bytes 884744 | tf_op jit(solution)/shard_map/ppermute | solution.py:19
  114.7 2.7 %collective-permute-start.15 = (bf16[48,1536]{1,0:T(8,128)(2,1)S(1)}, bf16[48,1536]{1,0:T(8,128)(2,1)S(1)}, u32[]{:S(2)}, u32[]{:S(2)}) collective-permute-start(bf16[48,1536]{1,0:T(8,128)(2,1)S(1)} %slice.45), channel_id=1, source_target_pairs={{0,4},{4,8},{8,12},{12,16},{16,20},{20,24},{24,28},{28,0},{1,5},{5... | collective-permute-start | bytes 442376 | tf_op jit(solution)/shard_map/ppermute | solution.py:19
  117.4 3.8 %collective-permute-start.16 = (bf16[48,1536]{1,0:T(8,128)(2,1)S(1)}, bf16[48,1536]{1,0:T(8,128)(2,1)S(1)}, u32[]{:S(2)}, u32[]{:S(2)}) collective-permute-start(bf16[48,1536]{1,0:T(8,128)(2,1)S(1)} %slice.46), channel_id=1, source_target_pairs={{0,28},{4,0},{8,4},{12,8},{16,12},{20,16},{24,20},{28,24},{1,29},{... | collective-permute-start | bytes 442376 | tf_op jit(solution)/shard_map/ppermute | solution.py:19
  125.3 7.1 %fusion.2 = f32[1536,768]{1,0:T(8,128)S(1)} fusion(bf16[1536,1536]{1,0:T(8,128)(2,1)} %bitcast.24, bf16[2,1536,768]{2,1,0:T(8,128)(2,1)} %bitcast.120, s32[]{:T(128)S(6)} %select_n.279), kind=kOutput, calls=%fused_computation.6 | convolution fusion | flops 3623878656 | bytes 11796484 | tf_op jit(solution)/shard_map/dot_general | solution.py:90
  134.7 11.4 %collective-permute-start.17 = (bf16[1536,384]{1,0:T(8,128)(2,1)S(1)}, bf16[1536,384]{1,0:T(8,128)(2,1)}, u32[]{:S(2)}, u32[]{:S(2)}) collective-permute-start(bf16[1536,384]{1,0:T(8,128)(2,1)S(1)} %slice.57), channel_id=1, source_target_pairs={{0,1},{1,0},{2,3},{3,2},{4,5},{5,4},{6,7},{7,6},{8,9},{9,8},{10,11... | collective-permute-start | bytes 3538952 | tf_op jit(solution)/shard_map/ppermute | solution.py:27
  146.0 5.9 %fusion = f32[1536,768]{1,0:T(8,128)S(1)} fusion(bf16[1536,1536]{1,0:T(8,128)(2,1)} %bitcast.24, bf16[2,1536,768]{2,1,0:T(8,128)(2,1)S(1)} %bitcast.121, s32[]{:T(128)S(6)} %select_n.285), kind=kOutput, calls=%fused_computation.4 | convolution fusion | flops 3623878656 | bytes 11796484 | tf_op jit(solution)/shard_map/dot_general | solution.py:90
  151.9 2.1 copy-done.1
  157.2 2.2 slice_add_fusion.1
  160.3 2.2 slice_add_fusion
  166.8 3.5 %collective-permute-start.22 = (bf16[384,384]{0,1:T(8,128)(2,1)}, bf16[384,384]{0,1:T(8,128)(2,1)}, u32[]{:S(2)}, u32[]{:S(2)}) collective-permute-start(bf16[384,384]{0,1:T(8,128)(2,1)} %bitcast.119), channel_id=1, source_target_pairs={{0,32},{32,64},{64,96},{96,0},{1,33},{33,65},{65,97},{97,1},{2,34}... | collective-permute-start | bytes 884744 | tf_op jit(solution)/shard_map/ppermute | solution.py:23
  172.2 2.2 collective-permute-start.23
  175.3 4.0 %collective-permute-start.24 = (bf16[384,384]{0,1:T(8,128)(2,1)}, bf16[384,384]{0,1:T(8,128)(2,1)}, u32[]{:S(2)}, u32[]{:S(2)}) collective-permute-start(bf16[384,384]{0,1:T(8,128)(2,1)} %bitcast.118), channel_id=1, source_target_pairs={{0,96},{32,0},{64,32},{96,64},{1,97},{33,1},{65,33},{97,65},{2,98}... | collective-permute-start | bytes 884744 | tf_op jit(solution)/shard_map/ppermute | solution.py:23
  183.0 4.0 %collective-permute-start.19 = (bf16[384,384]{0,1:T(8,128)(2,1)}, bf16[384,384]{0,1:T(8,128)(2,1)}, u32[]{:S(2)}, u32[]{:S(2)}) collective-permute-start(bf16[384,384]{0,1:T(8,128)(2,1)} %bitcast.33), channel_id=1, source_target_pairs={{0,64},{32,96},{64,0},{96,32},{1,65},{33,97},{65,1},{97,33},{2,66}... | collective-permute-start | bytes 884744 | tf_op jit(solution)/shard_map/ppermute | solution.py:23
  189.1 3.0 %collective-permute-start.20 = (bf16[384,384]{0,1:T(8,128)(2,1)}, bf16[384,384]{0,1:T(8,128)(2,1)}, u32[]{:S(2)}, u32[]{:S(2)}) collective-permute-start(bf16[384,384]{0,1:T(8,128)(2,1)} %bitcast.34), channel_id=1, source_target_pairs={{0,96},{32,0},{64,32},{96,64},{1,97},{33,1},{65,33},{97,65},{2,98}... | collective-permute-start | bytes 884744 | tf_op jit(solution)/shard_map/ppermute | solution.py:23
  194.0 7.7 %collective-permute-start.26 = (f32[1,384]{1,0:T(1,128)S(1)}, f32[1,384]{1,0:T(1,128)S(1)}, u32[]{:S(2)}, u32[]{:S(2)}) collective-permute-start(f32[1,384]{1,0:T(1,128)S(1)} %broadcast_in_dim.92), channel_id=1, source_target_pairs={{0,2},{2,0},{1,3},{3,1},{4,6},{6,4},{5,7},{7,5},{8,10},{10,8},{9,1... | collective-permute-start | bytes 4616 | tf_op jit(solution)/shard_map/ppermute | solution.py:27
  205.7 6.9 %all-to-all-start.1 = ((f32[16,1,384]{2,1,0:T(1,128)}), f32[16,1,384]{2,1,0:T(1,128)S(1)}, u32[]{:S(2)}, u32[]{:S(2)}) async-start(f32[16,1,384]{2,1,0:T(1,128)} %broadcast_in_dim.94), calls=%async_computation.1 | async-start | bytes 49152 | tf_op jit(solution)/shard_map/all_to_all | solution.py:108
  212.7 11.1 %all-to-all-done.1 = f32[16,1,384]{2,1,0:T(1,128)S(1)} async-done(((f32[16,1,384]{2,1,0:T(1,128)}), f32[16,1,384]{2,1,0:T(1,128)S(1)}, u32[]{:S(2)}, u32[]{:S(2)}) %all-to-all-start.1) | async-done | bytes 24608 | tf_op jit(solution)/shard_map/all_to_all | solution.py:108
  (107 shorter events, 56.9 us)
Async XLA Ops:
  12.7 26.9 %all-to-all-start = ((bf16[8,4,48,384]{3,1,2,0:T(4,128)(2,1)}), bf16[8,4,48,384]{3,1,2,0:T(4,128)(2,1)S(1)}, u32[]{:S(2)}, u32[]{:S(2)}) async-start(bf16[8,4,48,384]{3,1,2,0:T(4,128)(2,1)} %pad_maximum_fusion), calls=%async_computation | async-start | bytes 2359296 | tf_op jit(solution)/shard_map/all_to_all | solution.py:70
  23.0 102.3 %all-gather.2.cloned.1.call-start = ((), (), s32[]{:S(2)}) async-start(), calls=%async_computation.2 | async-start | bytes 5308416 | tf_op jit(solution)/shard_map/all_gather | solution.py:75
  43.0 16.9 %collective-permute-start = (bf16[96,1536]{1,0:T(8,128)(2,1)S(1)}, bf16[96,1536]{1,0:T(8,128)(2,1)S(1)}, u32[]{:S(2)}, u32[]{:S(2)}) collective-permute-start(bf16[96,1536]{1,0:T(8,128)(2,1)S(1)} %get-tuple-element.24), channel_id=1, source_target_pairs={{0,4},{4,8},{8,12},{12,16},{16,20},{20,24},{24,28},{28,0},{1,5},{5... | collective-permute-start | bytes 884744 | tf_op jit(solution)/shard_map/ppermute | solution.py:19
  45.0 15.0 %collective-permute-start.1 = (bf16[96,1536]{1,0:T(8,128)(2,1)S(1)}, bf16[96,1536]{1,0:T(8,128)(2,1)S(1)}, u32[]{:S(2)}, u32[]{:S(2)}) collective-permute-start(bf16[96,1536]{1,0:T(8,128)(2,1)S(1)} %get-tuple-element.23), channel_id=1, source_target_pairs={{0,2},{2,0},{1,3},{3,1},{4,6},{6,4},{5,7},{7,5},{8,10},{10,8},{9,1... | collective-permute-start | bytes 884744 | tf_op jit(solution)/shard_map/ppermute | solution.py:27
  52.3 18.5 %collective-permute-start.2 = (bf16[96,1536]{1,0:T(8,128)(2,1)S(1)}, bf16[96,1536]{1,0:T(8,128)(2,1)S(1)}, u32[]{:S(2)}, u32[]{:S(2)}) collective-permute-start(bf16[96,1536]{1,0:T(8,128)(2,1)S(1)} %get-tuple-element.24), channel_id=1, source_target_pairs={{0,28},{4,0},{8,4},{12,8},{16,12},{20,16},{24,20},{28,24},{1,29},{... | collective-permute-start | bytes 884744 | tf_op jit(solution)/shard_map/ppermute | solution.py:19
  60.0 27.7 %collective-permute-start.9 = (bf16[96,1536]{1,0:T(8,128)(2,1)S(1)}, bf16[96,1536]{1,0:T(8,128)(2,1)S(1)}, u32[]{:S(2)}, u32[]{:S(2)}) collective-permute-start(bf16[96,1536]{1,0:T(8,128)(2,1)S(1)} %collective-permute-done.1), channel_id=1, source_target_pairs={{0,4},{4,8},{8,12},{12,16},{16,20},{20,24},{24,28},{28,0},{1,5},{5... | collective-permute-start | bytes 884744 | tf_op jit(solution)/shard_map/ppermute | solution.py:19
  63.7 28.4 %collective-permute-start.10 = (bf16[96,1536]{1,0:T(8,128)(2,1)S(1)}, bf16[96,1536]{1,0:T(8,128)(2,1)S(1)}, u32[]{:S(2)}, u32[]{:S(2)}) collective-permute-start(bf16[96,1536]{1,0:T(8,128)(2,1)S(1)} %collective-permute-done.1), channel_id=1, source_target_pairs={{0,28},{4,0},{8,4},{12,8},{16,12},{20,16},{24,20},{28,24},{1,29},{... | collective-permute-start | bytes 884744 | tf_op jit(solution)/shard_map/ppermute | solution.py:19
  68.9 10.5 %collective-permute-start.3 = (bf16[96,1536]{1,0:T(8,128)(2,1)S(1)}, bf16[96,1536]{1,0:T(8,128)(2,1)S(1)}, u32[]{:S(2)}, u32[]{:S(2)}) collective-permute-start(bf16[96,1536]{1,0:T(8,128)(2,1)S(1)} %collective-permute-done), channel_id=1, source_target_pairs={{0,4},{4,8},{8,12},{12,16},{16,20},{20,24},{24,28},{28,0},{1,5},{5... | collective-permute-start | bytes 884744 | tf_op jit(solution)/shard_map/ppermute | solution.py:19
  70.9 14.9 %collective-permute-start.4 = (bf16[96,1536]{1,0:T(8,128)(2,1)S(1)}, bf16[96,1536]{1,0:T(8,128)(2,1)S(1)}, u32[]{:S(2)}, u32[]{:S(2)}) collective-permute-start(bf16[96,1536]{1,0:T(8,128)(2,1)S(1)} %collective-permute-done.2), channel_id=1, source_target_pairs={{0,28},{4,0},{8,4},{12,8},{16,12},{20,16},{24,20},{28,24},{1,29},{... | collective-permute-start | bytes 884744 | tf_op jit(solution)/shard_map/ppermute | solution.py:19
  79.4 16.3 %collective-permute-start.5 = (bf16[96,1536]{1,0:T(8,128)(2,1)S(1)}, bf16[96,1536]{1,0:T(8,128)(2,1)S(1)}, u32[]{:S(2)}, u32[]{:S(2)}) collective-permute-start(bf16[96,1536]{1,0:T(8,128)(2,1)S(1)} %collective-permute-done.3), channel_id=1, source_target_pairs={{0,4},{4,8},{8,12},{12,16},{16,20},{20,24},{24,28},{28,0},{1,5},{5... | collective-permute-start | bytes 884744 | tf_op jit(solution)/shard_map/ppermute | solution.py:19
  85.8 13.1 %collective-permute-start.6 = (bf16[96,1536]{1,0:T(8,128)(2,1)S(1)}, bf16[96,1536]{1,0:T(8,128)(2,1)S(1)}, u32[]{:S(2)}, u32[]{:S(2)}) collective-permute-start(bf16[96,1536]{1,0:T(8,128)(2,1)S(1)} %collective-permute-done.4), channel_id=1, source_target_pairs={{0,28},{4,0},{8,4},{12,8},{16,12},{20,16},{24,20},{28,24},{1,29},{... | collective-permute-start | bytes 884744 | tf_op jit(solution)/shard_map/ppermute | solution.py:19
  87.7 14.6 %collective-permute-start.11 = (bf16[96,1536]{1,0:T(8,128)(2,1)S(1)}, bf16[96,1536]{1,0:T(8,128)(2,1)S(1)}, u32[]{:S(2)}, u32[]{:S(2)}) collective-permute-start(bf16[96,1536]{1,0:T(8,128)(2,1)S(1)} %collective-permute-done.9), channel_id=1, source_target_pairs={{0,4},{4,8},{8,12},{12,16},{16,20},{20,24},{24,28},{28,0},{1,5},{5... | collective-permute-start | bytes 884744 | tf_op jit(solution)/shard_map/ppermute | solution.py:19
  92.1 12.9 %collective-permute-start.12 = (bf16[96,1536]{1,0:T(8,128)(2,1)S(1)}, bf16[96,1536]{1,0:T(8,128)(2,1)S(1)}, u32[]{:S(2)}, u32[]{:S(2)}) collective-permute-start(bf16[96,1536]{1,0:T(8,128)(2,1)S(1)} %collective-permute-done.10), channel_id=1, source_target_pairs={{0,28},{4,0},{8,4},{12,8},{16,12},{20,16},{24,20},{28,24},{1,29},{... | collective-permute-start | bytes 884744 | tf_op jit(solution)/shard_map/ppermute | solution.py:19
  95.7 14.6 %collective-permute-start.7 = (bf16[48,1536]{1,0:T(8,128)(2,1)S(1)}, bf16[48,1536]{1,0:T(8,128)(2,1)S(1)}, u32[]{:S(2)}, u32[]{:S(2)}) collective-permute-start(bf16[48,1536]{1,0:T(8,128)(2,1)S(1)} %slice.43), channel_id=1, source_target_pairs={{0,4},{4,8},{8,12},{12,16},{16,20},{20,24},{24,28},{28,0},{1,5},{5... | collective-permute-start | bytes 442376 | tf_op jit(solution)/shard_map/ppermute | solution.py:19
  98.9 11.4 %collective-permute-start.8 = (bf16[48,1536]{1,0:T(8,128)(2,1)S(1)}, bf16[48,1536]{1,0:T(8,128)(2,1)S(1)}, u32[]{:S(2)}, u32[]{:S(2)}) collective-permute-start(bf16[48,1536]{1,0:T(8,128)(2,1)S(1)} %slice.44), channel_id=1, source_target_pairs={{0,28},{4,0},{8,4},{12,8},{16,12},{20,16},{24,20},{28,24},{1,29},{... | collective-permute-start | bytes 442376 | tf_op jit(solution)/shard_map/ppermute | solution.py:19
  102.3 12.4 %collective-permute-start.13 = (bf16[96,1536]{1,0:T(8,128)(2,1)S(1)}, bf16[96,1536]{1,0:T(8,128)(2,1)S(1)}, u32[]{:S(2)}, u32[]{:S(2)}) collective-permute-start(bf16[96,1536]{1,0:T(8,128)(2,1)S(1)} %collective-permute-done.11), channel_id=1, source_target_pairs={{0,4},{4,8},{8,12},{12,16},{16,20},{20,24},{24,28},{28,0},{1,5},{5... | collective-permute-start | bytes 884744 | tf_op jit(solution)/shard_map/ppermute | solution.py:19
  105.0 12.4 %collective-permute-start.14 = (bf16[96,1536]{1,0:T(8,128)(2,1)S(1)}, bf16[96,1536]{1,0:T(8,128)(2,1)S(1)}, u32[]{:S(2)}, u32[]{:S(2)}) collective-permute-start(bf16[96,1536]{1,0:T(8,128)(2,1)S(1)} %collective-permute-done.12), channel_id=1, source_target_pairs={{0,28},{4,0},{8,4},{12,8},{16,12},{20,16},{24,20},{28,24},{1,29},{... | collective-permute-start | bytes 884744 | tf_op jit(solution)/shard_map/ppermute | solution.py:19
  114.7 8.0 %collective-permute-start.15 = (bf16[48,1536]{1,0:T(8,128)(2,1)S(1)}, bf16[48,1536]{1,0:T(8,128)(2,1)S(1)}, u32[]{:S(2)}, u32[]{:S(2)}) collective-permute-start(bf16[48,1536]{1,0:T(8,128)(2,1)S(1)} %slice.45), channel_id=1, source_target_pairs={{0,4},{4,8},{8,12},{12,16},{16,20},{20,24},{24,28},{28,0},{1,5},{5... | collective-permute-start | bytes 442376 | tf_op jit(solution)/shard_map/ppermute | solution.py:19
  117.4 7.1 %collective-permute-start.16 = (bf16[48,1536]{1,0:T(8,128)(2,1)S(1)}, bf16[48,1536]{1,0:T(8,128)(2,1)S(1)}, u32[]{:S(2)}, u32[]{:S(2)}) collective-permute-start(bf16[48,1536]{1,0:T(8,128)(2,1)S(1)} %slice.46), channel_id=1, source_target_pairs={{0,28},{4,0},{8,4},{12,8},{16,12},{20,16},{24,20},{28,24},{1,29},{... | collective-permute-start | bytes 442376 | tf_op jit(solution)/shard_map/ppermute | solution.py:19
  125.3 20.7 %copy-start.4 = (bf16[8,384,768]{2,1,0:T(8,128)(2,1)S(1)}, bf16[8,384,768]{2,1,0:T(8,128)(2,1)}, u32[]{:S(2)}) copy-start(bf16[8,384,768]{2,1,0:T(8,128)(2,1)} %all-gather.2.cloned.1.call-done) | copy-start | bytes 14155780
  134.7 22.5 %collective-permute-start.17 = (bf16[1536,384]{1,0:T(8,128)(2,1)S(1)}, bf16[1536,384]{1,0:T(8,128)(2,1)}, u32[]{:S(2)}, u32[]{:S(2)}) collective-permute-start(bf16[1536,384]{1,0:T(8,128)(2,1)S(1)} %slice.57), channel_id=1, source_target_pairs={{0,1},{1,0},{2,3},{3,2},{4,5},{5,4},{6,7},{7,6},{8,9},{9,8},{10,11... | collective-permute-start | bytes 3538952 | tf_op jit(solution)/shard_map/ppermute | solution.py:27
  155.2 5.1 %collective-permute-start.21 = (bf16[1536,384]{1,0:T(8,128)(2,1)}, bf16[1536,384]{1,0:T(8,128)(2,1)}, u32[]{:S(2)}, u32[]{:S(2)}) collective-permute-start(bf16[1536,384]{1,0:T(8,128)(2,1)} %slice.56), channel_id=1, source_target_pairs={{0,1},{1,0},{2,3},{3,2},{4,5},{5,4},{6,7},{7,6},{8,9},{9,8},{10,11... | collective-permute-start | bytes 3538952 | tf_op jit(solution)/shard_map/ppermute | solution.py:27
  166.8 22.2 %collective-permute-start.22 = (bf16[384,384]{0,1:T(8,128)(2,1)}, bf16[384,384]{0,1:T(8,128)(2,1)}, u32[]{:S(2)}, u32[]{:S(2)}) collective-permute-start(bf16[384,384]{0,1:T(8,128)(2,1)} %bitcast.119), channel_id=1, source_target_pairs={{0,32},{32,64},{64,96},{96,0},{1,33},{33,65},{65,97},{97,1},{2,34}... | collective-permute-start | bytes 884744 | tf_op jit(solution)/shard_map/ppermute | solution.py:23
  172.2 20.4 %collective-permute-start.23 = (bf16[384,384]{0,1:T(8,128)(2,1)}, bf16[384,384]{0,1:T(8,128)(2,1)}, u32[]{:S(2)}, u32[]{:S(2)}) collective-permute-start(bf16[384,384]{0,1:T(8,128)(2,1)} %bitcast.117), channel_id=1, source_target_pairs={{0,64},{32,96},{64,0},{96,32},{1,65},{33,97},{65,1},{97,33},{2,66}... | collective-permute-start | bytes 884744 | tf_op jit(solution)/shard_map/ppermute | solution.py:23
  175.3 17.3 %collective-permute-start.24 = (bf16[384,384]{0,1:T(8,128)(2,1)}, bf16[384,384]{0,1:T(8,128)(2,1)}, u32[]{:S(2)}, u32[]{:S(2)}) collective-permute-start(bf16[384,384]{0,1:T(8,128)(2,1)} %bitcast.118), channel_id=1, source_target_pairs={{0,96},{32,0},{64,32},{96,64},{1,97},{33,1},{65,33},{97,65},{2,98}... | collective-permute-start | bytes 884744 | tf_op jit(solution)/shard_map/ppermute | solution.py:23
  180.2 23.5 %collective-permute-start.18 = (bf16[384,384]{0,1:T(8,128)(2,1)}, bf16[384,384]{0,1:T(8,128)(2,1)}, u32[]{:S(2)}, u32[]{:S(2)}) collective-permute-start(bf16[384,384]{0,1:T(8,128)(2,1)} %bitcast.32), channel_id=1, source_target_pairs={{0,32},{32,64},{64,96},{96,0},{1,33},{33,65},{65,97},{97,1},{2,34}... | collective-permute-start | bytes 884744 | tf_op jit(solution)/shard_map/ppermute | solution.py:23
  183.0 29.7 %copy-start.3 = (s32[6,3]{0,1:T(4,128)S(1)}, s32[6,3]{0,1:T(4,128)}, u32[]{:S(2)}) copy-start(s32[6,3]{0,1:T(4,128)} %param.5) | copy-start | bytes 220
  183.0 20.7 %collective-permute-start.19 = (bf16[384,384]{0,1:T(8,128)(2,1)}, bf16[384,384]{0,1:T(8,128)(2,1)}, u32[]{:S(2)}, u32[]{:S(2)}) collective-permute-start(bf16[384,384]{0,1:T(8,128)(2,1)} %bitcast.33), channel_id=1, source_target_pairs={{0,64},{32,96},{64,0},{96,32},{1,65},{33,97},{65,1},{97,33},{2,66}... | collective-permute-start | bytes 884744 | tf_op jit(solution)/shard_map/ppermute | solution.py:23
  189.1 14.6 %collective-permute-start.20 = (bf16[384,384]{0,1:T(8,128)(2,1)}, bf16[384,384]{0,1:T(8,128)(2,1)}, u32[]{:S(2)}, u32[]{:S(2)}) collective-permute-start(bf16[384,384]{0,1:T(8,128)(2,1)} %bitcast.34), channel_id=1, source_target_pairs={{0,96},{32,0},{64,32},{96,64},{1,97},{33,1},{65,33},{97,65},{2,98}... | collective-permute-start | bytes 884744 | tf_op jit(solution)/shard_map/ppermute | solution.py:23
  194.0 11.1 %collective-permute-start.26 = (f32[1,384]{1,0:T(1,128)S(1)}, f32[1,384]{1,0:T(1,128)S(1)}, u32[]{:S(2)}, u32[]{:S(2)}) collective-permute-start(f32[1,384]{1,0:T(1,128)S(1)} %broadcast_in_dim.92), channel_id=1, source_target_pairs={{0,2},{2,0},{1,3},{3,1},{4,6},{6,4},{5,7},{7,5},{8,10},{10,8},{9,1... | collective-permute-start | bytes 4616 | tf_op jit(solution)/shard_map/ppermute | solution.py:27
  201.8 22.1 %collective-permute-start.25 = (bf16[384,384]{0,1:T(8,128)(2,1)S(1)}, bf16[384,384]{0,1:T(8,128)(2,1)S(1)}, u32[]{:S(2)}, u32[]{:S(2)}) collective-permute-start(bf16[384,384]{0,1:T(8,128)(2,1)S(1)} %get-tuple-element.12), channel_id=1, source_target_pairs={{0,2},{2,0},{1,3},{3,1},{4,6},{6,4},{5,7},{7,5},{8,10},{10,8},{9,1... | collective-permute-start | bytes 884744 | tf_op jit(solution)/shard_map/ppermute | solution.py:27
  205.7 18.1 %all-to-all-start.1 = ((f32[16,1,384]{2,1,0:T(1,128)}), f32[16,1,384]{2,1,0:T(1,128)S(1)}, u32[]{:S(2)}, u32[]{:S(2)}) async-start(f32[16,1,384]{2,1,0:T(1,128)} %broadcast_in_dim.94), calls=%async_computation.1 | async-start | bytes 49152 | tf_op jit(solution)/shard_map/all_to_all | solution.py:108
  (3 other events, 5.7 us)
Sparse Core Ops, SparseCore 0:
  42.4 69.7 all-gather.1

commit v3 on v2

v3 whole, which is shorter than its diff:
```python
import functools

import jax
import jax.numpy as jnp
from jax import lax
from jax.experimental import pallas as pl
from jax.experimental.pallas import tpu as pltpu
from jax.sharding import Mesh
from jax.sharding import PartitionSpec as P

Z_LO, X, Y, Z_HI, CORE = 4, 4, 8, 2, 2
ROWS, UNIT, TILE = 768, 384, 128
HALF = ROWS // 2
SUB = UNIT // (X * CORE)
WIDE = X * HALF
DEPTH = Y * Z_HI * CORE * SUB
VMEM = pl.BlockSpec(memory_space=pltpu.VMEM)
SMEM = pl.BlockSpec(memory_space=pltpu.SMEM)
HBM = pl.BlockSpec(memory_space=pltpu.HBM)
BF16, F32 = jnp.bfloat16, jnp.float32


def call(body, outs, ins, args, scratch=(), flops=0, vmem=48):
    shapes = [jax.ShapeDtypeStruct(shape, dtype) for shape, dtype in outs]
    moved = sum(a.size * a.dtype.itemsize for a in list(args) + shapes)
    return pl.pallas_call(
        body,
        out_shape=shapes,
        in_specs=ins,
        out_specs=[VMEM] * len(outs),
        scratch_shapes=scratch,
        compiler_params=pltpu.CompilerParams(vmem_limit_bytes=vmem << 20),
        cost_estimate=pl.CostEstimate(flops=flops, bytes_accessed=moved, transcendentals=0),
    )(*args)


def shift_y(shard, step):
    return lax.ppermute(shard, "y", [(i, (i + step) % Y) for i in range(Y)])


def shift_x(shard, step):
    return lax.ppermute(shard, "x", [(i, (i + step) % X) for i in range(X)])


def swap(shard, axis):
    return lax.ppermute(shard, axis, [(0, 1), (1, 0)])


def spread_over(array):
    return lax.all_to_all(array, ("x", "core"), split_axis=0, concat_axis=0, tiled=True)


def weigh(place, mask, values, both, far, weighted):
    zhi = place[0]
    for i in range(ROWS // TILE):
        for j in range(UNIT // TILE):
            at = (slice(i * TILE, (i + 1) * TILE), slice(j * TILE, (j + 1) * TILE))
            weighted[at] = values[at] * mask[i, j].astype(F32)
    for chunk in range(X * CORE):
        for part in range(CORE):
            start = part * UNIT + chunk * SUB
            both[chunk, 1 + part] = weighted[start : start + SUB].astype(BF16)
    near = weighted[pl.ds(pl.multiple_of(zhi * HALF, HALF), HALF)].T.astype(BF16)
    for chunk in range(X * CORE):
        both[chunk, 0] = near[chunk * SUB : (chunk + 1) * SUB]
    far[...] = weighted[pl.ds(pl.multiple_of((1 - zhi) * HALF, HALF), HALF)].T.astype(BF16)


def settle(place, both, near, right, stack):
    core = place[1]
    for x in range(X):
        for part in range(CORE):
            near[part * SUB : (part + 1) * SUB, x * HALF : (x + 1) * HALF] = both[x, part, 0]
    for own in range(2):
        source = core if own else 1 - core
        for x in range(X):
            for part in range(CORE):
                at = (x * CORE + part) * SUB
                stack[at : at + SUB] = both[x, source, 1 + part].astype(F32)
        right[0, own * UNIT : (own + 1) * UNIT] = stack[...].T.astype(BF16)


def multiply(order, place, *refs):
    shards, right = refs[: len(order)], refs[len(order)]
    outs, (a, b, sems) = refs[len(order) + 1 : -3], refs[-3:]
    y, zhi = place[0], place[1]
    copies = []
    for shard, (far, d, offset, length) in zip(shards, order):
        k_hi = 1 - zhi if far else zhi
        start = (lax.rem(y + Y - d, Y) * Z_HI + k_hi) * (CORE * SUB) + offset
        start = pl.multiple_of(start, SUB)
        copies.append(
            pltpu.make_async_copy(shard, a.at[pl.ds(start, length)], sems.at[len(copies)])
        )
    for own in range(2):
        for lo in range(Z_LO):
            origin = (zhi if own else 1 - zhi) * Z_LO + lo
            target = b.at[own, :, lo * UNIT : (lo + 1) * UNIT]
            copies.append(pltpu.make_async_copy(right.at[origin], target, sems.at[len(copies)]))
    for copy in copies:
        copy.start()
    for copy in copies[:-Z_LO]:
        copy.wait()
    step = 512
    for own in range(2):
        theirs, ours = outs[2 * own : 2 * own + 2]
        if own:
            for copy in copies[-Z_LO:]:
                copy.wait()

        @pl.loop(0, WIDE // step)
        def _(i):
            at = pl.ds(pl.multiple_of(i * step, step), step)
            product = jnp.dot(b[own], a[:, at], preferred_element_type=F32)
            theirs[:, at] = product[:UNIT].astype(BF16)
            ours[:, at] = product[UNIT:]


def add_core(place, ours, sent, first, second, third, own):
    x = place[0]
    pieces = [own, first, second, third]
    for step in range(X):
        at = pl.ds(pl.multiple_of(lax.rem(x + step, X) * HALF, HALF), HALF)
        total = ours[:, at] + sent[:, at].astype(F32)
        pieces[step][...] = total.astype(pieces[step].dtype)


def add_x(own, first, second, third, total, sums):
    all_x = own[...] + first[...].astype(F32) + (second[...].astype(F32) + third[...].astype(F32))
    turned = all_x.T
    total[...] = turned.astype(total.dtype)
    sums[...] = jnp.sum(turned * turned, axis=0, keepdims=True)


def finish(place, keep, mine, other, sums, flows):
    zhi = place[0]
    scale = jnp.sum(sums[:, 0], axis=0, keepdims=True) / (ROWS * Z_LO * X) + 1e-06
    for own in range(2):
        base = (zhi if own else 1 - zhi) * (HALF // TILE)
        source = mine if own else other
        for i in range(HALF // TILE):
            rows = pl.ds(pl.multiple_of((base + i) * TILE, TILE), TILE)
            for j in range(UNIT // TILE):
                cols = slice(j * TILE, (j + 1) * TILE)
                value = source[i * TILE : (i + 1) * TILE, cols].astype(F32)
                kept = keep[base + i, j].astype(F32)
                flows[rows, cols] = kept * (value * value) / scale[:, cols]


def in_order(first, second):
    return lax.optimization_barrier((first, second))


def rings(near, far):
    shards, order = [near], [(0, 0, 0, CORE * SUB)]
    ends = [[near, near], [far, far]]
    for d in range(1, Y // 2):
        for which in (0, 1):
            up, down = ends[which]
            up, down = shift_y(up, 1), shift_y(down, -1)
            if d == 1 and which == 0:
                up, far = in_order(up, far)
                ends[1] = [far, far]
                shards.append(far)
                order.append((1, 0, 0, CORE * SUB))
            ends[which] = [up, down]
            shards += [up, down]
            order += [(which, d, 0, CORE * SUB), (which, Y - d, 0, CORE * SUB)]
    for which in (0, 1):
        up, down = ends[which]
        shards += [shift_y(up[:SUB], 1), shift_y(down[SUB:], -1)]
        order += [(which, Y // 2, 0, SUB), (which, Y // 2, SUB, SUB)]
    return shards, tuple(order)


def local(values, tile_mask, keep_mask):
    x, y, core, zhi = (lax.axis_index(a) for a in ("x", "y", "core", "zhi"))
    place = jnp.stack([zhi, core])

    both, far = call(
        weigh,
        [((X * CORE, 3, SUB, UNIT), BF16), ((UNIT, HALF), BF16)],
        [SMEM, SMEM, VMEM],
        (place, tile_mask, values),
        [pltpu.VMEM((ROWS, UNIT), F32)],
    )
    far = swap(far, "zhi")
    both = spread_over(both)
    both, far = in_order(both, far)
    far = spread_over(far.reshape(X * CORE, SUB, HALF))
    near, right = call(
        settle,
        [((CORE * SUB, WIDE), BF16), ((1, CORE * UNIT, UNIT), BF16)],
        [SMEM, VMEM],
        (place, both.reshape(X, CORE, 3, SUB, UNIT)),
        [pltpu.VMEM((UNIT, UNIT), F32)],
    )
    right = lax.all_gather(right, ("zhi", "zlo"), axis=0, tiled=True)
    far = far.reshape(X, CORE * SUB, HALF).transpose(1, 0, 2).reshape(CORE * SUB, WIDE)
    shards, order = rings(near, far)

    theirs, ours, theirs_near, ours_near = call(
        functools.partial(multiply, order),
        [((UNIT, WIDE), BF16), ((UNIT, WIDE), F32)] * 2,
        [SMEM] + [HBM] * (len(shards) + 1),
        (jnp.stack([y, zhi]), *shards, right),
        [
            pltpu.VMEM((DEPTH, WIDE), BF16),
            pltpu.VMEM((2, CORE * UNIT, DEPTH), BF16),
            pltpu.SemaphoreType.DMA((len(shards) + 2 * Z_LO,)),
        ],
        flops=4 * CORE * UNIT * DEPTH * WIDE,
        vmem=60,
    )

    def over_x(ours, sent):
        pieces = call(
            add_core,
            [((UNIT, HALF), BF16)] * 3 + [((UNIT, HALF), F32)],
            [SMEM, VMEM, VMEM],
            (x[None], ours, sent),
        )
        return pieces[3], *(shift_x(pieces[step - 1], step) for step in range(1, X))

    def total(pieces, dtype):
        return call(add_x, [((HALF, UNIT), dtype), ((1, UNIT), F32)], [VMEM] * 4, pieces)

    pieces = over_x(ours, swap(theirs, "core"))
    pieces_near = over_x(ours_near, swap(theirs_near, "core"))
    other, sums = total(pieces, BF16)
    sums, other = swap(sums, "zhi"), swap(other, "zhi")
    mine, own_sums = total(pieces_near, F32)
    sums = jnp.broadcast_to(sums + own_sums, (Z_LO * X, 1, UNIT))
    sums = lax.all_to_all(sums, ("zlo", "x"), split_axis=0, concat_axis=0, tiled=True)
    return call(
        finish,
        [((ROWS, UNIT), F32)],
        [SMEM, SMEM, VMEM, VMEM, VMEM],
        (zhi[None], keep_mask, mine, other, sums),
    )[0]


def solution(mesh):
    physical = Mesh(
        mesh.devices.reshape(Z_LO, X, Y, Z_HI, CORE), ("zlo", "x", "y", "zhi", "core")
    )
    spec = P(("zlo", "x"), ("y", "zhi", "core"))
    return jax.shard_map(
        local, mesh=physical, in_specs=(spec, spec, spec), out_specs=spec, check_vma=False
    )
```

time: 235 us -> 202 us (0.86)
  the two profiles are of different devices: /device:TPU:1 before, /device:TPU:24 now
where the time goes in v3:
time: 202 us; the launch traced here: 200 us
  starting transfers between devices  122 us (60%)
  waiting for transfers between devices  38.6 us (19%)
  Pallas kernels  20.3 us (10%)
  between operations  14.1 us (7%)
  local copies, waits for them, and re-layouts  5.12 us (3%)
    ppermute x16, starting transfers between devices, shift_y(): return lax.ppermute(shard, 'y', [(i, (i + step) % Y) for i in range(Y)])  53.4 us
    ppermute x5, starting transfers between devices, swap(): return lax.ppermute(shard, axis, [(0, 1), (1, 0)])  30.9 us
    ppermute x6, starting transfers between devices, shift_x(): return lax.ppermute(shard, 'x', [(i, (i + step) % X) for i in range(X)])  20.4 us
    pallas_call x8, Pallas kernels, call(): pl.pallas_call(body, out_shape=shapes, in_specs=ins, out_specs=[VMEM] * l...  20.3 us
    ppermute x5, waiting for transfers between devices, swap(): return lax.ppermute(shard, axis, [(0, 1), (1, 0)])  17.4 us
    all_to_all x2, starting transfers between devices, spread_over(): lax.all_to_all(array, ('x', 'core'), split_axis=0, concat_axis=0, tiled=T...  8.76 us
    all_to_all x1, starting transfers between devices, local(): lax.all_to_all(sums, ('zlo', 'x'), split_axis=0, concat_axis=0, tiled=True)  8.18 us
    all_to_all x1, waiting for transfers between devices, local(): lax.all_to_all(sums, ('zlo', 'x'), split_axis=0, concat_axis=0, tiled=True)  7.97 us
  transfers between devices with their start and end apart: 31, of which 7 were waited for; matrix products, arithmetic and copies ran while one was open for 1% of the time, Pallas kernels for 1%

profile of v3, /device:TPU:24, one launch (start us, length us, event | category | flops | bytes accessed | tf_op | source)
XLA Modules:
  0.0 200.4 jit_solution(12515979131662337991)
XLA Ops:
  10.5 4.3 %all-to-all-start = ((bf16[8,3,48,384]{3,2,1,0:T(8,128)(2,1)}), bf16[8,3,48,384]{3,2,1,0:T(8,128)(2,1)S(1)}, u32[]{:S(2)}, u32[]{:S(2)}) async-start(bf16[8,3,48,384]{3,2,1,0:T(8,128)(2,1)} %get-tuple-element.29), calls=%async_computation | async-start | bytes 1769472 | tf_op jit(solution)/shard_map/all_to_all | solution.py:50
  14.8 10.9 %collective-permute-start = (bf16[384,384]{1,0:T(8,128)(2,1)S(1)}, bf16[384,384]{1,0:T(8,128)(2,1)}, u32[]{:S(2)}, u32[]{:S(2)}) collective-permute-start(bf16[384,384]{1,0:T(8,128)(2,1)S(1)} %get-tuple-element.30), channel_id=1, source_target_pairs={{0,2},{2,0},{1,3},{3,1},{4,6},{6,4},{5,7},{7,5},{8,10},{10,8},{9,1... | collective-permute-start | bytes 884744 | tf_op jit(solution)/shard_map/ppermute | solution.py:46
  25.8 7.9 %collective-permute-done = bf16[384,384]{1,0:T(8,128)(2,1)} collective-permute-done((bf16[384,384]{1,0:T(8,128)(2,1)S(1)}, bf16[384,384]{1,0:T(8,128)(2,1)}, u32[]{:S(2)}, u32[]{:S(2)}) %collective-permute-start) | collective-permute-done | bytes 294944 | tf_op jit(solution)/shard_map/ppermute | solution.py:46
  35.3 4.7 %collective-permute-start.1 = (bf16[96,1536]{1,0:T(8,128)(2,1)S(1)}, bf16[96,1536]{1,0:T(8,128)(2,1)S(1)}, u32[]{:S(2)}, u32[]{:S(2)}) collective-permute-start(bf16[96,1536]{1,0:T(8,128)(2,1)S(1)} %get-tuple-element.32.refs_0_), channel_id=1, source_target_pairs={{0,4},{4,8},{8,12},{12,16},{16,20},{20,24},{24,28},{28,0},{1,5},{5... | collective-permute-start | bytes 884744 | tf_op jit(solution)/shard_map/ppermute | solution.py:38
  40.0 4.5 %all-to-all-start.1 = ((bf16[8,48,384]{2,1,0:T(8,128)(2,1)}), bf16[8,48,384]{2,1,0:T(8,128)(2,1)S(1)}, u32[]{:S(2)}, u32[]{:S(2)}) async-start(bf16[8,48,384]{2,1,0:T(8,128)(2,1)} %bitcast.5), calls=%async_computation.1 | async-start | bytes 589824 | tf_op jit(solution)/shard_map/all_to_all | solution.py:50
  46.3 6.0 %all-to-all-done.1 = bf16[8,48,384]{2,1,0:T(8,128)(2,1)S(1)} async-done(((bf16[8,48,384]{2,1,0:T(8,128)(2,1)}), bf16[8,48,384]{2,1,0:T(8,128)(2,1)S(1)}, u32[]{:S(2)}, u32[]{:S(2)}) %all-to-all-start.1) | async-done | bytes 294944 | tf_op jit(solution)/shard_map/all_to_all | solution.py:50
  52.4 2.6 %collective-permute-start.3 = (bf16[96,1536]{1,0:T(8,128)(2,1)S(1)}, bf16[96,1536]{1,0:T(8,128)(2,1)S(1)}, u32[]{:S(2)}, u32[]{:S(2)}) collective-permute-start(bf16[96,1536]{1,0:T(8,128)(2,1)S(1)} %bitcast.13), channel_id=1, source_target_pairs={{0,4},{4,8},{8,12},{12,16},{16,20},{20,24},{24,28},{28,0},{1,5},{5... | collective-permute-start | bytes 884744 | tf_op jit(solution)/shard_map/ppermute | solution.py:38
  55.0 3.3 %collective-permute-start.4 = (bf16[96,1536]{1,0:T(8,128)(2,1)S(1)}, bf16[96,1536]{1,0:T(8,128)(2,1)S(1)}, u32[]{:S(2)}, u32[]{:S(2)}) collective-permute-start(bf16[96,1536]{1,0:T(8,128)(2,1)S(1)} %bitcast.14), channel_id=1, source_target_pairs={{0,28},{4,0},{8,4},{12,8},{16,12},{20,16},{24,20},{28,24},{1,29},{... | collective-permute-start | bytes 884744 | tf_op jit(solution)/shard_map/ppermute | solution.py:38
  58.2 3.8 %collective-permute-start.5 = (bf16[96,1536]{1,0:T(8,128)(2,1)S(1)}, bf16[96,1536]{1,0:T(8,128)(2,1)S(1)}, u32[]{:S(2)}, u32[]{:S(2)}) collective-permute-start(bf16[96,1536]{1,0:T(8,128)(2,1)S(1)} %collective-permute-done.1.refs_2_), channel_id=1, source_target_pairs={{0,4},{4,8},{8,12},{12,16},{16,20},{20,24},{24,28},{28,0},{1,5},{5... | collective-permute-start | bytes 884744 | tf_op jit(solution)/shard_map/ppermute | solution.py:38
  62.1 2.0 %collective-permute-start.6 = (bf16[96,1536]{1,0:T(8,128)(2,1)S(1)}, bf16[96,1536]{1,0:T(8,128)(2,1)S(1)}, u32[]{:S(2)}, u32[]{:S(2)}) collective-permute-start(bf16[96,1536]{1,0:T(8,128)(2,1)S(1)} %collective-permute-done.2.refs_3_), channel_id=1, source_target_pairs={{0,28},{4,0},{8,4},{12,8},{16,12},{20,16},{24,20},{28,24},{1,29},{... | collective-permute-start | bytes 884744 | tf_op jit(solution)/shard_map/ppermute | solution.py:38
  64.1 5.0 %collective-permute-start.7 = (bf16[96,1536]{1,0:T(8,128)(2,1)S(1)}, bf16[96,1536]{1,0:T(8,128)(2,1)S(1)}, u32[]{:S(2)}, u32[]{:S(2)}) collective-permute-start(bf16[96,1536]{1,0:T(8,128)(2,1)S(1)} %collective-permute-done.3.refs_4_), channel_id=1, source_target_pairs={{0,4},{4,8},{8,12},{12,16},{16,20},{20,24},{24,28},{28,0},{1,5},{5... | collective-permute-start | bytes 884744 | tf_op jit(solution)/shard_map/ppermute | solution.py:38
  69.2 1.9 collective-permute-start.8
  71.1 5.1 %collective-permute-start.9 = (bf16[96,1536]{1,0:T(8,128)(2,1)S(1)}, bf16[96,1536]{1,0:T(8,128)(2,1)S(1)}, u32[]{:S(2)}, u32[]{:S(2)}) collective-permute-start(bf16[96,1536]{1,0:T(8,128)(2,1)S(1)} %collective-permute-done.5.refs_6_), channel_id=1, source_target_pairs={{0,4},{4,8},{8,12},{12,16},{16,20},{20,24},{24,28},{28,0},{1,5},{5... | collective-permute-start | bytes 884744 | tf_op jit(solution)/shard_map/ppermute | solution.py:38
  76.3 1.9 collective-permute-start.10
  78.2 5.1 %collective-permute-start.11 = (bf16[96,1536]{1,0:T(8,128)(2,1)S(1)}, bf16[96,1536]{1,0:T(8,128)(2,1)S(1)}, u32[]{:S(2)}, u32[]{:S(2)}) collective-permute-start(bf16[96,1536]{1,0:T(8,128)(2,1)S(1)} %collective-permute-done.7.refs_8_), channel_id=1, source_target_pairs={{0,4},{4,8},{8,12},{12,16},{16,20},{20,24},{24,28},{28,0},{1,5},{5... | collective-permute-start | bytes 884744 | tf_op jit(solution)/shard_map/ppermute | solution.py:38
  85.4 5.1 %collective-permute-start.13 = (bf16[48,1536]{1,0:T(8,128)(2,1)S(1)}, bf16[48,1536]{1,0:T(8,128)(2,1)}, u32[]{:S(2)}, u32[]{:S(2)}) collective-permute-start(bf16[48,1536]{1,0:T(8,128)(2,1)S(1)} %slice.16), channel_id=1, source_target_pairs={{0,4},{4,8},{8,12},{12,16},{16,20},{20,24},{24,28},{28,0},{1,5},{5... | collective-permute-start | bytes 442376 | tf_op jit(solution)/shard_map/ppermute | solution.py:38
  90.5 1.9 collective-permute-start.14
  92.5 5.1 %collective-permute-start.15 = (bf16[48,1536]{1,0:T(8,128)(2,1)S(1)}, bf16[48,1536]{1,0:T(8,128)(2,1)S(1)}, u32[]{:S(2)}, u32[]{:S(2)}) collective-permute-start(bf16[48,1536]{1,0:T(8,128)(2,1)S(1)} %slice.18), channel_id=1, source_target_pairs={{0,4},{4,8},{8,12},{12,16},{16,20},{20,24},{24,28},{28,0},{1,5},{5... | collective-permute-start | bytes 442376 | tf_op jit(solution)/shard_map/ppermute | solution.py:38
  100.3 5.7 %collective-permute-done.16.refs_17_ = bf16[48,1536]{1,0:T(8,128)(2,1)S(1)} collective-permute-done((bf16[48,1536]{1,0:T(8,128)(2,1)S(1)}, bf16[48,1536]{1,0:T(8,128)(2,1)S(1)}, u32[]{:S(2)}, u32[]{:S(2)}) %collective-permute-start.16) | collective-permute-done | bytes 147488 | tf_op jit(solution)/shard_map/ppermute | solution.py:38
  106.6 14.0 %shard_map.39 = (bf16[384,1536]{1,0:T(8,128)(2,1)}, f32[384,1536]{1,0:T(8,128)}, bf16[384,1536]{1,0:T(8,128)(2,1)}, f32[384,1536]{1,0:T(8,128)}) custom-call(s32[2]{0:T(128)} %pad_add_fusion.place, bf16[96,1536]{1,0:T(8,128)(2,1)} %copy-done.3, bf16[96,1536]{1,0:T(8,128)(2,1)} %bitcast.15, bf16[96,1536]{1,0:T(8,128)(2,1)} %copy-done.10, ...), custom_call_target="tpu_custom_call" | custom-call | flops 7247757312 | bytes 16515080 | tf_op jit(solution)/shard_map/pallas_call | solution.py:26
  122.5 2.4 %collective-permute-start.17 = (bf16[384,1536]{1,0:T(8,128)(2,1)}, bf16[384,1536]{1,0:T(8,128)(2,1)S(1)}, u32[]{:S(2)}, u32[]{:S(2)}) collective-permute-start(bf16[384,1536]{1,0:T(8,128)(2,1)} %get-tuple-element.38), channel_id=1, source_target_pairs={{0,1},{1,0},{2,3},{3,2},{4,5},{5,4},{6,7},{7,6},{8,9},{9,8},{10,11... | collective-permute-start | bytes 3538952 | tf_op jit(solution)/shard_map/ppermute | solution.py:46
  127.5 2.9 %collective-permute-start.22 = (bf16[384,384]{1,0:T(8,128)(2,1)S(1)}, bf16[384,384]{1,0:T(8,128)(2,1)S(1)}, u32[]{:S(2)}, u32[]{:S(2)}) collective-permute-start(bf16[384,384]{1,0:T(8,128)(2,1)S(1)} %get-tuple-element.47), channel_id=1, source_target_pairs={{0,32},{32,64},{64,96},{96,0},{1,33},{33,65},{65,97},{97,1},{2,34}... | collective-permute-start | bytes 884744 | tf_op jit(solution)/shard_map/ppermute | solution.py:42
  130.4 4.6 %collective-permute-start.23 = (bf16[384,384]{1,0:T(8,128)(2,1)S(1)}, bf16[384,384]{1,0:T(8,128)(2,1)S(1)}, u32[]{:S(2)}, u32[]{:S(2)}) collective-permute-start(bf16[384,384]{1,0:T(8,128)(2,1)S(1)} %get-tuple-element.48), channel_id=1, source_target_pairs={{0,64},{32,96},{64,0},{96,32},{1,65},{33,97},{65,1},{97,33},{2,66}... | collective-permute-start | bytes 884744 | tf_op jit(solution)/shard_map/ppermute | solution.py:42
  135.0 3.4 %collective-permute-start.24 = (bf16[384,384]{1,0:T(8,128)(2,1)S(1)}, bf16[384,384]{1,0:T(8,128)(2,1)S(1)}, u32[]{:S(2)}, u32[]{:S(2)}) collective-permute-start(bf16[384,384]{1,0:T(8,128)(2,1)S(1)} %get-tuple-element.49), channel_id=1, source_target_pairs={{0,96},{32,0},{64,32},{96,64},{1,97},{33,1},{65,33},{97,65},{2,98}... | collective-permute-start | bytes 884744 | tf_op jit(solution)/shard_map/ppermute | solution.py:42
  138.6 2.5 %collective-permute-start.18 = (bf16[384,384]{1,0:T(8,128)(2,1)S(1)}, bf16[384,384]{1,0:T(8,128)(2,1)S(1)}, u32[]{:S(2)}, u32[]{:S(2)}) collective-permute-start(bf16[384,384]{1,0:T(8,128)(2,1)S(1)} %get-tuple-element.40), channel_id=1, source_target_pairs={{0,32},{32,64},{64,96},{96,0},{1,33},{33,65},{65,97},{97,1},{2,34}... | collective-permute-start | bytes 884744 | tf_op jit(solution)/shard_map/ppermute | solution.py:42
  141.1 2.8 %collective-permute-start.19 = (bf16[384,384]{1,0:T(8,128)(2,1)S(1)}, bf16[384,384]{1,0:T(8,128)(2,1)S(1)}, u32[]{:S(2)}, u32[]{:S(2)}) collective-permute-start(bf16[384,384]{1,0:T(8,128)(2,1)S(1)} %get-tuple-element.41), channel_id=1, source_target_pairs={{0,64},{32,96},{64,0},{96,32},{1,65},{33,97},{65,1},{97,33},{2,66}... | collective-permute-start | bytes 884744 | tf_op jit(solution)/shard_map/ppermute | solution.py:42
  143.9 4.3 %collective-permute-start.20 = (bf16[384,384]{1,0:T(8,128)(2,1)S(1)}, bf16[384,384]{1,0:T(8,128)(2,1)S(1)}, u32[]{:S(2)}, u32[]{:S(2)}) collective-permute-start(bf16[384,384]{1,0:T(8,128)(2,1)S(1)} %get-tuple-element.42), channel_id=1, source_target_pairs={{0,96},{32,0},{64,32},{96,64},{1,97},{33,1},{65,33},{97,65},{2,98}... | collective-permute-start | bytes 884744 | tf_op jit(solution)/shard_map/ppermute | solution.py:42
  150.0 13.7 %collective-permute-start.25 = (bf16[384,384]{1,0:T(8,128)(2,1)S(1)}, bf16[384,384]{1,0:T(8,128)(2,1)S(1)}, u32[]{:S(2)}, u32[]{:S(2)}) collective-permute-start(bf16[384,384]{1,0:T(8,128)(2,1)S(1)} %get-tuple-element.50), channel_id=1, source_target_pairs={{0,2},{2,0},{1,3},{3,1},{4,6},{6,4},{5,7},{7,5},{8,10},{10,8},{9,1... | collective-permute-start | bytes 884744 | tf_op jit(solution)/shard_map/ppermute | solution.py:46
  163.8 1.9 collective-permute-start.26
  166.0 8.9 %collective-permute-done.26 = f32[1,384]{1,0:T(1,128)S(1)} collective-permute-done((f32[1,384]{1,0:T(1,128)S(1)}, f32[1,384]{1,0:T(1,128)S(1)}, u32[]{:S(2)}, u32[]{:S(2)}) %collective-permute-start.26) | collective-permute-done | bytes 1568 | tf_op jit(solution)/shard_map/ppermute | solution.py:46
  175.5 8.2 %all-to-all-start.2 = ((f32[16,1,384]{2,1,0:T(1,128)}), f32[16,1,384]{2,1,0:T(1,128)S(1)}, u32[]{:S(2)}, u32[]{:S(2)}) async-start(f32[16,1,384]{2,1,0:T(1,128)} %broadcast_in_dim.12), calls=%async_computation.2 | async-start | bytes 49152 | tf_op jit(solution)/shard_map/all_to_all | solution.py:234
  183.8 8.0 %all-to-all-done.2.sums = f32[16,1,384]{2,1,0:T(1,128)S(1)} async-done(((f32[16,1,384]{2,1,0:T(1,128)}), f32[16,1,384]{2,1,0:T(1,128)S(1)}, u32[]{:S(2)}, u32[]{:S(2)}) %all-to-all-start.2) | async-done | bytes 24608 | tf_op jit(solution)/shard_map/all_to_all | solution.py:234
  (90 shorter events, 22.1 us)
Async XLA Ops:
  10.5 23.1 %all-to-all-start = ((bf16[8,3,48,384]{3,2,1,0:T(8,128)(2,1)}), bf16[8,3,48,384]{3,2,1,0:T(8,128)(2,1)S(1)}, u32[]{:S(2)}, u32[]{:S(2)}) async-start(bf16[8,3,48,384]{3,2,1,0:T(8,128)(2,1)} %get-tuple-element.29), calls=%async_computation | async-start | bytes 1769472 | tf_op jit(solution)/shard_map/all_to_all | solution.py:50
  14.8 91.2 %all-gather.2.cloned.1.call-start = ((), (), s32[]{:S(2)}) async-start(), calls=%async_computation.3 | async-start | bytes 5308416 | tf_op jit(solution)/shard_map/all_gather | solution.py:198
  14.8 18.8 %collective-permute-start = (bf16[384,384]{1,0:T(8,128)(2,1)S(1)}, bf16[384,384]{1,0:T(8,128)(2,1)}, u32[]{:S(2)}, u32[]{:S(2)}) collective-permute-start(bf16[384,384]{1,0:T(8,128)(2,1)S(1)} %get-tuple-element.30), channel_id=1, source_target_pairs={{0,2},{2,0},{1,3},{3,1},{4,6},{6,4},{5,7},{7,5},{8,10},{10,8},{9,1... | collective-permute-start | bytes 884744 | tf_op jit(solution)/shard_map/ppermute | solution.py:46
  35.2 55.3 %copy-start.3 = (bf16[96,1536]{1,0:T(8,128)(2,1)}, bf16[96,1536]{1,0:T(8,128)(2,1)S(1)}, u32[]{:S(2)}) copy-start(bf16[96,1536]{1,0:T(8,128)(2,1)S(1)} %get-tuple-element.32.refs_0_) | copy-start | bytes 884740
  35.3 17.1 %collective-permute-start.1 = (bf16[96,1536]{1,0:T(8,128)(2,1)S(1)}, bf16[96,1536]{1,0:T(8,128)(2,1)S(1)}, u32[]{:S(2)}, u32[]{:S(2)}) collective-permute-start(bf16[96,1536]{1,0:T(8,128)(2,1)S(1)} %get-tuple-element.32.refs_0_), channel_id=1, source_target_pairs={{0,4},{4,8},{8,12},{12,16},{16,20},{20,24},{24,28},{28,0},{1,5},{5... | collective-permute-start | bytes 884744 | tf_op jit(solution)/shard_map/ppermute | solution.py:38
  40.0 12.3 %all-to-all-start.1 = ((bf16[8,48,384]{2,1,0:T(8,128)(2,1)}), bf16[8,48,384]{2,1,0:T(8,128)(2,1)S(1)}, u32[]{:S(2)}, u32[]{:S(2)}) async-start(bf16[8,48,384]{2,1,0:T(8,128)(2,1)} %bitcast.5), calls=%async_computation.1 | async-start | bytes 589824 | tf_op jit(solution)/shard_map/all_to_all | solution.py:50
  44.4 17.6 %collective-permute-start.2 = (bf16[96,1536]{1,0:T(8,128)(2,1)S(1)}, bf16[96,1536]{1,0:T(8,128)(2,1)S(1)}, u32[]{:S(2)}, u32[]{:S(2)}) collective-permute-start(bf16[96,1536]{1,0:T(8,128)(2,1)S(1)} %get-tuple-element.32.refs_0_), channel_id=1, source_target_pairs={{0,28},{4,0},{8,4},{12,8},{16,12},{20,16},{24,20},{28,24},{1,29},{... | collective-permute-start | bytes 884744 | tf_op jit(solution)/shard_map/ppermute | solution.py:38
  52.4 11.7 %collective-permute-start.3 = (bf16[96,1536]{1,0:T(8,128)(2,1)S(1)}, bf16[96,1536]{1,0:T(8,128)(2,1)S(1)}, u32[]{:S(2)}, u32[]{:S(2)}) collective-permute-start(bf16[96,1536]{1,0:T(8,128)(2,1)S(1)} %bitcast.13), channel_id=1, source_target_pairs={{0,4},{4,8},{8,12},{12,16},{16,20},{20,24},{24,28},{28,0},{1,5},{5... | collective-permute-start | bytes 884744 | tf_op jit(solution)/shard_map/ppermute | solution.py:38
  55.0 14.2 %collective-permute-start.4 = (bf16[96,1536]{1,0:T(8,128)(2,1)S(1)}, bf16[96,1536]{1,0:T(8,128)(2,1)S(1)}, u32[]{:S(2)}, u32[]{:S(2)}) collective-permute-start(bf16[96,1536]{1,0:T(8,128)(2,1)S(1)} %bitcast.14), channel_id=1, source_target_pairs={{0,28},{4,0},{8,4},{12,8},{16,12},{20,16},{24,20},{28,24},{1,29},{... | collective-permute-start | bytes 884744 | tf_op jit(solution)/shard_map/ppermute | solution.py:38
  58.2 12.9 %collective-permute-start.5 = (bf16[96,1536]{1,0:T(8,128)(2,1)S(1)}, bf16[96,1536]{1,0:T(8,128)(2,1)S(1)}, u32[]{:S(2)}, u32[]{:S(2)}) collective-permute-start(bf16[96,1536]{1,0:T(8,128)(2,1)S(1)} %collective-permute-done.1.refs_2_), channel_id=1, source_target_pairs={{0,4},{4,8},{8,12},{12,16},{16,20},{20,24},{24,28},{28,0},{1,5},{5... | collective-permute-start | bytes 884744 | tf_op jit(solution)/shard_map/ppermute | solution.py:38
  62.1 14.2 %collective-permute-start.6 = (bf16[96,1536]{1,0:T(8,128)(2,1)S(1)}, bf16[96,1536]{1,0:T(8,128)(2,1)S(1)}, u32[]{:S(2)}, u32[]{:S(2)}) collective-permute-start(bf16[96,1536]{1,0:T(8,128)(2,1)S(1)} %collective-permute-done.2.refs_3_), channel_id=1, source_target_pairs={{0,28},{4,0},{8,4},{12,8},{16,12},{20,16},{24,20},{28,24},{1,29},{... | collective-permute-start | bytes 884744 | tf_op jit(solution)/shard_map/ppermute | solution.py:38
  64.1 14.1 %collective-permute-start.7 = (bf16[96,1536]{1,0:T(8,128)(2,1)S(1)}, bf16[96,1536]{1,0:T(8,128)(2,1)S(1)}, u32[]{:S(2)}, u32[]{:S(2)}) collective-permute-start(bf16[96,1536]{1,0:T(8,128)(2,1)S(1)} %collective-permute-done.3.refs_4_), channel_id=1, source_target_pairs={{0,4},{4,8},{8,12},{12,16},{16,20},{20,24},{24,28},{28,0},{1,5},{5... | collective-permute-start | bytes 884744 | tf_op jit(solution)/shard_map/ppermute | solution.py:38
  69.2 14.2 %collective-permute-start.8 = (bf16[96,1536]{1,0:T(8,128)(2,1)S(1)}, bf16[96,1536]{1,0:T(8,128)(2,1)S(1)}, u32[]{:S(2)}, u32[]{:S(2)}) collective-permute-start(bf16[96,1536]{1,0:T(8,128)(2,1)S(1)} %collective-permute-done.4.refs_5_), channel_id=1, source_target_pairs={{0,28},{4,0},{8,4},{12,8},{16,12},{20,16},{24,20},{28,24},{1,29},{... | collective-permute-start | bytes 884744 | tf_op jit(solution)/shard_map/ppermute | solution.py:38
  71.1 14.2 %collective-permute-start.9 = (bf16[96,1536]{1,0:T(8,128)(2,1)S(1)}, bf16[96,1536]{1,0:T(8,128)(2,1)S(1)}, u32[]{:S(2)}, u32[]{:S(2)}) collective-permute-start(bf16[96,1536]{1,0:T(8,128)(2,1)S(1)} %collective-permute-done.5.refs_6_), channel_id=1, source_target_pairs={{0,4},{4,8},{8,12},{12,16},{16,20},{20,24},{24,28},{28,0},{1,5},{5... | collective-permute-start | bytes 884744 | tf_op jit(solution)/shard_map/ppermute | solution.py:38
  76.3 14.2 %collective-permute-start.10 = (bf16[96,1536]{1,0:T(8,128)(2,1)S(1)}, bf16[96,1536]{1,0:T(8,128)(2,1)S(1)}, u32[]{:S(2)}, u32[]{:S(2)}) collective-permute-start(bf16[96,1536]{1,0:T(8,128)(2,1)S(1)} %collective-permute-done.6.refs_7_), channel_id=1, source_target_pairs={{0,28},{4,0},{8,4},{12,8},{16,12},{20,16},{24,20},{28,24},{1,29},{... | collective-permute-start | bytes 884744 | tf_op jit(solution)/shard_map/ppermute | solution.py:38
  78.2 14.3 %collective-permute-start.11 = (bf16[96,1536]{1,0:T(8,128)(2,1)S(1)}, bf16[96,1536]{1,0:T(8,128)(2,1)S(1)}, u32[]{:S(2)}, u32[]{:S(2)}) collective-permute-start(bf16[96,1536]{1,0:T(8,128)(2,1)S(1)} %collective-permute-done.7.refs_8_), channel_id=1, source_target_pairs={{0,4},{4,8},{8,12},{12,16},{16,20},{20,24},{24,28},{28,0},{1,5},{5... | collective-permute-start | bytes 884744 | tf_op jit(solution)/shard_map/ppermute | solution.py:38
  83.4 14.3 %collective-permute-start.12 = (bf16[96,1536]{1,0:T(8,128)(2,1)S(1)}, bf16[96,1536]{1,0:T(8,128)(2,1)S(1)}, u32[]{:S(2)}, u32[]{:S(2)}) collective-permute-start(bf16[96,1536]{1,0:T(8,128)(2,1)S(1)} %collective-permute-done.8.refs_9_), channel_id=1, source_target_pairs={{0,28},{4,0},{8,4},{12,8},{16,12},{20,16},{24,20},{28,24},{1,29},{... | collective-permute-start | bytes 884744 | tf_op jit(solution)/shard_map/ppermute | solution.py:38
  85.4 14.9 %collective-permute-start.13 = (bf16[48,1536]{1,0:T(8,128)(2,1)S(1)}, bf16[48,1536]{1,0:T(8,128)(2,1)}, u32[]{:S(2)}, u32[]{:S(2)}) collective-permute-start(bf16[48,1536]{1,0:T(8,128)(2,1)S(1)} %slice.16), channel_id=1, source_target_pairs={{0,4},{4,8},{8,12},{12,16},{16,20},{20,24},{24,28},{28,0},{1,5},{5... | collective-permute-start | bytes 442376 | tf_op jit(solution)/shard_map/ppermute | solution.py:38
  90.5 9.7 %collective-permute-start.14 = (bf16[48,1536]{1,0:T(8,128)(2,1)S(1)}, bf16[48,1536]{1,0:T(8,128)(2,1)}, u32[]{:S(2)}, u32[]{:S(2)}) collective-permute-start(bf16[48,1536]{1,0:T(8,128)(2,1)S(1)} %slice.17), channel_id=1, source_target_pairs={{0,28},{4,0},{8,4},{12,8},{16,12},{20,16},{24,20},{28,24},{1,29},{... | collective-permute-start | bytes 442376 | tf_op jit(solution)/shard_map/ppermute | solution.py:38
  92.5 7.8 %collective-permute-start.15 = (bf16[48,1536]{1,0:T(8,128)(2,1)S(1)}, bf16[48,1536]{1,0:T(8,128)(2,1)S(1)}, u32[]{:S(2)}, u32[]{:S(2)}) collective-permute-start(bf16[48,1536]{1,0:T(8,128)(2,1)S(1)} %slice.18), channel_id=1, source_target_pairs={{0,4},{4,8},{8,12},{12,16},{16,20},{20,24},{24,28},{28,0},{1,5},{5... | collective-permute-start | bytes 442376 | tf_op jit(solution)/shard_map/ppermute | solution.py:38
  97.7 8.2 %collective-permute-start.16 = (bf16[48,1536]{1,0:T(8,128)(2,1)S(1)}, bf16[48,1536]{1,0:T(8,128)(2,1)S(1)}, u32[]{:S(2)}, u32[]{:S(2)}) collective-permute-start(bf16[48,1536]{1,0:T(8,128)(2,1)S(1)} %slice.19), channel_id=1, source_target_pairs={{0,28},{4,0},{8,4},{12,8},{16,12},{20,16},{24,20},{28,24},{1,29},{... | collective-permute-start | bytes 442376 | tf_op jit(solution)/shard_map/ppermute | solution.py:38
  120.6 5.0 %collective-permute-start.21 = (bf16[384,1536]{1,0:T(8,128)(2,1)}, bf16[384,1536]{1,0:T(8,128)(2,1)S(1)}, u32[]{:S(2)}, u32[]{:S(2)}) collective-permute-start(bf16[384,1536]{1,0:T(8,128)(2,1)} %get-tuple-element.45), channel_id=1, source_target_pairs={{0,1},{1,0},{2,3},{3,2},{4,5},{5,4},{6,7},{7,6},{8,9},{9,8},{10,11... | collective-permute-start | bytes 3538952 | tf_op jit(solution)/shard_map/ppermute | solution.py:46
  122.5 15.8 %collective-permute-start.17 = (bf16[384,1536]{1,0:T(8,128)(2,1)}, bf16[384,1536]{1,0:T(8,128)(2,1)S(1)}, u32[]{:S(2)}, u32[]{:S(2)}) collective-permute-start(bf16[384,1536]{1,0:T(8,128)(2,1)} %get-tuple-element.38), channel_id=1, source_target_pairs={{0,1},{1,0},{2,3},{3,2},{4,5},{5,4},{6,7},{7,6},{8,9},{9,8},{10,11... | collective-permute-start | bytes 3538952 | tf_op jit(solution)/shard_map/ppermute | solution.py:46
  127.5 16.4 %collective-permute-start.22 = (bf16[384,384]{1,0:T(8,128)(2,1)S(1)}, bf16[384,384]{1,0:T(8,128)(2,1)S(1)}, u32[]{:S(2)}, u32[]{:S(2)}) collective-permute-start(bf16[384,384]{1,0:T(8,128)(2,1)S(1)} %get-tuple-element.47), channel_id=1, source_target_pairs={{0,32},{32,64},{64,96},{96,0},{1,33},{33,65},{65,97},{97,1},{2,34}... | collective-permute-start | bytes 884744 | tf_op jit(solution)/shard_map/ppermute | solution.py:42
  130.4 17.9 %collective-permute-start.23 = (bf16[384,384]{1,0:T(8,128)(2,1)S(1)}, bf16[384,384]{1,0:T(8,128)(2,1)S(1)}, u32[]{:S(2)}, u32[]{:S(2)}) collective-permute-start(bf16[384,384]{1,0:T(8,128)(2,1)S(1)} %get-tuple-element.48), channel_id=1, source_target_pairs={{0,64},{32,96},{64,0},{96,32},{1,65},{33,97},{65,1},{97,33},{2,66}... | collective-permute-start | bytes 884744 | tf_op jit(solution)/shard_map/ppermute | solution.py:42
  135.0 14.8 %collective-permute-start.24 = (bf16[384,384]{1,0:T(8,128)(2,1)S(1)}, bf16[384,384]{1,0:T(8,128)(2,1)S(1)}, u32[]{:S(2)}, u32[]{:S(2)}) collective-permute-start(bf16[384,384]{1,0:T(8,128)(2,1)S(1)} %get-tuple-element.49), channel_id=1, source_target_pairs={{0,96},{32,0},{64,32},{96,64},{1,97},{33,1},{65,33},{97,65},{2,98}... | collective-permute-start | bytes 884744 | tf_op jit(solution)/shard_map/ppermute | solution.py:42
  138.6 27.1 %collective-permute-start.18 = (bf16[384,384]{1,0:T(8,128)(2,1)S(1)}, bf16[384,384]{1,0:T(8,128)(2,1)S(1)}, u32[]{:S(2)}, u32[]{:S(2)}) collective-permute-start(bf16[384,384]{1,0:T(8,128)(2,1)S(1)} %get-tuple-element.40), channel_id=1, source_target_pairs={{0,32},{32,64},{64,96},{96,0},{1,33},{33,65},{65,97},{97,1},{2,34}... | collective-permute-start | bytes 884744 | tf_op jit(solution)/shard_map/ppermute | solution.py:42
  141.1 24.6 %collective-permute-start.19 = (bf16[384,384]{1,0:T(8,128)(2,1)S(1)}, bf16[384,384]{1,0:T(8,128)(2,1)S(1)}, u32[]{:S(2)}, u32[]{:S(2)}) collective-permute-start(bf16[384,384]{1,0:T(8,128)(2,1)S(1)} %get-tuple-element.41), channel_id=1, source_target_pairs={{0,64},{32,96},{64,0},{96,32},{1,65},{33,97},{65,1},{97,33},{2,66}... | collective-permute-start | bytes 884744 | tf_op jit(solution)/shard_map/ppermute | solution.py:42
  143.9 21.8 %collective-permute-start.20 = (bf16[384,384]{1,0:T(8,128)(2,1)S(1)}, bf16[384,384]{1,0:T(8,128)(2,1)S(1)}, u32[]{:S(2)}, u32[]{:S(2)}) collective-permute-start(bf16[384,384]{1,0:T(8,128)(2,1)S(1)} %get-tuple-element.42), channel_id=1, source_target_pairs={{0,96},{32,0},{64,32},{96,64},{1,97},{33,1},{65,33},{97,65},{2,98}... | collective-permute-start | bytes 884744 | tf_op jit(solution)/shard_map/ppermute | solution.py:42
  150.0 41.8 %collective-permute-start.25 = (bf16[384,384]{1,0:T(8,128)(2,1)S(1)}, bf16[384,384]{1,0:T(8,128)(2,1)S(1)}, u32[]{:S(2)}, u32[]{:S(2)}) collective-permute-start(bf16[384,384]{1,0:T(8,128)(2,1)S(1)} %get-tuple-element.50), channel_id=1, source_target_pairs={{0,2},{2,0},{1,3},{3,1},{4,6},{6,4},{5,7},{7,5},{8,10},{10,8},{9,1... | collective-permute-start | bytes 884744 | tf_op jit(solution)/shard_map/ppermute | solution.py:46
  163.8 11.1 %collective-permute-start.26 = (f32[1,384]{1,0:T(1,128)S(1)}, f32[1,384]{1,0:T(1,128)S(1)}, u32[]{:S(2)}, u32[]{:S(2)}) collective-permute-start(f32[1,384]{1,0:T(1,128)S(1)} %get-tuple-element.51), channel_id=1, source_target_pairs={{0,2},{2,0},{1,3},{3,1},{4,6},{6,4},{5,7},{7,5},{8,10},{10,8},{9,1... | collective-permute-start | bytes 4616 | tf_op jit(solution)/shard_map/ppermute | solution.py:46
  175.5 16.3 %all-to-all-start.2 = ((f32[16,1,384]{2,1,0:T(1,128)}), f32[16,1,384]{2,1,0:T(1,128)S(1)}, u32[]{:S(2)}, u32[]{:S(2)}) async-start(f32[16,1,384]{2,1,0:T(1,128)} %broadcast_in_dim.12), calls=%async_computation.2 | async-start | bytes 49152 | tf_op jit(solution)/shard_map/all_to_all | solution.py:234
  (19 other events, 419.2 us)
Sparse Core Ops, SparseCore 0:
  35.4 70.4 all-gather.1

commit v4 on v3

v4 whole, which is shorter than its diff:
```python
import functools

import jax
import jax.numpy as jnp
from jax import lax
from jax.experimental import pallas as pl
from jax.experimental.pallas import tpu as pltpu
from jax.sharding import Mesh
from jax.sharding import PartitionSpec as P

Z_LO, X, Y, Z_HI, CORE = 4, 4, 8, 2, 2
ROWS, UNIT, TILE = 768, 384, 128
HALF = ROWS // 2
SUB = UNIT // (X * CORE)
DEEP = Z_HI * CORE * SUB
DEPTH = Y * DEEP
PARTS = (256, 128)
VMEM = pl.BlockSpec(memory_space=pltpu.VMEM)
SMEM = pl.BlockSpec(memory_space=pltpu.SMEM)
HBM = pl.BlockSpec(memory_space=pltpu.HBM)
BF16, F32 = jnp.bfloat16, jnp.float32


def call(body, outs, ins, args, scratch=(), flops=0, vmem=48):
    shapes = [jax.ShapeDtypeStruct(shape, dtype) for shape, dtype in outs]
    moved = sum(a.size * a.dtype.itemsize for a in list(args) + shapes)
    return pl.pallas_call(
        body,
        out_shape=shapes,
        in_specs=ins,
        out_specs=[VMEM] * len(outs),
        scratch_shapes=scratch,
        compiler_params=pltpu.CompilerParams(vmem_limit_bytes=vmem << 20),
        cost_estimate=pl.CostEstimate(flops=flops, bytes_accessed=moved, transcendentals=0),
    )(*args)


def shift_y(shard, step):
    return lax.ppermute(shard, "y", [(i, (i + step) % Y) for i in range(Y)])


def shift_x(shard, step):
    return lax.ppermute(shard, "x", [(i, (i + step) % X) for i in range(X)])


def swap(shard, axis):
    return lax.ppermute(shard, axis, [(0, 1), (1, 0)])


def spread_over(array):
    return lax.all_to_all(array, ("x", "core"), split_axis=0, concat_axis=0, tiled=True)


def weigh(place, mask, values, right, near, far, weighted):
    zhi = place[0]
    for i in range(ROWS // TILE):
        for j in range(UNIT // TILE):
            at = (slice(i * TILE, (i + 1) * TILE), slice(j * TILE, (j + 1) * TILE))
            weighted[at] = values[at] * mask[i, j].astype(F32)
    for chunk in range(X * CORE):
        for part in range(CORE):
            start = part * UNIT + chunk * SUB
            right[chunk, part] = weighted[start : start + SUB].astype(BF16)
    near[...] = weighted[pl.ds(pl.multiple_of(zhi * HALF, HALF), HALF)].T.astype(BF16)
    far[...] = weighted[pl.ds(pl.multiple_of((1 - zhi) * HALF, HALF), HALF)].T.astype(BF16)


def settle_right(place, both, right, stack):
    core = place[1]
    for own in range(2):
        source = core if own else 1 - core
        for x in range(X):
            for part in range(CORE):
                at = (x * CORE + part) * SUB
                stack[at : at + SUB] = both[x, source, part].astype(F32)
        right[0, own * UNIT : (own + 1) * UNIT] = stack[...].T.astype(BF16)


def settle_left(place, both, *parts):
    zhi = place[0]
    for k_hi in range(Z_HI):
        source = 1 - zhi if k_hi else zhi
        for x in range(X):
            for core in range(CORE):
                rows = slice((k_hi * CORE + core) * SUB, (k_hi * CORE + core + 1) * SUB)
                start = 0
                for part, width in zip(parts, PARTS):
                    cols = slice(x * width, (x + 1) * width)
                    part[rows, cols] = both[x, core, source, :, start : start + width]
                    start += width


def multiply(order, place, *refs):
    shards, right = refs[: len(order)], refs[len(order)]
    theirs, ours, a, b, sems = refs[len(order) + 1 :]
    y = place[0]
    copies = []
    for shard, (d, offset, length) in zip(shards, order):
        start = pl.multiple_of(lax.rem(y + Y - d, Y) * DEEP + offset, DEEP // 2)
        copies.append(
            pltpu.make_async_copy(shard, a.at[pl.ds(start, length)], sems.at[len(copies)])
        )
    for hi in range(Z_HI):
        for lo in range(Z_LO):
            target = b.at[hi, :, lo * UNIT : (lo + 1) * UNIT]
            copies.append(
                pltpu.make_async_copy(right.at[hi * Z_LO + lo], target, sems.at[len(copies)])
            )
    for copy in copies:
        copy.start()
    for copy in copies[:-Z_LO]:
        copy.wait()
    step = 512
    for hi in range(Z_HI):
        if hi:
            for copy in copies[-Z_LO:]:
                copy.wait()

        @pl.loop(0, a.shape[1] // step)
        def _(i):
            at = pl.ds(pl.multiple_of(i * step, step), step)
            product = jnp.dot(b[hi], a[:, at], preferred_element_type=F32)
            theirs[hi * UNIT : (hi + 1) * UNIT, at] = product[:UNIT].astype(BF16)
            ours[hi * UNIT : (hi + 1) * UNIT, at] = product[UNIT:]


def add_core(place, ours, sent, first, second, third, own):
    x = place[0]
    width = own.shape[1]
    pieces = [own, first, second, third]
    for step in range(X):
        at = pl.ds(pl.multiple_of(lax.rem(x + step, X) * width, width), width)
        total = ours[:, at] + sent[:, at].astype(F32)
        pieces[step][...] = total.astype(pieces[step].dtype)


def add_x(place, own, first, second, third, mine, other, sums):
    zhi = place[0]
    for same in range(2):
        hi = zhi if same else 1 - zhi
        at = pl.ds(pl.multiple_of(hi * UNIT, UNIT), UNIT)
        all_x = own[at] + first[at].astype(F32) + (second[at].astype(F32) + third[at].astype(F32))
        turned = all_x.T
        if same:
            mine[...] = turned
        else:
            other[...] = turned.astype(BF16)
        sums[:, at] = jnp.sum(turned * turned, axis=0, keepdims=True)


def finish(place, keep, sums, *refs):
    zhi = place[0]
    parts, flows = refs[:-1], refs[-1]
    at = pl.ds(pl.multiple_of(zhi * UNIT, UNIT), UNIT)
    scale = jnp.sum(sums[:, 0, at], axis=0, keepdims=True) / (ROWS * Z_LO * X) + 1e-06
    for own in range(2):
        tile = (zhi if own else 1 - zhi) * (HALF // TILE)
        for part, width in zip(parts[:2] if own else parts[2:], PARTS):
            for i in range(width // TILE):
                rows = pl.ds(pl.multiple_of(tile * TILE, TILE), TILE)
                for j in range(UNIT // TILE):
                    cols = slice(j * TILE, (j + 1) * TILE)
                    value = part[i * TILE : (i + 1) * TILE, cols].astype(F32)
                    kept = keep[tile, j].astype(F32)
                    flows[rows, cols] = kept * (value * value) / scale[:, cols]
                tile += 1


def in_order(first, second):
    return lax.optimization_barrier((first, second))


def rings(first, second):
    shards, ends = [[first], [second]], [[first, first], [second, second]]
    order = [(0, 0, DEEP)]
    half = DEEP // 2
    arrived = {}
    for d in range(1, Y // 2 + 1):
        for which in range(2):
            if which == 0 and d >= 3:
                arrived[d - 2], ends[0] = in_order(arrived[d - 2], ends[0])
            up, down = ends[which]
            if d == Y // 2:
                up, down = up[:half], down[half:]
            ends[which] = [shift_y(up, 1), shift_y(down, -1)]
            if which == 0:
                shards[0] += ends[0]
            else:
                arrived[d] = ends[1]
        order += [(d, 0, DEEP), (Y - d, 0, DEEP)] if d < Y // 2 else [(d, 0, half), (d, half, half)]
    last = Y // 2
    arrived[last - 1], shards[0][-2:] = in_order(arrived[last - 1], shards[0][-2:])
    for d in range(1, last + 1):
        shards[1] += arrived[d]
    return shards, tuple(order)


def local(values, tile_mask, keep_mask):
    x, y, core, zhi = (lax.axis_index(a) for a in ("x", "y", "core", "zhi"))
    place = jnp.stack([zhi, core])

    right, near, far = call(
        weigh,
        [((X * CORE, CORE, SUB, UNIT), BF16), ((UNIT, HALF), BF16), ((UNIT, HALF), BF16)],
        [SMEM, SMEM, VMEM],
        (place, tile_mask, values),
        [pltpu.VMEM((ROWS, UNIT), F32)],
    )
    far = swap(far, "zhi")
    right = spread_over(right)
    right, far = in_order(right, far)
    left = jnp.stack([piece.reshape(X * CORE, SUB, HALF) for piece in (near, far)], 1)
    left = spread_over(left)
    right = call(
        settle_right,
        [((1, CORE * UNIT, UNIT), BF16)],
        [SMEM, VMEM],
        (place, right.reshape(X, CORE, CORE, SUB, UNIT)),
        [pltpu.VMEM((UNIT, UNIT), F32)],
    )[0]
    right = lax.all_gather(right, ("zhi", "zlo"), axis=0, tiled=True)
    starts = call(
        settle_left,
        [((DEEP, X * width), BF16) for width in PARTS],
        [SMEM, VMEM],
        (place, left.reshape(X, CORE, Z_HI, SUB, HALF)),
    )
    shards, order = rings(*starts)

    def part(shards, width, earlier=None):
        theirs, ours = call(
            functools.partial(multiply, order),
            [((Z_HI * UNIT, X * width), BF16), ((Z_HI * UNIT, X * width), F32)],
            [SMEM] + [HBM] * (len(shards) + 1),
            (y[None], *shards, right),
            [
                pltpu.VMEM((DEPTH, X * width), BF16),
                pltpu.VMEM((Z_HI, CORE * UNIT, DEPTH), BF16),
                pltpu.SemaphoreType.DMA((len(shards) + Z_HI * Z_LO,)),
            ],
            flops=4 * CORE * UNIT * DEPTH * X * width,
            vmem=60,
        )
        if earlier is not None:
            earlier, theirs = in_order(earlier, theirs)
        pieces = call(
            add_core,
            [((Z_HI * UNIT, width), BF16)] * 3 + [((Z_HI * UNIT, width), F32)],
            [SMEM, VMEM, VMEM],
            (x[None], ours, swap(theirs, "core")),
        )
        return pieces, earlier

    def over_x(pieces, width):
        mine, other, sums = call(
            add_x,
            [((width, UNIT), F32), ((width, UNIT), BF16), ((1, Z_HI * UNIT), F32)],
            [SMEM] + [VMEM] * 4,
            (zhi[None], pieces[3], *(shift_x(pieces[step - 1], step) for step in range(1, X))),
        )
        return mine, swap(other, "zhi"), sums

    first, _ = part(shards[0], PARTS[0])
    second, first = part(shards[1], PARTS[1], first)
    done = [over_x(first, PARTS[0]), over_x(second, PARTS[1])]
    mine, other, sums = zip(*done)
    sums = jnp.broadcast_to(sum(sums), (Z_LO * X * Z_HI, 1, Z_HI * UNIT))
    sums = lax.all_to_all(sums, ("zlo", "x", "zhi"), split_axis=0, concat_axis=0, tiled=True)
    return call(
        finish,
        [((ROWS, UNIT), F32)],
        [SMEM, SMEM] + [VMEM] * 5,
        (zhi[None], keep_mask, sums, *mine, *other),
    )[0]


def solution(mesh):
    physical = Mesh(
        mesh.devices.reshape(Z_LO, X, Y, Z_HI, CORE), ("zlo", "x", "y", "zhi", "core")
    )
    spec = P(("zlo", "x"), ("y", "zhi", "core"))
    return jax.shard_map(
        local, mesh=physical, in_specs=(spec, spec, spec), out_specs=spec, check_vma=False
    )
```

time: 202 us -> 228 us (1.13)
  the two profiles are of different devices: /device:TPU:24 before, /device:TPU:1 now
where the time goes in v4:
time: 228 us; the launch traced here: 224 us
  starting transfers between devices  126 us (55%)
  waiting for transfers between devices  39.3 us (17%)
  Pallas kernels  25.7 us (11%)
  blocking collectives  15.6 us (7%)
  between operations  14 us (6%)
  local copies, waits for them, and re-layouts  3.57 us (2%)
    ppermute x16, starting transfers between devices, shift_y(): return lax.ppermute(shard, 'y', [(i, (i + step) % Y) for i in range(Y)])  53.6 us
    ppermute x5, starting transfers between devices, swap(): return lax.ppermute(shard, axis, [(0, 1), (1, 0)])  34.5 us
    pallas_call x10, Pallas kernels, call(): pl.pallas_call(body, out_shape=shapes, in_specs=ins, out_specs=[VMEM] * l...  25.7 us
    ppermute x16, waiting for transfers between devices, shift_y(): return lax.ppermute(shard, 'y', [(i, (i + step) % Y) for i in range(Y)])  19.8 us
    ppermute x6, starting transfers between devices, shift_x(): return lax.ppermute(shard, 'x', [(i, (i + step) % X) for i in range(X)])  16.6 us
    all_to_all x1, blocking collectives, spread_over(): lax.all_to_all(array, ('x', 'core'), split_axis=0, concat_axis=0, tiled=T...  15.6 us
    ppermute x5, waiting for transfers between devices, swap(): return lax.ppermute(shard, axis, [(0, 1), (1, 0)])  12 us
    all_to_all x1, starting transfers between devices, local(): lax.all_to_all(sums, ('zlo', 'x', 'zhi'), split_axis=0, concat_axis=0, ti...  10.4 us
  transfers between devices with their start and end apart: 30, of which 12 were waited for; matrix products, arithmetic and copies ran while one was open for 0% of the time, Pallas kernels for 3%

profile of v4, /device:TPU:1, one launch (start us, length us, event | category | flops | bytes accessed | tf_op | source)
XLA Modules:
  0.0 223.9 jit_solution(8561169439335816910)
XLA Ops:
  10.4 10.3 %all-to-all-start = ((bf16[8,2,48,384]{3,2,1,0:T(8,128)(2,1)}), bf16[8,2,48,384]{3,2,1,0:T(8,128)(2,1)S(1)}, u32[]{:S(2)}, u32[]{:S(2)}) async-start(bf16[8,2,48,384]{3,2,1,0:T(8,128)(2,1)} %get-tuple-element.48), calls=%async_computation | async-start | bytes 1179648 | tf_op jit(solution)/shard_map/all_to_all | solution.py:51
  20.7 6.1 %collective-permute-start = (bf16[384,384]{1,0:T(8,128)(2,1)S(1)}, bf16[384,384]{1,0:T(8,128)(2,1)S(1)}, u32[]{:S(2)}, u32[]{:S(2)}) collective-permute-start(bf16[384,384]{1,0:T(8,128)(2,1)S(1)} %get-tuple-element.49), channel_id=1, source_target_pairs={{0,2},{2,0},{1,3},{3,1},{4,6},{6,4},{5,7},{7,5},{8,10},{10,8},{9,1... | collective-permute-start | bytes 884744 | tf_op jit(solution)/shard_map/ppermute | solution.py:47
  26.8 9.2 %collective-permute-done = bf16[384,384]{1,0:T(8,128)(2,1)S(1)} collective-permute-done((bf16[384,384]{1,0:T(8,128)(2,1)S(1)}, bf16[384,384]{1,0:T(8,128)(2,1)S(1)}, u32[]{:S(2)}, u32[]{:S(2)}) %collective-permute-start) | collective-permute-done | bytes 294944 | tf_op jit(solution)/shard_map/ppermute | solution.py:47
  37.7 15.6 %all_to_all.15 = bf16[8,2,48,384]{3,2,1,0:T(8,128)(2,1)S(1)} all-to-all(bf16[8,2,48,384]{3,2,1,0:T(8,128)(2,1)S(1)} %pad_maximum_fusion), channel_id=1, replica_groups=mesh['zlo'=4,'x'=4,'y'=8,'zhi'=2,'core'=2] {'x','core'}, dimensions={0} | all-to-all | bytes 1179648 | tf_op jit(solution)/shard_map/all_to_all | solution.py:51
  55.9 4.6 %collective-permute-start.2 = (bf16[192,1024]{1,0:T(8,128)(2,1)S(1)}, bf16[192,1024]{1,0:T(8,128)(2,1)S(1)}, u32[]{:S(2)}, u32[]{:S(2)}) collective-permute-start(bf16[192,1024]{1,0:T(8,128)(2,1)S(1)} %get-tuple-element.51.refs_0_), channel_id=1, source_target_pairs={{0,28},{4,0},{8,4},{12,8},{16,12},{20,16},{24,20},{28,24},{1,29},{... | collective-permute-start | bytes 1179656 | tf_op jit(solution)/shard_map/ppermute | solution.py:39
  60.5 6.6 %collective-permute-done.1.refs_1_ = bf16[192,1024]{1,0:T(8,128)(2,1)S(1)} collective-permute-done((bf16[192,1024]{1,0:T(8,128)(2,1)S(1)}, bf16[192,1024]{1,0:T(8,128)(2,1)S(1)}, u32[]{:S(2)}, u32[]{:S(2)}) %collective-permute-start.1) | collective-permute-done | bytes 393248 | tf_op jit(solution)/shard_map/ppermute | solution.py:39
  69.1 4.6 %collective-permute-start.4 = (bf16[192,1024]{1,0:T(8,128)(2,1)S(1)}, bf16[192,1024]{1,0:T(8,128)(2,1)S(1)}, u32[]{:S(2)}, u32[]{:S(2)}) collective-permute-start(bf16[192,1024]{1,0:T(8,128)(2,1)S(1)} %collective-permute-done.2.refs_2_), channel_id=1, source_target_pairs={{0,28},{4,0},{8,4},{12,8},{16,12},{20,16},{24,20},{28,24},{1,29},{... | collective-permute-start | bytes 1179656 | tf_op jit(solution)/shard_map/ppermute | solution.py:39
  75.6 4.6 %collective-permute-start.6 = (bf16[192,512]{1,0:T(8,128)(2,1)S(1)}, bf16[192,512]{1,0:T(8,128)(2,1)S(1)}, u32[]{:S(2)}, u32[]{:S(2)}) collective-permute-start(bf16[192,512]{1,0:T(8,128)(2,1)S(1)} %get-tuple-element.52.refs_0_), channel_id=1, source_target_pairs={{0,28},{4,0},{8,4},{12,8},{16,12},{20,16},{24,20},{28,24},{1,29},{... | collective-permute-start | bytes 589832 | tf_op jit(solution)/shard_map/ppermute | solution.py:39
  80.2 3.7 %collective-permute-done.5.refs_1_ = bf16[192,512]{1,0:T(8,128)(2,1)S(1)} collective-permute-done((bf16[192,512]{1,0:T(8,128)(2,1)S(1)}, bf16[192,512]{1,0:T(8,128)(2,1)S(1)}, u32[]{:S(2)}, u32[]{:S(2)}) %collective-permute-start.5) | collective-permute-done | bytes 196640 | tf_op jit(solution)/shard_map/ppermute | solution.py:39
  86.9 5.4 %collective-permute-start.8 = (bf16[192,1024]{1,0:T(8,128)(2,1)S(1)}, bf16[192,1024]{1,0:T(8,128)(2,1)S(1)}, u32[]{:S(2)}, u32[]{:S(2)}) collective-permute-start(bf16[192,1024]{1,0:T(8,128)(2,1)S(1)} %collective-permute-done.4.refs_4_), channel_id=1, source_target_pairs={{0,28},{4,0},{8,4},{12,8},{16,12},{20,16},{24,20},{28,24},{1,29},{... | collective-permute-start | bytes 1179656 | tf_op jit(solution)/shard_map/ppermute | solution.py:39
  92.3 1.9 collective-permute-start.9
  94.2 4.6 %collective-permute-start.11 = (bf16[192,512]{1,0:T(8,128)(2,1)S(1)}, bf16[192,512]{1,0:T(8,128)(2,1)}, u32[]{:S(2)}, u32[]{:S(2)}) collective-permute-start(bf16[192,512]{1,0:T(8,128)(2,1)S(1)} %collective-permute-done.6.refs_2_), channel_id=1, source_target_pairs={{0,28},{4,0},{8,4},{12,8},{16,12},{20,16},{24,20},{28,24},{1,29},{... | collective-permute-start | bytes 589832 | tf_op jit(solution)/shard_map/ppermute | solution.py:39
  98.8 3.7 %collective-permute-done.9.refs_3_ = bf16[192,512]{1,0:T(8,128)(2,1)} collective-permute-done((bf16[192,512]{1,0:T(8,128)(2,1)S(1)}, bf16[192,512]{1,0:T(8,128)(2,1)}, u32[]{:S(2)}, u32[]{:S(2)}) %collective-permute-start.9) | collective-permute-done | bytes 196640 | tf_op jit(solution)/shard_map/ppermute | solution.py:39
  104.4 4.6 %collective-permute-start.12 = (bf16[192,512]{1,0:T(8,128)(2,1)}, bf16[192,512]{1,0:T(8,128)(2,1)S(1)}, u32[]{:S(2)}, u32[]{:S(2)}) collective-permute-start(bf16[192,512]{1,0:T(8,128)(2,1)} %collective-permute-done.11.refs_4_), channel_id=1, source_target_pairs={{0,28},{4,0},{8,4},{12,8},{16,12},{20,16},{24,20},{28,24},{1,29},{... | collective-permute-start | bytes 589832 | tf_op jit(solution)/shard_map/ppermute | solution.py:39
  111.0 4.6 %collective-permute-start.14 = (bf16[96,1024]{1,0:T(8,128)(2,1)S(1)}, bf16[96,1024]{1,0:T(8,128)(2,1)}, u32[]{:S(2)}, u32[]{:S(2)}) collective-permute-start(bf16[96,1024]{1,0:T(8,128)(2,1)S(1)} %slice.13), channel_id=1, source_target_pairs={{0,28},{4,0},{8,4},{12,8},{16,12},{20,16},{24,20},{28,24},{1,29},{... | collective-permute-start | bytes 589832 | tf_op jit(solution)/shard_map/ppermute | solution.py:39
  118.3 10.3 %shard_map.40 = (bf16[768,1024]{1,0:T(8,128)(2,1)}, f32[768,1024]{1,0:T(8,128)}) custom-call(s32[1]{0:T(128)} %bitcast.2.place, bf16[192,1024]{1,0:T(8,128)(2,1)} %copy-done.2, bf16[192,1024]{1,0:T(8,128)(2,1)} %copy-done.10, bf16[192,1024]{1,0:T(8,128)(2,1)} %copy-done.11, bf16[192,1024]{1,0:T(8,128)(2,1)} %copy-done.12, bf16[192,1024]{1,0:T(8,128)(2,1)} %copy-done.13, ...), custom_call_target="tpu_custom_call" | custom-call | flops 4831838208 | bytes 12582916 | tf_op jit(solution)/shard_map/pallas_call | solution.py:27
  128.6 5.8 %collective-permute-start.15 = (bf16[768,1024]{1,0:T(8,128)(2,1)}, bf16[768,1024]{1,0:T(8,128)(2,1)S(1)}, u32[]{:S(2)}, u32[]{:S(2)}) collective-permute-start(bf16[768,1024]{1,0:T(8,128)(2,1)} %get-tuple-element.61), channel_id=1, source_target_pairs={{0,1},{1,0},{2,3},{3,2},{4,5},{5,4},{6,7},{7,6},{8,9},{9,8},{10,11... | collective-permute-start | bytes 4718600 | tf_op jit(solution)/shard_map/ppermute | solution.py:47
  136.4 5.4 %collective-permute-start.17 = (bf16[96,512]{1,0:T(8,128)(2,1)S(1)}, bf16[96,512]{1,0:T(8,128)(2,1)S(1)}, u32[]{:S(2)}, u32[]{:S(2)}) collective-permute-start(bf16[96,512]{1,0:T(8,128)(2,1)S(1)} %slice.17), channel_id=1, source_target_pairs={{0,28},{4,0},{8,4},{12,8},{16,12},{20,16},{24,20},{28,24},{1,29},{... | collective-permute-start | bytes 294920 | tf_op jit(solution)/shard_map/ppermute | solution.py:39
  144.7 6.4 %shard_map.42 = (bf16[768,512]{1,0:T(8,128)(2,1)}, f32[768,512]{1,0:T(8,128)}) custom-call(s32[1]{0:T(128)} %bitcast.2.place, bf16[192,512]{1,0:T(8,128)(2,1)} %copy-done.3, bf16[192,512]{1,0:T(8,128)(2,1)} %copy-done.14, bf16[192,512]{1,0:T(8,128)(2,1)} %copy-done.15, bf16[192,512]{1,0:T(8,128)(2,1)} %collective-permute-done.9.refs_3_, ...), custom_call_target="tpu_custom_call" | custom-call | flops 2415919104 | bytes 8650756 | tf_op jit(solution)/shard_map/pallas_call | solution.py:27
  151.2 2.5 %shard_map.41 = (bf16[768,256]{1,0:T(8,128)(2,1)S(1)}, bf16[768,256]{1,0:T(8,128)(2,1)S(1)}, bf16[768,256]{1,0:T(8,128)(2,1)S(1)}, f32[768,256]{1,0:T(8,128)S(1)}) custom-call(s32[1]{0:T(128)} %bitcast.1.place, f32[768,1024]{1,0:T(8,128)} %get-tuple-element.60.ours, bf16[768,1024]{1,0:T(8,128)(2,1)S(1)} %collective-permute-done.15.sent), custom_call_target="tpu_custom_call" | custom-call | bytes 6684676 | tf_op jit(solution)/shard_map/pallas_call | solution.py:27
  153.6 2.7 %collective-permute-start.21 = (bf16[768,512]{1,0:T(8,128)(2,1)S(1)}, bf16[768,512]{1,0:T(8,128)(2,1)S(1)}, u32[]{:S(2)}, u32[]{:S(2)}) collective-permute-start(bf16[768,512]{1,0:T(8,128)(2,1)S(1)} %copy-done.9), channel_id=1, source_target_pairs={{0,1},{1,0},{2,3},{3,2},{4,5},{5,4},{6,7},{7,6},{8,9},{9,8},{10,11... | collective-permute-start | bytes 2359304 | tf_op jit(solution)/shard_map/ppermute | solution.py:47
  156.3 2.2 collective-permute-start.18
  158.5 3.7 %collective-permute-start.19 = (bf16[768,256]{1,0:T(8,128)(2,1)S(1)}, bf16[768,256]{1,0:T(8,128)(2,1)S(1)}, u32[]{:S(2)}, u32[]{:S(2)}) collective-permute-start(bf16[768,256]{1,0:T(8,128)(2,1)S(1)} %get-tuple-element.75), channel_id=1, source_target_pairs={{0,64},{32,96},{64,0},{96,32},{1,65},{33,97},{65,1},{97,33},{2,66}... | collective-permute-start | bytes 1179656 | tf_op jit(solution)/shard_map/ppermute | solution.py:43
  162.2 2.6 %collective-permute-start.20 = (bf16[768,256]{1,0:T(8,128)(2,1)S(1)}, bf16[768,256]{1,0:T(8,128)(2,1)S(1)}, u32[]{:S(2)}, u32[]{:S(2)}) collective-permute-start(bf16[768,256]{1,0:T(8,128)(2,1)S(1)} %get-tuple-element.76), channel_id=1, source_target_pairs={{0,96},{32,0},{64,32},{96,64},{1,97},{33,1},{65,33},{97,65},{2,98}... | collective-permute-start | bytes 1179656 | tf_op jit(solution)/shard_map/ppermute | solution.py:43
  165.2 2.7 %collective-permute-start.22 = (bf16[768,128]{1,0:T(8,128)(2,1)S(1)}, bf16[768,128]{1,0:T(8,128)(2,1)S(1)}, u32[]{:S(2)}, u32[]{:S(2)}) collective-permute-start(bf16[768,128]{1,0:T(8,128)(2,1)S(1)} %get-tuple-element.81), channel_id=1, source_target_pairs={{0,32},{32,64},{64,96},{96,0},{1,33},{33,65},{65,97},{97,1},{2,34}... | collective-permute-start | bytes 589832 | tf_op jit(solution)/shard_map/ppermute | solution.py:43
  167.9 3.5 %collective-permute-start.23 = (bf16[768,128]{1,0:T(8,128)(2,1)S(1)}, bf16[768,128]{1,0:T(8,128)(2,1)S(1)}, u32[]{:S(2)}, u32[]{:S(2)}) collective-permute-start(bf16[768,128]{1,0:T(8,128)(2,1)S(1)} %get-tuple-element.82), channel_id=1, source_target_pairs={{0,64},{32,96},{64,0},{96,32},{1,65},{33,97},{65,1},{97,33},{2,66}... | collective-permute-start | bytes 589832 | tf_op jit(solution)/shard_map/ppermute | solution.py:43
  171.3 7.1 %collective-permute-done.18.first = bf16[768,256]{1,0:T(8,128)(2,1)S(1)} collective-permute-done((bf16[768,256]{1,0:T(8,128)(2,1)S(1)}, bf16[768,256]{1,0:T(8,128)(2,1)S(1)}, u32[]{:S(2)}, u32[]{:S(2)}) %collective-permute-start.18) | collective-permute-done | bytes 393248 | tf_op jit(solution)/shard_map/ppermute | solution.py:43
  178.4 2.0 collective-permute-start.24
  181.1 12.8 %collective-permute-start.25 = (bf16[256,384]{1,0:T(8,128)(2,1)S(1)}, bf16[256,384]{1,0:T(8,128)(2,1)S(1)}, u32[]{:S(2)}, u32[]{:S(2)}) collective-permute-start(bf16[256,384]{1,0:T(8,128)(2,1)S(1)} %get-tuple-element.87), channel_id=1, source_target_pairs={{0,2},{2,0},{1,3},{3,1},{4,6},{6,4},{5,7},{7,5},{8,10},{10,8},{9,1... | collective-permute-start | bytes 589832 | tf_op jit(solution)/shard_map/ppermute | solution.py:47
  194.9 10.4 %all-to-all-start.2 = ((f32[32,1,768]{2,1,0:T(1,128)}), f32[32,1,768]{2,1,0:T(1,128)S(1)}, u32[]{:S(2)}, u32[]{:S(2)}) async-start(f32[32,1,768]{2,1,0:T(1,128)} %broadcast_in_dim.19), calls=%async_computation.2 | async-start | bytes 196608 | tf_op jit(solution)/shard_map/all_to_all | solution.py:268
  205.3 7.0 %collective-permute-start.26 = (bf16[128,384]{1,0:T(8,128)(2,1)S(1)}, bf16[128,384]{1,0:T(8,128)(2,1)S(1)}, u32[]{:S(2)}, u32[]{:S(2)}) collective-permute-start(bf16[128,384]{1,0:T(8,128)(2,1)S(1)} %get-tuple-element.88), channel_id=1, source_target_pairs={{0,2},{2,0},{1,3},{3,1},{4,6},{6,4},{5,7},{7,5},{8,10},{10,8},{9,1... | collective-permute-start | bytes 294920 | tf_op jit(solution)/shard_map/ppermute | solution.py:47
  212.5 2.8 %collective-permute-done.26.refs_3_ = bf16[128,384]{1,0:T(8,128)(2,1)S(1)} collective-permute-done((bf16[128,384]{1,0:T(8,128)(2,1)S(1)}, bf16[128,384]{1,0:T(8,128)(2,1)S(1)}, u32[]{:S(2)}, u32[]{:S(2)}) %collective-permute-start.26) | collective-permute-done | bytes 98336 | tf_op jit(solution)/shard_map/ppermute | solution.py:47
  (86 shorter events, 29.9 us)
Async XLA Ops:
  10.4 25.6 %all-to-all-start = ((bf16[8,2,48,384]{3,2,1,0:T(8,128)(2,1)}), bf16[8,2,48,384]{3,2,1,0:T(8,128)(2,1)S(1)}, u32[]{:S(2)}, u32[]{:S(2)}) async-start(bf16[8,2,48,384]{3,2,1,0:T(8,128)(2,1)} %get-tuple-element.48), calls=%async_computation | async-start | bytes 1179648 | tf_op jit(solution)/shard_map/all_to_all | solution.py:51
  20.7 97.5 %all-gather.2.cloned.1.call-start = ((), (), s32[]{:S(2)}) async-start(), calls=%async_computation.3 | async-start | bytes 5308416 | tf_op jit(solution)/shard_map/all_gather | solution.py:221
  20.7 15.3 %collective-permute-start = (bf16[384,384]{1,0:T(8,128)(2,1)S(1)}, bf16[384,384]{1,0:T(8,128)(2,1)S(1)}, u32[]{:S(2)}, u32[]{:S(2)}) collective-permute-start(bf16[384,384]{1,0:T(8,128)(2,1)S(1)} %get-tuple-element.49), channel_id=1, source_target_pairs={{0,2},{2,0},{1,3},{3,1},{4,6},{6,4},{5,7},{7,5},{8,10},{10,8},{9,1... | collective-permute-start | bytes 884744 | tf_op jit(solution)/shard_map/ppermute | solution.py:47
  54.0 64.2 %copy-start.2 = (bf16[192,1024]{1,0:T(8,128)(2,1)}, bf16[192,1024]{1,0:T(8,128)(2,1)S(1)}, u32[]{:S(2)}) copy-start(bf16[192,1024]{1,0:T(8,128)(2,1)S(1)} %get-tuple-element.51.refs_0_) | copy-start | bytes 1179652
  54.0 74.6 %copy-start.3 = (bf16[192,512]{1,0:T(8,128)(2,1)}, bf16[192,512]{1,0:T(8,128)(2,1)S(1)}, u32[]{:S(2)}) copy-start(bf16[192,512]{1,0:T(8,128)(2,1)S(1)} %get-tuple-element.52.refs_0_) | copy-start | bytes 589828
  54.0 13.1 %collective-permute-start.1 = (bf16[192,1024]{1,0:T(8,128)(2,1)S(1)}, bf16[192,1024]{1,0:T(8,128)(2,1)S(1)}, u32[]{:S(2)}, u32[]{:S(2)}) collective-permute-start(bf16[192,1024]{1,0:T(8,128)(2,1)S(1)} %get-tuple-element.51.refs_0_), channel_id=1, source_target_pairs={{0,4},{4,8},{8,12},{12,16},{16,20},{20,24},{24,28},{28,0},{1,5},{5... | collective-permute-start | bytes 1179656 | tf_op jit(solution)/shard_map/ppermute | solution.py:39
  55.9 13.1 %collective-permute-start.2 = (bf16[192,1024]{1,0:T(8,128)(2,1)S(1)}, bf16[192,1024]{1,0:T(8,128)(2,1)S(1)}, u32[]{:S(2)}, u32[]{:S(2)}) collective-permute-start(bf16[192,1024]{1,0:T(8,128)(2,1)S(1)} %get-tuple-element.51.refs_0_), channel_id=1, source_target_pairs={{0,28},{4,0},{8,4},{12,8},{16,12},{20,16},{24,20},{28,24},{1,29},{... | collective-permute-start | bytes 1179656 | tf_op jit(solution)/shard_map/ppermute | solution.py:39
  67.1 17.8 %collective-permute-start.3 = (bf16[192,1024]{1,0:T(8,128)(2,1)S(1)}, bf16[192,1024]{1,0:T(8,128)(2,1)S(1)}, u32[]{:S(2)}, u32[]{:S(2)}) collective-permute-start(bf16[192,1024]{1,0:T(8,128)(2,1)S(1)} %collective-permute-done.1.refs_1_), channel_id=1, source_target_pairs={{0,4},{4,8},{8,12},{12,16},{16,20},{20,24},{24,28},{28,0},{1,5},{5... | collective-permute-start | bytes 1179656 | tf_op jit(solution)/shard_map/ppermute | solution.py:39
  69.1 15.9 %collective-permute-start.4 = (bf16[192,1024]{1,0:T(8,128)(2,1)S(1)}, bf16[192,1024]{1,0:T(8,128)(2,1)S(1)}, u32[]{:S(2)}, u32[]{:S(2)}) collective-permute-start(bf16[192,1024]{1,0:T(8,128)(2,1)S(1)} %collective-permute-done.2.refs_2_), channel_id=1, source_target_pairs={{0,28},{4,0},{8,4},{12,8},{16,12},{20,16},{24,20},{28,24},{1,29},{... | collective-permute-start | bytes 1179656 | tf_op jit(solution)/shard_map/ppermute | solution.py:39
  73.6 10.2 %collective-permute-start.5 = (bf16[192,512]{1,0:T(8,128)(2,1)S(1)}, bf16[192,512]{1,0:T(8,128)(2,1)S(1)}, u32[]{:S(2)}, u32[]{:S(2)}) collective-permute-start(bf16[192,512]{1,0:T(8,128)(2,1)S(1)} %get-tuple-element.52.refs_0_), channel_id=1, source_target_pairs={{0,4},{4,8},{8,12},{12,16},{16,20},{20,24},{24,28},{28,0},{1,5},{5... | collective-permute-start | bytes 589832 | tf_op jit(solution)/shard_map/ppermute | solution.py:39
  75.6 9.3 %collective-permute-start.6 = (bf16[192,512]{1,0:T(8,128)(2,1)S(1)}, bf16[192,512]{1,0:T(8,128)(2,1)S(1)}, u32[]{:S(2)}, u32[]{:S(2)}) collective-permute-start(bf16[192,512]{1,0:T(8,128)(2,1)S(1)} %get-tuple-element.52.refs_0_), channel_id=1, source_target_pairs={{0,28},{4,0},{8,4},{12,8},{16,12},{20,16},{24,20},{28,24},{1,29},{... | collective-permute-start | bytes 589832 | tf_op jit(solution)/shard_map/ppermute | solution.py:39
  84.9 24.1 %collective-permute-start.7 = (bf16[192,1024]{1,0:T(8,128)(2,1)S(1)}, bf16[192,1024]{1,0:T(8,128)(2,1)S(1)}, u32[]{:S(2)}, u32[]{:S(2)}) collective-permute-start(bf16[192,1024]{1,0:T(8,128)(2,1)S(1)} %collective-permute-done.3.refs_3_), channel_id=1, source_target_pairs={{0,4},{4,8},{8,12},{12,16},{16,20},{20,24},{24,28},{28,0},{1,5},{5... | collective-permute-start | bytes 1179656 | tf_op jit(solution)/shard_map/ppermute | solution.py:39
  86.9 22.2 %collective-permute-start.8 = (bf16[192,1024]{1,0:T(8,128)(2,1)S(1)}, bf16[192,1024]{1,0:T(8,128)(2,1)S(1)}, u32[]{:S(2)}, u32[]{:S(2)}) collective-permute-start(bf16[192,1024]{1,0:T(8,128)(2,1)S(1)} %collective-permute-done.4.refs_4_), channel_id=1, source_target_pairs={{0,28},{4,0},{8,4},{12,8},{16,12},{20,16},{24,20},{28,24},{1,29},{... | collective-permute-start | bytes 1179656 | tf_op jit(solution)/shard_map/ppermute | solution.py:39
  92.3 10.2 %collective-permute-start.9 = (bf16[192,512]{1,0:T(8,128)(2,1)S(1)}, bf16[192,512]{1,0:T(8,128)(2,1)}, u32[]{:S(2)}, u32[]{:S(2)}) collective-permute-start(bf16[192,512]{1,0:T(8,128)(2,1)S(1)} %collective-permute-done.5.refs_1_), channel_id=1, source_target_pairs={{0,4},{4,8},{8,12},{12,16},{16,20},{20,24},{24,28},{28,0},{1,5},{5... | collective-permute-start | bytes 589832 | tf_op jit(solution)/shard_map/ppermute | solution.py:39
  94.2 10.2 %collective-permute-start.11 = (bf16[192,512]{1,0:T(8,128)(2,1)S(1)}, bf16[192,512]{1,0:T(8,128)(2,1)}, u32[]{:S(2)}, u32[]{:S(2)}) collective-permute-start(bf16[192,512]{1,0:T(8,128)(2,1)S(1)} %collective-permute-done.6.refs_2_), channel_id=1, source_target_pairs={{0,28},{4,0},{8,4},{12,8},{16,12},{20,16},{24,20},{28,24},{1,29},{... | collective-permute-start | bytes 589832 | tf_op jit(solution)/shard_map/ppermute | solution.py:39
  102.5 13.1 %collective-permute-start.10 = (bf16[192,512]{1,0:T(8,128)(2,1)}, bf16[192,512]{1,0:T(8,128)(2,1)S(1)}, u32[]{:S(2)}, u32[]{:S(2)}) collective-permute-start(bf16[192,512]{1,0:T(8,128)(2,1)} %collective-permute-done.9.refs_3_), channel_id=1, source_target_pairs={{0,4},{4,8},{8,12},{12,16},{16,20},{20,24},{24,28},{28,0},{1,5},{5... | collective-permute-start | bytes 589832 | tf_op jit(solution)/shard_map/ppermute | solution.py:39
  104.4 11.2 %collective-permute-start.12 = (bf16[192,512]{1,0:T(8,128)(2,1)}, bf16[192,512]{1,0:T(8,128)(2,1)S(1)}, u32[]{:S(2)}, u32[]{:S(2)}) collective-permute-start(bf16[192,512]{1,0:T(8,128)(2,1)} %collective-permute-done.11.refs_4_), channel_id=1, source_target_pairs={{0,28},{4,0},{8,4},{12,8},{16,12},{20,16},{24,20},{28,24},{1,29},{... | collective-permute-start | bytes 589832 | tf_op jit(solution)/shard_map/ppermute | solution.py:39
  109.1 7.7 %collective-permute-start.13 = (bf16[96,1024]{1,0:T(8,128)(2,1)S(1)}, bf16[96,1024]{1,0:T(8,128)(2,1)}, u32[]{:S(2)}, u32[]{:S(2)}) collective-permute-start(bf16[96,1024]{1,0:T(8,128)(2,1)S(1)} %slice.12), channel_id=1, source_target_pairs={{0,4},{4,8},{8,12},{12,16},{16,20},{20,24},{24,28},{28,0},{1,5},{5... | collective-permute-start | bytes 589832 | tf_op jit(solution)/shard_map/ppermute | solution.py:39
  111.0 7.2 %collective-permute-start.14 = (bf16[96,1024]{1,0:T(8,128)(2,1)S(1)}, bf16[96,1024]{1,0:T(8,128)(2,1)}, u32[]{:S(2)}, u32[]{:S(2)}) collective-permute-start(bf16[96,1024]{1,0:T(8,128)(2,1)S(1)} %slice.13), channel_id=1, source_target_pairs={{0,28},{4,0},{8,4},{12,8},{16,12},{20,16},{24,20},{28,24},{1,29},{... | collective-permute-start | bytes 589832 | tf_op jit(solution)/shard_map/ppermute | solution.py:39
  128.6 22.5 %collective-permute-start.15 = (bf16[768,1024]{1,0:T(8,128)(2,1)}, bf16[768,1024]{1,0:T(8,128)(2,1)S(1)}, u32[]{:S(2)}, u32[]{:S(2)}) collective-permute-start(bf16[768,1024]{1,0:T(8,128)(2,1)} %get-tuple-element.61), channel_id=1, source_target_pairs={{0,1},{1,0},{2,3},{3,2},{4,5},{5,4},{6,7},{7,6},{8,9},{9,8},{10,11... | collective-permute-start | bytes 4718600 | tf_op jit(solution)/shard_map/ppermute | solution.py:47
  134.5 8.6 %collective-permute-start.16 = (bf16[96,512]{1,0:T(8,128)(2,1)S(1)}, bf16[96,512]{1,0:T(8,128)(2,1)S(1)}, u32[]{:S(2)}, u32[]{:S(2)}) collective-permute-start(bf16[96,512]{1,0:T(8,128)(2,1)S(1)} %slice.16), channel_id=1, source_target_pairs={{0,4},{4,8},{8,12},{12,16},{16,20},{20,24},{24,28},{28,0},{1,5},{5... | collective-permute-start | bytes 294920 | tf_op jit(solution)/shard_map/ppermute | solution.py:39
  136.4 7.6 %collective-permute-start.17 = (bf16[96,512]{1,0:T(8,128)(2,1)S(1)}, bf16[96,512]{1,0:T(8,128)(2,1)S(1)}, u32[]{:S(2)}, u32[]{:S(2)}) collective-permute-start(bf16[96,512]{1,0:T(8,128)(2,1)S(1)} %slice.17), channel_id=1, source_target_pairs={{0,28},{4,0},{8,4},{12,8},{16,12},{20,16},{24,20},{28,24},{1,29},{... | collective-permute-start | bytes 294920 | tf_op jit(solution)/shard_map/ppermute | solution.py:39
  153.6 11.2 %collective-permute-start.21 = (bf16[768,512]{1,0:T(8,128)(2,1)S(1)}, bf16[768,512]{1,0:T(8,128)(2,1)S(1)}, u32[]{:S(2)}, u32[]{:S(2)}) collective-permute-start(bf16[768,512]{1,0:T(8,128)(2,1)S(1)} %copy-done.9), channel_id=1, source_target_pairs={{0,1},{1,0},{2,3},{3,2},{4,5},{5,4},{6,7},{7,6},{8,9},{9,8},{10,11... | collective-permute-start | bytes 2359304 | tf_op jit(solution)/shard_map/ppermute | solution.py:47
  156.3 22.1 %collective-permute-start.18 = (bf16[768,256]{1,0:T(8,128)(2,1)S(1)}, bf16[768,256]{1,0:T(8,128)(2,1)S(1)}, u32[]{:S(2)}, u32[]{:S(2)}) collective-permute-start(bf16[768,256]{1,0:T(8,128)(2,1)S(1)} %get-tuple-element.74), channel_id=1, source_target_pairs={{0,32},{32,64},{64,96},{96,0},{1,33},{33,65},{65,97},{97,1},{2,34}... | collective-permute-start | bytes 1179656 | tf_op jit(solution)/shard_map/ppermute | solution.py:43
  158.5 21.9 %collective-permute-start.19 = (bf16[768,256]{1,0:T(8,128)(2,1)S(1)}, bf16[768,256]{1,0:T(8,128)(2,1)S(1)}, u32[]{:S(2)}, u32[]{:S(2)}) collective-permute-start(bf16[768,256]{1,0:T(8,128)(2,1)S(1)} %get-tuple-element.75), channel_id=1, source_target_pairs={{0,64},{32,96},{64,0},{96,32},{1,65},{33,97},{65,1},{97,33},{2,66}... | collective-permute-start | bytes 1179656 | tf_op jit(solution)/shard_map/ppermute | solution.py:43
  162.2 18.6 %collective-permute-start.20 = (bf16[768,256]{1,0:T(8,128)(2,1)S(1)}, bf16[768,256]{1,0:T(8,128)(2,1)S(1)}, u32[]{:S(2)}, u32[]{:S(2)}) collective-permute-start(bf16[768,256]{1,0:T(8,128)(2,1)S(1)} %get-tuple-element.76), channel_id=1, source_target_pairs={{0,96},{32,0},{64,32},{96,64},{1,97},{33,1},{65,33},{97,65},{2,98}... | collective-permute-start | bytes 1179656 | tf_op jit(solution)/shard_map/ppermute | solution.py:43
  165.2 28.8 %collective-permute-start.22 = (bf16[768,128]{1,0:T(8,128)(2,1)S(1)}, bf16[768,128]{1,0:T(8,128)(2,1)S(1)}, u32[]{:S(2)}, u32[]{:S(2)}) collective-permute-start(bf16[768,128]{1,0:T(8,128)(2,1)S(1)} %get-tuple-element.81), channel_id=1, source_target_pairs={{0,32},{32,64},{64,96},{96,0},{1,33},{33,65},{65,97},{97,1},{2,34}... | collective-permute-start | bytes 589832 | tf_op jit(solution)/shard_map/ppermute | solution.py:43
  167.9 26.1 %collective-permute-start.23 = (bf16[768,128]{1,0:T(8,128)(2,1)S(1)}, bf16[768,128]{1,0:T(8,128)(2,1)S(1)}, u32[]{:S(2)}, u32[]{:S(2)}) collective-permute-start(bf16[768,128]{1,0:T(8,128)(2,1)S(1)} %get-tuple-element.82), channel_id=1, source_target_pairs={{0,64},{32,96},{64,0},{96,32},{1,65},{33,97},{65,1},{97,33},{2,66}... | collective-permute-start | bytes 589832 | tf_op jit(solution)/shard_map/ppermute | solution.py:43
  178.4 15.6 %collective-permute-start.24 = (bf16[768,128]{1,0:T(8,128)(2,1)S(1)}, bf16[768,128]{1,0:T(8,128)(2,1)S(1)}, u32[]{:S(2)}, u32[]{:S(2)}) collective-permute-start(bf16[768,128]{1,0:T(8,128)(2,1)S(1)} %get-tuple-element.83), channel_id=1, source_target_pairs={{0,96},{32,0},{64,32},{96,64},{1,97},{33,1},{65,33},{97,65},{2,98}... | collective-permute-start | bytes 589832 | tf_op jit(solution)/shard_map/ppermute | solution.py:43
  181.1 31.3 %collective-permute-start.25 = (bf16[256,384]{1,0:T(8,128)(2,1)S(1)}, bf16[256,384]{1,0:T(8,128)(2,1)S(1)}, u32[]{:S(2)}, u32[]{:S(2)}) collective-permute-start(bf16[256,384]{1,0:T(8,128)(2,1)S(1)} %get-tuple-element.87), channel_id=1, source_target_pairs={{0,2},{2,0},{1,3},{3,1},{4,6},{6,4},{5,7},{7,5},{8,10},{10,8},{9,1... | collective-permute-start | bytes 589832 | tf_op jit(solution)/shard_map/ppermute | solution.py:47
  194.9 20.4 %all-to-all-start.2 = ((f32[32,1,768]{2,1,0:T(1,128)}), f32[32,1,768]{2,1,0:T(1,128)S(1)}, u32[]{:S(2)}, u32[]{:S(2)}) async-start(f32[32,1,768]{2,1,0:T(1,128)} %broadcast_in_dim.19), calls=%async_computation.2 | async-start | bytes 196608 | tf_op jit(solution)/shard_map/all_to_all | solution.py:268
  205.3 10.0 %collective-permute-start.26 = (bf16[128,384]{1,0:T(8,128)(2,1)S(1)}, bf16[128,384]{1,0:T(8,128)(2,1)S(1)}, u32[]{:S(2)}, u32[]{:S(2)}) collective-permute-start(bf16[128,384]{1,0:T(8,128)(2,1)S(1)} %get-tuple-element.88), channel_id=1, source_target_pairs={{0,2},{2,0},{1,3},{3,1},{4,6},{6,4},{5,7},{7,5},{8,10},{10,8},{9,1... | collective-permute-start | bytes 294920 | tf_op jit(solution)/shard_map/ppermute | solution.py:47
  (16 other events, 332.9 us)
Sparse Core Ops, SparseCore 0:
  37.8 68.9 all-gather.1

commit v5 on v3

--- a/solution.py
+++ b/solution.py
@@ -113,28 +113,34 @@
             at = pl.ds(pl.multiple_of(i * step, step), step)
             product = jnp.dot(b[own], a[:, at], preferred_element_type=F32)
             theirs[:, at] = product[:UNIT].astype(BF16)
-            ours[:, at] = product[UNIT:]
-
-
-def add_core(place, ours, sent, first, second, third, own):
-    x = place[0]
-    pieces = [own, first, second, third]
+            ours[:, at] = product[UNIT:].astype(BF16)
+
+
+def add_core(ours, sent, pieces):
+    for x in range(X):
+        at = slice(x * HALF, (x + 1) * HALF)
+        pieces[x] = (ours[:, at].astype(F32) + sent[:, at].astype(F32)).astype(BF16)
+
+
+def add_core_apart(place, ours, sent, *pieces):
     for step in range(X):
-        at = pl.ds(pl.multiple_of(lax.rem(x + step, X) * HALF, HALF), HALF)
-        total = ours[:, at] + sent[:, at].astype(F32)
-        pieces[step][...] = total.astype(pieces[step].dtype)
-
-
-def add_x(own, first, second, third, total, sums):
-    all_x = own[...] + first[...].astype(F32) + (second[...].astype(F32) + third[...].astype(F32))
-    turned = all_x.T
+        at = pl.ds(pl.multiple_of(lax.rem(place[0] + step, X) * HALF, HALF), HALF)
+        pieces[step][...] = (ours[:, at].astype(F32) + sent[:, at].astype(F32)).astype(BF16)
+
+
+def add_x(*refs):
+    pieces, total, sums = refs[:-2], refs[-2], refs[-1]
+    if len(pieces) == 1:
+        pieces = [pieces[0].at[x] for x in range(X)]
+    turned = sum(piece[...].astype(F32) for piece in pieces).T
     total[...] = turned.astype(total.dtype)
     sums[...] = jnp.sum(turned * turned, axis=0, keepdims=True)
 
 
 def finish(place, keep, mine, other, sums, flows):
     zhi = place[0]
-    scale = jnp.sum(sums[:, 0], axis=0, keepdims=True) / (ROWS * Z_LO * X) + 1e-06
+    at = pl.ds(pl.multiple_of(zhi * UNIT, UNIT), UNIT)
+    scale = jnp.sum(sums[:, 0, at], axis=0, keepdims=True) / (ROWS * Z_LO * X) + 1e-06
     for own in range(2):
         base = (zhi if own else 1 - zhi) * (HALF // TILE)
         source = mine if own else other
@@ -201,7 +207,7 @@
 
     theirs, ours, theirs_near, ours_near = call(
         functools.partial(multiply, order),
-        [((UNIT, WIDE), BF16), ((UNIT, WIDE), F32)] * 2,
+        [((UNIT, WIDE), BF16)] * 4,
         [SMEM] + [HBM] * (len(shards) + 1),
         (jnp.stack([y, zhi]), *shards, right),
         [
@@ -213,25 +219,30 @@
         vmem=60,
     )
 
-    def over_x(ours, sent):
-        pieces = call(
-            add_core,
-            [((UNIT, HALF), BF16)] * 3 + [((UNIT, HALF), F32)],
-            [SMEM, VMEM, VMEM],
-            (x[None], ours, sent),
+    def total(pieces, dtype):
+        return call(
+            add_x, [((HALF, UNIT), dtype), ((1, UNIT), F32)], [VMEM] * len(pieces), pieces
         )
-        return pieces[3], *(shift_x(pieces[step - 1], step) for step in range(1, X))
-
-    def total(pieces, dtype):
-        return call(add_x, [((HALF, UNIT), dtype), ((1, UNIT), F32)], [VMEM] * 4, pieces)
-
-    pieces = over_x(ours, swap(theirs, "core"))
-    pieces_near = over_x(ours_near, swap(theirs_near, "core"))
-    other, sums = total(pieces, BF16)
-    sums, other = swap(sums, "zhi"), swap(other, "zhi")
-    mine, own_sums = total(pieces_near, F32)
-    sums = jnp.broadcast_to(sums + own_sums, (Z_LO * X, 1, UNIT))
-    sums = lax.all_to_all(sums, ("zlo", "x"), split_axis=0, concat_axis=0, tiled=True)
+
+    pieces = call(
+        add_core, [((X, UNIT, HALF), BF16)], [VMEM, VMEM], (ours, swap(theirs, "core"))
+    )[0]
+    pieces = lax.all_to_all(pieces, "x", split_axis=0, concat_axis=0, tiled=True)
+    apart = call(
+        add_core_apart,
+        [((UNIT, HALF), BF16)] * X,
+        [SMEM, VMEM, VMEM],
+        (x[None], ours_near, swap(theirs_near, "core")),
+    )
+    apart = [apart[0]] + [shift_x(apart[step], step) for step in range(1, X)]
+    (other, sums), apart = in_order(total([pieces], BF16), apart)
+    other = swap(other, "zhi")
+    mine, own_sums = total(apart, F32)
+    sums = jnp.concatenate(
+        [jnp.where(zhi == 0, own_sums, sums), jnp.where(zhi == 0, sums, own_sums)], 1
+    )
+    sums = jnp.broadcast_to(sums, (Z_LO * X * Z_HI, 1, Z_HI * UNIT))
+    sums = lax.all_to_all(sums, ("zlo", "x", "zhi"), split_axis=0, concat_axis=0, tiled=True)
     return call(
         finish,
         [((ROWS, UNIT), F32)],

time: 202 us -> 205 us (1.015)
  the two profiles are of different devices: /device:TPU:24 before, /device:TPU:1 now
where the time goes in v5:
time: 205 us; the launch traced here: 202 us
  starting transfers between devices  110 us (54%)
  waiting for transfers between devices  50.4 us (25%)
  Pallas kernels  21.6 us (11%)
  between operations  14 us (7%)
  local copies, waits for them, and re-layouts  4.96 us (2%)
    ppermute x16, starting transfers between devices, shift_y(): return lax.ppermute(shard, 'y', [(i, (i + step) % Y) for i in range(Y)])  52.5 us
    ppermute x4, starting transfers between devices, swap(): return lax.ppermute(shard, axis, [(0, 1), (1, 0)])  21.9 us
    pallas_call x8, Pallas kernels, call(): pl.pallas_call(body, out_shape=shapes, in_specs=ins, out_specs=[VMEM] * l...  21.6 us
    all_to_all x2, starting transfers between devices, spread_over(): lax.all_to_all(array, ('x', 'core'), split_axis=0, concat_axis=0, tiled=T...  15.8 us
    all_to_all x1, waiting for transfers between devices, local(): lax.all_to_all(sums, ('zlo', 'x', 'zhi'), split_axis=0, concat_axis=0, ti...  14.6 us
    ppermute x3, waiting for transfers between devices, shift_x(): return lax.ppermute(shard, 'x', [(i, (i + step) % X) for i in range(X)])  12.4 us
    ppermute x3, starting transfers between devices, shift_x(): return lax.ppermute(shard, 'x', [(i, (i + step) % X) for i in range(X)])  10.9 us
    ppermute x4, waiting for transfers between devices, swap(): return lax.ppermute(shard, axis, [(0, 1), (1, 0)])  10.1 us
  transfers between devices with their start and end apart: 28, of which 10 were waited for; matrix products, arithmetic and copies ran while one was open for 1% of the time, Pallas kernels for 1%

profile of v5, /device:TPU:1, one launch (start us, length us, event | category | flops | bytes accessed | tf_op | source)
XLA Modules:
  0.0 201.7 jit_solution(2712955122694481329)
XLA Ops:
  10.5 10.3 %all-to-all-start = ((bf16[8,3,48,384]{3,2,1,0:T(8,128)(2,1)}), bf16[8,3,48,384]{3,2,1,0:T(8,128)(2,1)S(1)}, u32[]{:S(2)}, u32[]{:S(2)}) async-start(bf16[8,3,48,384]{3,2,1,0:T(8,128)(2,1)} %get-tuple-element.31), calls=%async_computation | async-start | bytes 1769472 | tf_op jit(solution)/shard_map/all_to_all | solution.py:50
  20.8 6.1 %collective-permute-start = (bf16[384,384]{1,0:T(8,128)(2,1)S(1)}, bf16[384,384]{1,0:T(8,128)(2,1)}, u32[]{:S(2)}, u32[]{:S(2)}) collective-permute-start(bf16[384,384]{1,0:T(8,128)(2,1)S(1)} %get-tuple-element.32), channel_id=1, source_target_pairs={{0,2},{2,0},{1,3},{3,1},{4,6},{6,4},{5,7},{7,5},{8,10},{10,8},{9,1... | collective-permute-start | bytes 884744 | tf_op jit(solution)/shard_map/ppermute | solution.py:46
  26.9 9.3 %collective-permute-done = bf16[384,384]{1,0:T(8,128)(2,1)} collective-permute-done((bf16[384,384]{1,0:T(8,128)(2,1)S(1)}, bf16[384,384]{1,0:T(8,128)(2,1)}, u32[]{:S(2)}, u32[]{:S(2)}) %collective-permute-start) | collective-permute-done | bytes 294944 | tf_op jit(solution)/shard_map/ppermute | solution.py:46
  37.9 1.9 collective-permute-start.1
  39.8 5.5 %all-to-all-start.1 = ((bf16[8,48,384]{2,1,0:T(8,128)(2,1)}), bf16[8,48,384]{2,1,0:T(8,128)(2,1)S(1)}, u32[]{:S(2)}, u32[]{:S(2)}) async-start(bf16[8,48,384]{2,1,0:T(8,128)(2,1)} %bitcast.4), calls=%async_computation.1 | async-start | bytes 589824 | tf_op jit(solution)/shard_map/all_to_all | solution.py:50
  45.3 4.8 %collective-permute-start.2 = (bf16[96,1536]{1,0:T(8,128)(2,1)S(1)}, bf16[96,1536]{1,0:T(8,128)(2,1)S(1)}, u32[]{:S(2)}, u32[]{:S(2)}) collective-permute-start(bf16[96,1536]{1,0:T(8,128)(2,1)S(1)} %get-tuple-element.34.refs_0_), channel_id=1, source_target_pairs={{0,28},{4,0},{8,4},{12,8},{16,12},{20,16},{24,20},{28,24},{1,29},{... | collective-permute-start | bytes 884744 | tf_op jit(solution)/shard_map/ppermute | solution.py:38
  50.2 2.0 all-to-all-done.1
  52.2 2.6 %collective-permute-start.3 = (bf16[96,1536]{1,0:T(8,128)(2,1)S(1)}, bf16[96,1536]{1,0:T(8,128)(2,1)S(1)}, u32[]{:S(2)}, u32[]{:S(2)}) collective-permute-start(bf16[96,1536]{1,0:T(8,128)(2,1)S(1)} %bitcast.13), channel_id=1, source_target_pairs={{0,4},{4,8},{8,12},{12,16},{16,20},{20,24},{24,28},{28,0},{1,5},{5... | collective-permute-start | bytes 884744 | tf_op jit(solution)/shard_map/ppermute | solution.py:38
  54.8 4.2 %collective-permute-start.4 = (bf16[96,1536]{1,0:T(8,128)(2,1)S(1)}, bf16[96,1536]{1,0:T(8,128)(2,1)S(1)}, u32[]{:S(2)}, u32[]{:S(2)}) collective-permute-start(bf16[96,1536]{1,0:T(8,128)(2,1)S(1)} %bitcast.14), channel_id=1, source_target_pairs={{0,28},{4,0},{8,4},{12,8},{16,12},{20,16},{24,20},{28,24},{1,29},{... | collective-permute-start | bytes 884744 | tf_op jit(solution)/shard_map/ppermute | solution.py:38
  59.0 1.9 collective-permute-start.5
  60.9 4.6 %collective-permute-start.6 = (bf16[96,1536]{1,0:T(8,128)(2,1)S(1)}, bf16[96,1536]{1,0:T(8,128)(2,1)S(1)}, u32[]{:S(2)}, u32[]{:S(2)}) collective-permute-start(bf16[96,1536]{1,0:T(8,128)(2,1)S(1)} %collective-permute-done.2.refs_3_), channel_id=1, source_target_pairs={{0,28},{4,0},{8,4},{12,8},{16,12},{20,16},{24,20},{28,24},{1,29},{... | collective-permute-start | bytes 884744 | tf_op jit(solution)/shard_map/ppermute | solution.py:38
  65.5 1.9 collective-permute-start.7
  67.5 4.6 %collective-permute-start.8 = (bf16[96,1536]{1,0:T(8,128)(2,1)S(1)}, bf16[96,1536]{1,0:T(8,128)(2,1)S(1)}, u32[]{:S(2)}, u32[]{:S(2)}) collective-permute-start(bf16[96,1536]{1,0:T(8,128)(2,1)S(1)} %collective-permute-done.4.refs_5_), channel_id=1, source_target_pairs={{0,28},{4,0},{8,4},{12,8},{16,12},{20,16},{24,20},{28,24},{1,29},{... | collective-permute-start | bytes 884744 | tf_op jit(solution)/shard_map/ppermute | solution.py:38
  74.0 4.6 %collective-permute-start.10 = (bf16[96,1536]{1,0:T(8,128)(2,1)S(1)}, bf16[96,1536]{1,0:T(8,128)(2,1)S(1)}, u32[]{:S(2)}, u32[]{:S(2)}) collective-permute-start(bf16[96,1536]{1,0:T(8,128)(2,1)S(1)} %collective-permute-done.6.refs_7_), channel_id=1, source_target_pairs={{0,28},{4,0},{8,4},{12,8},{16,12},{20,16},{24,20},{28,24},{1,29},{... | collective-permute-start | bytes 884744 | tf_op jit(solution)/shard_map/ppermute | solution.py:38
  80.6 4.6 %collective-permute-start.12 = (bf16[96,1536]{1,0:T(8,128)(2,1)S(1)}, bf16[96,1536]{1,0:T(8,128)(2,1)S(1)}, u32[]{:S(2)}, u32[]{:S(2)}) collective-permute-start(bf16[96,1536]{1,0:T(8,128)(2,1)S(1)} %collective-permute-done.8.refs_9_), channel_id=1, source_target_pairs={{0,28},{4,0},{8,4},{12,8},{16,12},{20,16},{24,20},{28,24},{1,29},{... | collective-permute-start | bytes 884744 | tf_op jit(solution)/shard_map/ppermute | solution.py:38
  85.2 1.9 collective-permute-start.13
  87.2 4.6 %collective-permute-start.14 = (bf16[48,1536]{1,0:T(8,128)(2,1)S(1)}, bf16[48,1536]{1,0:T(8,128)(2,1)}, u32[]{:S(2)}, u32[]{:S(2)}) collective-permute-start(bf16[48,1536]{1,0:T(8,128)(2,1)S(1)} %slice.17), channel_id=1, source_target_pairs={{0,28},{4,0},{8,4},{12,8},{16,12},{20,16},{24,20},{28,24},{1,29},{... | collective-permute-start | bytes 442376 | tf_op jit(solution)/shard_map/ppermute | solution.py:38
  91.8 1.9 collective-permute-start.15
  93.8 4.6 %collective-permute-start.16 = (bf16[48,1536]{1,0:T(8,128)(2,1)S(1)}, bf16[48,1536]{1,0:T(8,128)(2,1)S(1)}, u32[]{:S(2)}, u32[]{:S(2)}) collective-permute-start(bf16[48,1536]{1,0:T(8,128)(2,1)S(1)} %slice.19), channel_id=1, source_target_pairs={{0,28},{4,0},{8,4},{12,8},{16,12},{20,16},{24,20},{28,24},{1,29},{... | collective-permute-start | bytes 442376 | tf_op jit(solution)/shard_map/ppermute | solution.py:38
  100.5 6.5 %all-gather.2.cloned.1.call-done.refs_18_ = bf16[8,768,384]{2,1,0:T(8,128)(2,1)} async-done(((bf16[1,768,384]{2,1,0:T(8,128)(2,1)}), bf16[8,768,384]{2,1,0:T(8,128)(2,1)}) %all-gather.2.cloned.1.call-update) | async-done | bytes 4718608 | tf_op jit(solution)/shard_map/all_gather | solution.py:204
  107.1 13.5 %shard_map.39 = (bf16[384,1536]{1,0:T(8,128)(2,1)}, bf16[384,1536]{1,0:T(8,128)(2,1)}, bf16[384,1536]{1,0:T(8,128)(2,1)}, bf16[384,1536]{1,0:T(8,128)(2,1)}) custom-call(s32[2]{0:T(128)} %pad_add_fusion.place, bf16[96,1536]{1,0:T(8,128)(2,1)} %copy-done.5, bf16[96,1536]{1,0:T(8,128)(2,1)} %bitcast.15, bf16[96,1536]{1,0:T(8,128)(2,1)} %copy-done.12, ...), custom_call_target="tpu_custom_call" | custom-call | flops 7247757312 | bytes 14155784 | tf_op jit(solution)/shard_map/pallas_call | solution.py:26
  120.6 2.6 %collective-permute-start.17 = (bf16[384,1536]{1,0:T(8,128)(2,1)}, bf16[384,1536]{1,0:T(8,128)(2,1)S(1)}, u32[]{:S(2)}, u32[]{:S(2)}) collective-permute-start(bf16[384,1536]{1,0:T(8,128)(2,1)} %get-tuple-element.40), channel_id=1, source_target_pairs={{0,1},{1,0},{2,3},{3,2},{4,5},{5,4},{6,7},{7,6},{8,9},{9,8},{10,11... | collective-permute-start | bytes 3538952 | tf_op jit(solution)/shard_map/ppermute | solution.py:46
  128.4 4.1 %all-to-all-start.2 = ((bf16[4,384,384]{2,1,0:T(8,128)(2,1)}), bf16[4,384,384]{2,1,0:T(8,128)(2,1)S(1)}, u32[]{:S(2)}, u32[]{:S(2)}) async-start(bf16[4,384,384]{2,1,0:T(8,128)(2,1)} %shard_map.40), calls=%async_computation.2 | async-start | bytes 2359296 | tf_op jit(solution)/shard_map/all_to_all | solution.py:230
  134.3 3.5 %collective-permute-start.19 = (bf16[384,384]{1,0:T(8,128)(2,1)}, bf16[384,384]{1,0:T(8,128)(2,1)S(1)}, u32[]{:S(2)}, u32[]{:S(2)}) collective-permute-start(bf16[384,384]{1,0:T(8,128)(2,1)} %get-tuple-element.46), channel_id=1, source_target_pairs={{0,32},{32,64},{64,96},{96,0},{1,33},{33,65},{65,97},{97,1},{2,34}... | collective-permute-start | bytes 884744 | tf_op jit(solution)/shard_map/ppermute | solution.py:42
  137.8 4.3 %collective-permute-start.20 = (bf16[384,384]{1,0:T(8,128)(2,1)}, bf16[384,384]{1,0:T(8,128)(2,1)S(1)}, u32[]{:S(2)}, u32[]{:S(2)}) collective-permute-start(bf16[384,384]{1,0:T(8,128)(2,1)} %get-tuple-element.47), channel_id=1, source_target_pairs={{0,64},{32,96},{64,0},{96,32},{1,65},{33,97},{65,1},{97,33},{2,66}... | collective-permute-start | bytes 884744 | tf_op jit(solution)/shard_map/ppermute | solution.py:42
  142.1 3.1 %collective-permute-start.21 = (bf16[384,384]{1,0:T(8,128)(2,1)}, bf16[384,384]{1,0:T(8,128)(2,1)S(1)}, u32[]{:S(2)}, u32[]{:S(2)}) collective-permute-start(bf16[384,384]{1,0:T(8,128)(2,1)} %get-tuple-element.48), channel_id=1, source_target_pairs={{0,96},{32,0},{64,32},{96,64},{1,97},{33,1},{65,33},{97,65},{2,98}... | collective-permute-start | bytes 884744 | tf_op jit(solution)/shard_map/ppermute | solution.py:42
  145.2 3.3 %all-to-all-done.2.refs_0_ = bf16[4,384,384]{2,1,0:T(8,128)(2,1)S(1)} async-done(((bf16[4,384,384]{2,1,0:T(8,128)(2,1)}), bf16[4,384,384]{2,1,0:T(8,128)(2,1)S(1)}, u32[]{:S(2)}, u32[]{:S(2)}) %all-to-all-start.2) | async-done | bytes 1179680 | tf_op jit(solution)/shard_map/all_to_all | solution.py:230
  148.8 5.7 %collective-permute-done.19.refs_1_ = bf16[384,384]{1,0:T(8,128)(2,1)S(1)} collective-permute-done((bf16[384,384]{1,0:T(8,128)(2,1)}, bf16[384,384]{1,0:T(8,128)(2,1)S(1)}, u32[]{:S(2)}, u32[]{:S(2)}) %collective-permute-start.19) | collective-permute-done | bytes 294944 | tf_op jit(solution)/shard_map/ppermute | solution.py:42
  154.5 6.7 %collective-permute-done.20.refs_2_ = bf16[384,384]{1,0:T(8,128)(2,1)S(1)} collective-permute-done((bf16[384,384]{1,0:T(8,128)(2,1)}, bf16[384,384]{1,0:T(8,128)(2,1)S(1)}, u32[]{:S(2)}, u32[]{:S(2)}) %collective-permute-start.20) | collective-permute-done | bytes 294944 | tf_op jit(solution)/shard_map/ppermute | solution.py:42
  161.2 11.3 %collective-permute-start.22 = (bf16[384,384]{1,0:T(8,128)(2,1)S(1)}, bf16[384,384]{1,0:T(8,128)(2,1)S(1)}, u32[]{:S(2)}, u32[]{:S(2)}) collective-permute-start(bf16[384,384]{1,0:T(8,128)(2,1)S(1)} %get-tuple-element.54), channel_id=1, source_target_pairs={{0,2},{2,0},{1,3},{3,1},{4,6},{6,4},{5,7},{7,5},{8,10},{10,8},{9,1... | collective-permute-start | bytes 884744 | tf_op jit(solution)/shard_map/ppermute | solution.py:46
  173.5 4.9 %all-to-all-start.3 = ((f32[32,1,768]{2,1,0:T(1,128)}), f32[32,1,768]{2,1,0:T(1,128)S(1)}, u32[]{:S(2)}, u32[]{:S(2)}) async-start(f32[32,1,768]{2,1,0:T(1,128)} %broadcast_in_dim.11), calls=%async_computation.3 | async-start | bytes 196608 | tf_op jit(solution)/shard_map/all_to_all | solution.py:245
  178.5 14.6 %all-to-all-done.3.sums = f32[32,1,768]{2,1,0:T(1,128)S(1)} async-done(((f32[32,1,768]{2,1,0:T(1,128)}), f32[32,1,768]{2,1,0:T(1,128)S(1)}, u32[]{:S(2)}, u32[]{:S(2)}) %all-to-all-start.3) | async-done | bytes 98336 | tf_op jit(solution)/shard_map/all_to_all | solution.py:245
  (89 shorter events, 21.7 us)
Async XLA Ops:
  10.5 25.8 %all-to-all-start = ((bf16[8,3,48,384]{3,2,1,0:T(8,128)(2,1)}), bf16[8,3,48,384]{3,2,1,0:T(8,128)(2,1)S(1)}, u32[]{:S(2)}, u32[]{:S(2)}) async-start(bf16[8,3,48,384]{3,2,1,0:T(8,128)(2,1)} %get-tuple-element.31), calls=%async_computation | async-start | bytes 1769472 | tf_op jit(solution)/shard_map/all_to_all | solution.py:50
  20.8 86.2 %all-gather.2.cloned.1.call-start = ((), (), s32[]{:S(2)}) async-start(), calls=%async_computation.4 | async-start | bytes 5308416 | tf_op jit(solution)/shard_map/all_gather | solution.py:204
  20.8 15.4 %collective-permute-start = (bf16[384,384]{1,0:T(8,128)(2,1)S(1)}, bf16[384,384]{1,0:T(8,128)(2,1)}, u32[]{:S(2)}, u32[]{:S(2)}) collective-permute-start(bf16[384,384]{1,0:T(8,128)(2,1)S(1)} %get-tuple-element.32), channel_id=1, source_target_pairs={{0,2},{2,0},{1,3},{3,1},{4,6},{6,4},{5,7},{7,5},{8,10},{10,8},{9,1... | collective-permute-start | bytes 884744 | tf_op jit(solution)/shard_map/ppermute | solution.py:46
  37.9 49.3 %copy-start.5 = (bf16[96,1536]{1,0:T(8,128)(2,1)}, bf16[96,1536]{1,0:T(8,128)(2,1)S(1)}, u32[]{:S(2)}) copy-start(bf16[96,1536]{1,0:T(8,128)(2,1)S(1)} %get-tuple-element.34.refs_0_) | copy-start | bytes 884740
  37.9 14.3 %collective-permute-start.1 = (bf16[96,1536]{1,0:T(8,128)(2,1)S(1)}, bf16[96,1536]{1,0:T(8,128)(2,1)S(1)}, u32[]{:S(2)}, u32[]{:S(2)}) collective-permute-start(bf16[96,1536]{1,0:T(8,128)(2,1)S(1)} %get-tuple-element.34.refs_0_), channel_id=1, source_target_pairs={{0,4},{4,8},{8,12},{12,16},{16,20},{20,24},{24,28},{28,0},{1,5},{5... | collective-permute-start | bytes 884744 | tf_op jit(solution)/shard_map/ppermute | solution.py:38
  39.8 12.3 %all-to-all-start.1 = ((bf16[8,48,384]{2,1,0:T(8,128)(2,1)}), bf16[8,48,384]{2,1,0:T(8,128)(2,1)S(1)}, u32[]{:S(2)}, u32[]{:S(2)}) async-start(bf16[8,48,384]{2,1,0:T(8,128)(2,1)} %bitcast.4), calls=%async_computation.1 | async-start | bytes 589824 | tf_op jit(solution)/shard_map/all_to_all | solution.py:50
  45.3 15.6 %collective-permute-start.2 = (bf16[96,1536]{1,0:T(8,128)(2,1)S(1)}, bf16[96,1536]{1,0:T(8,128)(2,1)S(1)}, u32[]{:S(2)}, u32[]{:S(2)}) collective-permute-start(bf16[96,1536]{1,0:T(8,128)(2,1)S(1)} %get-tuple-element.34.refs_0_), channel_id=1, source_target_pairs={{0,28},{4,0},{8,4},{12,8},{16,12},{20,16},{24,20},{28,24},{1,29},{... | collective-permute-start | bytes 884744 | tf_op jit(solution)/shard_map/ppermute | solution.py:38
  52.2 54.8 %copy-start.6 = (bf16[4,12,8,384]{3,2,0,1:T(8,128)(2,1)}, bf16[4,12,8,384]{3,2,0,1:T(8,128)(2,1)S(1)}, u32[]{:S(2)}) copy-start(bf16[4,12,8,384]{3,2,0,1:T(8,128)(2,1)S(1)} %copy.12) | copy-start | bytes 884740
  52.2 54.8 %copy-start.12 = (bf16[96,1536]{1,0:T(8,128)(2,1)}, bf16[96,1536]{1,0:T(8,128)(2,1)S(1)}, u32[]{:S(2)}) copy-start(bf16[96,1536]{1,0:T(8,128)(2,1)S(1)} %collective-permute-done.1.refs_2_) | copy-start | bytes 884740
  52.2 13.3 %collective-permute-start.3 = (bf16[96,1536]{1,0:T(8,128)(2,1)S(1)}, bf16[96,1536]{1,0:T(8,128)(2,1)S(1)}, u32[]{:S(2)}, u32[]{:S(2)}) collective-permute-start(bf16[96,1536]{1,0:T(8,128)(2,1)S(1)} %bitcast.13), channel_id=1, source_target_pairs={{0,4},{4,8},{8,12},{12,16},{16,20},{20,24},{24,28},{28,0},{1,5},{5... | collective-permute-start | bytes 884744 | tf_op jit(solution)/shard_map/ppermute | solution.py:38
  54.8 12.7 %collective-permute-start.4 = (bf16[96,1536]{1,0:T(8,128)(2,1)S(1)}, bf16[96,1536]{1,0:T(8,128)(2,1)S(1)}, u32[]{:S(2)}, u32[]{:S(2)}) collective-permute-start(bf16[96,1536]{1,0:T(8,128)(2,1)S(1)} %bitcast.14), channel_id=1, source_target_pairs={{0,28},{4,0},{8,4},{12,8},{16,12},{20,16},{24,20},{28,24},{1,29},{... | collective-permute-start | bytes 884744 | tf_op jit(solution)/shard_map/ppermute | solution.py:38
  59.0 13.1 %collective-permute-start.5 = (bf16[96,1536]{1,0:T(8,128)(2,1)S(1)}, bf16[96,1536]{1,0:T(8,128)(2,1)S(1)}, u32[]{:S(2)}, u32[]{:S(2)}) collective-permute-start(bf16[96,1536]{1,0:T(8,128)(2,1)S(1)} %collective-permute-done.1.refs_2_), channel_id=1, source_target_pairs={{0,4},{4,8},{8,12},{12,16},{16,20},{20,24},{24,28},{28,0},{1,5},{5... | collective-permute-start | bytes 884744 | tf_op jit(solution)/shard_map/ppermute | solution.py:38
  60.9 46.1 %copy-start.13 = (bf16[96,1536]{1,0:T(8,128)(2,1)}, bf16[96,1536]{1,0:T(8,128)(2,1)S(1)}, u32[]{:S(2)}) copy-start(bf16[96,1536]{1,0:T(8,128)(2,1)S(1)} %collective-permute-done.2.refs_3_) | copy-start | bytes 884740
  60.9 13.1 %collective-permute-start.6 = (bf16[96,1536]{1,0:T(8,128)(2,1)S(1)}, bf16[96,1536]{1,0:T(8,128)(2,1)S(1)}, u32[]{:S(2)}, u32[]{:S(2)}) collective-permute-start(bf16[96,1536]{1,0:T(8,128)(2,1)S(1)} %collective-permute-done.2.refs_3_), channel_id=1, source_target_pairs={{0,28},{4,0},{8,4},{12,8},{16,12},{20,16},{24,20},{28,24},{1,29},{... | collective-permute-start | bytes 884744 | tf_op jit(solution)/shard_map/ppermute | solution.py:38
  65.5 13.1 %collective-permute-start.7 = (bf16[96,1536]{1,0:T(8,128)(2,1)S(1)}, bf16[96,1536]{1,0:T(8,128)(2,1)S(1)}, u32[]{:S(2)}, u32[]{:S(2)}) collective-permute-start(bf16[96,1536]{1,0:T(8,128)(2,1)S(1)} %collective-permute-done.3.refs_4_), channel_id=1, source_target_pairs={{0,4},{4,8},{8,12},{12,16},{16,20},{20,24},{24,28},{28,0},{1,5},{5... | collective-permute-start | bytes 884744 | tf_op jit(solution)/shard_map/ppermute | solution.py:38
  67.5 13.1 %collective-permute-start.8 = (bf16[96,1536]{1,0:T(8,128)(2,1)S(1)}, bf16[96,1536]{1,0:T(8,128)(2,1)S(1)}, u32[]{:S(2)}, u32[]{:S(2)}) collective-permute-start(bf16[96,1536]{1,0:T(8,128)(2,1)S(1)} %collective-permute-done.4.refs_5_), channel_id=1, source_target_pairs={{0,28},{4,0},{8,4},{12,8},{16,12},{20,16},{24,20},{28,24},{1,29},{... | collective-permute-start | bytes 884744 | tf_op jit(solution)/shard_map/ppermute | solution.py:38
  72.1 13.1 %collective-permute-start.9 = (bf16[96,1536]{1,0:T(8,128)(2,1)S(1)}, bf16[96,1536]{1,0:T(8,128)(2,1)S(1)}, u32[]{:S(2)}, u32[]{:S(2)}) collective-permute-start(bf16[96,1536]{1,0:T(8,128)(2,1)S(1)} %collective-permute-done.5.refs_6_), channel_id=1, source_target_pairs={{0,4},{4,8},{8,12},{12,16},{16,20},{20,24},{24,28},{28,0},{1,5},{5... | collective-permute-start | bytes 884744 | tf_op jit(solution)/shard_map/ppermute | solution.py:38
  74.0 13.1 %collective-permute-start.10 = (bf16[96,1536]{1,0:T(8,128)(2,1)S(1)}, bf16[96,1536]{1,0:T(8,128)(2,1)S(1)}, u32[]{:S(2)}, u32[]{:S(2)}) collective-permute-start(bf16[96,1536]{1,0:T(8,128)(2,1)S(1)} %collective-permute-done.6.refs_7_), channel_id=1, source_target_pairs={{0,28},{4,0},{8,4},{12,8},{16,12},{20,16},{24,20},{28,24},{1,29},{... | collective-permute-start | bytes 884744 | tf_op jit(solution)/shard_map/ppermute | solution.py:38
  78.6 13.1 %collective-permute-start.11 = (bf16[96,1536]{1,0:T(8,128)(2,1)S(1)}, bf16[96,1536]{1,0:T(8,128)(2,1)S(1)}, u32[]{:S(2)}, u32[]{:S(2)}) collective-permute-start(bf16[96,1536]{1,0:T(8,128)(2,1)S(1)} %collective-permute-done.7.refs_8_), channel_id=1, source_target_pairs={{0,4},{4,8},{8,12},{12,16},{16,20},{20,24},{24,28},{28,0},{1,5},{5... | collective-permute-start | bytes 884744 | tf_op jit(solution)/shard_map/ppermute | solution.py:38
  80.6 13.2 %collective-permute-start.12 = (bf16[96,1536]{1,0:T(8,128)(2,1)S(1)}, bf16[96,1536]{1,0:T(8,128)(2,1)S(1)}, u32[]{:S(2)}, u32[]{:S(2)}) collective-permute-start(bf16[96,1536]{1,0:T(8,128)(2,1)S(1)} %collective-permute-done.8.refs_9_), channel_id=1, source_target_pairs={{0,28},{4,0},{8,4},{12,8},{16,12},{20,16},{24,20},{28,24},{1,29},{... | collective-permute-start | bytes 884744 | tf_op jit(solution)/shard_map/ppermute | solution.py:38
  85.2 13.8 %collective-permute-start.13 = (bf16[48,1536]{1,0:T(8,128)(2,1)S(1)}, bf16[48,1536]{1,0:T(8,128)(2,1)}, u32[]{:S(2)}, u32[]{:S(2)}) collective-permute-start(bf16[48,1536]{1,0:T(8,128)(2,1)S(1)} %slice.16), channel_id=1, source_target_pairs={{0,4},{4,8},{8,12},{12,16},{16,20},{20,24},{24,28},{28,0},{1,5},{5... | collective-permute-start | bytes 442376 | tf_op jit(solution)/shard_map/ppermute | solution.py:38
  87.2 11.8 %collective-permute-start.14 = (bf16[48,1536]{1,0:T(8,128)(2,1)S(1)}, bf16[48,1536]{1,0:T(8,128)(2,1)}, u32[]{:S(2)}, u32[]{:S(2)}) collective-permute-start(bf16[48,1536]{1,0:T(8,128)(2,1)S(1)} %slice.17), channel_id=1, source_target_pairs={{0,28},{4,0},{8,4},{12,8},{16,12},{20,16},{24,20},{28,24},{1,29},{... | collective-permute-start | bytes 442376 | tf_op jit(solution)/shard_map/ppermute | solution.py:38
  91.8 7.5 %collective-permute-start.15 = (bf16[48,1536]{1,0:T(8,128)(2,1)S(1)}, bf16[48,1536]{1,0:T(8,128)(2,1)S(1)}, u32[]{:S(2)}, u32[]{:S(2)}) collective-permute-start(bf16[48,1536]{1,0:T(8,128)(2,1)S(1)} %slice.18), channel_id=1, source_target_pairs={{0,4},{4,8},{8,12},{12,16},{16,20},{20,24},{24,28},{28,0},{1,5},{5... | collective-permute-start | bytes 442376 | tf_op jit(solution)/shard_map/ppermute | solution.py:38
  93.8 6.7 %collective-permute-start.16 = (bf16[48,1536]{1,0:T(8,128)(2,1)S(1)}, bf16[48,1536]{1,0:T(8,128)(2,1)S(1)}, u32[]{:S(2)}, u32[]{:S(2)}) collective-permute-start(bf16[48,1536]{1,0:T(8,128)(2,1)S(1)} %slice.19), channel_id=1, source_target_pairs={{0,28},{4,0},{8,4},{12,8},{16,12},{20,16},{24,20},{28,24},{1,29},{... | collective-permute-start | bytes 442376 | tf_op jit(solution)/shard_map/ppermute | solution.py:38
  120.6 5.3 %collective-permute-start.17 = (bf16[384,1536]{1,0:T(8,128)(2,1)}, bf16[384,1536]{1,0:T(8,128)(2,1)S(1)}, u32[]{:S(2)}, u32[]{:S(2)}) collective-permute-start(bf16[384,1536]{1,0:T(8,128)(2,1)} %get-tuple-element.40), channel_id=1, source_target_pairs={{0,1},{1,0},{2,3},{3,2},{4,5},{5,4},{6,7},{7,6},{8,9},{9,8},{10,11... | collective-permute-start | bytes 3538952 | tf_op jit(solution)/shard_map/ppermute | solution.py:46
  123.2 9.3 %collective-permute-start.18 = (bf16[384,1536]{1,0:T(8,128)(2,1)}, bf16[384,1536]{1,0:T(8,128)(2,1)S(1)}, u32[]{:S(2)}, u32[]{:S(2)}) collective-permute-start(bf16[384,1536]{1,0:T(8,128)(2,1)} %get-tuple-element.44), channel_id=1, source_target_pairs={{0,1},{1,0},{2,3},{3,2},{4,5},{5,4},{6,7},{7,6},{8,9},{9,8},{10,11... | collective-permute-start | bytes 3538952 | tf_op jit(solution)/shard_map/ppermute | solution.py:46
  128.4 20.1 %all-to-all-start.2 = ((bf16[4,384,384]{2,1,0:T(8,128)(2,1)}), bf16[4,384,384]{2,1,0:T(8,128)(2,1)S(1)}, u32[]{:S(2)}, u32[]{:S(2)}) async-start(bf16[4,384,384]{2,1,0:T(8,128)(2,1)} %shard_map.40), calls=%async_computation.2 | async-start | bytes 2359296 | tf_op jit(solution)/shard_map/all_to_all | solution.py:230
  134.3 20.2 %collective-permute-start.19 = (bf16[384,384]{1,0:T(8,128)(2,1)}, bf16[384,384]{1,0:T(8,128)(2,1)S(1)}, u32[]{:S(2)}, u32[]{:S(2)}) collective-permute-start(bf16[384,384]{1,0:T(8,128)(2,1)} %get-tuple-element.46), channel_id=1, source_target_pairs={{0,32},{32,64},{64,96},{96,0},{1,33},{33,65},{65,97},{97,1},{2,34}... | collective-permute-start | bytes 884744 | tf_op jit(solution)/shard_map/ppermute | solution.py:42
  137.8 23.4 %collective-permute-start.20 = (bf16[384,384]{1,0:T(8,128)(2,1)}, bf16[384,384]{1,0:T(8,128)(2,1)S(1)}, u32[]{:S(2)}, u32[]{:S(2)}) collective-permute-start(bf16[384,384]{1,0:T(8,128)(2,1)} %get-tuple-element.47), channel_id=1, source_target_pairs={{0,64},{32,96},{64,0},{96,32},{1,65},{33,97},{65,1},{97,33},{2,66}... | collective-permute-start | bytes 884744 | tf_op jit(solution)/shard_map/ppermute | solution.py:42
  142.1 19.1 %collective-permute-start.21 = (bf16[384,384]{1,0:T(8,128)(2,1)}, bf16[384,384]{1,0:T(8,128)(2,1)S(1)}, u32[]{:S(2)}, u32[]{:S(2)}) collective-permute-start(bf16[384,384]{1,0:T(8,128)(2,1)} %get-tuple-element.48), channel_id=1, source_target_pairs={{0,96},{32,0},{64,32},{96,64},{1,97},{33,1},{65,33},{97,65},{2,98}... | collective-permute-start | bytes 884744 | tf_op jit(solution)/shard_map/ppermute | solution.py:42
  161.2 31.9 %collective-permute-start.22 = (bf16[384,384]{1,0:T(8,128)(2,1)S(1)}, bf16[384,384]{1,0:T(8,128)(2,1)S(1)}, u32[]{:S(2)}, u32[]{:S(2)}) collective-permute-start(bf16[384,384]{1,0:T(8,128)(2,1)S(1)} %get-tuple-element.54), channel_id=1, source_target_pairs={{0,2},{2,0},{1,3},{3,1},{4,6},{6,4},{5,7},{7,5},{8,10},{10,8},{9,1... | collective-permute-start | bytes 884744 | tf_op jit(solution)/shard_map/ppermute | solution.py:46
  173.5 19.5 %all-to-all-start.3 = ((f32[32,1,768]{2,1,0:T(1,128)}), f32[32,1,768]{2,1,0:T(1,128)S(1)}, u32[]{:S(2)}, u32[]{:S(2)}) async-start(f32[32,1,768]{2,1,0:T(1,128)} %broadcast_in_dim.11), calls=%async_computation.3 | async-start | bytes 196608 | tf_op jit(solution)/shard_map/all_to_all | solution.py:245
  (18 other events, 312.2 us)
Sparse Core Ops, SparseCore 0:
  38.0 68.9 all-gather.1

commit v6 on v3

--- a/solution.py
+++ b/solution.py
@@ -113,21 +113,18 @@
             at = pl.ds(pl.multiple_of(i * step, step), step)
             product = jnp.dot(b[own], a[:, at], preferred_element_type=F32)
             theirs[:, at] = product[:UNIT].astype(BF16)
-            ours[:, at] = product[UNIT:]
-
-
-def add_core(place, ours, sent, first, second, third, own):
-    x = place[0]
-    pieces = [own, first, second, third]
+            ours[:, at] = product[UNIT:].astype(BF16)
+
+
+def add_core(place, ours, sent, *pieces):
     for step in range(X):
-        at = pl.ds(pl.multiple_of(lax.rem(x + step, X) * HALF, HALF), HALF)
-        total = ours[:, at] + sent[:, at].astype(F32)
-        pieces[step][...] = total.astype(pieces[step].dtype)
-
-
-def add_x(own, first, second, third, total, sums):
-    all_x = own[...] + first[...].astype(F32) + (second[...].astype(F32) + third[...].astype(F32))
-    turned = all_x.T
+        at = pl.ds(pl.multiple_of(lax.rem(place[0] + step, X) * HALF, HALF), HALF)
+        pieces[step][...] = (ours[:, at].astype(F32) + sent[:, at].astype(F32)).astype(BF16)
+
+
+def add_x(*refs):
+    pieces, total, sums = refs[:X], refs[X], refs[X + 1]
+    turned = sum(piece[...].astype(F32) for piece in pieces).T
     total[...] = turned.astype(total.dtype)
     sums[...] = jnp.sum(turned * turned, axis=0, keepdims=True)
 
@@ -153,23 +150,37 @@
 
 def rings(near, far):
     shards, order = [near], [(0, 0, 0, CORE * SUB)]
-    ends = [[near, near], [far, far]]
-    for d in range(1, Y // 2):
-        for which in (0, 1):
-            up, down = ends[which]
-            up, down = shift_y(up, 1), shift_y(down, -1)
-            if d == 1 and which == 0:
-                up, far = in_order(up, far)
-                ends[1] = [far, far]
-                shards.append(far)
-                order.append((1, 0, 0, CORE * SUB))
-            ends[which] = [up, down]
-            shards += [up, down]
-            order += [(which, d, 0, CORE * SUB), (which, Y - d, 0, CORE * SUB)]
-    for which in (0, 1):
-        up, down = ends[which]
-        shards += [shift_y(up[:SUB], 1), shift_y(down[SUB:], -1)]
-        order += [(which, Y // 2, 0, SUB), (which, Y // 2, SUB, SUB)]
+    ups, downs = [near, far], [near, far]
+    ups[0] = shift_y(near, 1)
+    downs[0] = shift_y(near, -1)
+    ups[0], far = in_order(ups[0], far)
+    shards += [ups[0], downs[0], far]
+    order += [(0, 1, 0, CORE * SUB), (0, Y - 1, 0, CORE * SUB), (1, 0, 0, CORE * SUB)]
+    ups[1], downs[1] = far, far
+    last = Y // 2
+    for d in range(2, last + 2):
+        cut = [(0, d), (1, d - 1)]
+        up, down = list(ups), list(downs)
+        for which, distance in cut:
+            if distance == last:
+                up[which], down[which] = ups[which][:SUB], downs[which][SUB:]
+        live = [which for which, distance in cut if distance <= last]
+        for which in live:
+            ups[which] = shift_y(up[which], 1)
+        for which in live:
+            downs[which] = shift_y(down[which], -1)
+        for which, distance in cut:
+            if distance < last:
+                order += [(which, distance, 0, CORE * SUB), (which, Y - distance, 0, CORE * SUB)]
+            elif distance == last:
+                order += [(which, last, 0, SUB), (which, last, SUB, SUB)]
+            else:
+                continue
+            shards += [ups[which], downs[which]]
+        if d < last:
+            ups[:] = in_order(*ups)
+            downs[:] = in_order(*downs)
+            shards[-4:] = [ups[0], downs[0], ups[1], downs[1]]
     return shards, tuple(order)
 
 
@@ -201,7 +212,7 @@
 
     theirs, ours, theirs_near, ours_near = call(
         functools.partial(multiply, order),
-        [((UNIT, WIDE), BF16), ((UNIT, WIDE), F32)] * 2,
+        [((UNIT, WIDE), BF16)] * 4,
         [SMEM] + [HBM] * (len(shards) + 1),
         (jnp.stack([y, zhi]), *shards, right),
         [
@@ -213,23 +224,24 @@
         vmem=60,
     )
 
-    def over_x(ours, sent):
-        pieces = call(
+    def total(apart, dtype):
+        return call(add_x, [((HALF, UNIT), dtype), ((1, UNIT), F32)], [VMEM] * X, apart)
+
+    def over_x(ours, theirs):
+        apart = call(
             add_core,
-            [((UNIT, HALF), BF16)] * 3 + [((UNIT, HALF), F32)],
+            [((UNIT, HALF), BF16)] * X,
             [SMEM, VMEM, VMEM],
-            (x[None], ours, sent),
+            (x[None], ours, swap(theirs, "core")),
         )
-        return pieces[3], *(shift_x(pieces[step - 1], step) for step in range(1, X))
-
-    def total(pieces, dtype):
-        return call(add_x, [((HALF, UNIT), dtype), ((1, UNIT), F32)], [VMEM] * 4, pieces)
-
-    pieces = over_x(ours, swap(theirs, "core"))
-    pieces_near = over_x(ours_near, swap(theirs_near, "core"))
-    other, sums = total(pieces, BF16)
-    sums, other = swap(sums, "zhi"), swap(other, "zhi")
-    mine, own_sums = total(pieces_near, F32)
+        return [apart[0]] + [shift_x(apart[step], step) for step in range(1, X)]
+
+    apart = over_x(ours, theirs)
+    apart_near = over_x(ours_near, theirs_near)
+    other, sums = total(apart, BF16)
+    sums, other = in_order(swap(sums, "zhi"), other)
+    other = swap(other, "zhi")
+    mine, own_sums = total(apart_near, F32)
     sums = jnp.broadcast_to(sums + own_sums, (Z_LO * X, 1, UNIT))
     sums = lax.all_to_all(sums, ("zlo", "x"), split_axis=0, concat_axis=0, tiled=True)
     return call(

time: 202 us -> 212 us (1.050)
  the two profiles are of different devices: /device:TPU:24 before, /device:TPU:1 now
where the time goes in v6:
time: 212 us; the launch traced here: 210 us
  starting transfers between devices  119 us (56%)
  waiting for transfers between devices  39.1 us (18%)
  Pallas kernels  20 us (9%)
  between operations  14 us (7%)
  blocking collectives  13.2 us (6%)
  local copies, waits for them, and re-layouts  4.73 us (2%)
    ppermute x16, starting transfers between devices, shift_y(): return lax.ppermute(shard, 'y', [(i, (i + step) % Y) for i in range(Y)])  47.3 us
    ppermute x5, starting transfers between devices, swap(): return lax.ppermute(shard, axis, [(0, 1), (1, 0)])  35.6 us
    pallas_call x8, Pallas kernels, call(): pl.pallas_call(body, out_shape=shapes, in_specs=ins, out_specs=[VMEM] * l...  20 us
    ppermute x6, starting transfers between devices, shift_x(): return lax.ppermute(shard, 'x', [(i, (i + step) % X) for i in range(X)])  18.7 us
    ppermute x16, waiting for transfers between devices, shift_y(): return lax.ppermute(shard, 'y', [(i, (i + step) % Y) for i in range(Y)])  16.2 us
    all_to_all x1, blocking collectives, spread_over(): lax.all_to_all(array, ('x', 'core'), split_axis=0, concat_axis=0, tiled=T...  13.2 us
    ppermute x5, waiting for transfers between devices, swap(): return lax.ppermute(shard, axis, [(0, 1), (1, 0)])  10.9 us
    all_to_all x1, waiting for transfers between devices, local(): lax.all_to_all(sums, ('zlo', 'x'), split_axis=0, concat_axis=0, tiled=True)  10.6 us
  transfers between devices with their start and end apart: 30, of which 9 were waited for; matrix products, arithmetic and copies ran while one was open for 1% of the time, Pallas kernels for 1%

profile of v6, /device:TPU:1, one launch (start us, length us, event | category | flops | bytes accessed | tf_op | source)
XLA Modules:
  0.0 210.5 jit_solution(18137102129454319589)
XLA Ops:
  10.5 10.3 %all-to-all-start = ((bf16[8,3,48,384]{3,2,1,0:T(8,128)(2,1)}), bf16[8,3,48,384]{3,2,1,0:T(8,128)(2,1)S(1)}, u32[]{:S(2)}, u32[]{:S(2)}) async-start(bf16[8,3,48,384]{3,2,1,0:T(8,128)(2,1)} %get-tuple-element.39), calls=%async_computation | async-start | bytes 1769472 | tf_op jit(solution)/shard_map/all_to_all | solution.py:50
  20.8 6.1 %collective-permute-start = (bf16[384,384]{1,0:T(8,128)(2,1)S(1)}, bf16[384,384]{1,0:T(8,128)(2,1)S(1)}, u32[]{:S(2)}, u32[]{:S(2)}) collective-permute-start(bf16[384,384]{1,0:T(8,128)(2,1)S(1)} %get-tuple-element.40), channel_id=1, source_target_pairs={{0,2},{2,0},{1,3},{3,1},{4,6},{6,4},{5,7},{7,5},{8,10},{10,8},{9,1... | collective-permute-start | bytes 884744 | tf_op jit(solution)/shard_map/ppermute | solution.py:46
  26.9 9.2 %collective-permute-done = bf16[384,384]{1,0:T(8,128)(2,1)S(1)} collective-permute-done((bf16[384,384]{1,0:T(8,128)(2,1)S(1)}, bf16[384,384]{1,0:T(8,128)(2,1)S(1)}, u32[]{:S(2)}, u32[]{:S(2)}) %collective-permute-start) | collective-permute-done | bytes 294944 | tf_op jit(solution)/shard_map/ppermute | solution.py:46
  37.8 1.9 collective-permute-start.1
  39.7 4.6 %collective-permute-start.2 = (bf16[96,1536]{1,0:T(8,128)(2,1)S(1)}, bf16[96,1536]{1,0:T(8,128)(2,1)S(1)}, u32[]{:S(2)}, u32[]{:S(2)}) collective-permute-start(bf16[96,1536]{1,0:T(8,128)(2,1)S(1)} %get-tuple-element.42.refs_0_), channel_id=1, source_target_pairs={{0,28},{4,0},{8,4},{12,8},{16,12},{20,16},{24,20},{28,24},{1,29},{... | collective-permute-start | bytes 884744 | tf_op jit(solution)/shard_map/ppermute | solution.py:38
  44.3 13.2 %all_to_all.15 = bf16[8,48,384]{2,1,0:T(8,128)(2,1)S(1)} all-to-all(bf16[8,48,384]{2,1,0:T(8,128)(2,1)S(1)} %bitcast.16), channel_id=1, replica_groups=mesh['zlo'=4,'x'=4,'y'=8,'zhi'=2,'core'=2] {'x','core'}, dimensions={0} | all-to-all | bytes 589824 | tf_op jit(solution)/shard_map/all_to_all | solution.py:50
  59.5 2.8 %collective-permute-start.5 = (bf16[96,1536]{1,0:T(8,128)(2,1)S(1)}, bf16[96,1536]{1,0:T(8,128)(2,1)S(1)}, u32[]{:S(2)}, u32[]{:S(2)}) collective-permute-start(bf16[96,1536]{1,0:T(8,128)(2,1)S(1)} %collective-permute-done.2.refs_2_), channel_id=1, source_target_pairs={{0,28},{4,0},{8,4},{12,8},{16,12},{20,16},{24,20},{28,24},{1,29},{... | collective-permute-start | bytes 884744 | tf_op jit(solution)/shard_map/ppermute | solution.py:38
  62.3 2.5 %collective-permute-start.4 = (bf16[96,1536]{1,0:T(8,128)(2,1)S(1)}, bf16[96,1536]{1,0:T(8,128)(2,1)S(1)}, u32[]{:S(2)}, u32[]{:S(2)}) collective-permute-start(bf16[96,1536]{1,0:T(8,128)(2,1)S(1)} %bitcast.14), channel_id=1, source_target_pairs={{0,4},{4,8},{8,12},{12,16},{16,20},{20,24},{24,28},{28,0},{1,5},{5... | collective-permute-start | bytes 884744 | tf_op jit(solution)/shard_map/ppermute | solution.py:38
  64.8 3.4 %collective-permute-start.3 = (bf16[96,1536]{1,0:T(8,128)(2,1)S(1)}, bf16[96,1536]{1,0:T(8,128)(2,1)S(1)}, u32[]{:S(2)}, u32[]{:S(2)}) collective-permute-start(bf16[96,1536]{1,0:T(8,128)(2,1)S(1)} %collective-permute-done.1.refs_1_), channel_id=1, source_target_pairs={{0,4},{4,8},{8,12},{12,16},{16,20},{20,24},{24,28},{28,0},{1,5},{5... | collective-permute-start | bytes 884744 | tf_op jit(solution)/shard_map/ppermute | solution.py:38
  68.2 5.7 %collective-permute-done.5.refs_5_ = bf16[96,1536]{1,0:T(8,128)(2,1)S(1)} collective-permute-done((bf16[96,1536]{1,0:T(8,128)(2,1)S(1)}, bf16[96,1536]{1,0:T(8,128)(2,1)S(1)}, u32[]{:S(2)}, u32[]{:S(2)}) %collective-permute-start.5) | collective-permute-done | bytes 294944 | tf_op jit(solution)/shard_map/ppermute | solution.py:38
  73.8 3.3 %collective-permute-start.10 = (bf16[96,1536]{1,0:T(8,128)(2,1)S(1)}, bf16[96,1536]{1,0:T(8,128)(2,1)S(1)}, u32[]{:S(2)}, u32[]{:S(2)}) collective-permute-start(bf16[96,1536]{1,0:T(8,128)(2,1)S(1)} %collective-permute-done.6.refs_7_), channel_id=1, source_target_pairs={{0,28},{4,0},{8,4},{12,8},{16,12},{20,16},{24,20},{28,24},{1,29},{... | collective-permute-start | bytes 884744 | tf_op jit(solution)/shard_map/ppermute | solution.py:38
  79.2 3.4 %collective-permute-start.7 = (bf16[96,1536]{1,0:T(8,128)(2,1)S(1)}, bf16[96,1536]{1,0:T(8,128)(2,1)S(1)}, u32[]{:S(2)}, u32[]{:S(2)}) collective-permute-start(bf16[96,1536]{1,0:T(8,128)(2,1)S(1)} %collective-permute-done.3.refs_4_), channel_id=1, source_target_pairs={{0,4},{4,8},{8,12},{12,16},{16,20},{20,24},{24,28},{28,0},{1,5},{5... | collective-permute-start | bytes 884744 | tf_op jit(solution)/shard_map/ppermute | solution.py:38
  82.5 1.9 collective-permute-start.8
  84.5 4.8 %collective-permute-done.9.refs_9_ = bf16[96,1536]{1,0:T(8,128)(2,1)S(1)} collective-permute-done((bf16[96,1536]{1,0:T(8,128)(2,1)S(1)}, bf16[96,1536]{1,0:T(8,128)(2,1)S(1)}, u32[]{:S(2)}, u32[]{:S(2)}) %collective-permute-start.9) | collective-permute-done | bytes 294944 | tf_op jit(solution)/shard_map/ppermute | solution.py:38
  89.3 4.8 %collective-permute-start.14 = (bf16[96,1536]{1,0:T(8,128)(2,1)S(1)}, bf16[96,1536]{1,0:T(8,128)(2,1)S(1)}, u32[]{:S(2)}, u32[]{:S(2)}) collective-permute-start(bf16[96,1536]{1,0:T(8,128)(2,1)S(1)} %collective-permute-done.10.refs_11_), channel_id=1, source_target_pairs={{0,28},{4,0},{8,4},{12,8},{16,12},{20,16},{24,20},{28,24},{1,29},{... | collective-permute-start | bytes 884744 | tf_op jit(solution)/shard_map/ppermute | solution.py:38
  95.3 2.4 %collective-permute-start.13 = (bf16[96,1536]{1,0:T(8,128)(2,1)S(1)}, bf16[96,1536]{1,0:T(8,128)(2,1)S(1)}, u32[]{:S(2)}, u32[]{:S(2)}) collective-permute-start(bf16[96,1536]{1,0:T(8,128)(2,1)S(1)} %collective-permute-done.8.refs_10_), channel_id=1, source_target_pairs={{0,4},{4,8},{8,12},{12,16},{16,20},{20,24},{24,28},{28,0},{1,5},{5... | collective-permute-start | bytes 884744 | tf_op jit(solution)/shard_map/ppermute | solution.py:38
  97.7 4.1 %collective-permute-start.12 = (bf16[48,1536]{1,0:T(8,128)(2,1)S(1)}, bf16[48,1536]{1,0:T(8,128)(2,1)}, u32[]{:S(2)}, u32[]{:S(2)}) collective-permute-start(bf16[48,1536]{1,0:T(8,128)(2,1)S(1)} %slice.13), channel_id=1, source_target_pairs={{0,28},{4,0},{8,4},{12,8},{16,12},{20,16},{24,20},{28,24},{1,29},{... | collective-permute-start | bytes 442376 | tf_op jit(solution)/shard_map/ppermute | solution.py:38
  101.8 1.9 collective-permute-start.11
  103.8 4.6 %collective-permute-start.16 = (bf16[48,1536]{1,0:T(8,128)(2,1)S(1)}, bf16[48,1536]{1,0:T(8,128)(2,1)S(1)}, u32[]{:S(2)}, u32[]{:S(2)}) collective-permute-start(bf16[48,1536]{1,0:T(8,128)(2,1)S(1)} %slice.17), channel_id=1, source_target_pairs={{0,28},{4,0},{8,4},{12,8},{16,12},{20,16},{24,20},{28,24},{1,29},{... | collective-permute-start | bytes 442376 | tf_op jit(solution)/shard_map/ppermute | solution.py:38
  111.0 4.5 %collective-permute-done.15.refs_16_ = bf16[48,1536]{1,0:T(8,128)(2,1)S(1)} collective-permute-done((bf16[48,1536]{1,0:T(8,128)(2,1)S(1)}, bf16[48,1536]{1,0:T(8,128)(2,1)S(1)}, u32[]{:S(2)}, u32[]{:S(2)}) %collective-permute-start.15) | collective-permute-done | bytes 147488 | tf_op jit(solution)/shard_map/ppermute | solution.py:38
  116.2 13.6 %shard_map.39 = (bf16[384,1536]{1,0:T(8,128)(2,1)}, bf16[384,1536]{1,0:T(8,128)(2,1)}, bf16[384,1536]{1,0:T(8,128)(2,1)}, bf16[384,1536]{1,0:T(8,128)(2,1)}) custom-call(s32[2]{0:T(128)} %pad_add_fusion.place, bf16[96,1536]{1,0:T(8,128)(2,1)} %copy-done.3, bf16[96,1536]{1,0:T(8,128)(2,1)} %copy-done.10, bf16[96,1536]{1,0:T(8,128)(2,1)} %copy-done.11, ...), custom_call_target="tpu_custom_call" | custom-call | flops 7247757312 | bytes 14155784 | tf_op jit(solution)/shard_map/pallas_call | solution.py:26
  129.8 6.9 %collective-permute-start.21 = (bf16[384,1536]{1,0:T(8,128)(2,1)}, bf16[384,1536]{1,0:T(8,128)(2,1)S(1)}, u32[]{:S(2)}, u32[]{:S(2)}) collective-permute-start(bf16[384,1536]{1,0:T(8,128)(2,1)} %get-tuple-element.63), channel_id=1, source_target_pairs={{0,1},{1,0},{2,3},{3,2},{4,5},{5,4},{6,7},{7,6},{8,9},{9,8},{10,11... | collective-permute-start | bytes 3538952 | tf_op jit(solution)/shard_map/ppermute | solution.py:46
  140.9 2.3 %collective-permute-start.22 = (bf16[384,384]{1,0:T(8,128)(2,1)S(1)}, bf16[384,384]{1,0:T(8,128)(2,1)S(1)}, u32[]{:S(2)}, u32[]{:S(2)}) collective-permute-start(bf16[384,384]{1,0:T(8,128)(2,1)S(1)} %get-tuple-element.65), channel_id=1, source_target_pairs={{0,32},{32,64},{64,96},{96,0},{1,33},{33,65},{65,97},{97,1},{2,34}... | collective-permute-start | bytes 884744 | tf_op jit(solution)/shard_map/ppermute | solution.py:42
  143.3 3.7 %collective-permute-start.23 = (bf16[384,384]{1,0:T(8,128)(2,1)S(1)}, bf16[384,384]{1,0:T(8,128)(2,1)S(1)}, u32[]{:S(2)}, u32[]{:S(2)}) collective-permute-start(bf16[384,384]{1,0:T(8,128)(2,1)S(1)} %get-tuple-element.66), channel_id=1, source_target_pairs={{0,64},{32,96},{64,0},{96,32},{1,65},{33,97},{65,1},{97,33},{2,66}... | collective-permute-start | bytes 884744 | tf_op jit(solution)/shard_map/ppermute | solution.py:42
  147.0 2.5 %collective-permute-start.24 = (bf16[384,384]{1,0:T(8,128)(2,1)S(1)}, bf16[384,384]{1,0:T(8,128)(2,1)S(1)}, u32[]{:S(2)}, u32[]{:S(2)}) collective-permute-start(bf16[384,384]{1,0:T(8,128)(2,1)S(1)} %get-tuple-element.67), channel_id=1, source_target_pairs={{0,96},{32,0},{64,32},{96,64},{1,97},{33,1},{65,33},{97,65},{2,98}... | collective-permute-start | bytes 884744 | tf_op jit(solution)/shard_map/ppermute | solution.py:42
  149.9 2.7 %collective-permute-start.18 = (bf16[384,384]{1,0:T(8,128)(2,1)S(1)}, bf16[384,384]{1,0:T(8,128)(2,1)S(1)}, u32[]{:S(2)}, u32[]{:S(2)}) collective-permute-start(bf16[384,384]{1,0:T(8,128)(2,1)S(1)} %get-tuple-element.58), channel_id=1, source_target_pairs={{0,32},{32,64},{64,96},{96,0},{1,33},{33,65},{65,97},{97,1},{2,34}... | collective-permute-start | bytes 884744 | tf_op jit(solution)/shard_map/ppermute | solution.py:42
  152.6 3.4 %collective-permute-start.19 = (bf16[384,384]{1,0:T(8,128)(2,1)S(1)}, bf16[384,384]{1,0:T(8,128)(2,1)S(1)}, u32[]{:S(2)}, u32[]{:S(2)}) collective-permute-start(bf16[384,384]{1,0:T(8,128)(2,1)S(1)} %get-tuple-element.59), channel_id=1, source_target_pairs={{0,64},{32,96},{64,0},{96,32},{1,65},{33,97},{65,1},{97,33},{2,66}... | collective-permute-start | bytes 884744 | tf_op jit(solution)/shard_map/ppermute | solution.py:42
  156.1 4.0 %collective-permute-start.20 = (bf16[384,384]{1,0:T(8,128)(2,1)S(1)}, bf16[384,384]{1,0:T(8,128)(2,1)S(1)}, u32[]{:S(2)}, u32[]{:S(2)}) collective-permute-start(bf16[384,384]{1,0:T(8,128)(2,1)S(1)} %get-tuple-element.60), channel_id=1, source_target_pairs={{0,96},{32,0},{64,32},{96,64},{1,97},{33,1},{65,33},{97,65},{2,98}... | collective-permute-start | bytes 884744 | tf_op jit(solution)/shard_map/ppermute | solution.py:42
  161.7 13.4 %collective-permute-start.25 = (f32[1,384]{1,0:T(1,128)S(1)}, f32[1,384]{1,0:T(1,128)S(1)}, u32[]{:S(2)}, u32[]{:S(2)}) collective-permute-start(f32[1,384]{1,0:T(1,128)S(1)} %get-tuple-element.68), channel_id=1, source_target_pairs={{0,2},{2,0},{1,3},{3,1},{4,6},{6,4},{5,7},{7,5},{8,10},{10,8},{9,1... | collective-permute-start | bytes 4616 | tf_op jit(solution)/shard_map/ppermute | solution.py:46
  176.1 7.3 %collective-permute-start.26 = (bf16[384,384]{1,0:T(8,128)(2,1)S(1)}, bf16[384,384]{1,0:T(8,128)(2,1)S(1)}, u32[]{:S(2)}, u32[]{:S(2)}) collective-permute-start(bf16[384,384]{1,0:T(8,128)(2,1)S(1)} %get-tuple-element.70), channel_id=1, source_target_pairs={{0,2},{2,0},{1,3},{3,1},{4,6},{6,4},{5,7},{7,5},{8,10},{10,8},{9,1... | collective-permute-start | bytes 884744 | tf_op jit(solution)/shard_map/ppermute | solution.py:46
  184.3 6.8 %all-to-all-start.2 = ((f32[16,1,384]{2,1,0:T(1,128)}), f32[16,1,384]{2,1,0:T(1,128)S(1)}, u32[]{:S(2)}, u32[]{:S(2)}) async-start(f32[16,1,384]{2,1,0:T(1,128)} %broadcast_in_dim.12), calls=%async_computation.2 | async-start | bytes 49152 | tf_op jit(solution)/shard_map/all_to_all | solution.py:246
  191.2 10.6 %all-to-all-done.2.sums = f32[16,1,384]{2,1,0:T(1,128)S(1)} async-done(((f32[16,1,384]{2,1,0:T(1,128)}), f32[16,1,384]{2,1,0:T(1,128)S(1)}, u32[]{:S(2)}, u32[]{:S(2)}) %all-to-all-start.2) | async-done | bytes 24608 | tf_op jit(solution)/shard_map/all_to_all | solution.py:246
  (89 shorter events, 23.7 us)
Async XLA Ops:
  10.5 25.7 %all-to-all-start = ((bf16[8,3,48,384]{3,2,1,0:T(8,128)(2,1)}), bf16[8,3,48,384]{3,2,1,0:T(8,128)(2,1)S(1)}, u32[]{:S(2)}, u32[]{:S(2)}) async-start(bf16[8,3,48,384]{3,2,1,0:T(8,128)(2,1)} %get-tuple-element.39), calls=%async_computation | async-start | bytes 1769472 | tf_op jit(solution)/shard_map/all_to_all | solution.py:50
  20.8 94.7 %all-gather.2.cloned.1.call-start = ((), (), s32[]{:S(2)}) async-start(), calls=%async_computation.3 | async-start | bytes 5308416 | tf_op jit(solution)/shard_map/all_gather | solution.py:209
  20.8 15.3 %collective-permute-start = (bf16[384,384]{1,0:T(8,128)(2,1)S(1)}, bf16[384,384]{1,0:T(8,128)(2,1)S(1)}, u32[]{:S(2)}, u32[]{:S(2)}) collective-permute-start(bf16[384,384]{1,0:T(8,128)(2,1)S(1)} %get-tuple-element.40), channel_id=1, source_target_pairs={{0,2},{2,0},{1,3},{3,1},{4,6},{6,4},{5,7},{7,5},{8,10},{10,8},{9,1... | collective-permute-start | bytes 884744 | tf_op jit(solution)/shard_map/ppermute | solution.py:46
  37.8 64.1 %copy-start.3 = (bf16[96,1536]{1,0:T(8,128)(2,1)}, bf16[96,1536]{1,0:T(8,128)(2,1)S(1)}, u32[]{:S(2)}) copy-start(bf16[96,1536]{1,0:T(8,128)(2,1)S(1)} %get-tuple-element.42.refs_0_) | copy-start | bytes 884740
  37.8 19.7 %collective-permute-start.1 = (bf16[96,1536]{1,0:T(8,128)(2,1)S(1)}, bf16[96,1536]{1,0:T(8,128)(2,1)S(1)}, u32[]{:S(2)}, u32[]{:S(2)}) collective-permute-start(bf16[96,1536]{1,0:T(8,128)(2,1)S(1)} %get-tuple-element.42.refs_0_), channel_id=1, source_target_pairs={{0,4},{4,8},{8,12},{12,16},{16,20},{20,24},{24,28},{28,0},{1,5},{5... | collective-permute-start | bytes 884744 | tf_op jit(solution)/shard_map/ppermute | solution.py:38
  39.7 19.7 %collective-permute-start.2 = (bf16[96,1536]{1,0:T(8,128)(2,1)S(1)}, bf16[96,1536]{1,0:T(8,128)(2,1)S(1)}, u32[]{:S(2)}, u32[]{:S(2)}) collective-permute-start(bf16[96,1536]{1,0:T(8,128)(2,1)S(1)} %get-tuple-element.42.refs_0_), channel_id=1, source_target_pairs={{0,28},{4,0},{8,4},{12,8},{16,12},{20,16},{24,20},{28,24},{1,29},{... | collective-permute-start | bytes 884744 | tf_op jit(solution)/shard_map/ppermute | solution.py:38
  57.5 58.0 %copy-start.4 = (bf16[4,12,8,384]{3,2,0,1:T(8,128)(2,1)}, bf16[4,12,8,384]{3,2,0,1:T(8,128)(2,1)S(1)}, u32[]{:S(2)}) copy-start(bf16[4,12,8,384]{3,2,0,1:T(8,128)(2,1)S(1)} %copy.12) | copy-start | bytes 884740
  57.5 10.6 %collective-permute-start.6 = (bf16[96,1536]{1,0:T(8,128)(2,1)S(1)}, bf16[96,1536]{1,0:T(8,128)(2,1)S(1)}, u32[]{:S(2)}, u32[]{:S(2)}) collective-permute-start(bf16[96,1536]{1,0:T(8,128)(2,1)S(1)} %bitcast.13), channel_id=1, source_target_pairs={{0,28},{4,0},{8,4},{12,8},{16,12},{20,16},{24,20},{28,24},{1,29},{... | collective-permute-start | bytes 884744 | tf_op jit(solution)/shard_map/ppermute | solution.py:38
  59.5 14.4 %collective-permute-start.5 = (bf16[96,1536]{1,0:T(8,128)(2,1)S(1)}, bf16[96,1536]{1,0:T(8,128)(2,1)S(1)}, u32[]{:S(2)}, u32[]{:S(2)}) collective-permute-start(bf16[96,1536]{1,0:T(8,128)(2,1)S(1)} %collective-permute-done.2.refs_2_), channel_id=1, source_target_pairs={{0,28},{4,0},{8,4},{12,8},{16,12},{20,16},{24,20},{28,24},{1,29},{... | collective-permute-start | bytes 884744 | tf_op jit(solution)/shard_map/ppermute | solution.py:38
  62.3 16.9 %collective-permute-start.4 = (bf16[96,1536]{1,0:T(8,128)(2,1)S(1)}, bf16[96,1536]{1,0:T(8,128)(2,1)S(1)}, u32[]{:S(2)}, u32[]{:S(2)}) collective-permute-start(bf16[96,1536]{1,0:T(8,128)(2,1)S(1)} %bitcast.14), channel_id=1, source_target_pairs={{0,4},{4,8},{8,12},{12,16},{16,20},{20,24},{24,28},{28,0},{1,5},{5... | collective-permute-start | bytes 884744 | tf_op jit(solution)/shard_map/ppermute | solution.py:38
  64.8 14.4 %collective-permute-start.3 = (bf16[96,1536]{1,0:T(8,128)(2,1)S(1)}, bf16[96,1536]{1,0:T(8,128)(2,1)S(1)}, u32[]{:S(2)}, u32[]{:S(2)}) collective-permute-start(bf16[96,1536]{1,0:T(8,128)(2,1)S(1)} %collective-permute-done.1.refs_1_), channel_id=1, source_target_pairs={{0,4},{4,8},{8,12},{12,16},{16,20},{20,24},{24,28},{28,0},{1,5},{5... | collective-permute-start | bytes 884744 | tf_op jit(solution)/shard_map/ppermute | solution.py:38
  73.8 10.6 %collective-permute-start.10 = (bf16[96,1536]{1,0:T(8,128)(2,1)S(1)}, bf16[96,1536]{1,0:T(8,128)(2,1)S(1)}, u32[]{:S(2)}, u32[]{:S(2)}) collective-permute-start(bf16[96,1536]{1,0:T(8,128)(2,1)S(1)} %collective-permute-done.6.refs_7_), channel_id=1, source_target_pairs={{0,28},{4,0},{8,4},{12,8},{16,12},{20,16},{24,20},{28,24},{1,29},{... | collective-permute-start | bytes 884744 | tf_op jit(solution)/shard_map/ppermute | solution.py:38
  77.2 12.1 %collective-permute-start.9 = (bf16[96,1536]{1,0:T(8,128)(2,1)S(1)}, bf16[96,1536]{1,0:T(8,128)(2,1)S(1)}, u32[]{:S(2)}, u32[]{:S(2)}) collective-permute-start(bf16[96,1536]{1,0:T(8,128)(2,1)S(1)} %collective-permute-done.5.refs_5_), channel_id=1, source_target_pairs={{0,28},{4,0},{8,4},{12,8},{16,12},{20,16},{24,20},{28,24},{1,29},{... | collective-permute-start | bytes 884744 | tf_op jit(solution)/shard_map/ppermute | solution.py:38
  79.2 15.0 %collective-permute-start.7 = (bf16[96,1536]{1,0:T(8,128)(2,1)S(1)}, bf16[96,1536]{1,0:T(8,128)(2,1)S(1)}, u32[]{:S(2)}, u32[]{:S(2)}) collective-permute-start(bf16[96,1536]{1,0:T(8,128)(2,1)S(1)} %collective-permute-done.3.refs_4_), channel_id=1, source_target_pairs={{0,4},{4,8},{8,12},{12,16},{16,20},{20,24},{24,28},{28,0},{1,5},{5... | collective-permute-start | bytes 884744 | tf_op jit(solution)/shard_map/ppermute | solution.py:38
  82.5 12.7 %collective-permute-start.8 = (bf16[96,1536]{1,0:T(8,128)(2,1)S(1)}, bf16[96,1536]{1,0:T(8,128)(2,1)S(1)}, u32[]{:S(2)}, u32[]{:S(2)}) collective-permute-start(bf16[96,1536]{1,0:T(8,128)(2,1)S(1)} %collective-permute-done.4.refs_6_), channel_id=1, source_target_pairs={{0,4},{4,8},{8,12},{12,16},{16,20},{20,24},{24,28},{28,0},{1,5},{5... | collective-permute-start | bytes 884744 | tf_op jit(solution)/shard_map/ppermute | solution.py:38
  89.3 14.4 %collective-permute-start.14 = (bf16[96,1536]{1,0:T(8,128)(2,1)S(1)}, bf16[96,1536]{1,0:T(8,128)(2,1)S(1)}, u32[]{:S(2)}, u32[]{:S(2)}) collective-permute-start(bf16[96,1536]{1,0:T(8,128)(2,1)S(1)} %collective-permute-done.10.refs_11_), channel_id=1, source_target_pairs={{0,28},{4,0},{8,4},{12,8},{16,12},{20,16},{24,20},{28,24},{1,29},{... | collective-permute-start | bytes 884744 | tf_op jit(solution)/shard_map/ppermute | solution.py:38
  95.3 13.1 %collective-permute-start.13 = (bf16[96,1536]{1,0:T(8,128)(2,1)S(1)}, bf16[96,1536]{1,0:T(8,128)(2,1)S(1)}, u32[]{:S(2)}, u32[]{:S(2)}) collective-permute-start(bf16[96,1536]{1,0:T(8,128)(2,1)S(1)} %collective-permute-done.8.refs_10_), channel_id=1, source_target_pairs={{0,4},{4,8},{8,12},{12,16},{16,20},{20,24},{24,28},{28,0},{1,5},{5... | collective-permute-start | bytes 884744 | tf_op jit(solution)/shard_map/ppermute | solution.py:38
  97.7 13.3 %collective-permute-start.12 = (bf16[48,1536]{1,0:T(8,128)(2,1)S(1)}, bf16[48,1536]{1,0:T(8,128)(2,1)}, u32[]{:S(2)}, u32[]{:S(2)}) collective-permute-start(bf16[48,1536]{1,0:T(8,128)(2,1)S(1)} %slice.13), channel_id=1, source_target_pairs={{0,28},{4,0},{8,4},{12,8},{16,12},{20,16},{24,20},{28,24},{1,29},{... | collective-permute-start | bytes 442376 | tf_op jit(solution)/shard_map/ppermute | solution.py:38
  101.8 9.2 %collective-permute-start.11 = (bf16[48,1536]{1,0:T(8,128)(2,1)S(1)}, bf16[48,1536]{1,0:T(8,128)(2,1)}, u32[]{:S(2)}, u32[]{:S(2)}) collective-permute-start(bf16[48,1536]{1,0:T(8,128)(2,1)S(1)} %slice.12), channel_id=1, source_target_pairs={{0,4},{4,8},{8,12},{12,16},{16,20},{20,24},{24,28},{28,0},{1,5},{5... | collective-permute-start | bytes 442376 | tf_op jit(solution)/shard_map/ppermute | solution.py:38
  103.8 7.2 %collective-permute-start.16 = (bf16[48,1536]{1,0:T(8,128)(2,1)S(1)}, bf16[48,1536]{1,0:T(8,128)(2,1)S(1)}, u32[]{:S(2)}, u32[]{:S(2)}) collective-permute-start(bf16[48,1536]{1,0:T(8,128)(2,1)S(1)} %slice.17), channel_id=1, source_target_pairs={{0,28},{4,0},{8,4},{12,8},{16,12},{20,16},{24,20},{28,24},{1,29},{... | collective-permute-start | bytes 442376 | tf_op jit(solution)/shard_map/ppermute | solution.py:38
  108.4 7.1 %collective-permute-start.15 = (bf16[48,1536]{1,0:T(8,128)(2,1)S(1)}, bf16[48,1536]{1,0:T(8,128)(2,1)S(1)}, u32[]{:S(2)}, u32[]{:S(2)}) collective-permute-start(bf16[48,1536]{1,0:T(8,128)(2,1)S(1)} %slice.16), channel_id=1, source_target_pairs={{0,4},{4,8},{8,12},{12,16},{16,20},{20,24},{24,28},{28,0},{1,5},{5... | collective-permute-start | bytes 442376 | tf_op jit(solution)/shard_map/ppermute | solution.py:38
  129.8 9.6 %collective-permute-start.21 = (bf16[384,1536]{1,0:T(8,128)(2,1)}, bf16[384,1536]{1,0:T(8,128)(2,1)S(1)}, u32[]{:S(2)}, u32[]{:S(2)}) collective-permute-start(bf16[384,1536]{1,0:T(8,128)(2,1)} %get-tuple-element.63), channel_id=1, source_target_pairs={{0,1},{1,0},{2,3},{3,2},{4,5},{5,4},{6,7},{7,6},{8,9},{9,8},{10,11... | collective-permute-start | bytes 3538952 | tf_op jit(solution)/shard_map/ppermute | solution.py:46
  136.7 12.8 %collective-permute-start.17 = (bf16[384,1536]{1,0:T(8,128)(2,1)}, bf16[384,1536]{1,0:T(8,128)(2,1)S(1)}, u32[]{:S(2)}, u32[]{:S(2)}) collective-permute-start(bf16[384,1536]{1,0:T(8,128)(2,1)} %get-tuple-element.56), channel_id=1, source_target_pairs={{0,1},{1,0},{2,3},{3,2},{4,5},{5,4},{6,7},{7,6},{8,9},{9,8},{10,11... | collective-permute-start | bytes 3538952 | tf_op jit(solution)/shard_map/ppermute | solution.py:46
  140.9 15.1 %collective-permute-start.22 = (bf16[384,384]{1,0:T(8,128)(2,1)S(1)}, bf16[384,384]{1,0:T(8,128)(2,1)S(1)}, u32[]{:S(2)}, u32[]{:S(2)}) collective-permute-start(bf16[384,384]{1,0:T(8,128)(2,1)S(1)} %get-tuple-element.65), channel_id=1, source_target_pairs={{0,32},{32,64},{64,96},{96,0},{1,33},{33,65},{65,97},{97,1},{2,34}... | collective-permute-start | bytes 884744 | tf_op jit(solution)/shard_map/ppermute | solution.py:42
  143.3 16.8 %collective-permute-start.23 = (bf16[384,384]{1,0:T(8,128)(2,1)S(1)}, bf16[384,384]{1,0:T(8,128)(2,1)S(1)}, u32[]{:S(2)}, u32[]{:S(2)}) collective-permute-start(bf16[384,384]{1,0:T(8,128)(2,1)S(1)} %get-tuple-element.66), channel_id=1, source_target_pairs={{0,64},{32,96},{64,0},{96,32},{1,65},{33,97},{65,1},{97,33},{2,66}... | collective-permute-start | bytes 884744 | tf_op jit(solution)/shard_map/ppermute | solution.py:42
  147.0 14.4 %collective-permute-start.24 = (bf16[384,384]{1,0:T(8,128)(2,1)S(1)}, bf16[384,384]{1,0:T(8,128)(2,1)S(1)}, u32[]{:S(2)}, u32[]{:S(2)}) collective-permute-start(bf16[384,384]{1,0:T(8,128)(2,1)S(1)} %get-tuple-element.67), channel_id=1, source_target_pairs={{0,96},{32,0},{64,32},{96,64},{1,97},{33,1},{65,33},{97,65},{2,98}... | collective-permute-start | bytes 884744 | tf_op jit(solution)/shard_map/ppermute | solution.py:42
  149.9 33.5 %collective-permute-start.18 = (bf16[384,384]{1,0:T(8,128)(2,1)S(1)}, bf16[384,384]{1,0:T(8,128)(2,1)S(1)}, u32[]{:S(2)}, u32[]{:S(2)}) collective-permute-start(bf16[384,384]{1,0:T(8,128)(2,1)S(1)} %get-tuple-element.58), channel_id=1, source_target_pairs={{0,32},{32,64},{64,96},{96,0},{1,33},{33,65},{65,97},{97,1},{2,34}... | collective-permute-start | bytes 884744 | tf_op jit(solution)/shard_map/ppermute | solution.py:42
  152.6 30.7 %collective-permute-start.19 = (bf16[384,384]{1,0:T(8,128)(2,1)S(1)}, bf16[384,384]{1,0:T(8,128)(2,1)S(1)}, u32[]{:S(2)}, u32[]{:S(2)}) collective-permute-start(bf16[384,384]{1,0:T(8,128)(2,1)S(1)} %get-tuple-element.59), channel_id=1, source_target_pairs={{0,64},{32,96},{64,0},{96,32},{1,65},{33,97},{65,1},{97,33},{2,66}... | collective-permute-start | bytes 884744 | tf_op jit(solution)/shard_map/ppermute | solution.py:42
  156.1 27.3 %collective-permute-start.20 = (bf16[384,384]{1,0:T(8,128)(2,1)S(1)}, bf16[384,384]{1,0:T(8,128)(2,1)S(1)}, u32[]{:S(2)}, u32[]{:S(2)}) collective-permute-start(bf16[384,384]{1,0:T(8,128)(2,1)S(1)} %get-tuple-element.60), channel_id=1, source_target_pairs={{0,96},{32,0},{64,32},{96,64},{1,97},{33,1},{65,33},{97,65},{2,98}... | collective-permute-start | bytes 884744 | tf_op jit(solution)/shard_map/ppermute | solution.py:42
  161.7 14.4 %collective-permute-start.25 = (f32[1,384]{1,0:T(1,128)S(1)}, f32[1,384]{1,0:T(1,128)S(1)}, u32[]{:S(2)}, u32[]{:S(2)}) collective-permute-start(f32[1,384]{1,0:T(1,128)S(1)} %get-tuple-element.68), channel_id=1, source_target_pairs={{0,2},{2,0},{1,3},{3,1},{4,6},{6,4},{5,7},{7,5},{8,10},{10,8},{9,1... | collective-permute-start | bytes 4616 | tf_op jit(solution)/shard_map/ppermute | solution.py:46
  176.1 25.8 %collective-permute-start.26 = (bf16[384,384]{1,0:T(8,128)(2,1)S(1)}, bf16[384,384]{1,0:T(8,128)(2,1)S(1)}, u32[]{:S(2)}, u32[]{:S(2)}) collective-permute-start(bf16[384,384]{1,0:T(8,128)(2,1)S(1)} %get-tuple-element.70), channel_id=1, source_target_pairs={{0,2},{2,0},{1,3},{3,1},{4,6},{6,4},{5,7},{7,5},{8,10},{10,8},{9,1... | collective-permute-start | bytes 884744 | tf_op jit(solution)/shard_map/ppermute | solution.py:46
  184.3 17.6 %all-to-all-start.2 = ((f32[16,1,384]{2,1,0:T(1,128)}), f32[16,1,384]{2,1,0:T(1,128)S(1)}, u32[]{:S(2)}, u32[]{:S(2)}) async-start(f32[16,1,384]{2,1,0:T(1,128)} %broadcast_in_dim.12), calls=%async_computation.2 | async-start | bytes 49152 | tf_op jit(solution)/shard_map/all_to_all | solution.py:246
  (18 other events, 379.9 us)
Sparse Core Ops, SparseCore 0:
  37.9 68.9 all-gather.1

commit v7 on v3

--- a/solution.py
+++ b/solution.py
@@ -46,11 +46,7 @@
     return lax.ppermute(shard, axis, [(0, 1), (1, 0)])
 
 
-def spread_over(array):
-    return lax.all_to_all(array, ("x", "core"), split_axis=0, concat_axis=0, tiled=True)
-
-
-def weigh(place, mask, values, both, far, weighted):
+def weigh(place, mask, values, both, weighted):
     zhi = place[0]
     for i in range(ROWS // TILE):
         for j in range(UNIT // TILE):
@@ -59,24 +55,27 @@
     for chunk in range(X * CORE):
         for part in range(CORE):
             start = part * UNIT + chunk * SUB
-            both[chunk, 1 + part] = weighted[start : start + SUB].astype(BF16)
-    near = weighted[pl.ds(pl.multiple_of(zhi * HALF, HALF), HALF)].T.astype(BF16)
-    for chunk in range(X * CORE):
-        both[chunk, 0] = near[chunk * SUB : (chunk + 1) * SUB]
-    far[...] = weighted[pl.ds(pl.multiple_of((1 - zhi) * HALF, HALF), HALF)].T.astype(BF16)
-
-
-def settle(place, both, near, right, stack):
+            both[chunk, 2 + part] = weighted[start : start + SUB].astype(BF16)
+    for far in range(2):
+        start = (1 - zhi if far else zhi) * HALF
+        left = weighted[pl.ds(pl.multiple_of(start, HALF), HALF)].T.astype(BF16)
+        for chunk in range(X * CORE):
+            both[chunk, far] = left[chunk * SUB : (chunk + 1) * SUB]
+
+
+def settle(place, both, near, far, right, stack):
     core = place[1]
-    for x in range(X):
-        for part in range(CORE):
-            near[part * SUB : (part + 1) * SUB, x * HALF : (x + 1) * HALF] = both[x, part, 0]
+    for which, left in enumerate((near, far)):
+        for x in range(X):
+            for part in range(CORE):
+                at = (slice(part * SUB, (part + 1) * SUB), slice(x * HALF, (x + 1) * HALF))
+                left[at] = both[x, part, which]
     for own in range(2):
         source = core if own else 1 - core
         for x in range(X):
             for part in range(CORE):
                 at = (x * CORE + part) * SUB
-                stack[at : at + SUB] = both[x, source, 1 + part].astype(F32)
+                stack[at : at + SUB] = both[x, source, 2 + part].astype(F32)
         right[0, own * UNIT : (own + 1) * UNIT] = stack[...].T.astype(BF16)
 
 
@@ -113,21 +112,18 @@
             at = pl.ds(pl.multiple_of(i * step, step), step)
             product = jnp.dot(b[own], a[:, at], preferred_element_type=F32)
             theirs[:, at] = product[:UNIT].astype(BF16)
-            ours[:, at] = product[UNIT:]
-
-
-def add_core(place, ours, sent, first, second, third, own):
-    x = place[0]
-    pieces = [own, first, second, third]
+            ours[:, at] = product[UNIT:].astype(BF16)
+
+
+def add_core(place, ours, sent, *pieces):
     for step in range(X):
-        at = pl.ds(pl.multiple_of(lax.rem(x + step, X) * HALF, HALF), HALF)
-        total = ours[:, at] + sent[:, at].astype(F32)
-        pieces[step][...] = total.astype(pieces[step].dtype)
-
-
-def add_x(own, first, second, third, total, sums):
-    all_x = own[...] + first[...].astype(F32) + (second[...].astype(F32) + third[...].astype(F32))
-    turned = all_x.T
+        at = pl.ds(pl.multiple_of(lax.rem(place[0] + step, X) * HALF, HALF), HALF)
+        pieces[step][...] = (ours[:, at].astype(F32) + sent[:, at].astype(F32)).astype(BF16)
+
+
+def add_x(*refs):
+    pieces, total, sums = refs[:X], refs[X], refs[X + 1]
+    turned = sum(piece[...].astype(F32) for piece in pieces).T
     total[...] = turned.astype(total.dtype)
     sums[...] = jnp.sum(turned * turned, axis=0, keepdims=True)
 
@@ -159,7 +155,6 @@
             up, down = ends[which]
             up, down = shift_y(up, 1), shift_y(down, -1)
             if d == 1 and which == 0:
-                up, far = in_order(up, far)
                 ends[1] = [far, far]
                 shards.append(far)
                 order.append((1, 0, 0, CORE * SUB))
@@ -177,31 +172,27 @@
     x, y, core, zhi = (lax.axis_index(a) for a in ("x", "y", "core", "zhi"))
     place = jnp.stack([zhi, core])
 
-    both, far = call(
+    both = call(
         weigh,
-        [((X * CORE, 3, SUB, UNIT), BF16), ((UNIT, HALF), BF16)],
+        [((X * CORE, 4, SUB, UNIT), BF16)],
         [SMEM, SMEM, VMEM],
         (place, tile_mask, values),
         [pltpu.VMEM((ROWS, UNIT), F32)],
-    )
-    far = swap(far, "zhi")
-    both = spread_over(both)
-    both, far = in_order(both, far)
-    far = spread_over(far.reshape(X * CORE, SUB, HALF))
-    near, right = call(
+    )[0]
+    both = lax.all_to_all(both, ("x", "core"), split_axis=0, concat_axis=0, tiled=True)
+    near, far, right = call(
         settle,
-        [((CORE * SUB, WIDE), BF16), ((1, CORE * UNIT, UNIT), BF16)],
+        [((CORE * SUB, WIDE), BF16)] * 2 + [((1, CORE * UNIT, UNIT), BF16)],
         [SMEM, VMEM],
-        (place, both.reshape(X, CORE, 3, SUB, UNIT)),
+        (place, both.reshape(X, CORE, 4, SUB, UNIT)),
         [pltpu.VMEM((UNIT, UNIT), F32)],
     )
     right = lax.all_gather(right, ("zhi", "zlo"), axis=0, tiled=True)
-    far = far.reshape(X, CORE * SUB, HALF).transpose(1, 0, 2).reshape(CORE * SUB, WIDE)
-    shards, order = rings(near, far)
+    shards, order = rings(near, swap(far, "zhi"))
 
     theirs, ours, theirs_near, ours_near = call(
         functools.partial(multiply, order),
-        [((UNIT, WIDE), BF16), ((UNIT, WIDE), F32)] * 2,
+        [((UNIT, WIDE), BF16)] * 4,
         [SMEM] + [HBM] * (len(shards) + 1),
         (jnp.stack([y, zhi]), *shards, right),
         [
@@ -213,23 +204,24 @@
         vmem=60,
     )
 
-    def over_x(ours, sent):
-        pieces = call(
+    def total(apart, dtype):
+        return call(add_x, [((HALF, UNIT), dtype), ((1, UNIT), F32)], [VMEM] * X, apart)
+
+    def over_x(ours, theirs):
+        apart = call(
             add_core,
-            [((UNIT, HALF), BF16)] * 3 + [((UNIT, HALF), F32)],
+            [((UNIT, HALF), BF16)] * X,
             [SMEM, VMEM, VMEM],
-            (x[None], ours, sent),
+            (x[None], ours, swap(theirs, "core")),
         )
-        return pieces[3], *(shift_x(pieces[step - 1], step) for step in range(1, X))
-
-    def total(pieces, dtype):
-        return call(add_x, [((HALF, UNIT), dtype), ((1, UNIT), F32)], [VMEM] * 4, pieces)
-
-    pieces = over_x(ours, swap(theirs, "core"))
-    pieces_near = over_x(ours_near, swap(theirs_near, "core"))
-    other, sums = total(pieces, BF16)
-    sums, other = swap(sums, "zhi"), swap(other, "zhi")
-    mine, own_sums = total(pieces_near, F32)
+        return [apart[0]] + [shift_x(apart[step], step) for step in range(1, X)]
+
+    apart = over_x(ours, theirs)
+    apart_near = over_x(ours_near, theirs_near)
+    other, sums = total(apart, BF16)
+    sums, other = in_order(swap(sums, "zhi"), other)
+    other = swap(other, "zhi")
+    mine, own_sums = total(apart_near, F32)
     sums = jnp.broadcast_to(sums + own_sums, (Z_LO * X, 1, UNIT))
     sums = lax.all_to_all(sums, ("zlo", "x"), split_axis=0, concat_axis=0, tiled=True)
     return call(

time: 202 us -> 203 us (level)
  blocking collectives: 0 us -> 21.6 us
  waiting for transfers between devices: 38.6 us -> 24.8 us
  starting transfers between devices: 122 us -> 118 us
    all_to_all x0 -> x1, blocking collectives: none -> 21.6 us  [local(): lax.all_to_all(both, ('x', 'core'), split_axis=0, concat_axis=0, tiled=True)]
    ppermute x5, waiting for transfers between devices: 17.4 us -> 6.92 us  [swap(): return lax.ppermute(shard, axis, [(0, 1), (1, 0)])]
    all_to_all x2 -> x0, starting transfers between devices: 8.76 us -> none  [spread_over(): lax.all_to_all(array, ('x', 'core'), split_axis=0, concat_axis=0, tiled=T...]
    all_to_all x2 -> x0, waiting for transfers between devices: 5.98 us -> none  [spread_over(): lax.all_to_all(array, ('x', 'core'), split_axis=0, concat_axis=0, tiled=T...]
    all_to_all x1, starting transfers between devices: 8.18 us -> 12 us  [local(): lax.all_to_all(sums, ('zlo', 'x'), split_axis=0, concat_axis=0, tiled=True)]
    ppermute x6, starting transfers between devices: 20.4 us -> 17.8 us  [shift_x(): return lax.ppermute(shard, 'x', [(i, (i + step) % X) for i in range(X)])]
    ppermute x6, waiting for transfers between devices: 1.54 us -> 4.12 us  [shift_x(): return lax.ppermute(shard, 'x', [(i, (i + step) % X) for i in range(X)])]
    ppermute x16, starting transfers between devices: 53.4 us -> 55.8 us  [shift_y(): return lax.ppermute(shard, 'y', [(i, (i + step) % Y) for i in range(Y)])]
  transfers between devices with their start and end apart: 31 -> 29, of which waited for: 7 -> 7; matrix products, arithmetic and copies ran while one was open for 1% -> 1% of each run, Pallas kernels for 1% -> 1%
where the time goes in v7:
time: 203 us; the launch traced here: 202 us
  starting transfers between devices  118 us (58%)
  waiting for transfers between devices  24.8 us (12%)
  blocking collectives  21.6 us (11%)
  Pallas kernels  19.1 us (9%)
  between operations  14 us (7%)
  local copies, waits for them, and re-layouts  4.14 us (2%)
    ppermute x16, starting transfers between devices, shift_y(): return lax.ppermute(shard, 'y', [(i, (i + step) % Y) for i in range(Y)])  55.8 us
    ppermute x5, starting transfers between devices, swap(): return lax.ppermute(shard, axis, [(0, 1), (1, 0)])  32.2 us
    all_to_all x1, blocking collectives, local(): lax.all_to_all(both, ('x', 'core'), split_axis=0, concat_axis=0, tiled=True)  21.6 us
    pallas_call x8, Pallas kernels, call(): pl.pallas_call(body, out_shape=shapes, in_specs=ins, out_specs=[VMEM] * l...  19.1 us
    ppermute x6, starting transfers between devices, shift_x(): return lax.ppermute(shard, 'x', [(i, (i + step) % X) for i in range(X)])  17.8 us
    all_to_all x1, starting transfers between devices, local(): lax.all_to_all(sums, ('zlo', 'x'), split_axis=0, concat_axis=0, tiled=True)  12 us
    all_to_all x1, waiting for transfers between devices, local(): lax.all_to_all(sums, ('zlo', 'x'), split_axis=0, concat_axis=0, tiled=True)  7.97 us
    ppermute x5, waiting for transfers between devices, swap(): return lax.ppermute(shard, axis, [(0, 1), (1, 0)])  6.92 us
  transfers between devices with their start and end apart: 29, of which 7 were waited for; matrix products, arithmetic and copies ran while one was open for 1% of the time, Pallas kernels for 1%

profile of v7, /device:TPU:24, one launch (start us, length us, event | category | flops | bytes accessed | tf_op | source)
XLA Modules:
  0.0 202.2 jit_solution(18207293375259398879)
XLA Ops:
  9.6 21.6 %all_to_all.10 = bf16[8,4,48,384]{3,2,1,0:T(8,128)(2,1)S(1)} all-to-all(bf16[8,4,48,384]{3,2,1,0:T(8,128)(2,1)S(1)} %shard_map.37), channel_id=1, replica_groups=mesh['zlo'=4,'x'=4,'y'=8,'zhi'=2,'core'=2] {'x','core'}, dimensions={0} | all-to-all | bytes 2359296 | tf_op jit(solution)/shard_map/all_to_all | solution.py:182
  32.8 10.9 %collective-permute-start = (bf16[96,1536]{1,0:T(8,128)(2,1)S(1)}, bf16[96,1536]{1,0:T(8,128)(2,1)S(1)}, u32[]{:S(2)}, u32[]{:S(2)}) collective-permute-start(bf16[96,1536]{1,0:T(8,128)(2,1)S(1)} %get-tuple-element.27), channel_id=1, source_target_pairs={{0,2},{2,0},{1,3},{3,1},{4,6},{6,4},{5,7},{7,5},{8,10},{10,8},{9,1... | collective-permute-start | bytes 884744 | tf_op jit(solution)/shard_map/ppermute | solution.py:46
  43.8 4.7 %collective-permute-start.1 = (bf16[96,1536]{1,0:T(8,128)(2,1)S(1)}, bf16[96,1536]{1,0:T(8,128)(2,1)S(1)}, u32[]{:S(2)}, u32[]{:S(2)}) collective-permute-start(bf16[96,1536]{1,0:T(8,128)(2,1)S(1)} %get-tuple-element.26.refs_0_), channel_id=1, source_target_pairs={{0,4},{4,8},{8,12},{12,16},{16,20},{20,24},{24,28},{28,0},{1,5},{5... | collective-permute-start | bytes 884744 | tf_op jit(solution)/shard_map/ppermute | solution.py:38
  48.5 1.9 collective-permute-start.2
  50.4 4.8 %collective-permute-done.refs_1_ = bf16[96,1536]{1,0:T(8,128)(2,1)S(1)} collective-permute-done((bf16[96,1536]{1,0:T(8,128)(2,1)S(1)}, bf16[96,1536]{1,0:T(8,128)(2,1)S(1)}, u32[]{:S(2)}, u32[]{:S(2)}) %collective-permute-start) | collective-permute-done | bytes 294944 | tf_op jit(solution)/shard_map/ppermute | solution.py:46
  55.2 4.9 %collective-permute-start.3 = (bf16[96,1536]{1,0:T(8,128)(2,1)S(1)}, bf16[96,1536]{1,0:T(8,128)(2,1)S(1)}, u32[]{:S(2)}, u32[]{:S(2)}) collective-permute-start(bf16[96,1536]{1,0:T(8,128)(2,1)S(1)} %collective-permute-done.refs_1_), channel_id=1, source_target_pairs={{0,4},{4,8},{8,12},{12,16},{16,20},{20,24},{24,28},{28,0},{1,5},{5... | collective-permute-start | bytes 884744 | tf_op jit(solution)/shard_map/ppermute | solution.py:38
  60.1 1.9 collective-permute-start.4
  62.0 5.1 %collective-permute-start.5 = (bf16[96,1536]{1,0:T(8,128)(2,1)S(1)}, bf16[96,1536]{1,0:T(8,128)(2,1)S(1)}, u32[]{:S(2)}, u32[]{:S(2)}) collective-permute-start(bf16[96,1536]{1,0:T(8,128)(2,1)S(1)} %collective-permute-done.1.refs_2_), channel_id=1, source_target_pairs={{0,4},{4,8},{8,12},{12,16},{16,20},{20,24},{24,28},{28,0},{1,5},{5... | collective-permute-start | bytes 884744 | tf_op jit(solution)/shard_map/ppermute | solution.py:38
  67.2 1.9 collective-permute-start.6
  69.2 5.1 %collective-permute-start.7 = (bf16[96,1536]{1,0:T(8,128)(2,1)S(1)}, bf16[96,1536]{1,0:T(8,128)(2,1)S(1)}, u32[]{:S(2)}, u32[]{:S(2)}) collective-permute-start(bf16[96,1536]{1,0:T(8,128)(2,1)S(1)} %collective-permute-done.3.refs_4_), channel_id=1, source_target_pairs={{0,4},{4,8},{8,12},{12,16},{16,20},{20,24},{24,28},{28,0},{1,5},{5... | collective-permute-start | bytes 884744 | tf_op jit(solution)/shard_map/ppermute | solution.py:38
  74.3 1.9 collective-permute-start.8
  76.3 5.1 %collective-permute-start.9 = (bf16[96,1536]{1,0:T(8,128)(2,1)S(1)}, bf16[96,1536]{1,0:T(8,128)(2,1)S(1)}, u32[]{:S(2)}, u32[]{:S(2)}) collective-permute-start(bf16[96,1536]{1,0:T(8,128)(2,1)S(1)} %collective-permute-done.5.refs_6_), channel_id=1, source_target_pairs={{0,4},{4,8},{8,12},{12,16},{16,20},{20,24},{24,28},{28,0},{1,5},{5... | collective-permute-start | bytes 884744 | tf_op jit(solution)/shard_map/ppermute | solution.py:38
  81.4 1.9 collective-permute-start.10
  83.4 5.1 %collective-permute-start.11 = (bf16[96,1536]{1,0:T(8,128)(2,1)S(1)}, bf16[96,1536]{1,0:T(8,128)(2,1)S(1)}, u32[]{:S(2)}, u32[]{:S(2)}) collective-permute-start(bf16[96,1536]{1,0:T(8,128)(2,1)S(1)} %collective-permute-done.7.refs_8_), channel_id=1, source_target_pairs={{0,4},{4,8},{8,12},{12,16},{16,20},{20,24},{24,28},{28,0},{1,5},{5... | collective-permute-start | bytes 884744 | tf_op jit(solution)/shard_map/ppermute | solution.py:38
  88.5 1.9 collective-permute-start.12
  90.5 5.1 %collective-permute-start.13 = (bf16[48,1536]{1,0:T(8,128)(2,1)S(1)}, bf16[48,1536]{1,0:T(8,128)(2,1)}, u32[]{:S(2)}, u32[]{:S(2)}) collective-permute-start(bf16[48,1536]{1,0:T(8,128)(2,1)S(1)} %slice.16), channel_id=1, source_target_pairs={{0,4},{4,8},{8,12},{12,16},{16,20},{20,24},{24,28},{28,0},{1,5},{5... | collective-permute-start | bytes 442376 | tf_op jit(solution)/shard_map/ppermute | solution.py:38
  95.7 1.9 collective-permute-start.14
  97.7 5.1 %collective-permute-start.15 = (bf16[48,1536]{1,0:T(8,128)(2,1)S(1)}, bf16[48,1536]{1,0:T(8,128)(2,1)}, u32[]{:S(2)}, u32[]{:S(2)}) collective-permute-start(bf16[48,1536]{1,0:T(8,128)(2,1)S(1)} %slice.18), channel_id=1, source_target_pairs={{0,4},{4,8},{8,12},{12,16},{16,20},{20,24},{24,28},{28,0},{1,5},{5... | collective-permute-start | bytes 442376 | tf_op jit(solution)/shard_map/ppermute | solution.py:38
  102.9 1.9 collective-permute-start.16
  105.5 5.7 %collective-permute-done.16.refs_17_ = bf16[48,1536]{1,0:T(8,128)(2,1)} collective-permute-done((bf16[48,1536]{1,0:T(8,128)(2,1)S(1)}, bf16[48,1536]{1,0:T(8,128)(2,1)}, u32[]{:S(2)}, u32[]{:S(2)}) %collective-permute-start.16) | collective-permute-done | bytes 147488 | tf_op jit(solution)/shard_map/ppermute | solution.py:38
  111.3 13.6 %shard_map.39 = (bf16[384,1536]{1,0:T(8,128)(2,1)}, bf16[384,1536]{1,0:T(8,128)(2,1)}, bf16[384,1536]{1,0:T(8,128)(2,1)}, bf16[384,1536]{1,0:T(8,128)(2,1)}) custom-call(s32[2]{0:T(128)} %pad_add_fusion.place, bf16[96,1536]{1,0:T(8,128)(2,1)} %copy-done.3, bf16[96,1536]{1,0:T(8,128)(2,1)} %copy-done.9, bf16[96,1536]{1,0:T(8,128)(2,1)} %copy-done.10, ...), custom_call_target="tpu_custom_call" | custom-call | flops 7247757312 | bytes 14155784 | tf_op jit(solution)/shard_map/pallas_call | solution.py:26
  126.9 2.4 %collective-permute-start.17 = (bf16[384,1536]{1,0:T(8,128)(2,1)}, bf16[384,1536]{1,0:T(8,128)(2,1)S(1)}, u32[]{:S(2)}, u32[]{:S(2)}) collective-permute-start(bf16[384,1536]{1,0:T(8,128)(2,1)} %get-tuple-element.30), channel_id=1, source_target_pairs={{0,1},{1,0},{2,3},{3,2},{4,5},{5,4},{6,7},{7,6},{8,9},{9,8},{10,11... | collective-permute-start | bytes 3538952 | tf_op jit(solution)/shard_map/ppermute | solution.py:46
  131.5 2.1 %collective-permute-start.22 = (bf16[384,384]{1,0:T(8,128)(2,1)S(1)}, bf16[384,384]{1,0:T(8,128)(2,1)S(1)}, u32[]{:S(2)}, u32[]{:S(2)}) collective-permute-start(bf16[384,384]{1,0:T(8,128)(2,1)S(1)} %get-tuple-element.39), channel_id=1, source_target_pairs={{0,32},{32,64},{64,96},{96,0},{1,33},{33,65},{65,97},{97,1},{2,34}... | collective-permute-start | bytes 884744 | tf_op jit(solution)/shard_map/ppermute | solution.py:42
  133.5 1.9 collective-permute-start.23
  135.5 5.1 %collective-permute-start.24 = (bf16[384,384]{1,0:T(8,128)(2,1)S(1)}, bf16[384,384]{1,0:T(8,128)(2,1)S(1)}, u32[]{:S(2)}, u32[]{:S(2)}) collective-permute-start(bf16[384,384]{1,0:T(8,128)(2,1)S(1)} %get-tuple-element.41), channel_id=1, source_target_pairs={{0,96},{32,0},{64,32},{96,64},{1,97},{33,1},{65,33},{97,65},{2,98}... | collective-permute-start | bytes 884744 | tf_op jit(solution)/shard_map/ppermute | solution.py:42
  140.9 2.8 %collective-permute-start.18 = (bf16[384,384]{1,0:T(8,128)(2,1)S(1)}, bf16[384,384]{1,0:T(8,128)(2,1)S(1)}, u32[]{:S(2)}, u32[]{:S(2)}) collective-permute-start(bf16[384,384]{1,0:T(8,128)(2,1)S(1)} %get-tuple-element.32), channel_id=1, source_target_pairs={{0,32},{32,64},{64,96},{96,0},{1,33},{33,65},{65,97},{97,1},{2,34}... | collective-permute-start | bytes 884744 | tf_op jit(solution)/shard_map/ppermute | solution.py:42
  143.7 4.0 %collective-permute-start.19 = (bf16[384,384]{1,0:T(8,128)(2,1)S(1)}, bf16[384,384]{1,0:T(8,128)(2,1)S(1)}, u32[]{:S(2)}, u32[]{:S(2)}) collective-permute-start(bf16[384,384]{1,0:T(8,128)(2,1)S(1)} %get-tuple-element.33), channel_id=1, source_target_pairs={{0,64},{32,96},{64,0},{96,32},{1,65},{33,97},{65,1},{97,33},{2,66}... | collective-permute-start | bytes 884744 | tf_op jit(solution)/shard_map/ppermute | solution.py:42
  147.7 3.2 %collective-permute-done.22.refs_1_ = bf16[384,384]{1,0:T(8,128)(2,1)S(1)} collective-permute-done((bf16[384,384]{1,0:T(8,128)(2,1)S(1)}, bf16[384,384]{1,0:T(8,128)(2,1)S(1)}, u32[]{:S(2)}, u32[]{:S(2)}) %collective-permute-start.22) | collective-permute-done | bytes 294944 | tf_op jit(solution)/shard_map/ppermute | solution.py:42
  154.0 9.1 %collective-permute-start.25 = (f32[1,384]{1,0:T(1,128)S(1)}, f32[1,384]{1,0:T(1,128)S(1)}, u32[]{:S(2)}, u32[]{:S(2)}) collective-permute-start(f32[1,384]{1,0:T(1,128)S(1)} %get-tuple-element.42), channel_id=1, source_target_pairs={{0,2},{2,0},{1,3},{3,1},{4,6},{6,4},{5,7},{7,5},{8,10},{10,8},{9,1... | collective-permute-start | bytes 4616 | tf_op jit(solution)/shard_map/ppermute | solution.py:46
  164.7 7.8 %collective-permute-start.26 = (bf16[384,384]{1,0:T(8,128)(2,1)S(1)}, bf16[384,384]{1,0:T(8,128)(2,1)S(1)}, u32[]{:S(2)}, u32[]{:S(2)}) collective-permute-start(bf16[384,384]{1,0:T(8,128)(2,1)S(1)} %get-tuple-element.44), channel_id=1, source_target_pairs={{0,2},{2,0},{1,3},{3,1},{4,6},{6,4},{5,7},{7,5},{8,10},{10,8},{9,1... | collective-permute-start | bytes 884744 | tf_op jit(solution)/shard_map/ppermute | solution.py:46
  173.5 12.0 %all-to-all-start.1 = ((f32[16,1,384]{2,1,0:T(1,128)}), f32[16,1,384]{2,1,0:T(1,128)S(1)}, u32[]{:S(2)}, u32[]{:S(2)}) async-start(f32[16,1,384]{2,1,0:T(1,128)} %broadcast_in_dim.12), calls=%async_computation.1 | async-start | bytes 49152 | tf_op jit(solution)/shard_map/all_to_all | solution.py:226
  185.6 8.0 %all-to-all-done.1.sums = f32[16,1,384]{2,1,0:T(1,128)S(1)} async-done(((f32[16,1,384]{2,1,0:T(1,128)}), f32[16,1,384]{2,1,0:T(1,128)S(1)}, u32[]{:S(2)}, u32[]{:S(2)}) %all-to-all-start.1) | async-done | bytes 24608 | tf_op jit(solution)/shard_map/all_to_all | solution.py:226
  (82 shorter events, 17.3 us)
Async XLA Ops:
  6.5 104.7 %all-gather.2.cloned.1.call-start = ((), (), s32[]{:S(2)}) async-start(), calls=%async_computation.2 | async-start | bytes 5308416 | tf_op jit(solution)/shard_map/all_gather | solution.py:190
  32.8 78.4 %copy-start.3 = (bf16[96,1536]{1,0:T(8,128)(2,1)}, bf16[96,1536]{1,0:T(8,128)(2,1)S(1)}, u32[]{:S(2)}) copy-start(bf16[96,1536]{1,0:T(8,128)(2,1)S(1)} %get-tuple-element.26.refs_0_) | copy-start | bytes 884740
  32.8 22.3 %collective-permute-start = (bf16[96,1536]{1,0:T(8,128)(2,1)S(1)}, bf16[96,1536]{1,0:T(8,128)(2,1)S(1)}, u32[]{:S(2)}, u32[]{:S(2)}) collective-permute-start(bf16[96,1536]{1,0:T(8,128)(2,1)S(1)} %get-tuple-element.27), channel_id=1, source_target_pairs={{0,2},{2,0},{1,3},{3,1},{4,6},{6,4},{5,7},{7,5},{8,10},{10,8},{9,1... | collective-permute-start | bytes 884744 | tf_op jit(solution)/shard_map/ppermute | solution.py:46
  43.8 18.3 %collective-permute-start.1 = (bf16[96,1536]{1,0:T(8,128)(2,1)S(1)}, bf16[96,1536]{1,0:T(8,128)(2,1)S(1)}, u32[]{:S(2)}, u32[]{:S(2)}) collective-permute-start(bf16[96,1536]{1,0:T(8,128)(2,1)S(1)} %get-tuple-element.26.refs_0_), channel_id=1, source_target_pairs={{0,4},{4,8},{8,12},{12,16},{16,20},{20,24},{24,28},{28,0},{1,5},{5... | collective-permute-start | bytes 884744 | tf_op jit(solution)/shard_map/ppermute | solution.py:38
  48.5 18.7 %collective-permute-start.2 = (bf16[96,1536]{1,0:T(8,128)(2,1)S(1)}, bf16[96,1536]{1,0:T(8,128)(2,1)S(1)}, u32[]{:S(2)}, u32[]{:S(2)}) collective-permute-start(bf16[96,1536]{1,0:T(8,128)(2,1)S(1)} %get-tuple-element.26.refs_0_), channel_id=1, source_target_pairs={{0,28},{4,0},{8,4},{12,8},{16,12},{20,16},{24,20},{28,24},{1,29},{... | collective-permute-start | bytes 884744 | tf_op jit(solution)/shard_map/ppermute | solution.py:38
  55.2 56.1 %copy-start.9 = (bf16[96,1536]{1,0:T(8,128)(2,1)}, bf16[96,1536]{1,0:T(8,128)(2,1)S(1)}, u32[]{:S(2)}) copy-start(bf16[96,1536]{1,0:T(8,128)(2,1)S(1)} %collective-permute-done.refs_1_) | copy-start | bytes 884740
  55.2 14.0 %collective-permute-start.3 = (bf16[96,1536]{1,0:T(8,128)(2,1)S(1)}, bf16[96,1536]{1,0:T(8,128)(2,1)S(1)}, u32[]{:S(2)}, u32[]{:S(2)}) collective-permute-start(bf16[96,1536]{1,0:T(8,128)(2,1)S(1)} %collective-permute-done.refs_1_), channel_id=1, source_target_pairs={{0,4},{4,8},{8,12},{12,16},{16,20},{20,24},{24,28},{28,0},{1,5},{5... | collective-permute-start | bytes 884744 | tf_op jit(solution)/shard_map/ppermute | solution.py:38
  60.1 14.2 %collective-permute-start.4 = (bf16[96,1536]{1,0:T(8,128)(2,1)S(1)}, bf16[96,1536]{1,0:T(8,128)(2,1)S(1)}, u32[]{:S(2)}, u32[]{:S(2)}) collective-permute-start(bf16[96,1536]{1,0:T(8,128)(2,1)S(1)} %collective-permute-done.refs_1_), channel_id=1, source_target_pairs={{0,28},{4,0},{8,4},{12,8},{16,12},{20,16},{24,20},{28,24},{1,29},{... | collective-permute-start | bytes 884744 | tf_op jit(solution)/shard_map/ppermute | solution.py:38
  62.0 49.2 %copy-start.10 = (bf16[96,1536]{1,0:T(8,128)(2,1)}, bf16[96,1536]{1,0:T(8,128)(2,1)S(1)}, u32[]{:S(2)}) copy-start(bf16[96,1536]{1,0:T(8,128)(2,1)S(1)} %collective-permute-done.1.refs_2_) | copy-start | bytes 884740
  62.0 14.2 %collective-permute-start.5 = (bf16[96,1536]{1,0:T(8,128)(2,1)S(1)}, bf16[96,1536]{1,0:T(8,128)(2,1)S(1)}, u32[]{:S(2)}, u32[]{:S(2)}) collective-permute-start(bf16[96,1536]{1,0:T(8,128)(2,1)S(1)} %collective-permute-done.1.refs_2_), channel_id=1, source_target_pairs={{0,4},{4,8},{8,12},{12,16},{16,20},{20,24},{24,28},{28,0},{1,5},{5... | collective-permute-start | bytes 884744 | tf_op jit(solution)/shard_map/ppermute | solution.py:38
  67.2 14.2 %collective-permute-start.6 = (bf16[96,1536]{1,0:T(8,128)(2,1)S(1)}, bf16[96,1536]{1,0:T(8,128)(2,1)S(1)}, u32[]{:S(2)}, u32[]{:S(2)}) collective-permute-start(bf16[96,1536]{1,0:T(8,128)(2,1)S(1)} %collective-permute-done.2.refs_3_), channel_id=1, source_target_pairs={{0,28},{4,0},{8,4},{12,8},{16,12},{20,16},{24,20},{28,24},{1,29},{... | collective-permute-start | bytes 884744 | tf_op jit(solution)/shard_map/ppermute | solution.py:38
  69.2 14.2 %collective-permute-start.7 = (bf16[96,1536]{1,0:T(8,128)(2,1)S(1)}, bf16[96,1536]{1,0:T(8,128)(2,1)S(1)}, u32[]{:S(2)}, u32[]{:S(2)}) collective-permute-start(bf16[96,1536]{1,0:T(8,128)(2,1)S(1)} %collective-permute-done.3.refs_4_), channel_id=1, source_target_pairs={{0,4},{4,8},{8,12},{12,16},{16,20},{20,24},{24,28},{28,0},{1,5},{5... | collective-permute-start | bytes 884744 | tf_op jit(solution)/shard_map/ppermute | solution.py:38
  74.3 14.2 %collective-permute-start.8 = (bf16[96,1536]{1,0:T(8,128)(2,1)S(1)}, bf16[96,1536]{1,0:T(8,128)(2,1)S(1)}, u32[]{:S(2)}, u32[]{:S(2)}) collective-permute-start(bf16[96,1536]{1,0:T(8,128)(2,1)S(1)} %collective-permute-done.4.refs_5_), channel_id=1, source_target_pairs={{0,28},{4,0},{8,4},{12,8},{16,12},{20,16},{24,20},{28,24},{1,29},{... | collective-permute-start | bytes 884744 | tf_op jit(solution)/shard_map/ppermute | solution.py:38
  76.3 14.2 %collective-permute-start.9 = (bf16[96,1536]{1,0:T(8,128)(2,1)S(1)}, bf16[96,1536]{1,0:T(8,128)(2,1)S(1)}, u32[]{:S(2)}, u32[]{:S(2)}) collective-permute-start(bf16[96,1536]{1,0:T(8,128)(2,1)S(1)} %collective-permute-done.5.refs_6_), channel_id=1, source_target_pairs={{0,4},{4,8},{8,12},{12,16},{16,20},{20,24},{24,28},{28,0},{1,5},{5... | collective-permute-start | bytes 884744 | tf_op jit(solution)/shard_map/ppermute | solution.py:38
  81.4 14.2 %collective-permute-start.10 = (bf16[96,1536]{1,0:T(8,128)(2,1)S(1)}, bf16[96,1536]{1,0:T(8,128)(2,1)S(1)}, u32[]{:S(2)}, u32[]{:S(2)}) collective-permute-start(bf16[96,1536]{1,0:T(8,128)(2,1)S(1)} %collective-permute-done.6.refs_7_), channel_id=1, source_target_pairs={{0,28},{4,0},{8,4},{12,8},{16,12},{20,16},{24,20},{28,24},{1,29},{... | collective-permute-start | bytes 884744 | tf_op jit(solution)/shard_map/ppermute | solution.py:38
  83.4 14.3 %collective-permute-start.11 = (bf16[96,1536]{1,0:T(8,128)(2,1)S(1)}, bf16[96,1536]{1,0:T(8,128)(2,1)S(1)}, u32[]{:S(2)}, u32[]{:S(2)}) collective-permute-start(bf16[96,1536]{1,0:T(8,128)(2,1)S(1)} %collective-permute-done.7.refs_8_), channel_id=1, source_target_pairs={{0,4},{4,8},{8,12},{12,16},{16,20},{20,24},{24,28},{28,0},{1,5},{5... | collective-permute-start | bytes 884744 | tf_op jit(solution)/shard_map/ppermute | solution.py:38
  88.5 14.3 %collective-permute-start.12 = (bf16[96,1536]{1,0:T(8,128)(2,1)S(1)}, bf16[96,1536]{1,0:T(8,128)(2,1)S(1)}, u32[]{:S(2)}, u32[]{:S(2)}) collective-permute-start(bf16[96,1536]{1,0:T(8,128)(2,1)S(1)} %collective-permute-done.8.refs_9_), channel_id=1, source_target_pairs={{0,28},{4,0},{8,4},{12,8},{16,12},{20,16},{24,20},{28,24},{1,29},{... | collective-permute-start | bytes 884744 | tf_op jit(solution)/shard_map/ppermute | solution.py:38
  90.5 15.0 %collective-permute-start.13 = (bf16[48,1536]{1,0:T(8,128)(2,1)S(1)}, bf16[48,1536]{1,0:T(8,128)(2,1)}, u32[]{:S(2)}, u32[]{:S(2)}) collective-permute-start(bf16[48,1536]{1,0:T(8,128)(2,1)S(1)} %slice.16), channel_id=1, source_target_pairs={{0,4},{4,8},{8,12},{12,16},{16,20},{20,24},{24,28},{28,0},{1,5},{5... | collective-permute-start | bytes 442376 | tf_op jit(solution)/shard_map/ppermute | solution.py:38
  95.7 9.8 %collective-permute-start.14 = (bf16[48,1536]{1,0:T(8,128)(2,1)S(1)}, bf16[48,1536]{1,0:T(8,128)(2,1)}, u32[]{:S(2)}, u32[]{:S(2)}) collective-permute-start(bf16[48,1536]{1,0:T(8,128)(2,1)S(1)} %slice.17), channel_id=1, source_target_pairs={{0,28},{4,0},{8,4},{12,8},{16,12},{20,16},{24,20},{28,24},{1,29},{... | collective-permute-start | bytes 442376 | tf_op jit(solution)/shard_map/ppermute | solution.py:38
  97.7 7.8 %collective-permute-start.15 = (bf16[48,1536]{1,0:T(8,128)(2,1)S(1)}, bf16[48,1536]{1,0:T(8,128)(2,1)}, u32[]{:S(2)}, u32[]{:S(2)}) collective-permute-start(bf16[48,1536]{1,0:T(8,128)(2,1)S(1)} %slice.18), channel_id=1, source_target_pairs={{0,4},{4,8},{8,12},{12,16},{16,20},{20,24},{24,28},{28,0},{1,5},{5... | collective-permute-start | bytes 442376 | tf_op jit(solution)/shard_map/ppermute | solution.py:38
  102.9 8.4 %collective-permute-start.16 = (bf16[48,1536]{1,0:T(8,128)(2,1)S(1)}, bf16[48,1536]{1,0:T(8,128)(2,1)}, u32[]{:S(2)}, u32[]{:S(2)}) collective-permute-start(bf16[48,1536]{1,0:T(8,128)(2,1)S(1)} %slice.19), channel_id=1, source_target_pairs={{0,28},{4,0},{8,4},{12,8},{16,12},{20,16},{24,20},{28,24},{1,29},{... | collective-permute-start | bytes 442376 | tf_op jit(solution)/shard_map/ppermute | solution.py:38
  125.0 5.0 %collective-permute-start.21 = (bf16[384,1536]{1,0:T(8,128)(2,1)}, bf16[384,1536]{1,0:T(8,128)(2,1)S(1)}, u32[]{:S(2)}, u32[]{:S(2)}) collective-permute-start(bf16[384,1536]{1,0:T(8,128)(2,1)} %get-tuple-element.37), channel_id=1, source_target_pairs={{0,1},{1,0},{2,3},{3,2},{4,5},{5,4},{6,7},{7,6},{8,9},{9,8},{10,11... | collective-permute-start | bytes 3538952 | tf_op jit(solution)/shard_map/ppermute | solution.py:46
  126.9 13.7 %collective-permute-start.17 = (bf16[384,1536]{1,0:T(8,128)(2,1)}, bf16[384,1536]{1,0:T(8,128)(2,1)S(1)}, u32[]{:S(2)}, u32[]{:S(2)}) collective-permute-start(bf16[384,1536]{1,0:T(8,128)(2,1)} %get-tuple-element.30), channel_id=1, source_target_pairs={{0,1},{1,0},{2,3},{3,2},{4,5},{5,4},{6,7},{7,6},{8,9},{9,8},{10,11... | collective-permute-start | bytes 3538952 | tf_op jit(solution)/shard_map/ppermute | solution.py:46
  131.5 19.4 %collective-permute-start.22 = (bf16[384,384]{1,0:T(8,128)(2,1)S(1)}, bf16[384,384]{1,0:T(8,128)(2,1)S(1)}, u32[]{:S(2)}, u32[]{:S(2)}) collective-permute-start(bf16[384,384]{1,0:T(8,128)(2,1)S(1)} %get-tuple-element.39), channel_id=1, source_target_pairs={{0,32},{32,64},{64,96},{96,0},{1,33},{33,65},{65,97},{97,1},{2,34}... | collective-permute-start | bytes 884744 | tf_op jit(solution)/shard_map/ppermute | solution.py:42
  133.5 19.3 %collective-permute-start.23 = (bf16[384,384]{1,0:T(8,128)(2,1)S(1)}, bf16[384,384]{1,0:T(8,128)(2,1)S(1)}, u32[]{:S(2)}, u32[]{:S(2)}) collective-permute-start(bf16[384,384]{1,0:T(8,128)(2,1)S(1)} %get-tuple-element.40), channel_id=1, source_target_pairs={{0,64},{32,96},{64,0},{96,32},{1,65},{33,97},{65,1},{97,33},{2,66}... | collective-permute-start | bytes 884744 | tf_op jit(solution)/shard_map/ppermute | solution.py:42
  135.5 18.3 %collective-permute-start.24 = (bf16[384,384]{1,0:T(8,128)(2,1)S(1)}, bf16[384,384]{1,0:T(8,128)(2,1)S(1)}, u32[]{:S(2)}, u32[]{:S(2)}) collective-permute-start(bf16[384,384]{1,0:T(8,128)(2,1)S(1)} %get-tuple-element.41), channel_id=1, source_target_pairs={{0,96},{32,0},{64,32},{96,64},{1,97},{33,1},{65,33},{97,65},{2,98}... | collective-permute-start | bytes 884744 | tf_op jit(solution)/shard_map/ppermute | solution.py:42
  140.9 31.6 %collective-permute-start.18 = (bf16[384,384]{1,0:T(8,128)(2,1)S(1)}, bf16[384,384]{1,0:T(8,128)(2,1)S(1)}, u32[]{:S(2)}, u32[]{:S(2)}) collective-permute-start(bf16[384,384]{1,0:T(8,128)(2,1)S(1)} %get-tuple-element.32), channel_id=1, source_target_pairs={{0,32},{32,64},{64,96},{96,0},{1,33},{33,65},{65,97},{97,1},{2,34}... | collective-permute-start | bytes 884744 | tf_op jit(solution)/shard_map/ppermute | solution.py:42
  143.7 28.8 %collective-permute-start.19 = (bf16[384,384]{1,0:T(8,128)(2,1)S(1)}, bf16[384,384]{1,0:T(8,128)(2,1)S(1)}, u32[]{:S(2)}, u32[]{:S(2)}) collective-permute-start(bf16[384,384]{1,0:T(8,128)(2,1)S(1)} %get-tuple-element.33), channel_id=1, source_target_pairs={{0,64},{32,96},{64,0},{96,32},{1,65},{33,97},{65,1},{97,33},{2,66}... | collective-permute-start | bytes 884744 | tf_op jit(solution)/shard_map/ppermute | solution.py:42
  150.9 21.7 %collective-permute-start.20 = (bf16[384,384]{1,0:T(8,128)(2,1)S(1)}, bf16[384,384]{1,0:T(8,128)(2,1)S(1)}, u32[]{:S(2)}, u32[]{:S(2)}) collective-permute-start(bf16[384,384]{1,0:T(8,128)(2,1)S(1)} %get-tuple-element.34), channel_id=1, source_target_pairs={{0,96},{32,0},{64,32},{96,64},{1,97},{33,1},{65,33},{97,65},{2,98}... | collective-permute-start | bytes 884744 | tf_op jit(solution)/shard_map/ppermute | solution.py:42
  154.0 10.7 %collective-permute-start.25 = (f32[1,384]{1,0:T(1,128)S(1)}, f32[1,384]{1,0:T(1,128)S(1)}, u32[]{:S(2)}, u32[]{:S(2)}) collective-permute-start(f32[1,384]{1,0:T(1,128)S(1)} %get-tuple-element.42), channel_id=1, source_target_pairs={{0,2},{2,0},{1,3},{3,1},{4,6},{6,4},{5,7},{7,5},{8,10},{10,8},{9,1... | collective-permute-start | bytes 4616 | tf_op jit(solution)/shard_map/ppermute | solution.py:46
  164.7 28.9 %collective-permute-start.26 = (bf16[384,384]{1,0:T(8,128)(2,1)S(1)}, bf16[384,384]{1,0:T(8,128)(2,1)S(1)}, u32[]{:S(2)}, u32[]{:S(2)}) collective-permute-start(bf16[384,384]{1,0:T(8,128)(2,1)S(1)} %get-tuple-element.44), channel_id=1, source_target_pairs={{0,2},{2,0},{1,3},{3,1},{4,6},{6,4},{5,7},{7,5},{8,10},{10,8},{9,1... | collective-permute-start | bytes 884744 | tf_op jit(solution)/shard_map/ppermute | solution.py:46
  173.5 20.1 %all-to-all-start.1 = ((f32[16,1,384]{2,1,0:T(1,128)}), f32[16,1,384]{2,1,0:T(1,128)S(1)}, u32[]{:S(2)}, u32[]{:S(2)}) async-start(f32[16,1,384]{2,1,0:T(1,128)} %broadcast_in_dim.12), calls=%async_computation.1 | async-start | bytes 49152 | tf_op jit(solution)/shard_map/all_to_all | solution.py:226
  (15 other events, 289.6 us)
Sparse Core Ops, SparseCore 0:
  33.0 69.8 all-gather.1

commit v8 on v3

--- a/solution.py
+++ b/solution.py
@@ -113,21 +113,18 @@
             at = pl.ds(pl.multiple_of(i * step, step), step)
             product = jnp.dot(b[own], a[:, at], preferred_element_type=F32)
             theirs[:, at] = product[:UNIT].astype(BF16)
-            ours[:, at] = product[UNIT:]
-
-
-def add_core(place, ours, sent, first, second, third, own):
-    x = place[0]
-    pieces = [own, first, second, third]
+            ours[:, at] = product[UNIT:].astype(BF16)
+
+
+def add_core(place, ours, sent, *pieces):
     for step in range(X):
-        at = pl.ds(pl.multiple_of(lax.rem(x + step, X) * HALF, HALF), HALF)
-        total = ours[:, at] + sent[:, at].astype(F32)
-        pieces[step][...] = total.astype(pieces[step].dtype)
-
-
-def add_x(own, first, second, third, total, sums):
-    all_x = own[...] + first[...].astype(F32) + (second[...].astype(F32) + third[...].astype(F32))
-    turned = all_x.T
+        at = pl.ds(pl.multiple_of(lax.rem(place[0] + step, X) * HALF, HALF), HALF)
+        pieces[step][...] = (ours[:, at].astype(F32) + sent[:, at].astype(F32)).astype(BF16)
+
+
+def add_x(*refs):
+    pieces, total, sums = refs[:X], refs[X], refs[X + 1]
+    turned = sum(piece[...].astype(F32) for piece in pieces).T
     total[...] = turned.astype(total.dtype)
     sums[...] = jnp.sum(turned * turned, axis=0, keepdims=True)
 
@@ -201,7 +198,7 @@
 
     theirs, ours, theirs_near, ours_near = call(
         functools.partial(multiply, order),
-        [((UNIT, WIDE), BF16), ((UNIT, WIDE), F32)] * 2,
+        [((UNIT, WIDE), BF16)] * 4,
         [SMEM] + [HBM] * (len(shards) + 1),
         (jnp.stack([y, zhi]), *shards, right),
         [
@@ -213,23 +210,24 @@
         vmem=60,
     )
 
-    def over_x(ours, sent):
-        pieces = call(
+    def total(apart, dtype):
+        return call(add_x, [((HALF, UNIT), dtype), ((1, UNIT), F32)], [VMEM] * X, apart)
+
+    def over_x(ours, theirs):
+        apart = call(
             add_core,
-            [((UNIT, HALF), BF16)] * 3 + [((UNIT, HALF), F32)],
+            [((UNIT, HALF), BF16)] * X,
             [SMEM, VMEM, VMEM],
-            (x[None], ours, sent),
+            (x[None], ours, swap(theirs, "core")),
         )
-        return pieces[3], *(shift_x(pieces[step - 1], step) for step in range(1, X))
-
-    def total(pieces, dtype):
-        return call(add_x, [((HALF, UNIT), dtype), ((1, UNIT), F32)], [VMEM] * 4, pieces)
-
-    pieces = over_x(ours, swap(theirs, "core"))
-    pieces_near = over_x(ours_near, swap(theirs_near, "core"))
-    other, sums = total(pieces, BF16)
-    sums, other = swap(sums, "zhi"), swap(other, "zhi")
-    mine, own_sums = total(pieces_near, F32)
+        return [apart[0]] + [shift_x(apart[step], step) for step in range(1, X)]
+
+    apart = over_x(ours, theirs)
+    apart_near = over_x(ours_near, theirs_near)
+    other, sums = total(apart, BF16)
+    sums, other = in_order(swap(sums, "zhi"), other)
+    other = swap(other, "zhi")
+    mine, own_sums = total(apart_near, F32)
     sums = jnp.broadcast_to(sums + own_sums, (Z_LO * X, 1, UNIT))
     sums = lax.all_to_all(sums, ("zlo", "x"), split_axis=0, concat_axis=0, tiled=True)
     return call(

time: 202 us -> 198 us (0.980)
  the two profiles are of different devices: /device:TPU:24 before, /device:TPU:1 now
where the time goes in v8:
time: 198 us; the launch traced here: 195 us
  starting transfers between devices  124 us (63%)
  waiting for transfers between devices  32.6 us (16%)
  Pallas kernels  20 us (10%)
  between operations  14 us (7%)
  local copies, waits for them, and re-layouts  4.17 us (2%)
    ppermute x16, starting transfers between devices, shift_y(): return lax.ppermute(shard, 'y', [(i, (i + step) % Y) for i in range(Y)])  52.5 us
    ppermute x5, starting transfers between devices, swap(): return lax.ppermute(shard, axis, [(0, 1), (1, 0)])  29.3 us
    pallas_call x8, Pallas kernels, call(): pl.pallas_call(body, out_shape=shapes, in_specs=ins, out_specs=[VMEM] * l...  20 us
    ppermute x6, starting transfers between devices, shift_x(): return lax.ppermute(shard, 'x', [(i, (i + step) % X) for i in range(X)])  19 us
    all_to_all x2, starting transfers between devices, spread_over(): lax.all_to_all(array, ('x', 'core'), split_axis=0, concat_axis=0, tiled=T...  15.8 us
    ppermute x5, waiting for transfers between devices, swap(): return lax.ppermute(shard, axis, [(0, 1), (1, 0)])  11 us
    all_to_all x1, waiting for transfers between devices, local(): lax.all_to_all(sums, ('zlo', 'x'), split_axis=0, concat_axis=0, tiled=True)  10.5 us
    all_to_all x1, starting transfers between devices, local(): lax.all_to_all(sums, ('zlo', 'x'), split_axis=0, concat_axis=0, tiled=True)  6.96 us
  transfers between devices with their start and end apart: 31, of which 9 were waited for; matrix products, arithmetic and copies ran while one was open for 1% of the time, Pallas kernels for 1%

profile of v8, /device:TPU:1, one launch (start us, length us, event | category | flops | bytes accessed | tf_op | source)
XLA Modules:
  0.0 195.1 jit_solution(16980568006722233597)
XLA Ops:
  10.5 10.3 %all-to-all-start = ((bf16[8,3,48,384]{3,2,1,0:T(8,128)(2,1)}), bf16[8,3,48,384]{3,2,1,0:T(8,128)(2,1)S(1)}, u32[]{:S(2)}, u32[]{:S(2)}) async-start(bf16[8,3,48,384]{3,2,1,0:T(8,128)(2,1)} %get-tuple-element.31), calls=%async_computation | async-start | bytes 1769472 | tf_op jit(solution)/shard_map/all_to_all | solution.py:50
  20.8 6.1 %collective-permute-start = (bf16[384,384]{1,0:T(8,128)(2,1)S(1)}, bf16[384,384]{1,0:T(8,128)(2,1)}, u32[]{:S(2)}, u32[]{:S(2)}) collective-permute-start(bf16[384,384]{1,0:T(8,128)(2,1)S(1)} %get-tuple-element.32), channel_id=1, source_target_pairs={{0,2},{2,0},{1,3},{3,1},{4,6},{6,4},{5,7},{7,5},{8,10},{10,8},{9,1... | collective-permute-start | bytes 884744 | tf_op jit(solution)/shard_map/ppermute | solution.py:46
  26.9 9.3 %collective-permute-done = bf16[384,384]{1,0:T(8,128)(2,1)} collective-permute-done((bf16[384,384]{1,0:T(8,128)(2,1)S(1)}, bf16[384,384]{1,0:T(8,128)(2,1)}, u32[]{:S(2)}, u32[]{:S(2)}) %collective-permute-start) | collective-permute-done | bytes 294944 | tf_op jit(solution)/shard_map/ppermute | solution.py:46
  37.9 1.9 collective-permute-start.1
  39.8 5.5 %all-to-all-start.1 = ((bf16[8,48,384]{2,1,0:T(8,128)(2,1)}), bf16[8,48,384]{2,1,0:T(8,128)(2,1)S(1)}, u32[]{:S(2)}, u32[]{:S(2)}) async-start(bf16[8,48,384]{2,1,0:T(8,128)(2,1)} %bitcast.5), calls=%async_computation.1 | async-start | bytes 589824 | tf_op jit(solution)/shard_map/all_to_all | solution.py:50
  45.3 4.8 %collective-permute-start.2 = (bf16[96,1536]{1,0:T(8,128)(2,1)S(1)}, bf16[96,1536]{1,0:T(8,128)(2,1)S(1)}, u32[]{:S(2)}, u32[]{:S(2)}) collective-permute-start(bf16[96,1536]{1,0:T(8,128)(2,1)S(1)} %get-tuple-element.34.refs_0_), channel_id=1, source_target_pairs={{0,28},{4,0},{8,4},{12,8},{16,12},{20,16},{24,20},{28,24},{1,29},{... | collective-permute-start | bytes 884744 | tf_op jit(solution)/shard_map/ppermute | solution.py:38
  50.2 2.0 %all-to-all-done.1 = bf16[8,48,384]{2,1,0:T(8,128)(2,1)S(1)} async-done(((bf16[8,48,384]{2,1,0:T(8,128)(2,1)}), bf16[8,48,384]{2,1,0:T(8,128)(2,1)S(1)}, u32[]{:S(2)}, u32[]{:S(2)}) %all-to-all-start.1) | async-done | bytes 294944 | tf_op jit(solution)/shard_map/all_to_all | solution.py:50
  52.2 2.6 %collective-permute-start.3 = (bf16[96,1536]{1,0:T(8,128)(2,1)S(1)}, bf16[96,1536]{1,0:T(8,128)(2,1)S(1)}, u32[]{:S(2)}, u32[]{:S(2)}) collective-permute-start(bf16[96,1536]{1,0:T(8,128)(2,1)S(1)} %bitcast.13), channel_id=1, source_target_pairs={{0,4},{4,8},{8,12},{12,16},{16,20},{20,24},{24,28},{28,0},{1,5},{5... | collective-permute-start | bytes 884744 | tf_op jit(solution)/shard_map/ppermute | solution.py:38
  54.8 4.2 %collective-permute-start.4 = (bf16[96,1536]{1,0:T(8,128)(2,1)S(1)}, bf16[96,1536]{1,0:T(8,128)(2,1)S(1)}, u32[]{:S(2)}, u32[]{:S(2)}) collective-permute-start(bf16[96,1536]{1,0:T(8,128)(2,1)S(1)} %bitcast.14), channel_id=1, source_target_pairs={{0,28},{4,0},{8,4},{12,8},{16,12},{20,16},{24,20},{28,24},{1,29},{... | collective-permute-start | bytes 884744 | tf_op jit(solution)/shard_map/ppermute | solution.py:38
  59.0 1.9 collective-permute-start.5
  60.9 4.6 %collective-permute-start.6 = (bf16[96,1536]{1,0:T(8,128)(2,1)S(1)}, bf16[96,1536]{1,0:T(8,128)(2,1)S(1)}, u32[]{:S(2)}, u32[]{:S(2)}) collective-permute-start(bf16[96,1536]{1,0:T(8,128)(2,1)S(1)} %collective-permute-done.2.refs_3_), channel_id=1, source_target_pairs={{0,28},{4,0},{8,4},{12,8},{16,12},{20,16},{24,20},{28,24},{1,29},{... | collective-permute-start | bytes 884744 | tf_op jit(solution)/shard_map/ppermute | solution.py:38
  65.5 1.9 collective-permute-start.7
  67.5 4.6 %collective-permute-start.8 = (bf16[96,1536]{1,0:T(8,128)(2,1)S(1)}, bf16[96,1536]{1,0:T(8,128)(2,1)S(1)}, u32[]{:S(2)}, u32[]{:S(2)}) collective-permute-start(bf16[96,1536]{1,0:T(8,128)(2,1)S(1)} %collective-permute-done.4.refs_5_), channel_id=1, source_target_pairs={{0,28},{4,0},{8,4},{12,8},{16,12},{20,16},{24,20},{28,24},{1,29},{... | collective-permute-start | bytes 884744 | tf_op jit(solution)/shard_map/ppermute | solution.py:38
  74.0 4.6 %collective-permute-start.10 = (bf16[96,1536]{1,0:T(8,128)(2,1)S(1)}, bf16[96,1536]{1,0:T(8,128)(2,1)S(1)}, u32[]{:S(2)}, u32[]{:S(2)}) collective-permute-start(bf16[96,1536]{1,0:T(8,128)(2,1)S(1)} %collective-permute-done.6.refs_7_), channel_id=1, source_target_pairs={{0,28},{4,0},{8,4},{12,8},{16,12},{20,16},{24,20},{28,24},{1,29},{... | collective-permute-start | bytes 884744 | tf_op jit(solution)/shard_map/ppermute | solution.py:38
  80.6 4.6 %collective-permute-start.12 = (bf16[96,1536]{1,0:T(8,128)(2,1)S(1)}, bf16[96,1536]{1,0:T(8,128)(2,1)S(1)}, u32[]{:S(2)}, u32[]{:S(2)}) collective-permute-start(bf16[96,1536]{1,0:T(8,128)(2,1)S(1)} %collective-permute-done.8.refs_9_), channel_id=1, source_target_pairs={{0,28},{4,0},{8,4},{12,8},{16,12},{20,16},{24,20},{28,24},{1,29},{... | collective-permute-start | bytes 884744 | tf_op jit(solution)/shard_map/ppermute | solution.py:38
  85.2 1.9 collective-permute-start.13
  87.2 4.6 %collective-permute-start.14 = (bf16[48,1536]{1,0:T(8,128)(2,1)S(1)}, bf16[48,1536]{1,0:T(8,128)(2,1)}, u32[]{:S(2)}, u32[]{:S(2)}) collective-permute-start(bf16[48,1536]{1,0:T(8,128)(2,1)S(1)} %slice.17), channel_id=1, source_target_pairs={{0,28},{4,0},{8,4},{12,8},{16,12},{20,16},{24,20},{28,24},{1,29},{... | collective-permute-start | bytes 442376 | tf_op jit(solution)/shard_map/ppermute | solution.py:38
  91.8 1.9 collective-permute-start.15
  93.8 4.6 %collective-permute-start.16 = (bf16[48,1536]{1,0:T(8,128)(2,1)S(1)}, bf16[48,1536]{1,0:T(8,128)(2,1)S(1)}, u32[]{:S(2)}, u32[]{:S(2)}) collective-permute-start(bf16[48,1536]{1,0:T(8,128)(2,1)S(1)} %slice.19), channel_id=1, source_target_pairs={{0,28},{4,0},{8,4},{12,8},{16,12},{20,16},{24,20},{28,24},{1,29},{... | collective-permute-start | bytes 442376 | tf_op jit(solution)/shard_map/ppermute | solution.py:38
  100.5 6.5 %all-gather.2.cloned.1.call-done.refs_18_ = bf16[8,768,384]{2,1,0:T(8,128)(2,1)} async-done(((bf16[1,768,384]{2,1,0:T(8,128)(2,1)}), bf16[8,768,384]{2,1,0:T(8,128)(2,1)}) %all-gather.2.cloned.1.call-update) | async-done | bytes 4718608 | tf_op jit(solution)/shard_map/all_gather | solution.py:195
  107.1 13.6 %shard_map.39 = (bf16[384,1536]{1,0:T(8,128)(2,1)}, bf16[384,1536]{1,0:T(8,128)(2,1)}, bf16[384,1536]{1,0:T(8,128)(2,1)}, bf16[384,1536]{1,0:T(8,128)(2,1)}) custom-call(s32[2]{0:T(128)} %pad_add_fusion.place, bf16[96,1536]{1,0:T(8,128)(2,1)} %copy-done.3, bf16[96,1536]{1,0:T(8,128)(2,1)} %bitcast.15, bf16[96,1536]{1,0:T(8,128)(2,1)} %copy-done.10, ...), custom_call_target="tpu_custom_call" | custom-call | flops 7247757312 | bytes 14155784 | tf_op jit(solution)/shard_map/pallas_call | solution.py:26
  120.7 2.6 %collective-permute-start.21 = (bf16[384,1536]{1,0:T(8,128)(2,1)}, bf16[384,1536]{1,0:T(8,128)(2,1)S(1)}, u32[]{:S(2)}, u32[]{:S(2)}) collective-permute-start(bf16[384,1536]{1,0:T(8,128)(2,1)} %get-tuple-element.47), channel_id=1, source_target_pairs={{0,1},{1,0},{2,3},{3,2},{4,5},{5,4},{6,7},{7,6},{8,9},{9,8},{10,11... | collective-permute-start | bytes 3538952 | tf_op jit(solution)/shard_map/ppermute | solution.py:46
  127.5 3.2 %collective-permute-start.22 = (bf16[384,384]{1,0:T(8,128)(2,1)S(1)}, bf16[384,384]{1,0:T(8,128)(2,1)S(1)}, u32[]{:S(2)}, u32[]{:S(2)}) collective-permute-start(bf16[384,384]{1,0:T(8,128)(2,1)S(1)} %get-tuple-element.49), channel_id=1, source_target_pairs={{0,32},{32,64},{64,96},{96,0},{1,33},{33,65},{65,97},{97,1},{2,34}... | collective-permute-start | bytes 884744 | tf_op jit(solution)/shard_map/ppermute | solution.py:42
  130.7 4.3 %collective-permute-start.23 = (bf16[384,384]{1,0:T(8,128)(2,1)S(1)}, bf16[384,384]{1,0:T(8,128)(2,1)S(1)}, u32[]{:S(2)}, u32[]{:S(2)}) collective-permute-start(bf16[384,384]{1,0:T(8,128)(2,1)S(1)} %get-tuple-element.50), channel_id=1, source_target_pairs={{0,64},{32,96},{64,0},{96,32},{1,65},{33,97},{65,1},{97,33},{2,66}... | collective-permute-start | bytes 884744 | tf_op jit(solution)/shard_map/ppermute | solution.py:42
  135.0 3.1 %collective-permute-start.24 = (bf16[384,384]{1,0:T(8,128)(2,1)S(1)}, bf16[384,384]{1,0:T(8,128)(2,1)S(1)}, u32[]{:S(2)}, u32[]{:S(2)}) collective-permute-start(bf16[384,384]{1,0:T(8,128)(2,1)S(1)} %get-tuple-element.51), channel_id=1, source_target_pairs={{0,96},{32,0},{64,32},{96,64},{1,97},{33,1},{65,33},{97,65},{2,98}... | collective-permute-start | bytes 884744 | tf_op jit(solution)/shard_map/ppermute | solution.py:42
  138.5 2.2 %collective-permute-start.18 = (bf16[384,384]{1,0:T(8,128)(2,1)S(1)}, bf16[384,384]{1,0:T(8,128)(2,1)S(1)}, u32[]{:S(2)}, u32[]{:S(2)}) collective-permute-start(bf16[384,384]{1,0:T(8,128)(2,1)S(1)} %get-tuple-element.42), channel_id=1, source_target_pairs={{0,32},{32,64},{64,96},{96,0},{1,33},{33,65},{65,97},{97,1},{2,34}... | collective-permute-start | bytes 884744 | tf_op jit(solution)/shard_map/ppermute | solution.py:42
  140.7 2.8 %collective-permute-start.19 = (bf16[384,384]{1,0:T(8,128)(2,1)S(1)}, bf16[384,384]{1,0:T(8,128)(2,1)S(1)}, u32[]{:S(2)}, u32[]{:S(2)}) collective-permute-start(bf16[384,384]{1,0:T(8,128)(2,1)S(1)} %get-tuple-element.43), channel_id=1, source_target_pairs={{0,64},{32,96},{64,0},{96,32},{1,65},{33,97},{65,1},{97,33},{2,66}... | collective-permute-start | bytes 884744 | tf_op jit(solution)/shard_map/ppermute | solution.py:42
  143.5 3.4 %collective-permute-start.20 = (bf16[384,384]{1,0:T(8,128)(2,1)S(1)}, bf16[384,384]{1,0:T(8,128)(2,1)S(1)}, u32[]{:S(2)}, u32[]{:S(2)}) collective-permute-start(bf16[384,384]{1,0:T(8,128)(2,1)S(1)} %get-tuple-element.44), channel_id=1, source_target_pairs={{0,96},{32,0},{64,32},{96,64},{1,97},{33,1},{65,33},{97,65},{2,98}... | collective-permute-start | bytes 884744 | tf_op jit(solution)/shard_map/ppermute | solution.py:42
  148.3 11.4 %collective-permute-start.25 = (f32[1,384]{1,0:T(1,128)S(1)}, f32[1,384]{1,0:T(1,128)S(1)}, u32[]{:S(2)}, u32[]{:S(2)}) collective-permute-start(f32[1,384]{1,0:T(1,128)S(1)} %get-tuple-element.52), channel_id=1, source_target_pairs={{0,2},{2,0},{1,3},{3,1},{4,6},{6,4},{5,7},{7,5},{8,10},{10,8},{9,1... | collective-permute-start | bytes 4616 | tf_op jit(solution)/shard_map/ppermute | solution.py:46
  160.7 7.3 %collective-permute-start.26 = (bf16[384,384]{1,0:T(8,128)(2,1)S(1)}, bf16[384,384]{1,0:T(8,128)(2,1)S(1)}, u32[]{:S(2)}, u32[]{:S(2)}) collective-permute-start(bf16[384,384]{1,0:T(8,128)(2,1)S(1)} %get-tuple-element.54), channel_id=1, source_target_pairs={{0,2},{2,0},{1,3},{3,1},{4,6},{6,4},{5,7},{7,5},{8,10},{10,8},{9,1... | collective-permute-start | bytes 884744 | tf_op jit(solution)/shard_map/ppermute | solution.py:46
  168.9 7.0 %all-to-all-start.2 = ((f32[16,1,384]{2,1,0:T(1,128)}), f32[16,1,384]{2,1,0:T(1,128)S(1)}, u32[]{:S(2)}, u32[]{:S(2)}) async-start(f32[16,1,384]{2,1,0:T(1,128)} %broadcast_in_dim.12), calls=%async_computation.2 | async-start | bytes 49152 | tf_op jit(solution)/shard_map/all_to_all | solution.py:232
  175.9 10.5 %all-to-all-done.2.sums = f32[16,1,384]{2,1,0:T(1,128)S(1)} async-done(((f32[16,1,384]{2,1,0:T(1,128)}), f32[16,1,384]{2,1,0:T(1,128)S(1)}, u32[]{:S(2)}, u32[]{:S(2)}) %all-to-all-start.2) | async-done | bytes 24608 | tf_op jit(solution)/shard_map/all_to_all | solution.py:232
  (90 shorter events, 21.3 us)
Async XLA Ops:
  10.5 25.8 %all-to-all-start = ((bf16[8,3,48,384]{3,2,1,0:T(8,128)(2,1)}), bf16[8,3,48,384]{3,2,1,0:T(8,128)(2,1)S(1)}, u32[]{:S(2)}, u32[]{:S(2)}) async-start(bf16[8,3,48,384]{3,2,1,0:T(8,128)(2,1)} %get-tuple-element.31), calls=%async_computation | async-start | bytes 1769472 | tf_op jit(solution)/shard_map/all_to_all | solution.py:50
  20.8 86.2 %all-gather.2.cloned.1.call-start = ((), (), s32[]{:S(2)}) async-start(), calls=%async_computation.3 | async-start | bytes 5308416 | tf_op jit(solution)/shard_map/all_gather | solution.py:195
  20.8 15.4 %collective-permute-start = (bf16[384,384]{1,0:T(8,128)(2,1)S(1)}, bf16[384,384]{1,0:T(8,128)(2,1)}, u32[]{:S(2)}, u32[]{:S(2)}) collective-permute-start(bf16[384,384]{1,0:T(8,128)(2,1)S(1)} %get-tuple-element.32), channel_id=1, source_target_pairs={{0,2},{2,0},{1,3},{3,1},{4,6},{6,4},{5,7},{7,5},{8,10},{10,8},{9,1... | collective-permute-start | bytes 884744 | tf_op jit(solution)/shard_map/ppermute | solution.py:46
  37.9 14.3 %collective-permute-start.1 = (bf16[96,1536]{1,0:T(8,128)(2,1)S(1)}, bf16[96,1536]{1,0:T(8,128)(2,1)S(1)}, u32[]{:S(2)}, u32[]{:S(2)}) collective-permute-start(bf16[96,1536]{1,0:T(8,128)(2,1)S(1)} %get-tuple-element.34.refs_0_), channel_id=1, source_target_pairs={{0,4},{4,8},{8,12},{12,16},{16,20},{20,24},{24,28},{28,0},{1,5},{5... | collective-permute-start | bytes 884744 | tf_op jit(solution)/shard_map/ppermute | solution.py:38
  39.8 12.3 %all-to-all-start.1 = ((bf16[8,48,384]{2,1,0:T(8,128)(2,1)}), bf16[8,48,384]{2,1,0:T(8,128)(2,1)S(1)}, u32[]{:S(2)}, u32[]{:S(2)}) async-start(bf16[8,48,384]{2,1,0:T(8,128)(2,1)} %bitcast.5), calls=%async_computation.1 | async-start | bytes 589824 | tf_op jit(solution)/shard_map/all_to_all | solution.py:50
  45.3 15.6 %collective-permute-start.2 = (bf16[96,1536]{1,0:T(8,128)(2,1)S(1)}, bf16[96,1536]{1,0:T(8,128)(2,1)S(1)}, u32[]{:S(2)}, u32[]{:S(2)}) collective-permute-start(bf16[96,1536]{1,0:T(8,128)(2,1)S(1)} %get-tuple-element.34.refs_0_), channel_id=1, source_target_pairs={{0,28},{4,0},{8,4},{12,8},{16,12},{20,16},{24,20},{28,24},{1,29},{... | collective-permute-start | bytes 884744 | tf_op jit(solution)/shard_map/ppermute | solution.py:38
  52.2 54.8 %copy-start.4 = (bf16[4,12,8,384]{3,2,0,1:T(8,128)(2,1)}, bf16[4,12,8,384]{3,2,0,1:T(8,128)(2,1)S(1)}, u32[]{:S(2)}) copy-start(bf16[4,12,8,384]{3,2,0,1:T(8,128)(2,1)S(1)} %copy.12) | copy-start | bytes 884740
  52.2 13.3 %collective-permute-start.3 = (bf16[96,1536]{1,0:T(8,128)(2,1)S(1)}, bf16[96,1536]{1,0:T(8,128)(2,1)S(1)}, u32[]{:S(2)}, u32[]{:S(2)}) collective-permute-start(bf16[96,1536]{1,0:T(8,128)(2,1)S(1)} %bitcast.13), channel_id=1, source_target_pairs={{0,4},{4,8},{8,12},{12,16},{16,20},{20,24},{24,28},{28,0},{1,5},{5... | collective-permute-start | bytes 884744 | tf_op jit(solution)/shard_map/ppermute | solution.py:38
  54.8 12.7 %collective-permute-start.4 = (bf16[96,1536]{1,0:T(8,128)(2,1)S(1)}, bf16[96,1536]{1,0:T(8,128)(2,1)S(1)}, u32[]{:S(2)}, u32[]{:S(2)}) collective-permute-start(bf16[96,1536]{1,0:T(8,128)(2,1)S(1)} %bitcast.14), channel_id=1, source_target_pairs={{0,28},{4,0},{8,4},{12,8},{16,12},{20,16},{24,20},{28,24},{1,29},{... | collective-permute-start | bytes 884744 | tf_op jit(solution)/shard_map/ppermute | solution.py:38
  59.0 13.1 %collective-permute-start.5 = (bf16[96,1536]{1,0:T(8,128)(2,1)S(1)}, bf16[96,1536]{1,0:T(8,128)(2,1)S(1)}, u32[]{:S(2)}, u32[]{:S(2)}) collective-permute-start(bf16[96,1536]{1,0:T(8,128)(2,1)S(1)} %collective-permute-done.1.refs_2_), channel_id=1, source_target_pairs={{0,4},{4,8},{8,12},{12,16},{16,20},{20,24},{24,28},{28,0},{1,5},{5... | collective-permute-start | bytes 884744 | tf_op jit(solution)/shard_map/ppermute | solution.py:38
  60.9 13.1 %collective-permute-start.6 = (bf16[96,1536]{1,0:T(8,128)(2,1)S(1)}, bf16[96,1536]{1,0:T(8,128)(2,1)S(1)}, u32[]{:S(2)}, u32[]{:S(2)}) collective-permute-start(bf16[96,1536]{1,0:T(8,128)(2,1)S(1)} %collective-permute-done.2.refs_3_), channel_id=1, source_target_pairs={{0,28},{4,0},{8,4},{12,8},{16,12},{20,16},{24,20},{28,24},{1,29},{... | collective-permute-start | bytes 884744 | tf_op jit(solution)/shard_map/ppermute | solution.py:38
  65.5 13.1 %collective-permute-start.7 = (bf16[96,1536]{1,0:T(8,128)(2,1)S(1)}, bf16[96,1536]{1,0:T(8,128)(2,1)S(1)}, u32[]{:S(2)}, u32[]{:S(2)}) collective-permute-start(bf16[96,1536]{1,0:T(8,128)(2,1)S(1)} %collective-permute-done.3.refs_4_), channel_id=1, source_target_pairs={{0,4},{4,8},{8,12},{12,16},{16,20},{20,24},{24,28},{28,0},{1,5},{5... | collective-permute-start | bytes 884744 | tf_op jit(solution)/shard_map/ppermute | solution.py:38
  67.5 13.1 %collective-permute-start.8 = (bf16[96,1536]{1,0:T(8,128)(2,1)S(1)}, bf16[96,1536]{1,0:T(8,128)(2,1)S(1)}, u32[]{:S(2)}, u32[]{:S(2)}) collective-permute-start(bf16[96,1536]{1,0:T(8,128)(2,1)S(1)} %collective-permute-done.4.refs_5_), channel_id=1, source_target_pairs={{0,28},{4,0},{8,4},{12,8},{16,12},{20,16},{24,20},{28,24},{1,29},{... | collective-permute-start | bytes 884744 | tf_op jit(solution)/shard_map/ppermute | solution.py:38
  72.1 13.1 %collective-permute-start.9 = (bf16[96,1536]{1,0:T(8,128)(2,1)S(1)}, bf16[96,1536]{1,0:T(8,128)(2,1)S(1)}, u32[]{:S(2)}, u32[]{:S(2)}) collective-permute-start(bf16[96,1536]{1,0:T(8,128)(2,1)S(1)} %collective-permute-done.5.refs_6_), channel_id=1, source_target_pairs={{0,4},{4,8},{8,12},{12,16},{16,20},{20,24},{24,28},{28,0},{1,5},{5... | collective-permute-start | bytes 884744 | tf_op jit(solution)/shard_map/ppermute | solution.py:38
  74.0 13.1 %collective-permute-start.10 = (bf16[96,1536]{1,0:T(8,128)(2,1)S(1)}, bf16[96,1536]{1,0:T(8,128)(2,1)S(1)}, u32[]{:S(2)}, u32[]{:S(2)}) collective-permute-start(bf16[96,1536]{1,0:T(8,128)(2,1)S(1)} %collective-permute-done.6.refs_7_), channel_id=1, source_target_pairs={{0,28},{4,0},{8,4},{12,8},{16,12},{20,16},{24,20},{28,24},{1,29},{... | collective-permute-start | bytes 884744 | tf_op jit(solution)/shard_map/ppermute | solution.py:38
  78.6 13.1 %collective-permute-start.11 = (bf16[96,1536]{1,0:T(8,128)(2,1)S(1)}, bf16[96,1536]{1,0:T(8,128)(2,1)S(1)}, u32[]{:S(2)}, u32[]{:S(2)}) collective-permute-start(bf16[96,1536]{1,0:T(8,128)(2,1)S(1)} %collective-permute-done.7.refs_8_), channel_id=1, source_target_pairs={{0,4},{4,8},{8,12},{12,16},{16,20},{20,24},{24,28},{28,0},{1,5},{5... | collective-permute-start | bytes 884744 | tf_op jit(solution)/shard_map/ppermute | solution.py:38
  80.6 13.2 %collective-permute-start.12 = (bf16[96,1536]{1,0:T(8,128)(2,1)S(1)}, bf16[96,1536]{1,0:T(8,128)(2,1)S(1)}, u32[]{:S(2)}, u32[]{:S(2)}) collective-permute-start(bf16[96,1536]{1,0:T(8,128)(2,1)S(1)} %collective-permute-done.8.refs_9_), channel_id=1, source_target_pairs={{0,28},{4,0},{8,4},{12,8},{16,12},{20,16},{24,20},{28,24},{1,29},{... | collective-permute-start | bytes 884744 | tf_op jit(solution)/shard_map/ppermute | solution.py:38
  85.2 13.8 %collective-permute-start.13 = (bf16[48,1536]{1,0:T(8,128)(2,1)S(1)}, bf16[48,1536]{1,0:T(8,128)(2,1)}, u32[]{:S(2)}, u32[]{:S(2)}) collective-permute-start(bf16[48,1536]{1,0:T(8,128)(2,1)S(1)} %slice.16), channel_id=1, source_target_pairs={{0,4},{4,8},{8,12},{12,16},{16,20},{20,24},{24,28},{28,0},{1,5},{5... | collective-permute-start | bytes 442376 | tf_op jit(solution)/shard_map/ppermute | solution.py:38
  87.2 11.8 %collective-permute-start.14 = (bf16[48,1536]{1,0:T(8,128)(2,1)S(1)}, bf16[48,1536]{1,0:T(8,128)(2,1)}, u32[]{:S(2)}, u32[]{:S(2)}) collective-permute-start(bf16[48,1536]{1,0:T(8,128)(2,1)S(1)} %slice.17), channel_id=1, source_target_pairs={{0,28},{4,0},{8,4},{12,8},{16,12},{20,16},{24,20},{28,24},{1,29},{... | collective-permute-start | bytes 442376 | tf_op jit(solution)/shard_map/ppermute | solution.py:38
  91.8 7.5 %collective-permute-start.15 = (bf16[48,1536]{1,0:T(8,128)(2,1)S(1)}, bf16[48,1536]{1,0:T(8,128)(2,1)S(1)}, u32[]{:S(2)}, u32[]{:S(2)}) collective-permute-start(bf16[48,1536]{1,0:T(8,128)(2,1)S(1)} %slice.18), channel_id=1, source_target_pairs={{0,4},{4,8},{8,12},{12,16},{16,20},{20,24},{24,28},{28,0},{1,5},{5... | collective-permute-start | bytes 442376 | tf_op jit(solution)/shard_map/ppermute | solution.py:38
  93.8 6.7 %collective-permute-start.16 = (bf16[48,1536]{1,0:T(8,128)(2,1)S(1)}, bf16[48,1536]{1,0:T(8,128)(2,1)S(1)}, u32[]{:S(2)}, u32[]{:S(2)}) collective-permute-start(bf16[48,1536]{1,0:T(8,128)(2,1)S(1)} %slice.19), channel_id=1, source_target_pairs={{0,28},{4,0},{8,4},{12,8},{16,12},{20,16},{24,20},{28,24},{1,29},{... | collective-permute-start | bytes 442376 | tf_op jit(solution)/shard_map/ppermute | solution.py:38
  120.7 5.3 %collective-permute-start.21 = (bf16[384,1536]{1,0:T(8,128)(2,1)}, bf16[384,1536]{1,0:T(8,128)(2,1)S(1)}, u32[]{:S(2)}, u32[]{:S(2)}) collective-permute-start(bf16[384,1536]{1,0:T(8,128)(2,1)} %get-tuple-element.47), channel_id=1, source_target_pairs={{0,1},{1,0},{2,3},{3,2},{4,5},{5,4},{6,7},{7,6},{8,9},{9,8},{10,11... | collective-permute-start | bytes 3538952 | tf_op jit(solution)/shard_map/ppermute | solution.py:46
  123.3 14.9 %collective-permute-start.17 = (bf16[384,1536]{1,0:T(8,128)(2,1)}, bf16[384,1536]{1,0:T(8,128)(2,1)S(1)}, u32[]{:S(2)}, u32[]{:S(2)}) collective-permute-start(bf16[384,1536]{1,0:T(8,128)(2,1)} %get-tuple-element.40), channel_id=1, source_target_pairs={{0,1},{1,0},{2,3},{3,2},{4,5},{5,4},{6,7},{7,6},{8,9},{9,8},{10,11... | collective-permute-start | bytes 3538952 | tf_op jit(solution)/shard_map/ppermute | solution.py:46
  127.5 16.0 %collective-permute-start.22 = (bf16[384,384]{1,0:T(8,128)(2,1)S(1)}, bf16[384,384]{1,0:T(8,128)(2,1)S(1)}, u32[]{:S(2)}, u32[]{:S(2)}) collective-permute-start(bf16[384,384]{1,0:T(8,128)(2,1)S(1)} %get-tuple-element.49), channel_id=1, source_target_pairs={{0,32},{32,64},{64,96},{96,0},{1,33},{33,65},{65,97},{97,1},{2,34}... | collective-permute-start | bytes 884744 | tf_op jit(solution)/shard_map/ppermute | solution.py:42
  130.7 16.2 %collective-permute-start.23 = (bf16[384,384]{1,0:T(8,128)(2,1)S(1)}, bf16[384,384]{1,0:T(8,128)(2,1)S(1)}, u32[]{:S(2)}, u32[]{:S(2)}) collective-permute-start(bf16[384,384]{1,0:T(8,128)(2,1)S(1)} %get-tuple-element.50), channel_id=1, source_target_pairs={{0,64},{32,96},{64,0},{96,32},{1,65},{33,97},{65,1},{97,33},{2,66}... | collective-permute-start | bytes 884744 | tf_op jit(solution)/shard_map/ppermute | solution.py:42
  135.0 12.9 %collective-permute-start.24 = (bf16[384,384]{1,0:T(8,128)(2,1)S(1)}, bf16[384,384]{1,0:T(8,128)(2,1)S(1)}, u32[]{:S(2)}, u32[]{:S(2)}) collective-permute-start(bf16[384,384]{1,0:T(8,128)(2,1)S(1)} %get-tuple-element.51), channel_id=1, source_target_pairs={{0,96},{32,0},{64,32},{96,64},{1,97},{33,1},{65,33},{97,65},{2,98}... | collective-permute-start | bytes 884744 | tf_op jit(solution)/shard_map/ppermute | solution.py:42
  138.5 29.4 %collective-permute-start.18 = (bf16[384,384]{1,0:T(8,128)(2,1)S(1)}, bf16[384,384]{1,0:T(8,128)(2,1)S(1)}, u32[]{:S(2)}, u32[]{:S(2)}) collective-permute-start(bf16[384,384]{1,0:T(8,128)(2,1)S(1)} %get-tuple-element.42), channel_id=1, source_target_pairs={{0,32},{32,64},{64,96},{96,0},{1,33},{33,65},{65,97},{97,1},{2,34}... | collective-permute-start | bytes 884744 | tf_op jit(solution)/shard_map/ppermute | solution.py:42
  140.7 27.3 %collective-permute-start.19 = (bf16[384,384]{1,0:T(8,128)(2,1)S(1)}, bf16[384,384]{1,0:T(8,128)(2,1)S(1)}, u32[]{:S(2)}, u32[]{:S(2)}) collective-permute-start(bf16[384,384]{1,0:T(8,128)(2,1)S(1)} %get-tuple-element.43), channel_id=1, source_target_pairs={{0,64},{32,96},{64,0},{96,32},{1,65},{33,97},{65,1},{97,33},{2,66}... | collective-permute-start | bytes 884744 | tf_op jit(solution)/shard_map/ppermute | solution.py:42
  143.5 24.4 %collective-permute-start.20 = (bf16[384,384]{1,0:T(8,128)(2,1)S(1)}, bf16[384,384]{1,0:T(8,128)(2,1)S(1)}, u32[]{:S(2)}, u32[]{:S(2)}) collective-permute-start(bf16[384,384]{1,0:T(8,128)(2,1)S(1)} %get-tuple-element.44), channel_id=1, source_target_pairs={{0,96},{32,0},{64,32},{96,64},{1,97},{33,1},{65,33},{97,65},{2,98}... | collective-permute-start | bytes 884744 | tf_op jit(solution)/shard_map/ppermute | solution.py:42
  148.3 12.4 %collective-permute-start.25 = (f32[1,384]{1,0:T(1,128)S(1)}, f32[1,384]{1,0:T(1,128)S(1)}, u32[]{:S(2)}, u32[]{:S(2)}) collective-permute-start(f32[1,384]{1,0:T(1,128)S(1)} %get-tuple-element.52), channel_id=1, source_target_pairs={{0,2},{2,0},{1,3},{3,1},{4,6},{6,4},{5,7},{7,5},{8,10},{10,8},{9,1... | collective-permute-start | bytes 4616 | tf_op jit(solution)/shard_map/ppermute | solution.py:46
  160.7 25.8 %collective-permute-start.26 = (bf16[384,384]{1,0:T(8,128)(2,1)S(1)}, bf16[384,384]{1,0:T(8,128)(2,1)S(1)}, u32[]{:S(2)}, u32[]{:S(2)}) collective-permute-start(bf16[384,384]{1,0:T(8,128)(2,1)S(1)} %get-tuple-element.54), channel_id=1, source_target_pairs={{0,2},{2,0},{1,3},{3,1},{4,6},{6,4},{5,7},{7,5},{8,10},{10,8},{9,1... | collective-permute-start | bytes 884744 | tf_op jit(solution)/shard_map/ppermute | solution.py:46
  168.9 17.6 %all-to-all-start.2 = ((f32[16,1,384]{2,1,0:T(1,128)}), f32[16,1,384]{2,1,0:T(1,128)S(1)}, u32[]{:S(2)}, u32[]{:S(2)}) async-start(f32[16,1,384]{2,1,0:T(1,128)} %broadcast_in_dim.12), calls=%async_computation.2 | async-start | bytes 49152 | tf_op jit(solution)/shard_map/all_to_all | solution.py:232
  (19 other events, 425.0 us)
Sparse Core Ops, SparseCore 0:
  38.0 68.9 all-gather.1

commit v9 on v8

--- a/solution.py
+++ b/solution.py
@@ -18,6 +18,7 @@
 SMEM = pl.BlockSpec(memory_space=pltpu.SMEM)
 HBM = pl.BlockSpec(memory_space=pltpu.HBM)
 BF16, F32 = jnp.bfloat16, jnp.float32
+SUMS = 16
 
 
 def call(body, outs, ins, args, scratch=(), flops=0, vmem=48):
@@ -122,11 +123,27 @@
         pieces[step][...] = (ours[:, at].astype(F32) + sent[:, at].astype(F32)).astype(BF16)
 
 
+def summed(pieces):
+    turned = sum(piece[...].astype(F32) for piece in pieces).T
+    return turned, jnp.sum(turned * turned, axis=0, keepdims=True)
+
+
 def add_x(*refs):
     pieces, total, sums = refs[:X], refs[X], refs[X + 1]
-    turned = sum(piece[...].astype(F32) for piece in pieces).T
-    total[...] = turned.astype(total.dtype)
-    sums[...] = jnp.sum(turned * turned, axis=0, keepdims=True)
+    total[...], sums[...] = summed(pieces)
+
+
+def add_x_to_send(*refs):
+    pieces, total = refs[:X], refs[X]
+    turned, rest = summed(pieces)
+    total[:HALF] = turned.astype(BF16)
+    row = lax.broadcasted_iota(jnp.int32, (SUMS, UNIT), 0)
+    split = jnp.zeros((SUMS, UNIT), F32)
+    for which in range(3):
+        part = rest.astype(BF16).astype(F32)
+        split = jnp.where(row == which, part, split)
+        rest = rest - part
+    total[HALF:] = split.astype(BF16)
 
 
 def finish(place, keep, mine, other, sums, flows):
@@ -163,10 +180,8 @@
             ends[which] = [up, down]
             shards += [up, down]
             order += [(which, d, 0, CORE * SUB), (which, Y - d, 0, CORE * SUB)]
-    for which in (0, 1):
-        up, down = ends[which]
-        shards += [shift_y(up[:SUB], 1), shift_y(down[SUB:], -1)]
-        order += [(which, Y // 2, 0, SUB), (which, Y // 2, SUB, SUB)]
+    shards += [shift_y(ends[0][1], -1), shift_y(ends[1][0], 1)]
+    order += [(0, Y // 2, 0, CORE * SUB), (1, Y // 2, 0, CORE * SUB)]
     return shards, tuple(order)
 
 
@@ -210,25 +225,25 @@
         vmem=60,
     )
 
-    def total(apart, dtype):
-        return call(add_x, [((HALF, UNIT), dtype), ((1, UNIT), F32)], [VMEM] * X, apart)
-
-    def over_x(ours, theirs):
-        apart = call(
+    def over_cores(ours, theirs):
+        return call(
             add_core,
             [((UNIT, HALF), BF16)] * X,
             [SMEM, VMEM, VMEM],
             (x[None], ours, swap(theirs, "core")),
         )
+
+    def over_x(apart):
         return [apart[0]] + [shift_x(apart[step], step) for step in range(1, X)]
 
-    apart = over_x(ours, theirs)
-    apart_near = over_x(ours_near, theirs_near)
-    other, sums = total(apart, BF16)
-    sums, other = in_order(swap(sums, "zhi"), other)
+    apart = over_x(over_cores(ours, theirs))
+    apart_near, apart = in_order(over_cores(ours_near, theirs_near), apart)
+    apart_near = over_x(apart_near)
+    other = call(add_x_to_send, [((HALF + SUMS, UNIT), BF16)], [VMEM] * X, apart)[0]
     other = swap(other, "zhi")
-    mine, own_sums = total(apart_near, F32)
-    sums = jnp.broadcast_to(sums + own_sums, (Z_LO * X, 1, UNIT))
+    mine, sums = call(add_x, [((HALF, UNIT), F32), ((1, UNIT), F32)], [VMEM] * X, apart_near)
+    sums = sums + other[HALF : HALF + 3].astype(F32).sum(axis=0, keepdims=True)
+    sums = jnp.broadcast_to(sums, (Z_LO * X, 1, UNIT))
     sums = lax.all_to_all(sums, ("zlo", "x"), split_axis=0, concat_axis=0, tiled=True)
     return call(
         finish,

time: 198 us -> 199 us (level)
  waiting for transfers between devices: 32.6 us -> 55.7 us
  starting transfers between devices: 124 us -> 103 us
    ppermute x6, waiting for transfers between devices: 1.06 us -> 19.2 us  [shift_x(): return lax.ppermute(shard, 'x', [(i, (i + step) % X) for i in range(X)])]
    ppermute x5 -> x4, starting transfers between devices: 29.3 us -> 16.6 us  [swap(): return lax.ppermute(shard, axis, [(0, 1), (1, 0)])]
    ppermute x16 -> x14, starting transfers between devices: 52.5 us -> 43 us  [shift_y(): return lax.ppermute(shard, 'y', [(i, (i + step) % Y) for i in range(Y)])]
    ppermute x16 -> x14, waiting for transfers between devices: 1.54 us -> 8.46 us  [shift_y(): return lax.ppermute(shard, 'y', [(i, (i + step) % Y) for i in range(Y)])]
    all_to_all x1, waiting for transfers between devices: 10.5 us -> 6.82 us  [local(): lax.all_to_all(sums, ('zlo', 'x'), split_axis=0, concat_axis=0, tiled=True)]
    all_gather x1, waiting for transfers between devices: 6.51 us -> 9.23 us  [local(): right = lax.all_gather(right, ('zhi', 'zlo'), axis=0, tiled=True)]
    ppermute x5 -> x4, waiting for transfers between devices: 11 us -> 10.1 us  [swap(): return lax.ppermute(shard, axis, [(0, 1), (1, 0)])]
  transfers between devices with their start and end apart: 31 -> 28, of which waited for: 9 -> 15; matrix products, arithmetic and copies ran while one was open for 1% -> 0% of each run, Pallas kernels for 1% -> 0%
where the time goes in v9:
time: 199 us; the launch traced here: 197 us
  starting transfers between devices  103 us (52%)
  waiting for transfers between devices  55.7 us (28%)
  Pallas kernels  20 us (10%)
  between operations  13.9 us (7%)
  local copies, waits for them, and re-layouts  4.11 us (2%)
    ppermute x14, starting transfers between devices, shift_y(): return lax.ppermute(shard, 'y', [(i, (i + step) % Y) for i in range(Y)])  43 us
    ppermute x6, starting transfers between devices, shift_x(): return lax.ppermute(shard, 'x', [(i, (i + step) % X) for i in range(X)])  20.9 us
    pallas_call x8, Pallas kernels, call(): pl.pallas_call(body, out_shape=shapes, in_specs=ins, out_specs=[VMEM] * l...  20 us
    ppermute x6, waiting for transfers between devices, shift_x(): return lax.ppermute(shard, 'x', [(i, (i + step) % X) for i in range(X)])  19.2 us
    ppermute x4, starting transfers between devices, swap(): return lax.ppermute(shard, axis, [(0, 1), (1, 0)])  16.6 us
    all_to_all x2, starting transfers between devices, spread_over(): lax.all_to_all(array, ('x', 'core'), split_axis=0, concat_axis=0, tiled=T...  15.8 us
    ppermute x4, waiting for transfers between devices, swap(): return lax.ppermute(shard, axis, [(0, 1), (1, 0)])  10.1 us
    all_gather x1, waiting for transfers between devices, local(): right = lax.all_gather(right, ('zhi', 'zlo'), axis=0, tiled=True)  9.23 us
  transfers between devices with their start and end apart: 28, of which 15 were waited for; matrix products, arithmetic and copies ran while one was open for 0% of the time, Pallas kernels for 0%

profile of v9, /device:TPU:1, one launch (start us, length us, event | category | flops | bytes accessed | tf_op | source)
XLA Modules:
  0.0 197.3 jit_solution(1217480088835702377)
XLA Ops:
  10.5 10.3 %all-to-all-start = ((bf16[8,3,48,384]{3,2,1,0:T(8,128)(2,1)}), bf16[8,3,48,384]{3,2,1,0:T(8,128)(2,1)S(1)}, u32[]{:S(2)}, u32[]{:S(2)}) async-start(bf16[8,3,48,384]{3,2,1,0:T(8,128)(2,1)} %get-tuple-element.35), calls=%async_computation | async-start | bytes 1769472 | tf_op jit(solution)/shard_map/all_to_all | solution.py:51
  20.8 6.1 %collective-permute-start = (bf16[384,384]{1,0:T(8,128)(2,1)S(1)}, bf16[384,384]{1,0:T(8,128)(2,1)}, u32[]{:S(2)}, u32[]{:S(2)}) collective-permute-start(bf16[384,384]{1,0:T(8,128)(2,1)S(1)} %get-tuple-element.36), channel_id=1, source_target_pairs={{0,2},{2,0},{1,3},{3,1},{4,6},{6,4},{5,7},{7,5},{8,10},{10,8},{9,1... | collective-permute-start | bytes 884744 | tf_op jit(solution)/shard_map/ppermute | solution.py:47
  26.9 9.3 %collective-permute-done = bf16[384,384]{1,0:T(8,128)(2,1)} collective-permute-done((bf16[384,384]{1,0:T(8,128)(2,1)S(1)}, bf16[384,384]{1,0:T(8,128)(2,1)}, u32[]{:S(2)}, u32[]{:S(2)}) %collective-permute-start) | collective-permute-done | bytes 294944 | tf_op jit(solution)/shard_map/ppermute | solution.py:47
  37.9 1.9 collective-permute-start.1
  39.8 5.5 %all-to-all-start.1 = ((bf16[8,48,384]{2,1,0:T(8,128)(2,1)}), bf16[8,48,384]{2,1,0:T(8,128)(2,1)S(1)}, u32[]{:S(2)}, u32[]{:S(2)}) async-start(bf16[8,48,384]{2,1,0:T(8,128)(2,1)} %bitcast.5), calls=%async_computation.1 | async-start | bytes 589824 | tf_op jit(solution)/shard_map/all_to_all | solution.py:51
  45.3 4.8 %collective-permute-start.2 = (bf16[96,1536]{1,0:T(8,128)(2,1)S(1)}, bf16[96,1536]{1,0:T(8,128)(2,1)S(1)}, u32[]{:S(2)}, u32[]{:S(2)}) collective-permute-start(bf16[96,1536]{1,0:T(8,128)(2,1)S(1)} %get-tuple-element.38.refs_0_), channel_id=1, source_target_pairs={{0,28},{4,0},{8,4},{12,8},{16,12},{20,16},{24,20},{28,24},{1,29},{... | collective-permute-start | bytes 884744 | tf_op jit(solution)/shard_map/ppermute | solution.py:39
  50.2 2.0 all-to-all-done.1
  52.2 2.6 %collective-permute-start.3 = (bf16[96,1536]{1,0:T(8,128)(2,1)S(1)}, bf16[96,1536]{1,0:T(8,128)(2,1)S(1)}, u32[]{:S(2)}, u32[]{:S(2)}) collective-permute-start(bf16[96,1536]{1,0:T(8,128)(2,1)S(1)} %bitcast.13), channel_id=1, source_target_pairs={{0,4},{4,8},{8,12},{12,16},{16,20},{20,24},{24,28},{28,0},{1,5},{5... | collective-permute-start | bytes 884744 | tf_op jit(solution)/shard_map/ppermute | solution.py:39
  54.8 4.2 %collective-permute-start.4 = (bf16[96,1536]{1,0:T(8,128)(2,1)S(1)}, bf16[96,1536]{1,0:T(8,128)(2,1)S(1)}, u32[]{:S(2)}, u32[]{:S(2)}) collective-permute-start(bf16[96,1536]{1,0:T(8,128)(2,1)S(1)} %bitcast.14), channel_id=1, source_target_pairs={{0,28},{4,0},{8,4},{12,8},{16,12},{20,16},{24,20},{28,24},{1,29},{... | collective-permute-start | bytes 884744 | tf_op jit(solution)/shard_map/ppermute | solution.py:39
  59.0 3.4 %collective-permute-start.6 = (bf16[96,1536]{1,0:T(8,128)(2,1)S(1)}, bf16[96,1536]{1,0:T(8,128)(2,1)S(1)}, u32[]{:S(2)}, u32[]{:S(2)}) collective-permute-start(bf16[96,1536]{1,0:T(8,128)(2,1)S(1)} %collective-permute-done.2.refs_3_), channel_id=1, source_target_pairs={{0,28},{4,0},{8,4},{12,8},{16,12},{20,16},{24,20},{28,24},{1,29},{... | collective-permute-start | bytes 884744 | tf_op jit(solution)/shard_map/ppermute | solution.py:39
  65.3 2.3 %collective-permute-start.5 = (bf16[96,1536]{1,0:T(8,128)(2,1)S(1)}, bf16[96,1536]{1,0:T(8,128)(2,1)S(1)}, u32[]{:S(2)}, u32[]{:S(2)}) collective-permute-start(bf16[96,1536]{1,0:T(8,128)(2,1)S(1)} %collective-permute-done.1.refs_2_), channel_id=1, source_target_pairs={{0,4},{4,8},{8,12},{12,16},{16,20},{20,24},{24,28},{28,0},{1,5},{5... | collective-permute-start | bytes 884744 | tf_op jit(solution)/shard_map/ppermute | solution.py:39
  67.6 4.2 %collective-permute-start.8 = (bf16[96,1536]{1,0:T(8,128)(2,1)S(1)}, bf16[96,1536]{1,0:T(8,128)(2,1)S(1)}, u32[]{:S(2)}, u32[]{:S(2)}) collective-permute-start(bf16[96,1536]{1,0:T(8,128)(2,1)S(1)} %collective-permute-done.4.refs_5_), channel_id=1, source_target_pairs={{0,28},{4,0},{8,4},{12,8},{16,12},{20,16},{24,20},{28,24},{1,29},{... | collective-permute-start | bytes 884744 | tf_op jit(solution)/shard_map/ppermute | solution.py:39
  71.9 4.0 %collective-permute-start.10 = (bf16[96,1536]{1,0:T(8,128)(2,1)S(1)}, bf16[96,1536]{1,0:T(8,128)(2,1)S(1)}, u32[]{:S(2)}, u32[]{:S(2)}) collective-permute-start(bf16[96,1536]{1,0:T(8,128)(2,1)S(1)} %collective-permute-done.6.refs_7_), channel_id=1, source_target_pairs={{0,28},{4,0},{8,4},{12,8},{16,12},{20,16},{24,20},{28,24},{1,29},{... | collective-permute-start | bytes 884744 | tf_op jit(solution)/shard_map/ppermute | solution.py:39
  75.9 1.9 collective-permute-start.11
  77.9 2.0 %collective-permute-done.5.refs_6_ = bf16[96,1536]{1,0:T(8,128)(2,1)S(1)} collective-permute-done((bf16[96,1536]{1,0:T(8,128)(2,1)S(1)}, bf16[96,1536]{1,0:T(8,128)(2,1)S(1)}, u32[]{:S(2)}, u32[]{:S(2)}) %collective-permute-start.5) | collective-permute-done | bytes 294944 | tf_op jit(solution)/shard_map/ppermute | solution.py:39
  81.8 4.6 %collective-permute-start.12 = (bf16[96,1536]{1,0:T(8,128)(2,1)S(1)}, bf16[96,1536]{1,0:T(8,128)(2,1)}, u32[]{:S(2)}, u32[]{:S(2)}) collective-permute-start(bf16[96,1536]{1,0:T(8,128)(2,1)S(1)} %collective-permute-done.8.refs_9_), channel_id=1, source_target_pairs={{0,28},{4,0},{8,4},{12,8},{16,12},{20,16},{24,20},{28,24},{1,29},{... | collective-permute-start | bytes 884744 | tf_op jit(solution)/shard_map/ppermute | solution.py:39
  86.4 1.9 collective-permute-start.13
  88.3 3.4 %collective-permute-start.14 = (bf16[96,1536]{1,0:T(8,128)(2,1)S(1)}, bf16[96,1536]{1,0:T(8,128)(2,1)}, u32[]{:S(2)}, u32[]{:S(2)}) collective-permute-start(bf16[96,1536]{1,0:T(8,128)(2,1)S(1)} %collective-permute-done.11.refs_12_), channel_id=1, source_target_pairs={{0,4},{4,8},{8,12},{12,16},{16,20},{20,24},{24,28},{28,0},{1,5},{5... | collective-permute-start | bytes 884744 | tf_op jit(solution)/shard_map/ppermute | solution.py:39
  92.3 5.0 %collective-permute-done.13.refs_14_ = bf16[96,1536]{1,0:T(8,128)(2,1)} collective-permute-done((bf16[96,1536]{1,0:T(8,128)(2,1)S(1)}, bf16[96,1536]{1,0:T(8,128)(2,1)}, u32[]{:S(2)}, u32[]{:S(2)}) %collective-permute-start.13) | collective-permute-done | bytes 294944 | tf_op jit(solution)/shard_map/ppermute | solution.py:39
  97.8 9.2 %all-gather.2.cloned.1.call-done.refs_16_ = bf16[8,768,384]{2,1,0:T(8,128)(2,1)} async-done(((bf16[1,768,384]{2,1,0:T(8,128)(2,1)}), bf16[8,768,384]{2,1,0:T(8,128)(2,1)}) %all-gather.2.cloned.1.call-update) | async-done | bytes 4718608 | tf_op jit(solution)/shard_map/all_gather | solution.py:210
  107.1 13.6 %shard_map.39 = (bf16[384,1536]{1,0:T(8,128)(2,1)}, bf16[384,1536]{1,0:T(8,128)(2,1)}, bf16[384,1536]{1,0:T(8,128)(2,1)}, bf16[384,1536]{1,0:T(8,128)(2,1)}) custom-call(s32[2]{0:T(128)} %pad_add_fusion.place, bf16[96,1536]{1,0:T(8,128)(2,1)} %copy-done.3, bf16[96,1536]{1,0:T(8,128)(2,1)} %bitcast.15, bf16[96,1536]{1,0:T(8,128)(2,1)} %copy-done.6, ...), custom_call_target="tpu_custom_call" | custom-call | flops 7247757312 | bytes 14155784 | tf_op jit(solution)/shard_map/pallas_call | solution.py:27
  120.7 2.6 %collective-permute-start.16 = (bf16[384,1536]{1,0:T(8,128)(2,1)}, bf16[384,1536]{1,0:T(8,128)(2,1)S(1)}, u32[]{:S(2)}, u32[]{:S(2)}) collective-permute-start(bf16[384,1536]{1,0:T(8,128)(2,1)} %get-tuple-element.50), channel_id=1, source_target_pairs={{0,1},{1,0},{2,3},{3,2},{4,5},{5,4},{6,7},{7,6},{8,9},{9,8},{10,11... | collective-permute-start | bytes 3538952 | tf_op jit(solution)/shard_map/ppermute | solution.py:47
  127.5 3.2 %collective-permute-start.17 = (bf16[384,384]{1,0:T(8,128)(2,1)S(1)}, bf16[384,384]{1,0:T(8,128)(2,1)S(1)}, u32[]{:S(2)}, u32[]{:S(2)}) collective-permute-start(bf16[384,384]{1,0:T(8,128)(2,1)S(1)} %get-tuple-element.52), channel_id=1, source_target_pairs={{0,32},{32,64},{64,96},{96,0},{1,33},{33,65},{65,97},{97,1},{2,34}... | collective-permute-start | bytes 884744 | tf_op jit(solution)/shard_map/ppermute | solution.py:43
  130.8 4.3 %collective-permute-start.18 = (bf16[384,384]{1,0:T(8,128)(2,1)S(1)}, bf16[384,384]{1,0:T(8,128)(2,1)S(1)}, u32[]{:S(2)}, u32[]{:S(2)}) collective-permute-start(bf16[384,384]{1,0:T(8,128)(2,1)S(1)} %get-tuple-element.53), channel_id=1, source_target_pairs={{0,64},{32,96},{64,0},{96,32},{1,65},{33,97},{65,1},{97,33},{2,66}... | collective-permute-start | bytes 884744 | tf_op jit(solution)/shard_map/ppermute | solution.py:43
  135.1 3.1 %collective-permute-start.19 = (bf16[384,384]{1,0:T(8,128)(2,1)S(1)}, bf16[384,384]{1,0:T(8,128)(2,1)S(1)}, u32[]{:S(2)}, u32[]{:S(2)}) collective-permute-start(bf16[384,384]{1,0:T(8,128)(2,1)S(1)} %get-tuple-element.54), channel_id=1, source_target_pairs={{0,96},{32,0},{64,32},{96,64},{1,97},{33,1},{65,33},{97,65},{2,98}... | collective-permute-start | bytes 884744 | tf_op jit(solution)/shard_map/ppermute | solution.py:43
  139.0 7.2 %collective-permute-done.18.refs_2_ = bf16[384,384]{1,0:T(8,128)(2,1)S(1)} collective-permute-done((bf16[384,384]{1,0:T(8,128)(2,1)S(1)}, bf16[384,384]{1,0:T(8,128)(2,1)S(1)}, u32[]{:S(2)}, u32[]{:S(2)}) %collective-permute-start.18) | collective-permute-done | bytes 294944 | tf_op jit(solution)/shard_map/ppermute | solution.py:43
  147.8 6.0 %collective-permute-start.23 = (bf16[400,384]{1,0:T(8,128)(2,1)S(1)}, bf16[400,384]{1,0:T(8,128)(2,1)S(1)}, u32[]{:S(2)}, u32[]{:S(2)}) collective-permute-start(bf16[400,384]{1,0:T(8,128)(2,1)S(1)} %shard_map.43), channel_id=1, source_target_pairs={{0,2},{2,0},{1,3},{3,1},{4,6},{6,4},{5,7},{7,5},{8,10},{10,8},{9,1... | collective-permute-start | bytes 921608 | tf_op jit(solution)/shard_map/ppermute | solution.py:47
  153.8 3.5 %collective-permute-start.20 = (bf16[384,384]{1,0:T(8,128)(2,1)S(1)}, bf16[384,384]{1,0:T(8,128)(2,1)S(1)}, u32[]{:S(2)}, u32[]{:S(2)}) collective-permute-start(bf16[384,384]{1,0:T(8,128)(2,1)S(1)} %get-tuple-element.56), channel_id=1, source_target_pairs={{0,32},{32,64},{64,96},{96,0},{1,33},{33,65},{65,97},{97,1},{2,34}... | collective-permute-start | bytes 884744 | tf_op jit(solution)/shard_map/ppermute | solution.py:43
  157.3 4.9 %collective-permute-start.21 = (bf16[384,384]{1,0:T(8,128)(2,1)S(1)}, bf16[384,384]{1,0:T(8,128)(2,1)S(1)}, u32[]{:S(2)}, u32[]{:S(2)}) collective-permute-start(bf16[384,384]{1,0:T(8,128)(2,1)S(1)} %get-tuple-element.57), channel_id=1, source_target_pairs={{0,64},{32,96},{64,0},{96,32},{1,65},{33,97},{65,1},{97,33},{2,66}... | collective-permute-start | bytes 884744 | tf_op jit(solution)/shard_map/ppermute | solution.py:43
  165.0 7.8 %collective-permute-done.21.refs_2_ = bf16[384,384]{1,0:T(8,128)(2,1)S(1)} collective-permute-done((bf16[384,384]{1,0:T(8,128)(2,1)S(1)}, bf16[384,384]{1,0:T(8,128)(2,1)S(1)}, u32[]{:S(2)}, u32[]{:S(2)}) %collective-permute-start.21) | collective-permute-done | bytes 294944 | tf_op jit(solution)/shard_map/ppermute | solution.py:43
  175.2 6.5 %all-to-all-start.2 = ((f32[16,1,384]{2,1,0:T(1,128)}), f32[16,1,384]{2,1,0:T(1,128)S(1)}, u32[]{:S(2)}, u32[]{:S(2)}) async-start(f32[16,1,384]{2,1,0:T(1,128)} %broadcast_in_dim.16), calls=%async_computation.2 | async-start | bytes 49152 | tf_op jit(solution)/shard_map/all_to_all | solution.py:247
  181.8 6.8 %all-to-all-done.2.sums = f32[16,1,384]{2,1,0:T(1,128)S(1)} async-done(((f32[16,1,384]{2,1,0:T(1,128)}), f32[16,1,384]{2,1,0:T(1,128)S(1)}, u32[]{:S(2)}, u32[]{:S(2)}) %all-to-all-start.2) | async-done | bytes 24608 | tf_op jit(solution)/shard_map/all_to_all | solution.py:247
  (73 shorter events, 25.2 us)
Async XLA Ops:
  10.5 25.8 %all-to-all-start = ((bf16[8,3,48,384]{3,2,1,0:T(8,128)(2,1)}), bf16[8,3,48,384]{3,2,1,0:T(8,128)(2,1)S(1)}, u32[]{:S(2)}, u32[]{:S(2)}) async-start(bf16[8,3,48,384]{3,2,1,0:T(8,128)(2,1)} %get-tuple-element.35), calls=%async_computation | async-start | bytes 1769472 | tf_op jit(solution)/shard_map/all_to_all | solution.py:51
  20.8 86.2 %all-gather.2.cloned.1.call-start = ((), (), s32[]{:S(2)}) async-start(), calls=%async_computation.3 | async-start | bytes 5308416 | tf_op jit(solution)/shard_map/all_gather | solution.py:210
  20.8 15.4 %collective-permute-start = (bf16[384,384]{1,0:T(8,128)(2,1)S(1)}, bf16[384,384]{1,0:T(8,128)(2,1)}, u32[]{:S(2)}, u32[]{:S(2)}) collective-permute-start(bf16[384,384]{1,0:T(8,128)(2,1)S(1)} %get-tuple-element.36), channel_id=1, source_target_pairs={{0,2},{2,0},{1,3},{3,1},{4,6},{6,4},{5,7},{7,5},{8,10},{10,8},{9,1... | collective-permute-start | bytes 884744 | tf_op jit(solution)/shard_map/ppermute | solution.py:47
  37.9 69.1 %copy-start.3 = (bf16[96,1536]{1,0:T(8,128)(2,1)}, bf16[96,1536]{1,0:T(8,128)(2,1)S(1)}, u32[]{:S(2)}) copy-start(bf16[96,1536]{1,0:T(8,128)(2,1)S(1)} %get-tuple-element.38.refs_0_) | copy-start | bytes 884740
  37.9 14.3 %collective-permute-start.1 = (bf16[96,1536]{1,0:T(8,128)(2,1)S(1)}, bf16[96,1536]{1,0:T(8,128)(2,1)S(1)}, u32[]{:S(2)}, u32[]{:S(2)}) collective-permute-start(bf16[96,1536]{1,0:T(8,128)(2,1)S(1)} %get-tuple-element.38.refs_0_), channel_id=1, source_target_pairs={{0,4},{4,8},{8,12},{12,16},{16,20},{20,24},{24,28},{28,0},{1,5},{5... | collective-permute-start | bytes 884744 | tf_op jit(solution)/shard_map/ppermute | solution.py:39
  39.8 12.3 %all-to-all-start.1 = ((bf16[8,48,384]{2,1,0:T(8,128)(2,1)}), bf16[8,48,384]{2,1,0:T(8,128)(2,1)S(1)}, u32[]{:S(2)}, u32[]{:S(2)}) async-start(bf16[8,48,384]{2,1,0:T(8,128)(2,1)} %bitcast.5), calls=%async_computation.1 | async-start | bytes 589824 | tf_op jit(solution)/shard_map/all_to_all | solution.py:51
  45.3 13.7 %collective-permute-start.2 = (bf16[96,1536]{1,0:T(8,128)(2,1)S(1)}, bf16[96,1536]{1,0:T(8,128)(2,1)S(1)}, u32[]{:S(2)}, u32[]{:S(2)}) collective-permute-start(bf16[96,1536]{1,0:T(8,128)(2,1)S(1)} %get-tuple-element.38.refs_0_), channel_id=1, source_target_pairs={{0,28},{4,0},{8,4},{12,8},{16,12},{20,16},{24,20},{28,24},{1,29},{... | collective-permute-start | bytes 884744 | tf_op jit(solution)/shard_map/ppermute | solution.py:39
  52.2 54.8 %copy-start.4 = (bf16[4,12,8,384]{3,2,0,1:T(8,128)(2,1)}, bf16[4,12,8,384]{3,2,0,1:T(8,128)(2,1)S(1)}, u32[]{:S(2)}) copy-start(bf16[4,12,8,384]{3,2,0,1:T(8,128)(2,1)S(1)} %copy.12) | copy-start | bytes 884740
  52.2 54.8 %copy-start.6 = (bf16[96,1536]{1,0:T(8,128)(2,1)}, bf16[96,1536]{1,0:T(8,128)(2,1)S(1)}, u32[]{:S(2)}) copy-start(bf16[96,1536]{1,0:T(8,128)(2,1)S(1)} %collective-permute-done.1.refs_2_) | copy-start | bytes 884740
  52.2 11.2 %collective-permute-start.3 = (bf16[96,1536]{1,0:T(8,128)(2,1)S(1)}, bf16[96,1536]{1,0:T(8,128)(2,1)S(1)}, u32[]{:S(2)}, u32[]{:S(2)}) collective-permute-start(bf16[96,1536]{1,0:T(8,128)(2,1)S(1)} %bitcast.13), channel_id=1, source_target_pairs={{0,4},{4,8},{8,12},{12,16},{16,20},{20,24},{24,28},{28,0},{1,5},{5... | collective-permute-start | bytes 884744 | tf_op jit(solution)/shard_map/ppermute | solution.py:39
  54.8 12.8 %collective-permute-start.4 = (bf16[96,1536]{1,0:T(8,128)(2,1)S(1)}, bf16[96,1536]{1,0:T(8,128)(2,1)S(1)}, u32[]{:S(2)}, u32[]{:S(2)}) collective-permute-start(bf16[96,1536]{1,0:T(8,128)(2,1)S(1)} %bitcast.14), channel_id=1, source_target_pairs={{0,28},{4,0},{8,4},{12,8},{16,12},{20,16},{24,20},{28,24},{1,29},{... | collective-permute-start | bytes 884744 | tf_op jit(solution)/shard_map/ppermute | solution.py:39
  59.0 48.0 %copy-start.7 = (bf16[96,1536]{1,0:T(8,128)(2,1)}, bf16[96,1536]{1,0:T(8,128)(2,1)S(1)}, u32[]{:S(2)}) copy-start(bf16[96,1536]{1,0:T(8,128)(2,1)S(1)} %collective-permute-done.2.refs_3_) | copy-start | bytes 884740
  59.0 12.9 %collective-permute-start.6 = (bf16[96,1536]{1,0:T(8,128)(2,1)S(1)}, bf16[96,1536]{1,0:T(8,128)(2,1)S(1)}, u32[]{:S(2)}, u32[]{:S(2)}) collective-permute-start(bf16[96,1536]{1,0:T(8,128)(2,1)S(1)} %collective-permute-done.2.refs_3_), channel_id=1, source_target_pairs={{0,28},{4,0},{8,4},{12,8},{16,12},{20,16},{24,20},{28,24},{1,29},{... | collective-permute-start | bytes 884744 | tf_op jit(solution)/shard_map/ppermute | solution.py:39
  63.4 12.5 %collective-permute-start.7 = (bf16[96,1536]{1,0:T(8,128)(2,1)S(1)}, bf16[96,1536]{1,0:T(8,128)(2,1)S(1)}, u32[]{:S(2)}, u32[]{:S(2)}) collective-permute-start(bf16[96,1536]{1,0:T(8,128)(2,1)S(1)} %collective-permute-done.3.refs_4_), channel_id=1, source_target_pairs={{0,4},{4,8},{8,12},{12,16},{16,20},{20,24},{24,28},{28,0},{1,5},{5... | collective-permute-start | bytes 884744 | tf_op jit(solution)/shard_map/ppermute | solution.py:39
  65.3 14.5 %collective-permute-start.5 = (bf16[96,1536]{1,0:T(8,128)(2,1)S(1)}, bf16[96,1536]{1,0:T(8,128)(2,1)S(1)}, u32[]{:S(2)}, u32[]{:S(2)}) collective-permute-start(bf16[96,1536]{1,0:T(8,128)(2,1)S(1)} %collective-permute-done.1.refs_2_), channel_id=1, source_target_pairs={{0,4},{4,8},{8,12},{12,16},{16,20},{20,24},{24,28},{28,0},{1,5},{5... | collective-permute-start | bytes 884744 | tf_op jit(solution)/shard_map/ppermute | solution.py:39
  67.6 14.1 %collective-permute-start.8 = (bf16[96,1536]{1,0:T(8,128)(2,1)S(1)}, bf16[96,1536]{1,0:T(8,128)(2,1)S(1)}, u32[]{:S(2)}, u32[]{:S(2)}) collective-permute-start(bf16[96,1536]{1,0:T(8,128)(2,1)S(1)} %collective-permute-done.4.refs_5_), channel_id=1, source_target_pairs={{0,28},{4,0},{8,4},{12,8},{16,12},{20,16},{24,20},{28,24},{1,29},{... | collective-permute-start | bytes 884744 | tf_op jit(solution)/shard_map/ppermute | solution.py:39
  71.9 14.5 %collective-permute-start.10 = (bf16[96,1536]{1,0:T(8,128)(2,1)S(1)}, bf16[96,1536]{1,0:T(8,128)(2,1)S(1)}, u32[]{:S(2)}, u32[]{:S(2)}) collective-permute-start(bf16[96,1536]{1,0:T(8,128)(2,1)S(1)} %collective-permute-done.6.refs_7_), channel_id=1, source_target_pairs={{0,28},{4,0},{8,4},{12,8},{16,12},{20,16},{24,20},{28,24},{1,29},{... | collective-permute-start | bytes 884744 | tf_op jit(solution)/shard_map/ppermute | solution.py:39
  75.9 12.4 %collective-permute-start.11 = (bf16[96,1536]{1,0:T(8,128)(2,1)S(1)}, bf16[96,1536]{1,0:T(8,128)(2,1)S(1)}, u32[]{:S(2)}, u32[]{:S(2)}) collective-permute-start(bf16[96,1536]{1,0:T(8,128)(2,1)S(1)} %collective-permute-done.7.refs_8_), channel_id=1, source_target_pairs={{0,4},{4,8},{8,12},{12,16},{16,20},{20,24},{24,28},{28,0},{1,5},{5... | collective-permute-start | bytes 884744 | tf_op jit(solution)/shard_map/ppermute | solution.py:39
  79.8 12.5 %collective-permute-start.9 = (bf16[96,1536]{1,0:T(8,128)(2,1)S(1)}, bf16[96,1536]{1,0:T(8,128)(2,1)}, u32[]{:S(2)}, u32[]{:S(2)}) collective-permute-start(bf16[96,1536]{1,0:T(8,128)(2,1)S(1)} %collective-permute-done.5.refs_6_), channel_id=1, source_target_pairs={{0,4},{4,8},{8,12},{12,16},{16,20},{20,24},{24,28},{28,0},{1,5},{5... | collective-permute-start | bytes 884744 | tf_op jit(solution)/shard_map/ppermute | solution.py:39
  81.8 10.6 %collective-permute-start.12 = (bf16[96,1536]{1,0:T(8,128)(2,1)S(1)}, bf16[96,1536]{1,0:T(8,128)(2,1)}, u32[]{:S(2)}, u32[]{:S(2)}) collective-permute-start(bf16[96,1536]{1,0:T(8,128)(2,1)S(1)} %collective-permute-done.8.refs_9_), channel_id=1, source_target_pairs={{0,28},{4,0},{8,4},{12,8},{16,12},{20,16},{24,20},{28,24},{1,29},{... | collective-permute-start | bytes 884744 | tf_op jit(solution)/shard_map/ppermute | solution.py:39
  86.4 10.9 %collective-permute-start.13 = (bf16[96,1536]{1,0:T(8,128)(2,1)S(1)}, bf16[96,1536]{1,0:T(8,128)(2,1)}, u32[]{:S(2)}, u32[]{:S(2)}) collective-permute-start(bf16[96,1536]{1,0:T(8,128)(2,1)S(1)} %collective-permute-done.10.refs_11_), channel_id=1, source_target_pairs={{0,28},{4,0},{8,4},{12,8},{16,12},{20,16},{24,20},{28,24},{1,29},{... | collective-permute-start | bytes 884744 | tf_op jit(solution)/shard_map/ppermute | solution.py:39
  88.3 9.4 %collective-permute-start.14 = (bf16[96,1536]{1,0:T(8,128)(2,1)S(1)}, bf16[96,1536]{1,0:T(8,128)(2,1)}, u32[]{:S(2)}, u32[]{:S(2)}) collective-permute-start(bf16[96,1536]{1,0:T(8,128)(2,1)S(1)} %collective-permute-done.11.refs_12_), channel_id=1, source_target_pairs={{0,4},{4,8},{8,12},{12,16},{16,20},{20,24},{24,28},{28,0},{1,5},{5... | collective-permute-start | bytes 884744 | tf_op jit(solution)/shard_map/ppermute | solution.py:39
  120.7 5.3 %collective-permute-start.16 = (bf16[384,1536]{1,0:T(8,128)(2,1)}, bf16[384,1536]{1,0:T(8,128)(2,1)S(1)}, u32[]{:S(2)}, u32[]{:S(2)}) collective-permute-start(bf16[384,1536]{1,0:T(8,128)(2,1)} %get-tuple-element.50), channel_id=1, source_target_pairs={{0,1},{1,0},{2,3},{3,2},{4,5},{5,4},{6,7},{7,6},{8,9},{9,8},{10,11... | collective-permute-start | bytes 3538952 | tf_op jit(solution)/shard_map/ppermute | solution.py:47
  123.3 14.9 %collective-permute-start.15 = (bf16[384,1536]{1,0:T(8,128)(2,1)}, bf16[384,1536]{1,0:T(8,128)(2,1)S(1)}, u32[]{:S(2)}, u32[]{:S(2)}) collective-permute-start(bf16[384,1536]{1,0:T(8,128)(2,1)} %get-tuple-element.44), channel_id=1, source_target_pairs={{0,1},{1,0},{2,3},{3,2},{4,5},{5,4},{6,7},{7,6},{8,9},{9,8},{10,11... | collective-permute-start | bytes 3538952 | tf_op jit(solution)/shard_map/ppermute | solution.py:47
  127.5 11.5 %collective-permute-start.17 = (bf16[384,384]{1,0:T(8,128)(2,1)S(1)}, bf16[384,384]{1,0:T(8,128)(2,1)S(1)}, u32[]{:S(2)}, u32[]{:S(2)}) collective-permute-start(bf16[384,384]{1,0:T(8,128)(2,1)S(1)} %get-tuple-element.52), channel_id=1, source_target_pairs={{0,32},{32,64},{64,96},{96,0},{1,33},{33,65},{65,97},{97,1},{2,34}... | collective-permute-start | bytes 884744 | tf_op jit(solution)/shard_map/ppermute | solution.py:43
  130.8 15.5 %collective-permute-start.18 = (bf16[384,384]{1,0:T(8,128)(2,1)S(1)}, bf16[384,384]{1,0:T(8,128)(2,1)S(1)}, u32[]{:S(2)}, u32[]{:S(2)}) collective-permute-start(bf16[384,384]{1,0:T(8,128)(2,1)S(1)} %get-tuple-element.53), channel_id=1, source_target_pairs={{0,64},{32,96},{64,0},{96,32},{1,65},{33,97},{65,1},{97,33},{2,66}... | collective-permute-start | bytes 884744 | tf_op jit(solution)/shard_map/ppermute | solution.py:43
  135.1 12.4 %collective-permute-start.19 = (bf16[384,384]{1,0:T(8,128)(2,1)S(1)}, bf16[384,384]{1,0:T(8,128)(2,1)S(1)}, u32[]{:S(2)}, u32[]{:S(2)}) collective-permute-start(bf16[384,384]{1,0:T(8,128)(2,1)S(1)} %get-tuple-element.54), channel_id=1, source_target_pairs={{0,96},{32,0},{64,32},{96,64},{1,97},{33,1},{65,33},{97,65},{2,98}... | collective-permute-start | bytes 884744 | tf_op jit(solution)/shard_map/ppermute | solution.py:43
  147.8 26.8 %collective-permute-start.23 = (bf16[400,384]{1,0:T(8,128)(2,1)S(1)}, bf16[400,384]{1,0:T(8,128)(2,1)S(1)}, u32[]{:S(2)}, u32[]{:S(2)}) collective-permute-start(bf16[400,384]{1,0:T(8,128)(2,1)S(1)} %shard_map.43), channel_id=1, source_target_pairs={{0,2},{2,0},{1,3},{3,1},{4,6},{6,4},{5,7},{7,5},{8,10},{10,8},{9,1... | collective-permute-start | bytes 921608 | tf_op jit(solution)/shard_map/ppermute | solution.py:47
  153.8 11.2 %collective-permute-start.20 = (bf16[384,384]{1,0:T(8,128)(2,1)S(1)}, bf16[384,384]{1,0:T(8,128)(2,1)S(1)}, u32[]{:S(2)}, u32[]{:S(2)}) collective-permute-start(bf16[384,384]{1,0:T(8,128)(2,1)S(1)} %get-tuple-element.56), channel_id=1, source_target_pairs={{0,32},{32,64},{64,96},{96,0},{1,33},{33,65},{65,97},{97,1},{2,34}... | collective-permute-start | bytes 884744 | tf_op jit(solution)/shard_map/ppermute | solution.py:43
  157.3 15.5 %collective-permute-start.21 = (bf16[384,384]{1,0:T(8,128)(2,1)S(1)}, bf16[384,384]{1,0:T(8,128)(2,1)S(1)}, u32[]{:S(2)}, u32[]{:S(2)}) collective-permute-start(bf16[384,384]{1,0:T(8,128)(2,1)S(1)} %get-tuple-element.57), channel_id=1, source_target_pairs={{0,64},{32,96},{64,0},{96,32},{1,65},{33,97},{65,1},{97,33},{2,66}... | collective-permute-start | bytes 884744 | tf_op jit(solution)/shard_map/ppermute | solution.py:43
  162.1 12.2 %collective-permute-start.22 = (bf16[384,384]{1,0:T(8,128)(2,1)S(1)}, bf16[384,384]{1,0:T(8,128)(2,1)S(1)}, u32[]{:S(2)}, u32[]{:S(2)}) collective-permute-start(bf16[384,384]{1,0:T(8,128)(2,1)S(1)} %get-tuple-element.58), channel_id=1, source_target_pairs={{0,96},{32,0},{64,32},{96,64},{1,97},{33,1},{65,33},{97,65},{2,98}... | collective-permute-start | bytes 884744 | tf_op jit(solution)/shard_map/ppermute | solution.py:43
  175.2 13.4 %all-to-all-start.2 = ((f32[16,1,384]{2,1,0:T(1,128)}), f32[16,1,384]{2,1,0:T(1,128)S(1)}, u32[]{:S(2)}, u32[]{:S(2)}) async-start(f32[16,1,384]{2,1,0:T(1,128)} %broadcast_in_dim.16), calls=%async_computation.2 | async-start | bytes 49152 | tf_op jit(solution)/shard_map/all_to_all | solution.py:247
  (12 other events, 288.9 us)
Sparse Core Ops, SparseCore 0:
  38.0 68.9 all-gather.1

commit v10 on v8

--- a/solution.py
+++ b/solution.py
@@ -163,10 +163,8 @@
             ends[which] = [up, down]
             shards += [up, down]
             order += [(which, d, 0, CORE * SUB), (which, Y - d, 0, CORE * SUB)]
-    for which in (0, 1):
-        up, down = ends[which]
-        shards += [shift_y(up[:SUB], 1), shift_y(down[SUB:], -1)]
-        order += [(which, Y // 2, 0, SUB), (which, Y // 2, SUB, SUB)]
+    shards += [shift_y(ends[0][1], -1), shift_y(ends[1][0], 1)]
+    order += [(0, Y // 2, 0, CORE * SUB), (1, Y // 2, 0, CORE * SUB)]
     return shards, tuple(order)
 
 

time: 198 us -> 191 us (0.965)
  starting transfers between devices: 124 us -> 107 us
  waiting for transfers between devices: 32.6 us -> 43.6 us
    ppermute x16 -> x14, starting transfers between devices: 52.5 us -> 43 us  [shift_y(): return lax.ppermute(shard, 'y', [(i, (i + step) % Y) for i in range(Y)])]
    ppermute x16 -> x14, waiting for transfers between devices: 1.54 us -> 8.49 us  [shift_y(): return lax.ppermute(shard, 'y', [(i, (i + step) % Y) for i in range(Y)])]
    ppermute x5, starting transfers between devices: 29.3 us -> 22.4 us  [swap(): return lax.ppermute(shard, axis, [(0, 1), (1, 0)])]
    all_gather x1, waiting for transfers between devices: 6.51 us -> 9.23 us  [local(): right = lax.all_gather(right, ('zhi', 'zlo'), axis=0, tiled=True)]
  transfers between devices with their start and end apart: 31 -> 29, of which waited for: 9 -> 11; matrix products, arithmetic and copies ran while one was open for 1% -> 1% of each run, Pallas kernels for 1% -> 1%
where the time goes in v10:
time: 191 us; the launch traced here: 190 us
  starting transfers between devices  107 us (56%)
  waiting for transfers between devices  43.6 us (23%)
  Pallas kernels  20 us (10%)
  between operations  13.9 us (7%)
  local copies, waits for them, and re-layouts  4.11 us (2%)
    ppermute x14, starting transfers between devices, shift_y(): return lax.ppermute(shard, 'y', [(i, (i + step) % Y) for i in range(Y)])  43 us
    ppermute x5, starting transfers between devices, swap(): return lax.ppermute(shard, axis, [(0, 1), (1, 0)])  22.4 us
    pallas_call x8, Pallas kernels, call(): pl.pallas_call(body, out_shape=shapes, in_specs=ins, out_specs=[VMEM] * l...  20 us
    ppermute x6, starting transfers between devices, shift_x(): return lax.ppermute(shard, 'x', [(i, (i + step) % X) for i in range(X)])  19 us
    all_to_all x2, starting transfers between devices, spread_over(): lax.all_to_all(array, ('x', 'core'), split_axis=0, concat_axis=0, tiled=T...  15.8 us
    ppermute x5, waiting for transfers between devices, swap(): return lax.ppermute(shard, axis, [(0, 1), (1, 0)])  12.4 us
    all_to_all x1, waiting for transfers between devices, local(): lax.all_to_all(sums, ('zlo', 'x'), split_axis=0, concat_axis=0, tiled=True)  10.5 us
    all_gather x1, waiting for transfers between devices, local(): right = lax.all_gather(right, ('zhi', 'zlo'), axis=0, tiled=True)  9.23 us
  transfers between devices with their start and end apart: 29, of which 11 were waited for; matrix products, arithmetic and copies ran while one was open for 1% of the time, Pallas kernels for 1%

profile of v10, /device:TPU:1, one launch (start us, length us, event | category | flops | bytes accessed | tf_op | source)
XLA Modules:
  0.0 189.6 jit_solution(18047119198869535185)
XLA Ops:
  10.5 10.3 %all-to-all-start = ((bf16[8,3,48,384]{3,2,1,0:T(8,128)(2,1)}), bf16[8,3,48,384]{3,2,1,0:T(8,128)(2,1)S(1)}, u32[]{:S(2)}, u32[]{:S(2)}) async-start(bf16[8,3,48,384]{3,2,1,0:T(8,128)(2,1)} %get-tuple-element.31), calls=%async_computation | async-start | bytes 1769472 | tf_op jit(solution)/shard_map/all_to_all | solution.py:50
  20.8 6.1 %collective-permute-start = (bf16[384,384]{1,0:T(8,128)(2,1)S(1)}, bf16[384,384]{1,0:T(8,128)(2,1)}, u32[]{:S(2)}, u32[]{:S(2)}) collective-permute-start(bf16[384,384]{1,0:T(8,128)(2,1)S(1)} %get-tuple-element.32), channel_id=1, source_target_pairs={{0,2},{2,0},{1,3},{3,1},{4,6},{6,4},{5,7},{7,5},{8,10},{10,8},{9,1... | collective-permute-start | bytes 884744 | tf_op jit(solution)/shard_map/ppermute | solution.py:46
  26.9 9.3 %collective-permute-done = bf16[384,384]{1,0:T(8,128)(2,1)} collective-permute-done((bf16[384,384]{1,0:T(8,128)(2,1)S(1)}, bf16[384,384]{1,0:T(8,128)(2,1)}, u32[]{:S(2)}, u32[]{:S(2)}) %collective-permute-start) | collective-permute-done | bytes 294944 | tf_op jit(solution)/shard_map/ppermute | solution.py:46
  37.9 1.9 %collective-permute-start.1 = (bf16[96,1536]{1,0:T(8,128)(2,1)S(1)}, bf16[96,1536]{1,0:T(8,128)(2,1)S(1)}, u32[]{:S(2)}, u32[]{:S(2)}) collective-permute-start(bf16[96,1536]{1,0:T(8,128)(2,1)S(1)} %get-tuple-element.34.refs_0_), channel_id=1, source_target_pairs={{0,4},{4,8},{8,12},{12,16},{16,20},{20,24},{24,28},{28,0},{1,5},{5... | collective-permute-start | bytes 884744 | tf_op jit(solution)/shard_map/ppermute | solution.py:38
  39.8 5.5 %all-to-all-start.1 = ((bf16[8,48,384]{2,1,0:T(8,128)(2,1)}), bf16[8,48,384]{2,1,0:T(8,128)(2,1)S(1)}, u32[]{:S(2)}, u32[]{:S(2)}) async-start(bf16[8,48,384]{2,1,0:T(8,128)(2,1)} %bitcast.5), calls=%async_computation.1 | async-start | bytes 589824 | tf_op jit(solution)/shard_map/all_to_all | solution.py:50
  45.3 4.8 %collective-permute-start.2 = (bf16[96,1536]{1,0:T(8,128)(2,1)S(1)}, bf16[96,1536]{1,0:T(8,128)(2,1)S(1)}, u32[]{:S(2)}, u32[]{:S(2)}) collective-permute-start(bf16[96,1536]{1,0:T(8,128)(2,1)S(1)} %get-tuple-element.34.refs_0_), channel_id=1, source_target_pairs={{0,28},{4,0},{8,4},{12,8},{16,12},{20,16},{24,20},{28,24},{1,29},{... | collective-permute-start | bytes 884744 | tf_op jit(solution)/shard_map/ppermute | solution.py:38
  50.2 2.0 %all-to-all-done.1 = bf16[8,48,384]{2,1,0:T(8,128)(2,1)S(1)} async-done(((bf16[8,48,384]{2,1,0:T(8,128)(2,1)}), bf16[8,48,384]{2,1,0:T(8,128)(2,1)S(1)}, u32[]{:S(2)}, u32[]{:S(2)}) %all-to-all-start.1) | async-done | bytes 294944 | tf_op jit(solution)/shard_map/all_to_all | solution.py:50
  52.2 2.6 %collective-permute-start.3 = (bf16[96,1536]{1,0:T(8,128)(2,1)S(1)}, bf16[96,1536]{1,0:T(8,128)(2,1)S(1)}, u32[]{:S(2)}, u32[]{:S(2)}) collective-permute-start(bf16[96,1536]{1,0:T(8,128)(2,1)S(1)} %bitcast.13), channel_id=1, source_target_pairs={{0,4},{4,8},{8,12},{12,16},{16,20},{20,24},{24,28},{28,0},{1,5},{5... | collective-permute-start | bytes 884744 | tf_op jit(solution)/shard_map/ppermute | solution.py:38
  54.8 4.2 %collective-permute-start.4 = (bf16[96,1536]{1,0:T(8,128)(2,1)S(1)}, bf16[96,1536]{1,0:T(8,128)(2,1)S(1)}, u32[]{:S(2)}, u32[]{:S(2)}) collective-permute-start(bf16[96,1536]{1,0:T(8,128)(2,1)S(1)} %bitcast.14), channel_id=1, source_target_pairs={{0,28},{4,0},{8,4},{12,8},{16,12},{20,16},{24,20},{28,24},{1,29},{... | collective-permute-start | bytes 884744 | tf_op jit(solution)/shard_map/ppermute | solution.py:38
  59.0 3.4 %collective-permute-start.6 = (bf16[96,1536]{1,0:T(8,128)(2,1)S(1)}, bf16[96,1536]{1,0:T(8,128)(2,1)S(1)}, u32[]{:S(2)}, u32[]{:S(2)}) collective-permute-start(bf16[96,1536]{1,0:T(8,128)(2,1)S(1)} %collective-permute-done.2.refs_3_), channel_id=1, source_target_pairs={{0,28},{4,0},{8,4},{12,8},{16,12},{20,16},{24,20},{28,24},{1,29},{... | collective-permute-start | bytes 884744 | tf_op jit(solution)/shard_map/ppermute | solution.py:38
  65.3 2.3 %collective-permute-start.5 = (bf16[96,1536]{1,0:T(8,128)(2,1)S(1)}, bf16[96,1536]{1,0:T(8,128)(2,1)S(1)}, u32[]{:S(2)}, u32[]{:S(2)}) collective-permute-start(bf16[96,1536]{1,0:T(8,128)(2,1)S(1)} %collective-permute-done.1.refs_2_), channel_id=1, source_target_pairs={{0,4},{4,8},{8,12},{12,16},{16,20},{20,24},{24,28},{28,0},{1,5},{5... | collective-permute-start | bytes 884744 | tf_op jit(solution)/shard_map/ppermute | solution.py:38
  67.6 4.2 %collective-permute-start.8 = (bf16[96,1536]{1,0:T(8,128)(2,1)S(1)}, bf16[96,1536]{1,0:T(8,128)(2,1)S(1)}, u32[]{:S(2)}, u32[]{:S(2)}) collective-permute-start(bf16[96,1536]{1,0:T(8,128)(2,1)S(1)} %collective-permute-done.4.refs_5_), channel_id=1, source_target_pairs={{0,28},{4,0},{8,4},{12,8},{16,12},{20,16},{24,20},{28,24},{1,29},{... | collective-permute-start | bytes 884744 | tf_op jit(solution)/shard_map/ppermute | solution.py:38
  71.9 4.0 %collective-permute-start.10 = (bf16[96,1536]{1,0:T(8,128)(2,1)S(1)}, bf16[96,1536]{1,0:T(8,128)(2,1)S(1)}, u32[]{:S(2)}, u32[]{:S(2)}) collective-permute-start(bf16[96,1536]{1,0:T(8,128)(2,1)S(1)} %collective-permute-done.6.refs_7_), channel_id=1, source_target_pairs={{0,28},{4,0},{8,4},{12,8},{16,12},{20,16},{24,20},{28,24},{1,29},{... | collective-permute-start | bytes 884744 | tf_op jit(solution)/shard_map/ppermute | solution.py:38
  77.9 2.0 %collective-permute-done.5.refs_6_ = bf16[96,1536]{1,0:T(8,128)(2,1)S(1)} collective-permute-done((bf16[96,1536]{1,0:T(8,128)(2,1)S(1)}, bf16[96,1536]{1,0:T(8,128)(2,1)S(1)}, u32[]{:S(2)}, u32[]{:S(2)}) %collective-permute-start.5) | collective-permute-done | bytes 294944 | tf_op jit(solution)/shard_map/ppermute | solution.py:38
  81.8 4.6 %collective-permute-start.12 = (bf16[96,1536]{1,0:T(8,128)(2,1)S(1)}, bf16[96,1536]{1,0:T(8,128)(2,1)}, u32[]{:S(2)}, u32[]{:S(2)}) collective-permute-start(bf16[96,1536]{1,0:T(8,128)(2,1)S(1)} %collective-permute-done.8.refs_9_), channel_id=1, source_target_pairs={{0,28},{4,0},{8,4},{12,8},{16,12},{20,16},{24,20},{28,24},{1,29},{... | collective-permute-start | bytes 884744 | tf_op jit(solution)/shard_map/ppermute | solution.py:38
  86.4 1.9 %collective-permute-start.13 = (bf16[96,1536]{1,0:T(8,128)(2,1)S(1)}, bf16[96,1536]{1,0:T(8,128)(2,1)}, u32[]{:S(2)}, u32[]{:S(2)}) collective-permute-start(bf16[96,1536]{1,0:T(8,128)(2,1)S(1)} %collective-permute-done.10.refs_11_), channel_id=1, source_target_pairs={{0,28},{4,0},{8,4},{12,8},{16,12},{20,16},{24,20},{28,24},{1,29},{... | collective-permute-start | bytes 884744 | tf_op jit(solution)/shard_map/ppermute | solution.py:38
  88.3 3.4 %collective-permute-start.14 = (bf16[96,1536]{1,0:T(8,128)(2,1)S(1)}, bf16[96,1536]{1,0:T(8,128)(2,1)}, u32[]{:S(2)}, u32[]{:S(2)}) collective-permute-start(bf16[96,1536]{1,0:T(8,128)(2,1)S(1)} %collective-permute-done.11.refs_12_), channel_id=1, source_target_pairs={{0,4},{4,8},{8,12},{12,16},{16,20},{20,24},{24,28},{28,0},{1,5},{5... | collective-permute-start | bytes 884744 | tf_op jit(solution)/shard_map/ppermute | solution.py:38
  92.3 5.0 %collective-permute-done.13.refs_14_ = bf16[96,1536]{1,0:T(8,128)(2,1)} collective-permute-done((bf16[96,1536]{1,0:T(8,128)(2,1)S(1)}, bf16[96,1536]{1,0:T(8,128)(2,1)}, u32[]{:S(2)}, u32[]{:S(2)}) %collective-permute-start.13) | collective-permute-done | bytes 294944 | tf_op jit(solution)/shard_map/ppermute | solution.py:38
  97.8 9.2 %all-gather.2.cloned.1.call-done.refs_16_ = bf16[8,768,384]{2,1,0:T(8,128)(2,1)} async-done(((bf16[1,768,384]{2,1,0:T(8,128)(2,1)}), bf16[8,768,384]{2,1,0:T(8,128)(2,1)}) %all-gather.2.cloned.1.call-update) | async-done | bytes 4718608 | tf_op jit(solution)/shard_map/all_gather | solution.py:193
  107.1 13.6 %shard_map.39 = (bf16[384,1536]{1,0:T(8,128)(2,1)}, bf16[384,1536]{1,0:T(8,128)(2,1)}, bf16[384,1536]{1,0:T(8,128)(2,1)}, bf16[384,1536]{1,0:T(8,128)(2,1)}) custom-call(s32[2]{0:T(128)} %pad_add_fusion.place, bf16[96,1536]{1,0:T(8,128)(2,1)} %copy-done.3, bf16[96,1536]{1,0:T(8,128)(2,1)} %bitcast.15, bf16[96,1536]{1,0:T(8,128)(2,1)} %copy-done.6, ...), custom_call_target="tpu_custom_call" | custom-call | flops 7247757312 | bytes 14155784 | tf_op jit(solution)/shard_map/pallas_call | solution.py:26
  120.7 2.6 %collective-permute-start.19 = (bf16[384,1536]{1,0:T(8,128)(2,1)}, bf16[384,1536]{1,0:T(8,128)(2,1)S(1)}, u32[]{:S(2)}, u32[]{:S(2)}) collective-permute-start(bf16[384,1536]{1,0:T(8,128)(2,1)} %get-tuple-element.47), channel_id=1, source_target_pairs={{0,1},{1,0},{2,3},{3,2},{4,5},{5,4},{6,7},{7,6},{8,9},{9,8},{10,11... | collective-permute-start | bytes 3538952 | tf_op jit(solution)/shard_map/ppermute | solution.py:46
  127.5 3.2 %collective-permute-start.20 = (bf16[384,384]{1,0:T(8,128)(2,1)S(1)}, bf16[384,384]{1,0:T(8,128)(2,1)S(1)}, u32[]{:S(2)}, u32[]{:S(2)}) collective-permute-start(bf16[384,384]{1,0:T(8,128)(2,1)S(1)} %get-tuple-element.49), channel_id=1, source_target_pairs={{0,32},{32,64},{64,96},{96,0},{1,33},{33,65},{65,97},{97,1},{2,34}... | collective-permute-start | bytes 884744 | tf_op jit(solution)/shard_map/ppermute | solution.py:42
  130.7 4.3 %collective-permute-start.21 = (bf16[384,384]{1,0:T(8,128)(2,1)S(1)}, bf16[384,384]{1,0:T(8,128)(2,1)S(1)}, u32[]{:S(2)}, u32[]{:S(2)}) collective-permute-start(bf16[384,384]{1,0:T(8,128)(2,1)S(1)} %get-tuple-element.50), channel_id=1, source_target_pairs={{0,64},{32,96},{64,0},{96,32},{1,65},{33,97},{65,1},{97,33},{2,66}... | collective-permute-start | bytes 884744 | tf_op jit(solution)/shard_map/ppermute | solution.py:42
  135.0 3.1 %collective-permute-start.22 = (bf16[384,384]{1,0:T(8,128)(2,1)S(1)}, bf16[384,384]{1,0:T(8,128)(2,1)S(1)}, u32[]{:S(2)}, u32[]{:S(2)}) collective-permute-start(bf16[384,384]{1,0:T(8,128)(2,1)S(1)} %get-tuple-element.51), channel_id=1, source_target_pairs={{0,96},{32,0},{64,32},{96,64},{1,97},{33,1},{65,33},{97,65},{2,98}... | collective-permute-start | bytes 884744 | tf_op jit(solution)/shard_map/ppermute | solution.py:42
  138.5 2.2 %collective-permute-start.16 = (bf16[384,384]{1,0:T(8,128)(2,1)S(1)}, bf16[384,384]{1,0:T(8,128)(2,1)S(1)}, u32[]{:S(2)}, u32[]{:S(2)}) collective-permute-start(bf16[384,384]{1,0:T(8,128)(2,1)S(1)} %get-tuple-element.42), channel_id=1, source_target_pairs={{0,32},{32,64},{64,96},{96,0},{1,33},{33,65},{65,97},{97,1},{2,34}... | collective-permute-start | bytes 884744 | tf_op jit(solution)/shard_map/ppermute | solution.py:42
  140.7 2.8 %collective-permute-start.17 = (bf16[384,384]{1,0:T(8,128)(2,1)S(1)}, bf16[384,384]{1,0:T(8,128)(2,1)S(1)}, u32[]{:S(2)}, u32[]{:S(2)}) collective-permute-start(bf16[384,384]{1,0:T(8,128)(2,1)S(1)} %get-tuple-element.43), channel_id=1, source_target_pairs={{0,64},{32,96},{64,0},{96,32},{1,65},{33,97},{65,1},{97,33},{2,66}... | collective-permute-start | bytes 884744 | tf_op jit(solution)/shard_map/ppermute | solution.py:42
  143.5 3.4 %collective-permute-start.18 = (bf16[384,384]{1,0:T(8,128)(2,1)S(1)}, bf16[384,384]{1,0:T(8,128)(2,1)S(1)}, u32[]{:S(2)}, u32[]{:S(2)}) collective-permute-start(bf16[384,384]{1,0:T(8,128)(2,1)S(1)} %get-tuple-element.44), channel_id=1, source_target_pairs={{0,96},{32,0},{64,32},{96,64},{1,97},{33,1},{65,33},{97,65},{2,98}... | collective-permute-start | bytes 884744 | tf_op jit(solution)/shard_map/ppermute | solution.py:42
  148.3 5.9 %collective-permute-start.23 = (f32[1,384]{1,0:T(1,128)S(1)}, f32[1,384]{1,0:T(1,128)S(1)}, u32[]{:S(2)}, u32[]{:S(2)}) collective-permute-start(f32[1,384]{1,0:T(1,128)S(1)} %get-tuple-element.52), channel_id=1, source_target_pairs={{0,2},{2,0},{1,3},{3,1},{4,6},{6,4},{5,7},{7,5},{8,10},{10,8},{9,1... | collective-permute-start | bytes 4616 | tf_op jit(solution)/shard_map/ppermute | solution.py:46
  154.2 2.3 %collective-permute-done.23 = f32[1,384]{1,0:T(1,128)S(1)} collective-permute-done((f32[1,384]{1,0:T(1,128)S(1)}, f32[1,384]{1,0:T(1,128)S(1)}, u32[]{:S(2)}, u32[]{:S(2)}) %collective-permute-start.23) | collective-permute-done | bytes 1568 | tf_op jit(solution)/shard_map/ppermute | solution.py:46
  156.5 5.9 %collective-permute-start.24 = (bf16[384,384]{1,0:T(8,128)(2,1)S(1)}, bf16[384,384]{1,0:T(8,128)(2,1)S(1)}, u32[]{:S(2)}, u32[]{:S(2)}) collective-permute-start(bf16[384,384]{1,0:T(8,128)(2,1)S(1)} %get-tuple-element.54), channel_id=1, source_target_pairs={{0,2},{2,0},{1,3},{3,1},{4,6},{6,4},{5,7},{7,5},{8,10},{10,8},{9,1... | collective-permute-start | bytes 884744 | tf_op jit(solution)/shard_map/ppermute | solution.py:46
  163.3 7.0 %all-to-all-start.2 = ((f32[16,1,384]{2,1,0:T(1,128)}), f32[16,1,384]{2,1,0:T(1,128)S(1)}, u32[]{:S(2)}, u32[]{:S(2)}) async-start(f32[16,1,384]{2,1,0:T(1,128)} %broadcast_in_dim.12), calls=%async_computation.2 | async-start | bytes 49152 | tf_op jit(solution)/shard_map/all_to_all | solution.py:230
  170.4 10.5 %all-to-all-done.2.sums = f32[16,1,384]{2,1,0:T(1,128)S(1)} async-done(((f32[16,1,384]{2,1,0:T(1,128)}), f32[16,1,384]{2,1,0:T(1,128)S(1)}, u32[]{:S(2)}, u32[]{:S(2)}) %all-to-all-start.2) | async-done | bytes 24608 | tf_op jit(solution)/shard_map/all_to_all | solution.py:230
  (74 shorter events, 22.1 us)
Async XLA Ops:
  10.5 25.8 %all-to-all-start = ((bf16[8,3,48,384]{3,2,1,0:T(8,128)(2,1)}), bf16[8,3,48,384]{3,2,1,0:T(8,128)(2,1)S(1)}, u32[]{:S(2)}, u32[]{:S(2)}) async-start(bf16[8,3,48,384]{3,2,1,0:T(8,128)(2,1)} %get-tuple-element.31), calls=%async_computation | async-start | bytes 1769472 | tf_op jit(solution)/shard_map/all_to_all | solution.py:50
  20.8 86.2 %all-gather.2.cloned.1.call-start = ((), (), s32[]{:S(2)}) async-start(), calls=%async_computation.3 | async-start | bytes 5308416 | tf_op jit(solution)/shard_map/all_gather | solution.py:193
  20.8 15.4 %collective-permute-start = (bf16[384,384]{1,0:T(8,128)(2,1)S(1)}, bf16[384,384]{1,0:T(8,128)(2,1)}, u32[]{:S(2)}, u32[]{:S(2)}) collective-permute-start(bf16[384,384]{1,0:T(8,128)(2,1)S(1)} %get-tuple-element.32), channel_id=1, source_target_pairs={{0,2},{2,0},{1,3},{3,1},{4,6},{6,4},{5,7},{7,5},{8,10},{10,8},{9,1... | collective-permute-start | bytes 884744 | tf_op jit(solution)/shard_map/ppermute | solution.py:46
  37.9 69.1 %copy-start.3 = (bf16[96,1536]{1,0:T(8,128)(2,1)}, bf16[96,1536]{1,0:T(8,128)(2,1)S(1)}, u32[]{:S(2)}) copy-start(bf16[96,1536]{1,0:T(8,128)(2,1)S(1)} %get-tuple-element.34.refs_0_) | copy-start | bytes 884740
  37.9 14.3 %collective-permute-start.1 = (bf16[96,1536]{1,0:T(8,128)(2,1)S(1)}, bf16[96,1536]{1,0:T(8,128)(2,1)S(1)}, u32[]{:S(2)}, u32[]{:S(2)}) collective-permute-start(bf16[96,1536]{1,0:T(8,128)(2,1)S(1)} %get-tuple-element.34.refs_0_), channel_id=1, source_target_pairs={{0,4},{4,8},{8,12},{12,16},{16,20},{20,24},{24,28},{28,0},{1,5},{5... | collective-permute-start | bytes 884744 | tf_op jit(solution)/shard_map/ppermute | solution.py:38
  39.8 12.3 %all-to-all-start.1 = ((bf16[8,48,384]{2,1,0:T(8,128)(2,1)}), bf16[8,48,384]{2,1,0:T(8,128)(2,1)S(1)}, u32[]{:S(2)}, u32[]{:S(2)}) async-start(bf16[8,48,384]{2,1,0:T(8,128)(2,1)} %bitcast.5), calls=%async_computation.1 | async-start | bytes 589824 | tf_op jit(solution)/shard_map/all_to_all | solution.py:50
  45.3 13.7 %collective-permute-start.2 = (bf16[96,1536]{1,0:T(8,128)(2,1)S(1)}, bf16[96,1536]{1,0:T(8,128)(2,1)S(1)}, u32[]{:S(2)}, u32[]{:S(2)}) collective-permute-start(bf16[96,1536]{1,0:T(8,128)(2,1)S(1)} %get-tuple-element.34.refs_0_), channel_id=1, source_target_pairs={{0,28},{4,0},{8,4},{12,8},{16,12},{20,16},{24,20},{28,24},{1,29},{... | collective-permute-start | bytes 884744 | tf_op jit(solution)/shard_map/ppermute | solution.py:38
  52.2 54.8 %copy-start.4 = (bf16[4,12,8,384]{3,2,0,1:T(8,128)(2,1)}, bf16[4,12,8,384]{3,2,0,1:T(8,128)(2,1)S(1)}, u32[]{:S(2)}) copy-start(bf16[4,12,8,384]{3,2,0,1:T(8,128)(2,1)S(1)} %copy.12) | copy-start | bytes 884740
  52.2 54.8 %copy-start.6 = (bf16[96,1536]{1,0:T(8,128)(2,1)}, bf16[96,1536]{1,0:T(8,128)(2,1)S(1)}, u32[]{:S(2)}) copy-start(bf16[96,1536]{1,0:T(8,128)(2,1)S(1)} %collective-permute-done.1.refs_2_) | copy-start | bytes 884740
  52.2 11.2 %collective-permute-start.3 = (bf16[96,1536]{1,0:T(8,128)(2,1)S(1)}, bf16[96,1536]{1,0:T(8,128)(2,1)S(1)}, u32[]{:S(2)}, u32[]{:S(2)}) collective-permute-start(bf16[96,1536]{1,0:T(8,128)(2,1)S(1)} %bitcast.13), channel_id=1, source_target_pairs={{0,4},{4,8},{8,12},{12,16},{16,20},{20,24},{24,28},{28,0},{1,5},{5... | collective-permute-start | bytes 884744 | tf_op jit(solution)/shard_map/ppermute | solution.py:38
  54.8 12.8 %collective-permute-start.4 = (bf16[96,1536]{1,0:T(8,128)(2,1)S(1)}, bf16[96,1536]{1,0:T(8,128)(2,1)S(1)}, u32[]{:S(2)}, u32[]{:S(2)}) collective-permute-start(bf16[96,1536]{1,0:T(8,128)(2,1)S(1)} %bitcast.14), channel_id=1, source_target_pairs={{0,28},{4,0},{8,4},{12,8},{16,12},{20,16},{24,20},{28,24},{1,29},{... | collective-permute-start | bytes 884744 | tf_op jit(solution)/shard_map/ppermute | solution.py:38
  59.0 12.9 %collective-permute-start.6 = (bf16[96,1536]{1,0:T(8,128)(2,1)S(1)}, bf16[96,1536]{1,0:T(8,128)(2,1)S(1)}, u32[]{:S(2)}, u32[]{:S(2)}) collective-permute-start(bf16[96,1536]{1,0:T(8,128)(2,1)S(1)} %collective-permute-done.2.refs_3_), channel_id=1, source_target_pairs={{0,28},{4,0},{8,4},{12,8},{16,12},{20,16},{24,20},{28,24},{1,29},{... | collective-permute-start | bytes 884744 | tf_op jit(solution)/shard_map/ppermute | solution.py:38
  63.4 12.5 %collective-permute-start.7 = (bf16[96,1536]{1,0:T(8,128)(2,1)S(1)}, bf16[96,1536]{1,0:T(8,128)(2,1)S(1)}, u32[]{:S(2)}, u32[]{:S(2)}) collective-permute-start(bf16[96,1536]{1,0:T(8,128)(2,1)S(1)} %collective-permute-done.3.refs_4_), channel_id=1, source_target_pairs={{0,4},{4,8},{8,12},{12,16},{16,20},{20,24},{24,28},{28,0},{1,5},{5... | collective-permute-start | bytes 884744 | tf_op jit(solution)/shard_map/ppermute | solution.py:38
  65.3 14.5 %collective-permute-start.5 = (bf16[96,1536]{1,0:T(8,128)(2,1)S(1)}, bf16[96,1536]{1,0:T(8,128)(2,1)S(1)}, u32[]{:S(2)}, u32[]{:S(2)}) collective-permute-start(bf16[96,1536]{1,0:T(8,128)(2,1)S(1)} %collective-permute-done.1.refs_2_), channel_id=1, source_target_pairs={{0,4},{4,8},{8,12},{12,16},{16,20},{20,24},{24,28},{28,0},{1,5},{5... | collective-permute-start | bytes 884744 | tf_op jit(solution)/shard_map/ppermute | solution.py:38
  67.6 14.1 %collective-permute-start.8 = (bf16[96,1536]{1,0:T(8,128)(2,1)S(1)}, bf16[96,1536]{1,0:T(8,128)(2,1)S(1)}, u32[]{:S(2)}, u32[]{:S(2)}) collective-permute-start(bf16[96,1536]{1,0:T(8,128)(2,1)S(1)} %collective-permute-done.4.refs_5_), channel_id=1, source_target_pairs={{0,28},{4,0},{8,4},{12,8},{16,12},{20,16},{24,20},{28,24},{1,29},{... | collective-permute-start | bytes 884744 | tf_op jit(solution)/shard_map/ppermute | solution.py:38
  71.9 14.5 %collective-permute-start.10 = (bf16[96,1536]{1,0:T(8,128)(2,1)S(1)}, bf16[96,1536]{1,0:T(8,128)(2,1)S(1)}, u32[]{:S(2)}, u32[]{:S(2)}) collective-permute-start(bf16[96,1536]{1,0:T(8,128)(2,1)S(1)} %collective-permute-done.6.refs_7_), channel_id=1, source_target_pairs={{0,28},{4,0},{8,4},{12,8},{16,12},{20,16},{24,20},{28,24},{1,29},{... | collective-permute-start | bytes 884744 | tf_op jit(solution)/shard_map/ppermute | solution.py:38
  75.9 12.4 %collective-permute-start.11 = (bf16[96,1536]{1,0:T(8,128)(2,1)S(1)}, bf16[96,1536]{1,0:T(8,128)(2,1)S(1)}, u32[]{:S(2)}, u32[]{:S(2)}) collective-permute-start(bf16[96,1536]{1,0:T(8,128)(2,1)S(1)} %collective-permute-done.7.refs_8_), channel_id=1, source_target_pairs={{0,4},{4,8},{8,12},{12,16},{16,20},{20,24},{24,28},{28,0},{1,5},{5... | collective-permute-start | bytes 884744 | tf_op jit(solution)/shard_map/ppermute | solution.py:38
  79.8 12.5 %collective-permute-start.9 = (bf16[96,1536]{1,0:T(8,128)(2,1)S(1)}, bf16[96,1536]{1,0:T(8,128)(2,1)}, u32[]{:S(2)}, u32[]{:S(2)}) collective-permute-start(bf16[96,1536]{1,0:T(8,128)(2,1)S(1)} %collective-permute-done.5.refs_6_), channel_id=1, source_target_pairs={{0,4},{4,8},{8,12},{12,16},{16,20},{20,24},{24,28},{28,0},{1,5},{5... | collective-permute-start | bytes 884744 | tf_op jit(solution)/shard_map/ppermute | solution.py:38
  81.8 10.5 %collective-permute-start.12 = (bf16[96,1536]{1,0:T(8,128)(2,1)S(1)}, bf16[96,1536]{1,0:T(8,128)(2,1)}, u32[]{:S(2)}, u32[]{:S(2)}) collective-permute-start(bf16[96,1536]{1,0:T(8,128)(2,1)S(1)} %collective-permute-done.8.refs_9_), channel_id=1, source_target_pairs={{0,28},{4,0},{8,4},{12,8},{16,12},{20,16},{24,20},{28,24},{1,29},{... | collective-permute-start | bytes 884744 | tf_op jit(solution)/shard_map/ppermute | solution.py:38
  86.4 10.9 %collective-permute-start.13 = (bf16[96,1536]{1,0:T(8,128)(2,1)S(1)}, bf16[96,1536]{1,0:T(8,128)(2,1)}, u32[]{:S(2)}, u32[]{:S(2)}) collective-permute-start(bf16[96,1536]{1,0:T(8,128)(2,1)S(1)} %collective-permute-done.10.refs_11_), channel_id=1, source_target_pairs={{0,28},{4,0},{8,4},{12,8},{16,12},{20,16},{24,20},{28,24},{1,29},{... | collective-permute-start | bytes 884744 | tf_op jit(solution)/shard_map/ppermute | solution.py:38
  88.3 9.4 %collective-permute-start.14 = (bf16[96,1536]{1,0:T(8,128)(2,1)S(1)}, bf16[96,1536]{1,0:T(8,128)(2,1)}, u32[]{:S(2)}, u32[]{:S(2)}) collective-permute-start(bf16[96,1536]{1,0:T(8,128)(2,1)S(1)} %collective-permute-done.11.refs_12_), channel_id=1, source_target_pairs={{0,4},{4,8},{8,12},{12,16},{16,20},{20,24},{24,28},{28,0},{1,5},{5... | collective-permute-start | bytes 884744 | tf_op jit(solution)/shard_map/ppermute | solution.py:38
  120.7 5.3 %collective-permute-start.19 = (bf16[384,1536]{1,0:T(8,128)(2,1)}, bf16[384,1536]{1,0:T(8,128)(2,1)S(1)}, u32[]{:S(2)}, u32[]{:S(2)}) collective-permute-start(bf16[384,1536]{1,0:T(8,128)(2,1)} %get-tuple-element.47), channel_id=1, source_target_pairs={{0,1},{1,0},{2,3},{3,2},{4,5},{5,4},{6,7},{7,6},{8,9},{9,8},{10,11... | collective-permute-start | bytes 3538952 | tf_op jit(solution)/shard_map/ppermute | solution.py:46
  123.3 14.9 %collective-permute-start.15 = (bf16[384,1536]{1,0:T(8,128)(2,1)}, bf16[384,1536]{1,0:T(8,128)(2,1)S(1)}, u32[]{:S(2)}, u32[]{:S(2)}) collective-permute-start(bf16[384,1536]{1,0:T(8,128)(2,1)} %get-tuple-element.40), channel_id=1, source_target_pairs={{0,1},{1,0},{2,3},{3,2},{4,5},{5,4},{6,7},{7,6},{8,9},{9,8},{10,11... | collective-permute-start | bytes 3538952 | tf_op jit(solution)/shard_map/ppermute | solution.py:46
  127.5 16.0 %collective-permute-start.20 = (bf16[384,384]{1,0:T(8,128)(2,1)S(1)}, bf16[384,384]{1,0:T(8,128)(2,1)S(1)}, u32[]{:S(2)}, u32[]{:S(2)}) collective-permute-start(bf16[384,384]{1,0:T(8,128)(2,1)S(1)} %get-tuple-element.49), channel_id=1, source_target_pairs={{0,32},{32,64},{64,96},{96,0},{1,33},{33,65},{65,97},{97,1},{2,34}... | collective-permute-start | bytes 884744 | tf_op jit(solution)/shard_map/ppermute | solution.py:42
  130.7 16.2 %collective-permute-start.21 = (bf16[384,384]{1,0:T(8,128)(2,1)S(1)}, bf16[384,384]{1,0:T(8,128)(2,1)S(1)}, u32[]{:S(2)}, u32[]{:S(2)}) collective-permute-start(bf16[384,384]{1,0:T(8,128)(2,1)S(1)} %get-tuple-element.50), channel_id=1, source_target_pairs={{0,64},{32,96},{64,0},{96,32},{1,65},{33,97},{65,1},{97,33},{2,66}... | collective-permute-start | bytes 884744 | tf_op jit(solution)/shard_map/ppermute | solution.py:42
  135.0 12.9 %collective-permute-start.22 = (bf16[384,384]{1,0:T(8,128)(2,1)S(1)}, bf16[384,384]{1,0:T(8,128)(2,1)S(1)}, u32[]{:S(2)}, u32[]{:S(2)}) collective-permute-start(bf16[384,384]{1,0:T(8,128)(2,1)S(1)} %get-tuple-element.51), channel_id=1, source_target_pairs={{0,96},{32,0},{64,32},{96,64},{1,97},{33,1},{65,33},{97,65},{2,98}... | collective-permute-start | bytes 884744 | tf_op jit(solution)/shard_map/ppermute | solution.py:42
  138.5 23.9 %collective-permute-start.16 = (bf16[384,384]{1,0:T(8,128)(2,1)S(1)}, bf16[384,384]{1,0:T(8,128)(2,1)S(1)}, u32[]{:S(2)}, u32[]{:S(2)}) collective-permute-start(bf16[384,384]{1,0:T(8,128)(2,1)S(1)} %get-tuple-element.42), channel_id=1, source_target_pairs={{0,32},{32,64},{64,96},{96,0},{1,33},{33,65},{65,97},{97,1},{2,34}... | collective-permute-start | bytes 884744 | tf_op jit(solution)/shard_map/ppermute | solution.py:42
  140.7 21.7 %collective-permute-start.17 = (bf16[384,384]{1,0:T(8,128)(2,1)S(1)}, bf16[384,384]{1,0:T(8,128)(2,1)S(1)}, u32[]{:S(2)}, u32[]{:S(2)}) collective-permute-start(bf16[384,384]{1,0:T(8,128)(2,1)S(1)} %get-tuple-element.43), channel_id=1, source_target_pairs={{0,64},{32,96},{64,0},{96,32},{1,65},{33,97},{65,1},{97,33},{2,66}... | collective-permute-start | bytes 884744 | tf_op jit(solution)/shard_map/ppermute | solution.py:42
  143.5 18.9 %collective-permute-start.18 = (bf16[384,384]{1,0:T(8,128)(2,1)S(1)}, bf16[384,384]{1,0:T(8,128)(2,1)S(1)}, u32[]{:S(2)}, u32[]{:S(2)}) collective-permute-start(bf16[384,384]{1,0:T(8,128)(2,1)S(1)} %get-tuple-element.44), channel_id=1, source_target_pairs={{0,96},{32,0},{64,32},{96,64},{1,97},{33,1},{65,33},{97,65},{2,98}... | collective-permute-start | bytes 884744 | tf_op jit(solution)/shard_map/ppermute | solution.py:42
  148.3 8.2 %collective-permute-start.23 = (f32[1,384]{1,0:T(1,128)S(1)}, f32[1,384]{1,0:T(1,128)S(1)}, u32[]{:S(2)}, u32[]{:S(2)}) collective-permute-start(f32[1,384]{1,0:T(1,128)S(1)} %get-tuple-element.52), channel_id=1, source_target_pairs={{0,2},{2,0},{1,3},{3,1},{4,6},{6,4},{5,7},{7,5},{8,10},{10,8},{9,1... | collective-permute-start | bytes 4616 | tf_op jit(solution)/shard_map/ppermute | solution.py:46
  156.5 24.5 %collective-permute-start.24 = (bf16[384,384]{1,0:T(8,128)(2,1)S(1)}, bf16[384,384]{1,0:T(8,128)(2,1)S(1)}, u32[]{:S(2)}, u32[]{:S(2)}) collective-permute-start(bf16[384,384]{1,0:T(8,128)(2,1)S(1)} %get-tuple-element.54), channel_id=1, source_target_pairs={{0,2},{2,0},{1,3},{3,1},{4,6},{6,4},{5,7},{7,5},{8,10},{10,8},{9,1... | collective-permute-start | bytes 884744 | tf_op jit(solution)/shard_map/ppermute | solution.py:46
  163.3 17.6 %all-to-all-start.2 = ((f32[16,1,384]{2,1,0:T(1,128)}), f32[16,1,384]{2,1,0:T(1,128)S(1)}, u32[]{:S(2)}, u32[]{:S(2)}) async-start(f32[16,1,384]{2,1,0:T(1,128)} %broadcast_in_dim.12), calls=%async_computation.2 | async-start | bytes 49152 | tf_op jit(solution)/shard_map/all_to_all | solution.py:230
  (13 other events, 325.0 us)
Sparse Core Ops, SparseCore 0:
  38.0 68.9 all-gather.1

commit v11 on v10

--- a/solution.py
+++ b/solution.py
@@ -181,8 +181,6 @@
     )
     far = swap(far, "zhi")
     both = spread_over(both)
-    both, far = in_order(both, far)
-    far = spread_over(far.reshape(X * CORE, SUB, HALF))
     near, right = call(
         settle,
         [((CORE * SUB, WIDE), BF16), ((1, CORE * UNIT, UNIT), BF16)],
@@ -190,6 +188,8 @@
         (place, both.reshape(X, CORE, 3, SUB, UNIT)),
         [pltpu.VMEM((UNIT, UNIT), F32)],
     )
+    right, far = in_order(right, far)
+    far = spread_over(far.reshape(X * CORE, SUB, HALF))
     right = lax.all_gather(right, ("zhi", "zlo"), axis=0, tiled=True)
     far = far.reshape(X, CORE * SUB, HALF).transpose(1, 0, 2).reshape(CORE * SUB, WIDE)
     shards, order = rings(near, far)
@@ -205,7 +205,7 @@
             pltpu.SemaphoreType.DMA((len(shards) + 2 * Z_LO,)),
         ],
         flops=4 * CORE * UNIT * DEPTH * WIDE,
-        vmem=60,
+        vmem=50,
     )
 
     def total(apart, dtype):

time: 191 us -> 189 us (0.990)
    ppermute x5, waiting for transfers between devices: 12.4 us -> 3.47 us  [swap(): return lax.ppermute(shard, axis, [(0, 1), (1, 0)])]
    all_to_all x2, waiting for transfers between devices: 1.97 us -> 9.33 us  [spread_over(): lax.all_to_all(array, ('x', 'core'), split_axis=0, concat_axis=0, tiled=T...]
  transfers between devices with their start and end apart: 29 -> 29, of which waited for: 11 -> 13; matrix products, arithmetic and copies ran while one was open for 1% -> 0% of each run, Pallas kernels for 1% -> 1%
where the time goes in v11:
time: 189 us; the launch traced here: 187 us
  starting transfers between devices  107 us (57%)
  waiting for transfers between devices  42.7 us (23%)
  Pallas kernels  19.6 us (10%)
  between operations  13.8 us (7%)
  local copies, waits for them, and re-layouts  4.06 us (2%)
    ppermute x14, starting transfers between devices, shift_y(): return lax.ppermute(shard, 'y', [(i, (i + step) % Y) for i in range(Y)])  43 us
    ppermute x5, starting transfers between devices, swap(): return lax.ppermute(shard, axis, [(0, 1), (1, 0)])  22.3 us
    pallas_call x8, Pallas kernels, call(): pl.pallas_call(body, out_shape=shapes, in_specs=ins, out_specs=[VMEM] * l...  19.6 us
    ppermute x6, starting transfers between devices, shift_x(): return lax.ppermute(shard, 'x', [(i, (i + step) % X) for i in range(X)])  19 us
    all_to_all x2, starting transfers between devices, spread_over(): lax.all_to_all(array, ('x', 'core'), split_axis=0, concat_axis=0, tiled=T...  15.8 us
    all_to_all x1, waiting for transfers between devices, local(): lax.all_to_all(sums, ('zlo', 'x'), split_axis=0, concat_axis=0, tiled=True)  10.5 us
    all_to_all x2, waiting for transfers between devices, spread_over(): lax.all_to_all(array, ('x', 'core'), split_axis=0, concat_axis=0, tiled=T...  9.33 us
    all_gather x1, waiting for transfers between devices, local(): right = lax.all_gather(right, ('zhi', 'zlo'), axis=0, tiled=True)  9.25 us
  transfers between devices with their start and end apart: 29, of which 13 were waited for; matrix products, arithmetic and copies ran while one was open for 0% of the time, Pallas kernels for 1%

profile of v11, /device:TPU:1, one launch (start us, length us, event | category | flops | bytes accessed | tf_op | source)
XLA Modules:
  0.0 187.4 jit_solution(4626635921654609595)
XLA Ops:
  10.5 10.3 %all-to-all-start = ((bf16[8,3,48,384]{3,2,1,0:T(8,128)(2,1)}), bf16[8,3,48,384]{3,2,1,0:T(8,128)(2,1)S(1)}, u32[]{:S(2)}, u32[]{:S(2)}) async-start(bf16[8,3,48,384]{3,2,1,0:T(8,128)(2,1)} %get-tuple-element.31), calls=%async_computation | async-start | bytes 1769472 | tf_op jit(solution)/shard_map/all_to_all | solution.py:50
  20.8 6.1 %collective-permute-start.1 = (bf16[384,384]{1,0:T(8,128)(2,1)S(1)}, bf16[384,384]{1,0:T(8,128)(2,1)}, u32[]{:S(2)}, u32[]{:S(2)}) collective-permute-start(bf16[384,384]{1,0:T(8,128)(2,1)S(1)} %get-tuple-element.34), channel_id=1, source_target_pairs={{0,2},{2,0},{1,3},{3,1},{4,6},{6,4},{5,7},{7,5},{8,10},{10,8},{9,1... | collective-permute-start | bytes 884744 | tf_op jit(solution)/shard_map/ppermute | solution.py:46
  26.9 7.4 %all-to-all-done = bf16[8,3,48,384]{3,2,1,0:T(8,128)(2,1)S(1)} async-done(((bf16[8,3,48,384]{3,2,1,0:T(8,128)(2,1)}), bf16[8,3,48,384]{3,2,1,0:T(8,128)(2,1)S(1)}, u32[]{:S(2)}, u32[]{:S(2)}) %all-to-all-start) | async-done | bytes 884768 | tf_op jit(solution)/shard_map/all_to_all | solution.py:50
  36.3 1.9 %collective-permute-start = (bf16[96,1536]{1,0:T(8,128)(2,1)S(1)}, bf16[96,1536]{1,0:T(8,128)(2,1)S(1)}, u32[]{:S(2)}, u32[]{:S(2)}) collective-permute-start(bf16[96,1536]{1,0:T(8,128)(2,1)S(1)} %get-tuple-element.32.refs_0_), channel_id=1, source_target_pairs={{0,4},{4,8},{8,12},{12,16},{16,20},{20,24},{24,28},{28,0},{1,5},{5... | collective-permute-start | bytes 884744 | tf_op jit(solution)/shard_map/ppermute | solution.py:38
  38.2 5.5 %all-to-all-start.1 = ((bf16[8,48,384]{2,1,0:T(8,128)(2,1)}), bf16[8,48,384]{2,1,0:T(8,128)(2,1)S(1)}, u32[]{:S(2)}, u32[]{:S(2)}) async-start(bf16[8,48,384]{2,1,0:T(8,128)(2,1)} %bitcast.5), calls=%async_computation.1 | async-start | bytes 589824 | tf_op jit(solution)/shard_map/all_to_all | solution.py:50
  43.7 4.8 %collective-permute-start.2 = (bf16[96,1536]{1,0:T(8,128)(2,1)S(1)}, bf16[96,1536]{1,0:T(8,128)(2,1)S(1)}, u32[]{:S(2)}, u32[]{:S(2)}) collective-permute-start(bf16[96,1536]{1,0:T(8,128)(2,1)S(1)} %get-tuple-element.32.refs_0_), channel_id=1, source_target_pairs={{0,28},{4,0},{8,4},{12,8},{16,12},{20,16},{24,20},{28,24},{1,29},{... | collective-permute-start | bytes 884744 | tf_op jit(solution)/shard_map/ppermute | solution.py:38
  48.6 2.0 %all-to-all-done.1 = bf16[8,48,384]{2,1,0:T(8,128)(2,1)S(1)} async-done(((bf16[8,48,384]{2,1,0:T(8,128)(2,1)}), bf16[8,48,384]{2,1,0:T(8,128)(2,1)S(1)}, u32[]{:S(2)}, u32[]{:S(2)}) %all-to-all-start.1) | async-done | bytes 294944 | tf_op jit(solution)/shard_map/all_to_all | solution.py:50
  50.6 2.6 %collective-permute-start.3 = (bf16[96,1536]{1,0:T(8,128)(2,1)S(1)}, bf16[96,1536]{1,0:T(8,128)(2,1)S(1)}, u32[]{:S(2)}, u32[]{:S(2)}) collective-permute-start(bf16[96,1536]{1,0:T(8,128)(2,1)S(1)} %bitcast.12), channel_id=1, source_target_pairs={{0,4},{4,8},{8,12},{12,16},{16,20},{20,24},{24,28},{28,0},{1,5},{5... | collective-permute-start | bytes 884744 | tf_op jit(solution)/shard_map/ppermute | solution.py:38
  53.2 4.2 %collective-permute-start.4 = (bf16[96,1536]{1,0:T(8,128)(2,1)S(1)}, bf16[96,1536]{1,0:T(8,128)(2,1)S(1)}, u32[]{:S(2)}, u32[]{:S(2)}) collective-permute-start(bf16[96,1536]{1,0:T(8,128)(2,1)S(1)} %bitcast.13), channel_id=1, source_target_pairs={{0,28},{4,0},{8,4},{12,8},{16,12},{20,16},{24,20},{28,24},{1,29},{... | collective-permute-start | bytes 884744 | tf_op jit(solution)/shard_map/ppermute | solution.py:38
  57.4 3.4 %collective-permute-start.6 = (bf16[96,1536]{1,0:T(8,128)(2,1)S(1)}, bf16[96,1536]{1,0:T(8,128)(2,1)S(1)}, u32[]{:S(2)}, u32[]{:S(2)}) collective-permute-start(bf16[96,1536]{1,0:T(8,128)(2,1)S(1)} %collective-permute-done.2.refs_3_), channel_id=1, source_target_pairs={{0,28},{4,0},{8,4},{12,8},{16,12},{20,16},{24,20},{28,24},{1,29},{... | collective-permute-start | bytes 884744 | tf_op jit(solution)/shard_map/ppermute | solution.py:38
  63.7 2.3 %collective-permute-start.5 = (bf16[96,1536]{1,0:T(8,128)(2,1)S(1)}, bf16[96,1536]{1,0:T(8,128)(2,1)S(1)}, u32[]{:S(2)}, u32[]{:S(2)}) collective-permute-start(bf16[96,1536]{1,0:T(8,128)(2,1)S(1)} %collective-permute-done.refs_2_), channel_id=1, source_target_pairs={{0,4},{4,8},{8,12},{12,16},{16,20},{20,24},{24,28},{28,0},{1,5},{5... | collective-permute-start | bytes 884744 | tf_op jit(solution)/shard_map/ppermute | solution.py:38
  66.0 4.2 %collective-permute-start.8 = (bf16[96,1536]{1,0:T(8,128)(2,1)S(1)}, bf16[96,1536]{1,0:T(8,128)(2,1)S(1)}, u32[]{:S(2)}, u32[]{:S(2)}) collective-permute-start(bf16[96,1536]{1,0:T(8,128)(2,1)S(1)} %collective-permute-done.4.refs_5_), channel_id=1, source_target_pairs={{0,28},{4,0},{8,4},{12,8},{16,12},{20,16},{24,20},{28,24},{1,29},{... | collective-permute-start | bytes 884744 | tf_op jit(solution)/shard_map/ppermute | solution.py:38
  70.2 4.0 %collective-permute-start.10 = (bf16[96,1536]{1,0:T(8,128)(2,1)S(1)}, bf16[96,1536]{1,0:T(8,128)(2,1)S(1)}, u32[]{:S(2)}, u32[]{:S(2)}) collective-permute-start(bf16[96,1536]{1,0:T(8,128)(2,1)S(1)} %collective-permute-done.6.refs_7_), channel_id=1, source_target_pairs={{0,28},{4,0},{8,4},{12,8},{16,12},{20,16},{24,20},{28,24},{1,29},{... | collective-permute-start | bytes 884744 | tf_op jit(solution)/shard_map/ppermute | solution.py:38
  76.2 2.0 %collective-permute-done.5.refs_6_ = bf16[96,1536]{1,0:T(8,128)(2,1)S(1)} collective-permute-done((bf16[96,1536]{1,0:T(8,128)(2,1)S(1)}, bf16[96,1536]{1,0:T(8,128)(2,1)S(1)}, u32[]{:S(2)}, u32[]{:S(2)}) %collective-permute-start.5) | collective-permute-done | bytes 294944 | tf_op jit(solution)/shard_map/ppermute | solution.py:38
  80.1 4.6 %collective-permute-start.12 = (bf16[96,1536]{1,0:T(8,128)(2,1)S(1)}, bf16[96,1536]{1,0:T(8,128)(2,1)}, u32[]{:S(2)}, u32[]{:S(2)}) collective-permute-start(bf16[96,1536]{1,0:T(8,128)(2,1)S(1)} %collective-permute-done.8.refs_9_), channel_id=1, source_target_pairs={{0,28},{4,0},{8,4},{12,8},{16,12},{20,16},{24,20},{28,24},{1,29},{... | collective-permute-start | bytes 884744 | tf_op jit(solution)/shard_map/ppermute | solution.py:38
  84.7 1.9 %collective-permute-start.13 = (bf16[96,1536]{1,0:T(8,128)(2,1)S(1)}, bf16[96,1536]{1,0:T(8,128)(2,1)}, u32[]{:S(2)}, u32[]{:S(2)}) collective-permute-start(bf16[96,1536]{1,0:T(8,128)(2,1)S(1)} %collective-permute-done.10.refs_11_), channel_id=1, source_target_pairs={{0,28},{4,0},{8,4},{12,8},{16,12},{20,16},{24,20},{28,24},{1,29},{... | collective-permute-start | bytes 884744 | tf_op jit(solution)/shard_map/ppermute | solution.py:38
  86.7 3.4 %collective-permute-start.14 = (bf16[96,1536]{1,0:T(8,128)(2,1)S(1)}, bf16[96,1536]{1,0:T(8,128)(2,1)}, u32[]{:S(2)}, u32[]{:S(2)}) collective-permute-start(bf16[96,1536]{1,0:T(8,128)(2,1)S(1)} %collective-permute-done.11.refs_12_), channel_id=1, source_target_pairs={{0,4},{4,8},{8,12},{12,16},{16,20},{20,24},{24,28},{28,0},{1,5},{5... | collective-permute-start | bytes 884744 | tf_op jit(solution)/shard_map/ppermute | solution.py:38
  90.5 5.2 %collective-permute-done.13.refs_14_ = bf16[96,1536]{1,0:T(8,128)(2,1)} collective-permute-done((bf16[96,1536]{1,0:T(8,128)(2,1)S(1)}, bf16[96,1536]{1,0:T(8,128)(2,1)}, u32[]{:S(2)}, u32[]{:S(2)}) %collective-permute-start.13) | collective-permute-done | bytes 294944 | tf_op jit(solution)/shard_map/ppermute | solution.py:38
  96.1 9.2 %all-gather.2.cloned.1.call-done.refs_16_ = bf16[8,768,384]{2,1,0:T(8,128)(2,1)} async-done(((bf16[1,768,384]{2,1,0:T(8,128)(2,1)}), bf16[8,768,384]{2,1,0:T(8,128)(2,1)}) %all-gather.2.cloned.1.call-update) | async-done | bytes 4718608 | tf_op jit(solution)/shard_map/all_gather | solution.py:193
  105.4 13.2 %shard_map.39 = (bf16[384,1536]{1,0:T(8,128)(2,1)}, bf16[384,1536]{1,0:T(8,128)(2,1)}, bf16[384,1536]{1,0:T(8,128)(2,1)}, bf16[384,1536]{1,0:T(8,128)(2,1)}) custom-call(s32[2]{0:T(128)S(1)} %pad_add_fusion.place, bf16[96,1536]{1,0:T(8,128)(2,1)S(1)} %get-tuple-element.32.refs_0_, bf16[96,1536]{1,0:T(8,128)(2,1)S(1)} %bitcast.14, ...), custom_call_target="tpu_custom_call" | custom-call | flops 7247757312 | bytes 14155784 | tf_op jit(solution)/shard_map/pallas_call | solution.py:26
  118.6 2.6 %collective-permute-start.19 = (bf16[384,1536]{1,0:T(8,128)(2,1)}, bf16[384,1536]{1,0:T(8,128)(2,1)S(1)}, u32[]{:S(2)}, u32[]{:S(2)}) collective-permute-start(bf16[384,1536]{1,0:T(8,128)(2,1)} %get-tuple-element.47), channel_id=1, source_target_pairs={{0,1},{1,0},{2,3},{3,2},{4,5},{5,4},{6,7},{7,6},{8,9},{9,8},{10,11... | collective-permute-start | bytes 3538952 | tf_op jit(solution)/shard_map/ppermute | solution.py:46
  125.4 3.2 %collective-permute-start.20 = (bf16[384,384]{1,0:T(8,128)(2,1)S(1)}, bf16[384,384]{1,0:T(8,128)(2,1)S(1)}, u32[]{:S(2)}, u32[]{:S(2)}) collective-permute-start(bf16[384,384]{1,0:T(8,128)(2,1)S(1)} %get-tuple-element.49), channel_id=1, source_target_pairs={{0,32},{32,64},{64,96},{96,0},{1,33},{33,65},{65,97},{97,1},{2,34}... | collective-permute-start | bytes 884744 | tf_op jit(solution)/shard_map/ppermute | solution.py:42
  128.6 4.3 %collective-permute-start.21 = (bf16[384,384]{1,0:T(8,128)(2,1)S(1)}, bf16[384,384]{1,0:T(8,128)(2,1)S(1)}, u32[]{:S(2)}, u32[]{:S(2)}) collective-permute-start(bf16[384,384]{1,0:T(8,128)(2,1)S(1)} %get-tuple-element.50), channel_id=1, source_target_pairs={{0,64},{32,96},{64,0},{96,32},{1,65},{33,97},{65,1},{97,33},{2,66}... | collective-permute-start | bytes 884744 | tf_op jit(solution)/shard_map/ppermute | solution.py:42
  132.9 3.1 %collective-permute-start.22 = (bf16[384,384]{1,0:T(8,128)(2,1)S(1)}, bf16[384,384]{1,0:T(8,128)(2,1)S(1)}, u32[]{:S(2)}, u32[]{:S(2)}) collective-permute-start(bf16[384,384]{1,0:T(8,128)(2,1)S(1)} %get-tuple-element.51), channel_id=1, source_target_pairs={{0,96},{32,0},{64,32},{96,64},{1,97},{33,1},{65,33},{97,65},{2,98}... | collective-permute-start | bytes 884744 | tf_op jit(solution)/shard_map/ppermute | solution.py:42
  136.4 2.2 %collective-permute-start.16 = (bf16[384,384]{1,0:T(8,128)(2,1)S(1)}, bf16[384,384]{1,0:T(8,128)(2,1)S(1)}, u32[]{:S(2)}, u32[]{:S(2)}) collective-permute-start(bf16[384,384]{1,0:T(8,128)(2,1)S(1)} %get-tuple-element.42), channel_id=1, source_target_pairs={{0,32},{32,64},{64,96},{96,0},{1,33},{33,65},{65,97},{97,1},{2,34}... | collective-permute-start | bytes 884744 | tf_op jit(solution)/shard_map/ppermute | solution.py:42
  138.6 2.8 %collective-permute-start.17 = (bf16[384,384]{1,0:T(8,128)(2,1)S(1)}, bf16[384,384]{1,0:T(8,128)(2,1)S(1)}, u32[]{:S(2)}, u32[]{:S(2)}) collective-permute-start(bf16[384,384]{1,0:T(8,128)(2,1)S(1)} %get-tuple-element.43), channel_id=1, source_target_pairs={{0,64},{32,96},{64,0},{96,32},{1,65},{33,97},{65,1},{97,33},{2,66}... | collective-permute-start | bytes 884744 | tf_op jit(solution)/shard_map/ppermute | solution.py:42
  141.4 3.4 %collective-permute-start.18 = (bf16[384,384]{1,0:T(8,128)(2,1)S(1)}, bf16[384,384]{1,0:T(8,128)(2,1)S(1)}, u32[]{:S(2)}, u32[]{:S(2)}) collective-permute-start(bf16[384,384]{1,0:T(8,128)(2,1)S(1)} %get-tuple-element.44), channel_id=1, source_target_pairs={{0,96},{32,0},{64,32},{96,64},{1,97},{33,1},{65,33},{97,65},{2,98}... | collective-permute-start | bytes 884744 | tf_op jit(solution)/shard_map/ppermute | solution.py:42
  146.2 5.8 %collective-permute-start.23 = (f32[1,384]{1,0:T(1,128)S(1)}, f32[1,384]{1,0:T(1,128)S(1)}, u32[]{:S(2)}, u32[]{:S(2)}) collective-permute-start(f32[1,384]{1,0:T(1,128)S(1)} %get-tuple-element.52), channel_id=1, source_target_pairs={{0,2},{2,0},{1,3},{3,1},{4,6},{6,4},{5,7},{7,5},{8,10},{10,8},{9,1... | collective-permute-start | bytes 4616 | tf_op jit(solution)/shard_map/ppermute | solution.py:46
  152.0 2.4 %collective-permute-done.23 = f32[1,384]{1,0:T(1,128)S(1)} collective-permute-done((f32[1,384]{1,0:T(1,128)S(1)}, f32[1,384]{1,0:T(1,128)S(1)}, u32[]{:S(2)}, u32[]{:S(2)}) %collective-permute-start.23) | collective-permute-done | bytes 1568 | tf_op jit(solution)/shard_map/ppermute | solution.py:46
  154.4 5.8 %collective-permute-start.24 = (bf16[384,384]{1,0:T(8,128)(2,1)S(1)}, bf16[384,384]{1,0:T(8,128)(2,1)S(1)}, u32[]{:S(2)}, u32[]{:S(2)}) collective-permute-start(bf16[384,384]{1,0:T(8,128)(2,1)S(1)} %get-tuple-element.54), channel_id=1, source_target_pairs={{0,2},{2,0},{1,3},{3,1},{4,6},{6,4},{5,7},{7,5},{8,10},{10,8},{9,1... | collective-permute-start | bytes 884744 | tf_op jit(solution)/shard_map/ppermute | solution.py:46
  161.2 7.0 %all-to-all-start.2 = ((f32[16,1,384]{2,1,0:T(1,128)}), f32[16,1,384]{2,1,0:T(1,128)S(1)}, u32[]{:S(2)}, u32[]{:S(2)}) async-start(f32[16,1,384]{2,1,0:T(1,128)} %broadcast_in_dim.12), calls=%async_computation.2 | async-start | bytes 49152 | tf_op jit(solution)/shard_map/all_to_all | solution.py:230
  168.3 10.5 %all-to-all-done.2.sums = f32[16,1,384]{2,1,0:T(1,128)S(1)} async-done(((f32[16,1,384]{2,1,0:T(1,128)}), f32[16,1,384]{2,1,0:T(1,128)S(1)}, u32[]{:S(2)}, u32[]{:S(2)}) %all-to-all-start.2) | async-done | bytes 24608 | tf_op jit(solution)/shard_map/all_to_all | solution.py:230
  (50 shorter events, 22.3 us)
Async XLA Ops:
  7.4 1.3 copy-start.2
  10.5 23.8 %all-to-all-start = ((bf16[8,3,48,384]{3,2,1,0:T(8,128)(2,1)}), bf16[8,3,48,384]{3,2,1,0:T(8,128)(2,1)S(1)}, u32[]{:S(2)}, u32[]{:S(2)}) async-start(bf16[8,3,48,384]{3,2,1,0:T(8,128)(2,1)} %get-tuple-element.31), calls=%async_computation | async-start | bytes 1769472 | tf_op jit(solution)/shard_map/all_to_all | solution.py:50
  20.8 84.6 %all-gather.2.cloned.1.call-start = ((), (), s32[]{:S(2)}) async-start(), calls=%async_computation.3 | async-start | bytes 5308416 | tf_op jit(solution)/shard_map/all_gather | solution.py:193
  20.8 15.4 %collective-permute-start.1 = (bf16[384,384]{1,0:T(8,128)(2,1)S(1)}, bf16[384,384]{1,0:T(8,128)(2,1)}, u32[]{:S(2)}, u32[]{:S(2)}) collective-permute-start(bf16[384,384]{1,0:T(8,128)(2,1)S(1)} %get-tuple-element.34), channel_id=1, source_target_pairs={{0,2},{2,0},{1,3},{3,1},{4,6},{6,4},{5,7},{7,5},{8,10},{10,8},{9,1... | collective-permute-start | bytes 884744 | tf_op jit(solution)/shard_map/ppermute | solution.py:46
  36.3 14.3 %collective-permute-start = (bf16[96,1536]{1,0:T(8,128)(2,1)S(1)}, bf16[96,1536]{1,0:T(8,128)(2,1)S(1)}, u32[]{:S(2)}, u32[]{:S(2)}) collective-permute-start(bf16[96,1536]{1,0:T(8,128)(2,1)S(1)} %get-tuple-element.32.refs_0_), channel_id=1, source_target_pairs={{0,4},{4,8},{8,12},{12,16},{16,20},{20,24},{24,28},{28,0},{1,5},{5... | collective-permute-start | bytes 884744 | tf_op jit(solution)/shard_map/ppermute | solution.py:38
  38.2 12.3 %all-to-all-start.1 = ((bf16[8,48,384]{2,1,0:T(8,128)(2,1)}), bf16[8,48,384]{2,1,0:T(8,128)(2,1)S(1)}, u32[]{:S(2)}, u32[]{:S(2)}) async-start(bf16[8,48,384]{2,1,0:T(8,128)(2,1)} %bitcast.5), calls=%async_computation.1 | async-start | bytes 589824 | tf_op jit(solution)/shard_map/all_to_all | solution.py:50
  43.7 13.6 %collective-permute-start.2 = (bf16[96,1536]{1,0:T(8,128)(2,1)S(1)}, bf16[96,1536]{1,0:T(8,128)(2,1)S(1)}, u32[]{:S(2)}, u32[]{:S(2)}) collective-permute-start(bf16[96,1536]{1,0:T(8,128)(2,1)S(1)} %get-tuple-element.32.refs_0_), channel_id=1, source_target_pairs={{0,28},{4,0},{8,4},{12,8},{16,12},{20,16},{24,20},{28,24},{1,29},{... | collective-permute-start | bytes 884744 | tf_op jit(solution)/shard_map/ppermute | solution.py:38
  50.6 11.2 %collective-permute-start.3 = (bf16[96,1536]{1,0:T(8,128)(2,1)S(1)}, bf16[96,1536]{1,0:T(8,128)(2,1)S(1)}, u32[]{:S(2)}, u32[]{:S(2)}) collective-permute-start(bf16[96,1536]{1,0:T(8,128)(2,1)S(1)} %bitcast.12), channel_id=1, source_target_pairs={{0,4},{4,8},{8,12},{12,16},{16,20},{20,24},{24,28},{28,0},{1,5},{5... | collective-permute-start | bytes 884744 | tf_op jit(solution)/shard_map/ppermute | solution.py:38
  53.2 12.8 %collective-permute-start.4 = (bf16[96,1536]{1,0:T(8,128)(2,1)S(1)}, bf16[96,1536]{1,0:T(8,128)(2,1)S(1)}, u32[]{:S(2)}, u32[]{:S(2)}) collective-permute-start(bf16[96,1536]{1,0:T(8,128)(2,1)S(1)} %bitcast.13), channel_id=1, source_target_pairs={{0,28},{4,0},{8,4},{12,8},{16,12},{20,16},{24,20},{28,24},{1,29},{... | collective-permute-start | bytes 884744 | tf_op jit(solution)/shard_map/ppermute | solution.py:38
  57.4 12.9 %collective-permute-start.6 = (bf16[96,1536]{1,0:T(8,128)(2,1)S(1)}, bf16[96,1536]{1,0:T(8,128)(2,1)S(1)}, u32[]{:S(2)}, u32[]{:S(2)}) collective-permute-start(bf16[96,1536]{1,0:T(8,128)(2,1)S(1)} %collective-permute-done.2.refs_3_), channel_id=1, source_target_pairs={{0,28},{4,0},{8,4},{12,8},{16,12},{20,16},{24,20},{28,24},{1,29},{... | collective-permute-start | bytes 884744 | tf_op jit(solution)/shard_map/ppermute | solution.py:38
  61.8 12.5 %collective-permute-start.7 = (bf16[96,1536]{1,0:T(8,128)(2,1)S(1)}, bf16[96,1536]{1,0:T(8,128)(2,1)S(1)}, u32[]{:S(2)}, u32[]{:S(2)}) collective-permute-start(bf16[96,1536]{1,0:T(8,128)(2,1)S(1)} %collective-permute-done.3.refs_4_), channel_id=1, source_target_pairs={{0,4},{4,8},{8,12},{12,16},{16,20},{20,24},{24,28},{28,0},{1,5},{5... | collective-permute-start | bytes 884744 | tf_op jit(solution)/shard_map/ppermute | solution.py:38
  63.7 14.5 %collective-permute-start.5 = (bf16[96,1536]{1,0:T(8,128)(2,1)S(1)}, bf16[96,1536]{1,0:T(8,128)(2,1)S(1)}, u32[]{:S(2)}, u32[]{:S(2)}) collective-permute-start(bf16[96,1536]{1,0:T(8,128)(2,1)S(1)} %collective-permute-done.refs_2_), channel_id=1, source_target_pairs={{0,4},{4,8},{8,12},{12,16},{16,20},{20,24},{24,28},{28,0},{1,5},{5... | collective-permute-start | bytes 884744 | tf_op jit(solution)/shard_map/ppermute | solution.py:38
  66.0 14.1 %collective-permute-start.8 = (bf16[96,1536]{1,0:T(8,128)(2,1)S(1)}, bf16[96,1536]{1,0:T(8,128)(2,1)S(1)}, u32[]{:S(2)}, u32[]{:S(2)}) collective-permute-start(bf16[96,1536]{1,0:T(8,128)(2,1)S(1)} %collective-permute-done.4.refs_5_), channel_id=1, source_target_pairs={{0,28},{4,0},{8,4},{12,8},{16,12},{20,16},{24,20},{28,24},{1,29},{... | collective-permute-start | bytes 884744 | tf_op jit(solution)/shard_map/ppermute | solution.py:38
  70.2 14.5 %collective-permute-start.10 = (bf16[96,1536]{1,0:T(8,128)(2,1)S(1)}, bf16[96,1536]{1,0:T(8,128)(2,1)S(1)}, u32[]{:S(2)}, u32[]{:S(2)}) collective-permute-start(bf16[96,1536]{1,0:T(8,128)(2,1)S(1)} %collective-permute-done.6.refs_7_), channel_id=1, source_target_pairs={{0,28},{4,0},{8,4},{12,8},{16,12},{20,16},{24,20},{28,24},{1,29},{... | collective-permute-start | bytes 884744 | tf_op jit(solution)/shard_map/ppermute | solution.py:38
  74.3 12.4 %collective-permute-start.11 = (bf16[96,1536]{1,0:T(8,128)(2,1)S(1)}, bf16[96,1536]{1,0:T(8,128)(2,1)S(1)}, u32[]{:S(2)}, u32[]{:S(2)}) collective-permute-start(bf16[96,1536]{1,0:T(8,128)(2,1)S(1)} %collective-permute-done.7.refs_8_), channel_id=1, source_target_pairs={{0,4},{4,8},{8,12},{12,16},{16,20},{20,24},{24,28},{28,0},{1,5},{5... | collective-permute-start | bytes 884744 | tf_op jit(solution)/shard_map/ppermute | solution.py:38
  78.2 12.3 %collective-permute-start.9 = (bf16[96,1536]{1,0:T(8,128)(2,1)S(1)}, bf16[96,1536]{1,0:T(8,128)(2,1)}, u32[]{:S(2)}, u32[]{:S(2)}) collective-permute-start(bf16[96,1536]{1,0:T(8,128)(2,1)S(1)} %collective-permute-done.5.refs_6_), channel_id=1, source_target_pairs={{0,4},{4,8},{8,12},{12,16},{16,20},{20,24},{24,28},{28,0},{1,5},{5... | collective-permute-start | bytes 884744 | tf_op jit(solution)/shard_map/ppermute | solution.py:38
  80.1 10.3 %collective-permute-start.12 = (bf16[96,1536]{1,0:T(8,128)(2,1)S(1)}, bf16[96,1536]{1,0:T(8,128)(2,1)}, u32[]{:S(2)}, u32[]{:S(2)}) collective-permute-start(bf16[96,1536]{1,0:T(8,128)(2,1)S(1)} %collective-permute-done.8.refs_9_), channel_id=1, source_target_pairs={{0,28},{4,0},{8,4},{12,8},{16,12},{20,16},{24,20},{28,24},{1,29},{... | collective-permute-start | bytes 884744 | tf_op jit(solution)/shard_map/ppermute | solution.py:38
  84.7 10.9 %collective-permute-start.13 = (bf16[96,1536]{1,0:T(8,128)(2,1)S(1)}, bf16[96,1536]{1,0:T(8,128)(2,1)}, u32[]{:S(2)}, u32[]{:S(2)}) collective-permute-start(bf16[96,1536]{1,0:T(8,128)(2,1)S(1)} %collective-permute-done.10.refs_11_), channel_id=1, source_target_pairs={{0,28},{4,0},{8,4},{12,8},{16,12},{20,16},{24,20},{28,24},{1,29},{... | collective-permute-start | bytes 884744 | tf_op jit(solution)/shard_map/ppermute | solution.py:38
  86.7 9.5 %collective-permute-start.14 = (bf16[96,1536]{1,0:T(8,128)(2,1)S(1)}, bf16[96,1536]{1,0:T(8,128)(2,1)}, u32[]{:S(2)}, u32[]{:S(2)}) collective-permute-start(bf16[96,1536]{1,0:T(8,128)(2,1)S(1)} %collective-permute-done.11.refs_12_), channel_id=1, source_target_pairs={{0,4},{4,8},{8,12},{12,16},{16,20},{20,24},{24,28},{28,0},{1,5},{5... | collective-permute-start | bytes 884744 | tf_op jit(solution)/shard_map/ppermute | solution.py:38
  118.6 5.3 %collective-permute-start.19 = (bf16[384,1536]{1,0:T(8,128)(2,1)}, bf16[384,1536]{1,0:T(8,128)(2,1)S(1)}, u32[]{:S(2)}, u32[]{:S(2)}) collective-permute-start(bf16[384,1536]{1,0:T(8,128)(2,1)} %get-tuple-element.47), channel_id=1, source_target_pairs={{0,1},{1,0},{2,3},{3,2},{4,5},{5,4},{6,7},{7,6},{8,9},{9,8},{10,11... | collective-permute-start | bytes 3538952 | tf_op jit(solution)/shard_map/ppermute | solution.py:46
  121.2 14.9 %collective-permute-start.15 = (bf16[384,1536]{1,0:T(8,128)(2,1)}, bf16[384,1536]{1,0:T(8,128)(2,1)S(1)}, u32[]{:S(2)}, u32[]{:S(2)}) collective-permute-start(bf16[384,1536]{1,0:T(8,128)(2,1)} %get-tuple-element.40), channel_id=1, source_target_pairs={{0,1},{1,0},{2,3},{3,2},{4,5},{5,4},{6,7},{7,6},{8,9},{9,8},{10,11... | collective-permute-start | bytes 3538952 | tf_op jit(solution)/shard_map/ppermute | solution.py:46
  125.1 10.9 %copy-start = (bf16[384,1536]{1,0:T(8,128)(2,1)S(1)}, bf16[384,1536]{1,0:T(8,128)(2,1)}, u32[]{:S(2)}) copy-start(bf16[384,1536]{1,0:T(8,128)(2,1)} %get-tuple-element.39.ours) | copy-start | bytes 3538948
  125.4 16.0 %collective-permute-start.20 = (bf16[384,384]{1,0:T(8,128)(2,1)S(1)}, bf16[384,384]{1,0:T(8,128)(2,1)S(1)}, u32[]{:S(2)}, u32[]{:S(2)}) collective-permute-start(bf16[384,384]{1,0:T(8,128)(2,1)S(1)} %get-tuple-element.49), channel_id=1, source_target_pairs={{0,32},{32,64},{64,96},{96,0},{1,33},{33,65},{65,97},{97,1},{2,34}... | collective-permute-start | bytes 884744 | tf_op jit(solution)/shard_map/ppermute | solution.py:42
  128.6 16.2 %collective-permute-start.21 = (bf16[384,384]{1,0:T(8,128)(2,1)S(1)}, bf16[384,384]{1,0:T(8,128)(2,1)S(1)}, u32[]{:S(2)}, u32[]{:S(2)}) collective-permute-start(bf16[384,384]{1,0:T(8,128)(2,1)S(1)} %get-tuple-element.50), channel_id=1, source_target_pairs={{0,64},{32,96},{64,0},{96,32},{1,65},{33,97},{65,1},{97,33},{2,66}... | collective-permute-start | bytes 884744 | tf_op jit(solution)/shard_map/ppermute | solution.py:42
  132.9 12.9 %collective-permute-start.22 = (bf16[384,384]{1,0:T(8,128)(2,1)S(1)}, bf16[384,384]{1,0:T(8,128)(2,1)S(1)}, u32[]{:S(2)}, u32[]{:S(2)}) collective-permute-start(bf16[384,384]{1,0:T(8,128)(2,1)S(1)} %get-tuple-element.51), channel_id=1, source_target_pairs={{0,96},{32,0},{64,32},{96,64},{1,97},{33,1},{65,33},{97,65},{2,98}... | collective-permute-start | bytes 884744 | tf_op jit(solution)/shard_map/ppermute | solution.py:42
  136.4 23.9 %collective-permute-start.16 = (bf16[384,384]{1,0:T(8,128)(2,1)S(1)}, bf16[384,384]{1,0:T(8,128)(2,1)S(1)}, u32[]{:S(2)}, u32[]{:S(2)}) collective-permute-start(bf16[384,384]{1,0:T(8,128)(2,1)S(1)} %get-tuple-element.42), channel_id=1, source_target_pairs={{0,32},{32,64},{64,96},{96,0},{1,33},{33,65},{65,97},{97,1},{2,34}... | collective-permute-start | bytes 884744 | tf_op jit(solution)/shard_map/ppermute | solution.py:42
  138.6 21.7 %collective-permute-start.17 = (bf16[384,384]{1,0:T(8,128)(2,1)S(1)}, bf16[384,384]{1,0:T(8,128)(2,1)S(1)}, u32[]{:S(2)}, u32[]{:S(2)}) collective-permute-start(bf16[384,384]{1,0:T(8,128)(2,1)S(1)} %get-tuple-element.43), channel_id=1, source_target_pairs={{0,64},{32,96},{64,0},{96,32},{1,65},{33,97},{65,1},{97,33},{2,66}... | collective-permute-start | bytes 884744 | tf_op jit(solution)/shard_map/ppermute | solution.py:42
  141.4 18.8 %collective-permute-start.18 = (bf16[384,384]{1,0:T(8,128)(2,1)S(1)}, bf16[384,384]{1,0:T(8,128)(2,1)S(1)}, u32[]{:S(2)}, u32[]{:S(2)}) collective-permute-start(bf16[384,384]{1,0:T(8,128)(2,1)S(1)} %get-tuple-element.44), channel_id=1, source_target_pairs={{0,96},{32,0},{64,32},{96,64},{1,97},{33,1},{65,33},{97,65},{2,98}... | collective-permute-start | bytes 884744 | tf_op jit(solution)/shard_map/ppermute | solution.py:42
  145.9 22.3 %copy-start.3 = (s32[6,3]{0,1:T(4,128)S(1)}, s32[6,3]{0,1:T(4,128)}, u32[]{:S(2)}) copy-start(s32[6,3]{0,1:T(4,128)} %param.5) | copy-start | bytes 220
  146.2 8.2 %collective-permute-start.23 = (f32[1,384]{1,0:T(1,128)S(1)}, f32[1,384]{1,0:T(1,128)S(1)}, u32[]{:S(2)}, u32[]{:S(2)}) collective-permute-start(f32[1,384]{1,0:T(1,128)S(1)} %get-tuple-element.52), channel_id=1, source_target_pairs={{0,2},{2,0},{1,3},{3,1},{4,6},{6,4},{5,7},{7,5},{8,10},{10,8},{9,1... | collective-permute-start | bytes 4616 | tf_op jit(solution)/shard_map/ppermute | solution.py:46
  154.4 24.4 %collective-permute-start.24 = (bf16[384,384]{1,0:T(8,128)(2,1)S(1)}, bf16[384,384]{1,0:T(8,128)(2,1)S(1)}, u32[]{:S(2)}, u32[]{:S(2)}) collective-permute-start(bf16[384,384]{1,0:T(8,128)(2,1)S(1)} %get-tuple-element.54), channel_id=1, source_target_pairs={{0,2},{2,0},{1,3},{3,1},{4,6},{6,4},{5,7},{7,5},{8,10},{10,8},{9,1... | collective-permute-start | bytes 884744 | tf_op jit(solution)/shard_map/ppermute | solution.py:46
  161.2 17.6 %all-to-all-start.2 = ((f32[16,1,384]{2,1,0:T(1,128)}), f32[16,1,384]{2,1,0:T(1,128)S(1)}, u32[]{:S(2)}, u32[]{:S(2)}) async-start(f32[16,1,384]{2,1,0:T(1,128)} %broadcast_in_dim.12), calls=%async_computation.2 | async-start | bytes 49152 | tf_op jit(solution)/shard_map/all_to_all | solution.py:230
  (1 other events, 1.3 us)
Sparse Core Ops, SparseCore 0:
  36.4 68.9 all-gather.1

commit v12 on v11

--- a/solution.py
+++ b/solution.py
@@ -107,10 +107,8 @@
         if own:
             for copy in copies[-Z_LO:]:
                 copy.wait()
-
-        @pl.loop(0, WIDE // step)
-        def _(i):
-            at = pl.ds(pl.multiple_of(i * step, step), step)
+        for start in range(0, WIDE, step):
+            at = slice(start, start + step)
             product = jnp.dot(b[own], a[:, at], preferred_element_type=F32)
             theirs[:, at] = product[:UNIT].astype(BF16)
             ours[:, at] = product[UNIT:].astype(BF16)

time: 189 us -> 188 us (level)
  no operation moved by 1% of the time
where the time goes in v12:
time: 188 us; the launch traced here: 187 us
  starting transfers between devices  107 us (57%)
  waiting for transfers between devices  42.7 us (23%)
  Pallas kernels  18.9 us (10%)
  between operations  13.8 us (7%)
  local copies, waits for them, and re-layouts  4.06 us (2%)
    ppermute x14, starting transfers between devices, shift_y(): return lax.ppermute(shard, 'y', [(i, (i + step) % Y) for i in range(Y)])  43 us
    ppermute x5, starting transfers between devices, swap(): return lax.ppermute(shard, axis, [(0, 1), (1, 0)])  22.3 us
    ppermute x6, starting transfers between devices, shift_x(): return lax.ppermute(shard, 'x', [(i, (i + step) % X) for i in range(X)])  19 us
    pallas_call x8, Pallas kernels, call(): pl.pallas_call(body, out_shape=shapes, in_specs=ins, out_specs=[VMEM] * l...  18.9 us
    all_to_all x2, starting transfers between devices, spread_over(): lax.all_to_all(array, ('x', 'core'), split_axis=0, concat_axis=0, tiled=T...  15.8 us
    all_to_all x1, waiting for transfers between devices, local(): lax.all_to_all(sums, ('zlo', 'x'), split_axis=0, concat_axis=0, tiled=True)  10.5 us
    all_to_all x2, waiting for transfers between devices, spread_over(): lax.all_to_all(array, ('x', 'core'), split_axis=0, concat_axis=0, tiled=T...  9.33 us
    all_gather x1, waiting for transfers between devices, local(): right = lax.all_gather(right, ('zhi', 'zlo'), axis=0, tiled=True)  9.25 us
  transfers between devices with their start and end apart: 29, of which 13 were waited for; matrix products, arithmetic and copies ran while one was open for 0% of the time, Pallas kernels for 1%

profile of v12, /device:TPU:1, one launch (start us, length us, event | category | flops | bytes accessed | tf_op | source)
XLA Modules:
  0.0 186.8 jit_solution(10057121506830009567)
XLA Ops:
  10.5 10.3 %all-to-all-start = ((bf16[8,3,48,384]{3,2,1,0:T(8,128)(2,1)}), bf16[8,3,48,384]{3,2,1,0:T(8,128)(2,1)S(1)}, u32[]{:S(2)}, u32[]{:S(2)}) async-start(bf16[8,3,48,384]{3,2,1,0:T(8,128)(2,1)} %get-tuple-element.31), calls=%async_computation | async-start | bytes 1769472 | tf_op jit(solution)/shard_map/all_to_all | solution.py:50
  20.8 6.1 %collective-permute-start.1 = (bf16[384,384]{1,0:T(8,128)(2,1)S(1)}, bf16[384,384]{1,0:T(8,128)(2,1)}, u32[]{:S(2)}, u32[]{:S(2)}) collective-permute-start(bf16[384,384]{1,0:T(8,128)(2,1)S(1)} %get-tuple-element.34), channel_id=1, source_target_pairs={{0,2},{2,0},{1,3},{3,1},{4,6},{6,4},{5,7},{7,5},{8,10},{10,8},{9,1... | collective-permute-start | bytes 884744 | tf_op jit(solution)/shard_map/ppermute | solution.py:46
  26.9 7.4 %all-to-all-done = bf16[8,3,48,384]{3,2,1,0:T(8,128)(2,1)S(1)} async-done(((bf16[8,3,48,384]{3,2,1,0:T(8,128)(2,1)}), bf16[8,3,48,384]{3,2,1,0:T(8,128)(2,1)S(1)}, u32[]{:S(2)}, u32[]{:S(2)}) %all-to-all-start) | async-done | bytes 884768 | tf_op jit(solution)/shard_map/all_to_all | solution.py:50
  36.3 1.9 %collective-permute-start = (bf16[96,1536]{1,0:T(8,128)(2,1)S(1)}, bf16[96,1536]{1,0:T(8,128)(2,1)S(1)}, u32[]{:S(2)}, u32[]{:S(2)}) collective-permute-start(bf16[96,1536]{1,0:T(8,128)(2,1)S(1)} %get-tuple-element.32.refs_0_), channel_id=1, source_target_pairs={{0,4},{4,8},{8,12},{12,16},{16,20},{20,24},{24,28},{28,0},{1,5},{5... | collective-permute-start | bytes 884744 | tf_op jit(solution)/shard_map/ppermute | solution.py:38
  38.2 5.5 %all-to-all-start.1 = ((bf16[8,48,384]{2,1,0:T(8,128)(2,1)}), bf16[8,48,384]{2,1,0:T(8,128)(2,1)S(1)}, u32[]{:S(2)}, u32[]{:S(2)}) async-start(bf16[8,48,384]{2,1,0:T(8,128)(2,1)} %bitcast.5), calls=%async_computation.1 | async-start | bytes 589824 | tf_op jit(solution)/shard_map/all_to_all | solution.py:50
  43.7 4.8 %collective-permute-start.2 = (bf16[96,1536]{1,0:T(8,128)(2,1)S(1)}, bf16[96,1536]{1,0:T(8,128)(2,1)S(1)}, u32[]{:S(2)}, u32[]{:S(2)}) collective-permute-start(bf16[96,1536]{1,0:T(8,128)(2,1)S(1)} %get-tuple-element.32.refs_0_), channel_id=1, source_target_pairs={{0,28},{4,0},{8,4},{12,8},{16,12},{20,16},{24,20},{28,24},{1,29},{... | collective-permute-start | bytes 884744 | tf_op jit(solution)/shard_map/ppermute | solution.py:38
  48.6 2.0 %all-to-all-done.1 = bf16[8,48,384]{2,1,0:T(8,128)(2,1)S(1)} async-done(((bf16[8,48,384]{2,1,0:T(8,128)(2,1)}), bf16[8,48,384]{2,1,0:T(8,128)(2,1)S(1)}, u32[]{:S(2)}, u32[]{:S(2)}) %all-to-all-start.1) | async-done | bytes 294944 | tf_op jit(solution)/shard_map/all_to_all | solution.py:50
  50.6 2.6 %collective-permute-start.3 = (bf16[96,1536]{1,0:T(8,128)(2,1)S(1)}, bf16[96,1536]{1,0:T(8,128)(2,1)S(1)}, u32[]{:S(2)}, u32[]{:S(2)}) collective-permute-start(bf16[96,1536]{1,0:T(8,128)(2,1)S(1)} %bitcast.12), channel_id=1, source_target_pairs={{0,4},{4,8},{8,12},{12,16},{16,20},{20,24},{24,28},{28,0},{1,5},{5... | collective-permute-start | bytes 884744 | tf_op jit(solution)/shard_map/ppermute | solution.py:38
  53.2 4.2 %collective-permute-start.4 = (bf16[96,1536]{1,0:T(8,128)(2,1)S(1)}, bf16[96,1536]{1,0:T(8,128)(2,1)S(1)}, u32[]{:S(2)}, u32[]{:S(2)}) collective-permute-start(bf16[96,1536]{1,0:T(8,128)(2,1)S(1)} %bitcast.13), channel_id=1, source_target_pairs={{0,28},{4,0},{8,4},{12,8},{16,12},{20,16},{24,20},{28,24},{1,29},{... | collective-permute-start | bytes 884744 | tf_op jit(solution)/shard_map/ppermute | solution.py:38
  57.4 3.4 %collective-permute-start.6 = (bf16[96,1536]{1,0:T(8,128)(2,1)S(1)}, bf16[96,1536]{1,0:T(8,128)(2,1)S(1)}, u32[]{:S(2)}, u32[]{:S(2)}) collective-permute-start(bf16[96,1536]{1,0:T(8,128)(2,1)S(1)} %collective-permute-done.2.refs_3_), channel_id=1, source_target_pairs={{0,28},{4,0},{8,4},{12,8},{16,12},{20,16},{24,20},{28,24},{1,29},{... | collective-permute-start | bytes 884744 | tf_op jit(solution)/shard_map/ppermute | solution.py:38
  63.7 2.3 %collective-permute-start.5 = (bf16[96,1536]{1,0:T(8,128)(2,1)S(1)}, bf16[96,1536]{1,0:T(8,128)(2,1)S(1)}, u32[]{:S(2)}, u32[]{:S(2)}) collective-permute-start(bf16[96,1536]{1,0:T(8,128)(2,1)S(1)} %collective-permute-done.refs_2_), channel_id=1, source_target_pairs={{0,4},{4,8},{8,12},{12,16},{16,20},{20,24},{24,28},{28,0},{1,5},{5... | collective-permute-start | bytes 884744 | tf_op jit(solution)/shard_map/ppermute | solution.py:38
  66.0 4.2 %collective-permute-start.8 = (bf16[96,1536]{1,0:T(8,128)(2,1)S(1)}, bf16[96,1536]{1,0:T(8,128)(2,1)S(1)}, u32[]{:S(2)}, u32[]{:S(2)}) collective-permute-start(bf16[96,1536]{1,0:T(8,128)(2,1)S(1)} %collective-permute-done.4.refs_5_), channel_id=1, source_target_pairs={{0,28},{4,0},{8,4},{12,8},{16,12},{20,16},{24,20},{28,24},{1,29},{... | collective-permute-start | bytes 884744 | tf_op jit(solution)/shard_map/ppermute | solution.py:38
  70.2 4.0 %collective-permute-start.10 = (bf16[96,1536]{1,0:T(8,128)(2,1)S(1)}, bf16[96,1536]{1,0:T(8,128)(2,1)S(1)}, u32[]{:S(2)}, u32[]{:S(2)}) collective-permute-start(bf16[96,1536]{1,0:T(8,128)(2,1)S(1)} %collective-permute-done.6.refs_7_), channel_id=1, source_target_pairs={{0,28},{4,0},{8,4},{12,8},{16,12},{20,16},{24,20},{28,24},{1,29},{... | collective-permute-start | bytes 884744 | tf_op jit(solution)/shard_map/ppermute | solution.py:38
  76.2 2.0 %collective-permute-done.5.refs_6_ = bf16[96,1536]{1,0:T(8,128)(2,1)S(1)} collective-permute-done((bf16[96,1536]{1,0:T(8,128)(2,1)S(1)}, bf16[96,1536]{1,0:T(8,128)(2,1)S(1)}, u32[]{:S(2)}, u32[]{:S(2)}) %collective-permute-start.5) | collective-permute-done | bytes 294944 | tf_op jit(solution)/shard_map/ppermute | solution.py:38
  80.1 4.6 %collective-permute-start.12 = (bf16[96,1536]{1,0:T(8,128)(2,1)S(1)}, bf16[96,1536]{1,0:T(8,128)(2,1)}, u32[]{:S(2)}, u32[]{:S(2)}) collective-permute-start(bf16[96,1536]{1,0:T(8,128)(2,1)S(1)} %collective-permute-done.8.refs_9_), channel_id=1, source_target_pairs={{0,28},{4,0},{8,4},{12,8},{16,12},{20,16},{24,20},{28,24},{1,29},{... | collective-permute-start | bytes 884744 | tf_op jit(solution)/shard_map/ppermute | solution.py:38
  84.7 1.9 %collective-permute-start.13 = (bf16[96,1536]{1,0:T(8,128)(2,1)S(1)}, bf16[96,1536]{1,0:T(8,128)(2,1)}, u32[]{:S(2)}, u32[]{:S(2)}) collective-permute-start(bf16[96,1536]{1,0:T(8,128)(2,1)S(1)} %collective-permute-done.10.refs_11_), channel_id=1, source_target_pairs={{0,28},{4,0},{8,4},{12,8},{16,12},{20,16},{24,20},{28,24},{1,29},{... | collective-permute-start | bytes 884744 | tf_op jit(solution)/shard_map/ppermute | solution.py:38
  86.7 3.4 %collective-permute-start.14 = (bf16[96,1536]{1,0:T(8,128)(2,1)S(1)}, bf16[96,1536]{1,0:T(8,128)(2,1)}, u32[]{:S(2)}, u32[]{:S(2)}) collective-permute-start(bf16[96,1536]{1,0:T(8,128)(2,1)S(1)} %collective-permute-done.11.refs_12_), channel_id=1, source_target_pairs={{0,4},{4,8},{8,12},{12,16},{16,20},{20,24},{24,28},{28,0},{1,5},{5... | collective-permute-start | bytes 884744 | tf_op jit(solution)/shard_map/ppermute | solution.py:38
  90.5 5.2 %collective-permute-done.13.refs_14_ = bf16[96,1536]{1,0:T(8,128)(2,1)} collective-permute-done((bf16[96,1536]{1,0:T(8,128)(2,1)S(1)}, bf16[96,1536]{1,0:T(8,128)(2,1)}, u32[]{:S(2)}, u32[]{:S(2)}) %collective-permute-start.13) | collective-permute-done | bytes 294944 | tf_op jit(solution)/shard_map/ppermute | solution.py:38
  96.1 9.2 %all-gather.2.cloned.1.call-done.refs_16_ = bf16[8,768,384]{2,1,0:T(8,128)(2,1)} async-done(((bf16[1,768,384]{2,1,0:T(8,128)(2,1)}), bf16[8,768,384]{2,1,0:T(8,128)(2,1)}) %all-gather.2.cloned.1.call-update) | async-done | bytes 4718608 | tf_op jit(solution)/shard_map/all_gather | solution.py:191
  105.4 12.5 %shard_map.39 = (bf16[384,1536]{1,0:T(8,128)(2,1)}, bf16[384,1536]{1,0:T(8,128)(2,1)}, bf16[384,1536]{1,0:T(8,128)(2,1)}, bf16[384,1536]{1,0:T(8,128)(2,1)}) custom-call(s32[2]{0:T(128)S(1)} %pad_add_fusion.place, bf16[96,1536]{1,0:T(8,128)(2,1)S(1)} %get-tuple-element.32.refs_0_, bf16[96,1536]{1,0:T(8,128)(2,1)S(1)} %bitcast.14, ...), custom_call_target="tpu_custom_call" | custom-call | flops 7247757312 | bytes 14155784 | tf_op jit(solution)/shard_map/pallas_call | solution.py:26
  117.9 2.6 %collective-permute-start.19 = (bf16[384,1536]{1,0:T(8,128)(2,1)}, bf16[384,1536]{1,0:T(8,128)(2,1)S(1)}, u32[]{:S(2)}, u32[]{:S(2)}) collective-permute-start(bf16[384,1536]{1,0:T(8,128)(2,1)} %get-tuple-element.47), channel_id=1, source_target_pairs={{0,1},{1,0},{2,3},{3,2},{4,5},{5,4},{6,7},{7,6},{8,9},{9,8},{10,11... | collective-permute-start | bytes 3538952 | tf_op jit(solution)/shard_map/ppermute | solution.py:46
  124.7 3.2 %collective-permute-start.20 = (bf16[384,384]{1,0:T(8,128)(2,1)S(1)}, bf16[384,384]{1,0:T(8,128)(2,1)S(1)}, u32[]{:S(2)}, u32[]{:S(2)}) collective-permute-start(bf16[384,384]{1,0:T(8,128)(2,1)S(1)} %get-tuple-element.49), channel_id=1, source_target_pairs={{0,32},{32,64},{64,96},{96,0},{1,33},{33,65},{65,97},{97,1},{2,34}... | collective-permute-start | bytes 884744 | tf_op jit(solution)/shard_map/ppermute | solution.py:42
  127.9 4.3 %collective-permute-start.21 = (bf16[384,384]{1,0:T(8,128)(2,1)S(1)}, bf16[384,384]{1,0:T(8,128)(2,1)S(1)}, u32[]{:S(2)}, u32[]{:S(2)}) collective-permute-start(bf16[384,384]{1,0:T(8,128)(2,1)S(1)} %get-tuple-element.50), channel_id=1, source_target_pairs={{0,64},{32,96},{64,0},{96,32},{1,65},{33,97},{65,1},{97,33},{2,66}... | collective-permute-start | bytes 884744 | tf_op jit(solution)/shard_map/ppermute | solution.py:42
  132.2 3.1 %collective-permute-start.22 = (bf16[384,384]{1,0:T(8,128)(2,1)S(1)}, bf16[384,384]{1,0:T(8,128)(2,1)S(1)}, u32[]{:S(2)}, u32[]{:S(2)}) collective-permute-start(bf16[384,384]{1,0:T(8,128)(2,1)S(1)} %get-tuple-element.51), channel_id=1, source_target_pairs={{0,96},{32,0},{64,32},{96,64},{1,97},{33,1},{65,33},{97,65},{2,98}... | collective-permute-start | bytes 884744 | tf_op jit(solution)/shard_map/ppermute | solution.py:42
  135.7 2.2 %collective-permute-start.16 = (bf16[384,384]{1,0:T(8,128)(2,1)S(1)}, bf16[384,384]{1,0:T(8,128)(2,1)S(1)}, u32[]{:S(2)}, u32[]{:S(2)}) collective-permute-start(bf16[384,384]{1,0:T(8,128)(2,1)S(1)} %get-tuple-element.42), channel_id=1, source_target_pairs={{0,32},{32,64},{64,96},{96,0},{1,33},{33,65},{65,97},{97,1},{2,34}... | collective-permute-start | bytes 884744 | tf_op jit(solution)/shard_map/ppermute | solution.py:42
  137.9 2.8 %collective-permute-start.17 = (bf16[384,384]{1,0:T(8,128)(2,1)S(1)}, bf16[384,384]{1,0:T(8,128)(2,1)S(1)}, u32[]{:S(2)}, u32[]{:S(2)}) collective-permute-start(bf16[384,384]{1,0:T(8,128)(2,1)S(1)} %get-tuple-element.43), channel_id=1, source_target_pairs={{0,64},{32,96},{64,0},{96,32},{1,65},{33,97},{65,1},{97,33},{2,66}... | collective-permute-start | bytes 884744 | tf_op jit(solution)/shard_map/ppermute | solution.py:42
  140.7 3.4 %collective-permute-start.18 = (bf16[384,384]{1,0:T(8,128)(2,1)S(1)}, bf16[384,384]{1,0:T(8,128)(2,1)S(1)}, u32[]{:S(2)}, u32[]{:S(2)}) collective-permute-start(bf16[384,384]{1,0:T(8,128)(2,1)S(1)} %get-tuple-element.44), channel_id=1, source_target_pairs={{0,96},{32,0},{64,32},{96,64},{1,97},{33,1},{65,33},{97,65},{2,98}... | collective-permute-start | bytes 884744 | tf_op jit(solution)/shard_map/ppermute | solution.py:42
  145.5 5.8 %collective-permute-start.23 = (f32[1,384]{1,0:T(1,128)S(1)}, f32[1,384]{1,0:T(1,128)S(1)}, u32[]{:S(2)}, u32[]{:S(2)}) collective-permute-start(f32[1,384]{1,0:T(1,128)S(1)} %get-tuple-element.52), channel_id=1, source_target_pairs={{0,2},{2,0},{1,3},{3,1},{4,6},{6,4},{5,7},{7,5},{8,10},{10,8},{9,1... | collective-permute-start | bytes 4616 | tf_op jit(solution)/shard_map/ppermute | solution.py:46
  151.3 2.4 %collective-permute-done.23 = f32[1,384]{1,0:T(1,128)S(1)} collective-permute-done((f32[1,384]{1,0:T(1,128)S(1)}, f32[1,384]{1,0:T(1,128)S(1)}, u32[]{:S(2)}, u32[]{:S(2)}) %collective-permute-start.23) | collective-permute-done | bytes 1568 | tf_op jit(solution)/shard_map/ppermute | solution.py:46
  153.7 5.8 %collective-permute-start.24 = (bf16[384,384]{1,0:T(8,128)(2,1)S(1)}, bf16[384,384]{1,0:T(8,128)(2,1)S(1)}, u32[]{:S(2)}, u32[]{:S(2)}) collective-permute-start(bf16[384,384]{1,0:T(8,128)(2,1)S(1)} %get-tuple-element.54), channel_id=1, source_target_pairs={{0,2},{2,0},{1,3},{3,1},{4,6},{6,4},{5,7},{7,5},{8,10},{10,8},{9,1... | collective-permute-start | bytes 884744 | tf_op jit(solution)/shard_map/ppermute | solution.py:46
  160.5 7.0 %all-to-all-start.2 = ((f32[16,1,384]{2,1,0:T(1,128)}), f32[16,1,384]{2,1,0:T(1,128)S(1)}, u32[]{:S(2)}, u32[]{:S(2)}) async-start(f32[16,1,384]{2,1,0:T(1,128)} %broadcast_in_dim.12), calls=%async_computation.2 | async-start | bytes 49152 | tf_op jit(solution)/shard_map/all_to_all | solution.py:228
  167.6 10.5 %all-to-all-done.2.sums = f32[16,1,384]{2,1,0:T(1,128)S(1)} async-done(((f32[16,1,384]{2,1,0:T(1,128)}), f32[16,1,384]{2,1,0:T(1,128)S(1)}, u32[]{:S(2)}, u32[]{:S(2)}) %all-to-all-start.2) | async-done | bytes 24608 | tf_op jit(solution)/shard_map/all_to_all | solution.py:228
  (50 shorter events, 22.3 us)
Async XLA Ops:
  7.4 1.3 copy-start.2
  10.5 23.8 %all-to-all-start = ((bf16[8,3,48,384]{3,2,1,0:T(8,128)(2,1)}), bf16[8,3,48,384]{3,2,1,0:T(8,128)(2,1)S(1)}, u32[]{:S(2)}, u32[]{:S(2)}) async-start(bf16[8,3,48,384]{3,2,1,0:T(8,128)(2,1)} %get-tuple-element.31), calls=%async_computation | async-start | bytes 1769472 | tf_op jit(solution)/shard_map/all_to_all | solution.py:50
  20.8 84.6 %all-gather.2.cloned.1.call-start = ((), (), s32[]{:S(2)}) async-start(), calls=%async_computation.3 | async-start | bytes 5308416 | tf_op jit(solution)/shard_map/all_gather | solution.py:191
  20.8 15.4 %collective-permute-start.1 = (bf16[384,384]{1,0:T(8,128)(2,1)S(1)}, bf16[384,384]{1,0:T(8,128)(2,1)}, u32[]{:S(2)}, u32[]{:S(2)}) collective-permute-start(bf16[384,384]{1,0:T(8,128)(2,1)S(1)} %get-tuple-element.34), channel_id=1, source_target_pairs={{0,2},{2,0},{1,3},{3,1},{4,6},{6,4},{5,7},{7,5},{8,10},{10,8},{9,1... | collective-permute-start | bytes 884744 | tf_op jit(solution)/shard_map/ppermute | solution.py:46
  36.3 14.3 %collective-permute-start = (bf16[96,1536]{1,0:T(8,128)(2,1)S(1)}, bf16[96,1536]{1,0:T(8,128)(2,1)S(1)}, u32[]{:S(2)}, u32[]{:S(2)}) collective-permute-start(bf16[96,1536]{1,0:T(8,128)(2,1)S(1)} %get-tuple-element.32.refs_0_), channel_id=1, source_target_pairs={{0,4},{4,8},{8,12},{12,16},{16,20},{20,24},{24,28},{28,0},{1,5},{5... | collective-permute-start | bytes 884744 | tf_op jit(solution)/shard_map/ppermute | solution.py:38
  38.2 12.3 %all-to-all-start.1 = ((bf16[8,48,384]{2,1,0:T(8,128)(2,1)}), bf16[8,48,384]{2,1,0:T(8,128)(2,1)S(1)}, u32[]{:S(2)}, u32[]{:S(2)}) async-start(bf16[8,48,384]{2,1,0:T(8,128)(2,1)} %bitcast.5), calls=%async_computation.1 | async-start | bytes 589824 | tf_op jit(solution)/shard_map/all_to_all | solution.py:50
  43.7 13.6 %collective-permute-start.2 = (bf16[96,1536]{1,0:T(8,128)(2,1)S(1)}, bf16[96,1536]{1,0:T(8,128)(2,1)S(1)}, u32[]{:S(2)}, u32[]{:S(2)}) collective-permute-start(bf16[96,1536]{1,0:T(8,128)(2,1)S(1)} %get-tuple-element.32.refs_0_), channel_id=1, source_target_pairs={{0,28},{4,0},{8,4},{12,8},{16,12},{20,16},{24,20},{28,24},{1,29},{... | collective-permute-start | bytes 884744 | tf_op jit(solution)/shard_map/ppermute | solution.py:38
  50.6 11.2 %collective-permute-start.3 = (bf16[96,1536]{1,0:T(8,128)(2,1)S(1)}, bf16[96,1536]{1,0:T(8,128)(2,1)S(1)}, u32[]{:S(2)}, u32[]{:S(2)}) collective-permute-start(bf16[96,1536]{1,0:T(8,128)(2,1)S(1)} %bitcast.12), channel_id=1, source_target_pairs={{0,4},{4,8},{8,12},{12,16},{16,20},{20,24},{24,28},{28,0},{1,5},{5... | collective-permute-start | bytes 884744 | tf_op jit(solution)/shard_map/ppermute | solution.py:38
  53.2 12.8 %collective-permute-start.4 = (bf16[96,1536]{1,0:T(8,128)(2,1)S(1)}, bf16[96,1536]{1,0:T(8,128)(2,1)S(1)}, u32[]{:S(2)}, u32[]{:S(2)}) collective-permute-start(bf16[96,1536]{1,0:T(8,128)(2,1)S(1)} %bitcast.13), channel_id=1, source_target_pairs={{0,28},{4,0},{8,4},{12,8},{16,12},{20,16},{24,20},{28,24},{1,29},{... | collective-permute-start | bytes 884744 | tf_op jit(solution)/shard_map/ppermute | solution.py:38
  57.4 12.9 %collective-permute-start.6 = (bf16[96,1536]{1,0:T(8,128)(2,1)S(1)}, bf16[96,1536]{1,0:T(8,128)(2,1)S(1)}, u32[]{:S(2)}, u32[]{:S(2)}) collective-permute-start(bf16[96,1536]{1,0:T(8,128)(2,1)S(1)} %collective-permute-done.2.refs_3_), channel_id=1, source_target_pairs={{0,28},{4,0},{8,4},{12,8},{16,12},{20,16},{24,20},{28,24},{1,29},{... | collective-permute-start | bytes 884744 | tf_op jit(solution)/shard_map/ppermute | solution.py:38
  61.8 12.5 %collective-permute-start.7 = (bf16[96,1536]{1,0:T(8,128)(2,1)S(1)}, bf16[96,1536]{1,0:T(8,128)(2,1)S(1)}, u32[]{:S(2)}, u32[]{:S(2)}) collective-permute-start(bf16[96,1536]{1,0:T(8,128)(2,1)S(1)} %collective-permute-done.3.refs_4_), channel_id=1, source_target_pairs={{0,4},{4,8},{8,12},{12,16},{16,20},{20,24},{24,28},{28,0},{1,5},{5... | collective-permute-start | bytes 884744 | tf_op jit(solution)/shard_map/ppermute | solution.py:38
  63.7 14.5 %collective-permute-start.5 = (bf16[96,1536]{1,0:T(8,128)(2,1)S(1)}, bf16[96,1536]{1,0:T(8,128)(2,1)S(1)}, u32[]{:S(2)}, u32[]{:S(2)}) collective-permute-start(bf16[96,1536]{1,0:T(8,128)(2,1)S(1)} %collective-permute-done.refs_2_), channel_id=1, source_target_pairs={{0,4},{4,8},{8,12},{12,16},{16,20},{20,24},{24,28},{28,0},{1,5},{5... | collective-permute-start | bytes 884744 | tf_op jit(solution)/shard_map/ppermute | solution.py:38
  66.0 14.1 %collective-permute-start.8 = (bf16[96,1536]{1,0:T(8,128)(2,1)S(1)}, bf16[96,1536]{1,0:T(8,128)(2,1)S(1)}, u32[]{:S(2)}, u32[]{:S(2)}) collective-permute-start(bf16[96,1536]{1,0:T(8,128)(2,1)S(1)} %collective-permute-done.4.refs_5_), channel_id=1, source_target_pairs={{0,28},{4,0},{8,4},{12,8},{16,12},{20,16},{24,20},{28,24},{1,29},{... | collective-permute-start | bytes 884744 | tf_op jit(solution)/shard_map/ppermute | solution.py:38
  70.2 14.5 %collective-permute-start.10 = (bf16[96,1536]{1,0:T(8,128)(2,1)S(1)}, bf16[96,1536]{1,0:T(8,128)(2,1)S(1)}, u32[]{:S(2)}, u32[]{:S(2)}) collective-permute-start(bf16[96,1536]{1,0:T(8,128)(2,1)S(1)} %collective-permute-done.6.refs_7_), channel_id=1, source_target_pairs={{0,28},{4,0},{8,4},{12,8},{16,12},{20,16},{24,20},{28,24},{1,29},{... | collective-permute-start | bytes 884744 | tf_op jit(solution)/shard_map/ppermute | solution.py:38
  74.3 12.4 %collective-permute-start.11 = (bf16[96,1536]{1,0:T(8,128)(2,1)S(1)}, bf16[96,1536]{1,0:T(8,128)(2,1)S(1)}, u32[]{:S(2)}, u32[]{:S(2)}) collective-permute-start(bf16[96,1536]{1,0:T(8,128)(2,1)S(1)} %collective-permute-done.7.refs_8_), channel_id=1, source_target_pairs={{0,4},{4,8},{8,12},{12,16},{16,20},{20,24},{24,28},{28,0},{1,5},{5... | collective-permute-start | bytes 884744 | tf_op jit(solution)/shard_map/ppermute | solution.py:38
  78.2 12.3 %collective-permute-start.9 = (bf16[96,1536]{1,0:T(8,128)(2,1)S(1)}, bf16[96,1536]{1,0:T(8,128)(2,1)}, u32[]{:S(2)}, u32[]{:S(2)}) collective-permute-start(bf16[96,1536]{1,0:T(8,128)(2,1)S(1)} %collective-permute-done.5.refs_6_), channel_id=1, source_target_pairs={{0,4},{4,8},{8,12},{12,16},{16,20},{20,24},{24,28},{28,0},{1,5},{5... | collective-permute-start | bytes 884744 | tf_op jit(solution)/shard_map/ppermute | solution.py:38
  80.1 10.3 %collective-permute-start.12 = (bf16[96,1536]{1,0:T(8,128)(2,1)S(1)}, bf16[96,1536]{1,0:T(8,128)(2,1)}, u32[]{:S(2)}, u32[]{:S(2)}) collective-permute-start(bf16[96,1536]{1,0:T(8,128)(2,1)S(1)} %collective-permute-done.8.refs_9_), channel_id=1, source_target_pairs={{0,28},{4,0},{8,4},{12,8},{16,12},{20,16},{24,20},{28,24},{1,29},{... | collective-permute-start | bytes 884744 | tf_op jit(solution)/shard_map/ppermute | solution.py:38
  84.7 10.9 %collective-permute-start.13 = (bf16[96,1536]{1,0:T(8,128)(2,1)S(1)}, bf16[96,1536]{1,0:T(8,128)(2,1)}, u32[]{:S(2)}, u32[]{:S(2)}) collective-permute-start(bf16[96,1536]{1,0:T(8,128)(2,1)S(1)} %collective-permute-done.10.refs_11_), channel_id=1, source_target_pairs={{0,28},{4,0},{8,4},{12,8},{16,12},{20,16},{24,20},{28,24},{1,29},{... | collective-permute-start | bytes 884744 | tf_op jit(solution)/shard_map/ppermute | solution.py:38
  86.7 9.5 %collective-permute-start.14 = (bf16[96,1536]{1,0:T(8,128)(2,1)S(1)}, bf16[96,1536]{1,0:T(8,128)(2,1)}, u32[]{:S(2)}, u32[]{:S(2)}) collective-permute-start(bf16[96,1536]{1,0:T(8,128)(2,1)S(1)} %collective-permute-done.11.refs_12_), channel_id=1, source_target_pairs={{0,4},{4,8},{8,12},{12,16},{16,20},{20,24},{24,28},{28,0},{1,5},{5... | collective-permute-start | bytes 884744 | tf_op jit(solution)/shard_map/ppermute | solution.py:38
  117.9 5.3 %collective-permute-start.19 = (bf16[384,1536]{1,0:T(8,128)(2,1)}, bf16[384,1536]{1,0:T(8,128)(2,1)S(1)}, u32[]{:S(2)}, u32[]{:S(2)}) collective-permute-start(bf16[384,1536]{1,0:T(8,128)(2,1)} %get-tuple-element.47), channel_id=1, source_target_pairs={{0,1},{1,0},{2,3},{3,2},{4,5},{5,4},{6,7},{7,6},{8,9},{9,8},{10,11... | collective-permute-start | bytes 3538952 | tf_op jit(solution)/shard_map/ppermute | solution.py:46
  120.5 14.9 %collective-permute-start.15 = (bf16[384,1536]{1,0:T(8,128)(2,1)}, bf16[384,1536]{1,0:T(8,128)(2,1)S(1)}, u32[]{:S(2)}, u32[]{:S(2)}) collective-permute-start(bf16[384,1536]{1,0:T(8,128)(2,1)} %get-tuple-element.40), channel_id=1, source_target_pairs={{0,1},{1,0},{2,3},{3,2},{4,5},{5,4},{6,7},{7,6},{8,9},{9,8},{10,11... | collective-permute-start | bytes 3538952 | tf_op jit(solution)/shard_map/ppermute | solution.py:46
  124.4 10.9 %copy-start = (bf16[384,1536]{1,0:T(8,128)(2,1)S(1)}, bf16[384,1536]{1,0:T(8,128)(2,1)}, u32[]{:S(2)}) copy-start(bf16[384,1536]{1,0:T(8,128)(2,1)} %get-tuple-element.39.ours) | copy-start | bytes 3538948
  124.7 16.0 %collective-permute-start.20 = (bf16[384,384]{1,0:T(8,128)(2,1)S(1)}, bf16[384,384]{1,0:T(8,128)(2,1)S(1)}, u32[]{:S(2)}, u32[]{:S(2)}) collective-permute-start(bf16[384,384]{1,0:T(8,128)(2,1)S(1)} %get-tuple-element.49), channel_id=1, source_target_pairs={{0,32},{32,64},{64,96},{96,0},{1,33},{33,65},{65,97},{97,1},{2,34}... | collective-permute-start | bytes 884744 | tf_op jit(solution)/shard_map/ppermute | solution.py:42
  127.9 16.2 %collective-permute-start.21 = (bf16[384,384]{1,0:T(8,128)(2,1)S(1)}, bf16[384,384]{1,0:T(8,128)(2,1)S(1)}, u32[]{:S(2)}, u32[]{:S(2)}) collective-permute-start(bf16[384,384]{1,0:T(8,128)(2,1)S(1)} %get-tuple-element.50), channel_id=1, source_target_pairs={{0,64},{32,96},{64,0},{96,32},{1,65},{33,97},{65,1},{97,33},{2,66}... | collective-permute-start | bytes 884744 | tf_op jit(solution)/shard_map/ppermute | solution.py:42
  132.2 12.9 %collective-permute-start.22 = (bf16[384,384]{1,0:T(8,128)(2,1)S(1)}, bf16[384,384]{1,0:T(8,128)(2,1)S(1)}, u32[]{:S(2)}, u32[]{:S(2)}) collective-permute-start(bf16[384,384]{1,0:T(8,128)(2,1)S(1)} %get-tuple-element.51), channel_id=1, source_target_pairs={{0,96},{32,0},{64,32},{96,64},{1,97},{33,1},{65,33},{97,65},{2,98}... | collective-permute-start | bytes 884744 | tf_op jit(solution)/shard_map/ppermute | solution.py:42
  135.7 23.9 %collective-permute-start.16 = (bf16[384,384]{1,0:T(8,128)(2,1)S(1)}, bf16[384,384]{1,0:T(8,128)(2,1)S(1)}, u32[]{:S(2)}, u32[]{:S(2)}) collective-permute-start(bf16[384,384]{1,0:T(8,128)(2,1)S(1)} %get-tuple-element.42), channel_id=1, source_target_pairs={{0,32},{32,64},{64,96},{96,0},{1,33},{33,65},{65,97},{97,1},{2,34}... | collective-permute-start | bytes 884744 | tf_op jit(solution)/shard_map/ppermute | solution.py:42
  137.9 21.7 %collective-permute-start.17 = (bf16[384,384]{1,0:T(8,128)(2,1)S(1)}, bf16[384,384]{1,0:T(8,128)(2,1)S(1)}, u32[]{:S(2)}, u32[]{:S(2)}) collective-permute-start(bf16[384,384]{1,0:T(8,128)(2,1)S(1)} %get-tuple-element.43), channel_id=1, source_target_pairs={{0,64},{32,96},{64,0},{96,32},{1,65},{33,97},{65,1},{97,33},{2,66}... | collective-permute-start | bytes 884744 | tf_op jit(solution)/shard_map/ppermute | solution.py:42
  140.7 18.8 %collective-permute-start.18 = (bf16[384,384]{1,0:T(8,128)(2,1)S(1)}, bf16[384,384]{1,0:T(8,128)(2,1)S(1)}, u32[]{:S(2)}, u32[]{:S(2)}) collective-permute-start(bf16[384,384]{1,0:T(8,128)(2,1)S(1)} %get-tuple-element.44), channel_id=1, source_target_pairs={{0,96},{32,0},{64,32},{96,64},{1,97},{33,1},{65,33},{97,65},{2,98}... | collective-permute-start | bytes 884744 | tf_op jit(solution)/shard_map/ppermute | solution.py:42
  145.2 22.3 %copy-start.3 = (s32[6,3]{0,1:T(4,128)S(1)}, s32[6,3]{0,1:T(4,128)}, u32[]{:S(2)}) copy-start(s32[6,3]{0,1:T(4,128)} %param.5) | copy-start | bytes 220
  145.5 8.2 %collective-permute-start.23 = (f32[1,384]{1,0:T(1,128)S(1)}, f32[1,384]{1,0:T(1,128)S(1)}, u32[]{:S(2)}, u32[]{:S(2)}) collective-permute-start(f32[1,384]{1,0:T(1,128)S(1)} %get-tuple-element.52), channel_id=1, source_target_pairs={{0,2},{2,0},{1,3},{3,1},{4,6},{6,4},{5,7},{7,5},{8,10},{10,8},{9,1... | collective-permute-start | bytes 4616 | tf_op jit(solution)/shard_map/ppermute | solution.py:46
  153.7 24.4 %collective-permute-start.24 = (bf16[384,384]{1,0:T(8,128)(2,1)S(1)}, bf16[384,384]{1,0:T(8,128)(2,1)S(1)}, u32[]{:S(2)}, u32[]{:S(2)}) collective-permute-start(bf16[384,384]{1,0:T(8,128)(2,1)S(1)} %get-tuple-element.54), channel_id=1, source_target_pairs={{0,2},{2,0},{1,3},{3,1},{4,6},{6,4},{5,7},{7,5},{8,10},{10,8},{9,1... | collective-permute-start | bytes 884744 | tf_op jit(solution)/shard_map/ppermute | solution.py:46
  160.5 17.6 %all-to-all-start.2 = ((f32[16,1,384]{2,1,0:T(1,128)}), f32[16,1,384]{2,1,0:T(1,128)S(1)}, u32[]{:S(2)}, u32[]{:S(2)}) async-start(f32[16,1,384]{2,1,0:T(1,128)} %broadcast_in_dim.12), calls=%async_computation.2 | async-start | bytes 49152 | tf_op jit(solution)/shard_map/all_to_all | solution.py:228
  (1 other events, 1.3 us)
Sparse Core Ops, SparseCore 0:
  36.4 68.9 all-gather.1

commit v13 on v12

--- a/solution.py
+++ b/solution.py
@@ -125,6 +125,14 @@
     turned = sum(piece[...].astype(F32) for piece in pieces).T
     total[...] = turned.astype(total.dtype)
     sums[...] = jnp.sum(turned * turned, axis=0, keepdims=True)
+
+
+def add_x_last(*refs):
+    pieces, earlier, total, sums = refs[:X], refs[X], refs[X + 1], refs[X + 2]
+    turned = sum(piece[...].astype(F32) for piece in pieces).T
+    total[...] = turned
+    both = jnp.sum(turned * turned, axis=0, keepdims=True) + earlier[...]
+    sums[...] = jnp.broadcast_to(both[None], sums.shape)
 
 
 def finish(place, keep, mine, other, sums, flows):
@@ -223,8 +231,12 @@
     other, sums = total(apart, BF16)
     sums, other = in_order(swap(sums, "zhi"), other)
     other = swap(other, "zhi")
-    mine, own_sums = total(apart_near, F32)
-    sums = jnp.broadcast_to(sums + own_sums, (Z_LO * X, 1, UNIT))
+    mine, sums = call(
+        add_x_last,
+        [((HALF, UNIT), F32), ((Z_LO * X, 1, UNIT), F32)],
+        [VMEM] * (X + 1),
+        (*apart_near, sums),
+    )
     sums = lax.all_to_all(sums, ("zlo", "x"), split_axis=0, concat_axis=0, tiled=True)
     return call(
         finish,

time: 188 us -> 188 us (level)
  transfers between devices with their start and end apart: 29 -> 29, of which waited for: 13 -> 13; matrix products, arithmetic and copies ran while one was open for 0% -> 0% of each run, Pallas kernels for 1% -> 2%
where the time goes in v13:
time: 188 us; the launch traced here: 187 us
  starting transfers between devices  107 us (57%)
  waiting for transfers between devices  42.7 us (23%)
  Pallas kernels  19.5 us (10%)
  between operations  13.8 us (7%)
  local copies, waits for them, and re-layouts  3.44 us (2%)
    ppermute x14, starting transfers between devices, shift_y(): return lax.ppermute(shard, 'y', [(i, (i + step) % Y) for i in range(Y)])  43 us
    ppermute x5, starting transfers between devices, swap(): return lax.ppermute(shard, axis, [(0, 1), (1, 0)])  22.3 us
    pallas_call x8, Pallas kernels, call(): pl.pallas_call(body, out_shape=shapes, in_specs=ins, out_specs=[VMEM] * l...  19.5 us
    ppermute x6, starting transfers between devices, shift_x(): return lax.ppermute(shard, 'x', [(i, (i + step) % X) for i in range(X)])  19 us
    all_to_all x2, starting transfers between devices, spread_over(): lax.all_to_all(array, ('x', 'core'), split_axis=0, concat_axis=0, tiled=T...  15.8 us
    all_to_all x1, waiting for transfers between devices, local(): lax.all_to_all(sums, ('zlo', 'x'), split_axis=0, concat_axis=0, tiled=True)  10.5 us
    all_to_all x2, waiting for transfers between devices, spread_over(): lax.all_to_all(array, ('x', 'core'), split_axis=0, concat_axis=0, tiled=T...  9.33 us
    all_gather x1, waiting for transfers between devices, local(): right = lax.all_gather(right, ('zhi', 'zlo'), axis=0, tiled=True)  9.25 us
  transfers between devices with their start and end apart: 29, of which 13 were waited for; matrix products, arithmetic and copies ran while one was open for 0% of the time, Pallas kernels for 2%

profile of v13, /device:TPU:1, one launch (start us, length us, event | category | flops | bytes accessed | tf_op | source)
XLA Modules:
  0.0 186.8 jit_solution(15476886872068780616)
XLA Ops:
  10.5 10.3 %all-to-all-start = ((bf16[8,3,48,384]{3,2,1,0:T(8,128)(2,1)}), bf16[8,3,48,384]{3,2,1,0:T(8,128)(2,1)S(1)}, u32[]{:S(2)}, u32[]{:S(2)}) async-start(bf16[8,3,48,384]{3,2,1,0:T(8,128)(2,1)} %get-tuple-element.31), calls=%async_computation | async-start | bytes 1769472 | tf_op jit(solution)/shard_map/all_to_all | solution.py:50
  20.8 6.1 %collective-permute-start.1 = (bf16[384,384]{1,0:T(8,128)(2,1)S(1)}, bf16[384,384]{1,0:T(8,128)(2,1)}, u32[]{:S(2)}, u32[]{:S(2)}) collective-permute-start(bf16[384,384]{1,0:T(8,128)(2,1)S(1)} %get-tuple-element.34), channel_id=1, source_target_pairs={{0,2},{2,0},{1,3},{3,1},{4,6},{6,4},{5,7},{7,5},{8,10},{10,8},{9,1... | collective-permute-start | bytes 884744 | tf_op jit(solution)/shard_map/ppermute | solution.py:46
  26.9 7.4 %all-to-all-done = bf16[8,3,48,384]{3,2,1,0:T(8,128)(2,1)S(1)} async-done(((bf16[8,3,48,384]{3,2,1,0:T(8,128)(2,1)}), bf16[8,3,48,384]{3,2,1,0:T(8,128)(2,1)S(1)}, u32[]{:S(2)}, u32[]{:S(2)}) %all-to-all-start) | async-done | bytes 884768 | tf_op jit(solution)/shard_map/all_to_all | solution.py:50
  36.3 1.9 %collective-permute-start = (bf16[96,1536]{1,0:T(8,128)(2,1)S(1)}, bf16[96,1536]{1,0:T(8,128)(2,1)S(1)}, u32[]{:S(2)}, u32[]{:S(2)}) collective-permute-start(bf16[96,1536]{1,0:T(8,128)(2,1)S(1)} %get-tuple-element.32.refs_0_), channel_id=1, source_target_pairs={{0,4},{4,8},{8,12},{12,16},{16,20},{20,24},{24,28},{28,0},{1,5},{5... | collective-permute-start | bytes 884744 | tf_op jit(solution)/shard_map/ppermute | solution.py:38
  38.2 5.5 %all-to-all-start.1 = ((bf16[8,48,384]{2,1,0:T(8,128)(2,1)}), bf16[8,48,384]{2,1,0:T(8,128)(2,1)S(1)}, u32[]{:S(2)}, u32[]{:S(2)}) async-start(bf16[8,48,384]{2,1,0:T(8,128)(2,1)} %bitcast.5), calls=%async_computation.1 | async-start | bytes 589824 | tf_op jit(solution)/shard_map/all_to_all | solution.py:50
  43.7 4.8 %collective-permute-start.2 = (bf16[96,1536]{1,0:T(8,128)(2,1)S(1)}, bf16[96,1536]{1,0:T(8,128)(2,1)S(1)}, u32[]{:S(2)}, u32[]{:S(2)}) collective-permute-start(bf16[96,1536]{1,0:T(8,128)(2,1)S(1)} %get-tuple-element.32.refs_0_), channel_id=1, source_target_pairs={{0,28},{4,0},{8,4},{12,8},{16,12},{20,16},{24,20},{28,24},{1,29},{... | collective-permute-start | bytes 884744 | tf_op jit(solution)/shard_map/ppermute | solution.py:38
  48.6 2.0 %all-to-all-done.1 = bf16[8,48,384]{2,1,0:T(8,128)(2,1)S(1)} async-done(((bf16[8,48,384]{2,1,0:T(8,128)(2,1)}), bf16[8,48,384]{2,1,0:T(8,128)(2,1)S(1)}, u32[]{:S(2)}, u32[]{:S(2)}) %all-to-all-start.1) | async-done | bytes 294944 | tf_op jit(solution)/shard_map/all_to_all | solution.py:50
  50.6 2.6 %collective-permute-start.3 = (bf16[96,1536]{1,0:T(8,128)(2,1)S(1)}, bf16[96,1536]{1,0:T(8,128)(2,1)S(1)}, u32[]{:S(2)}, u32[]{:S(2)}) collective-permute-start(bf16[96,1536]{1,0:T(8,128)(2,1)S(1)} %bitcast.12), channel_id=1, source_target_pairs={{0,4},{4,8},{8,12},{12,16},{16,20},{20,24},{24,28},{28,0},{1,5},{5... | collective-permute-start | bytes 884744 | tf_op jit(solution)/shard_map/ppermute | solution.py:38
  53.2 4.2 %collective-permute-start.4 = (bf16[96,1536]{1,0:T(8,128)(2,1)S(1)}, bf16[96,1536]{1,0:T(8,128)(2,1)S(1)}, u32[]{:S(2)}, u32[]{:S(2)}) collective-permute-start(bf16[96,1536]{1,0:T(8,128)(2,1)S(1)} %bitcast.13), channel_id=1, source_target_pairs={{0,28},{4,0},{8,4},{12,8},{16,12},{20,16},{24,20},{28,24},{1,29},{... | collective-permute-start | bytes 884744 | tf_op jit(solution)/shard_map/ppermute | solution.py:38
  57.4 3.4 %collective-permute-start.6 = (bf16[96,1536]{1,0:T(8,128)(2,1)S(1)}, bf16[96,1536]{1,0:T(8,128)(2,1)S(1)}, u32[]{:S(2)}, u32[]{:S(2)}) collective-permute-start(bf16[96,1536]{1,0:T(8,128)(2,1)S(1)} %collective-permute-done.2.refs_3_), channel_id=1, source_target_pairs={{0,28},{4,0},{8,4},{12,8},{16,12},{20,16},{24,20},{28,24},{1,29},{... | collective-permute-start | bytes 884744 | tf_op jit(solution)/shard_map/ppermute | solution.py:38
  63.7 2.3 %collective-permute-start.5 = (bf16[96,1536]{1,0:T(8,128)(2,1)S(1)}, bf16[96,1536]{1,0:T(8,128)(2,1)S(1)}, u32[]{:S(2)}, u32[]{:S(2)}) collective-permute-start(bf16[96,1536]{1,0:T(8,128)(2,1)S(1)} %collective-permute-done.refs_2_), channel_id=1, source_target_pairs={{0,4},{4,8},{8,12},{12,16},{16,20},{20,24},{24,28},{28,0},{1,5},{5... | collective-permute-start | bytes 884744 | tf_op jit(solution)/shard_map/ppermute | solution.py:38
  66.0 4.2 %collective-permute-start.8 = (bf16[96,1536]{1,0:T(8,128)(2,1)S(1)}, bf16[96,1536]{1,0:T(8,128)(2,1)S(1)}, u32[]{:S(2)}, u32[]{:S(2)}) collective-permute-start(bf16[96,1536]{1,0:T(8,128)(2,1)S(1)} %collective-permute-done.4.refs_5_), channel_id=1, source_target_pairs={{0,28},{4,0},{8,4},{12,8},{16,12},{20,16},{24,20},{28,24},{1,29},{... | collective-permute-start | bytes 884744 | tf_op jit(solution)/shard_map/ppermute | solution.py:38
  70.2 4.0 %collective-permute-start.10 = (bf16[96,1536]{1,0:T(8,128)(2,1)S(1)}, bf16[96,1536]{1,0:T(8,128)(2,1)S(1)}, u32[]{:S(2)}, u32[]{:S(2)}) collective-permute-start(bf16[96,1536]{1,0:T(8,128)(2,1)S(1)} %collective-permute-done.6.refs_7_), channel_id=1, source_target_pairs={{0,28},{4,0},{8,4},{12,8},{16,12},{20,16},{24,20},{28,24},{1,29},{... | collective-permute-start | bytes 884744 | tf_op jit(solution)/shard_map/ppermute | solution.py:38
  76.2 2.0 %collective-permute-done.5.refs_6_ = bf16[96,1536]{1,0:T(8,128)(2,1)S(1)} collective-permute-done((bf16[96,1536]{1,0:T(8,128)(2,1)S(1)}, bf16[96,1536]{1,0:T(8,128)(2,1)S(1)}, u32[]{:S(2)}, u32[]{:S(2)}) %collective-permute-start.5) | collective-permute-done | bytes 294944 | tf_op jit(solution)/shard_map/ppermute | solution.py:38
  80.1 4.6 %collective-permute-start.12 = (bf16[96,1536]{1,0:T(8,128)(2,1)S(1)}, bf16[96,1536]{1,0:T(8,128)(2,1)}, u32[]{:S(2)}, u32[]{:S(2)}) collective-permute-start(bf16[96,1536]{1,0:T(8,128)(2,1)S(1)} %collective-permute-done.8.refs_9_), channel_id=1, source_target_pairs={{0,28},{4,0},{8,4},{12,8},{16,12},{20,16},{24,20},{28,24},{1,29},{... | collective-permute-start | bytes 884744 | tf_op jit(solution)/shard_map/ppermute | solution.py:38
  84.7 1.9 %collective-permute-start.13 = (bf16[96,1536]{1,0:T(8,128)(2,1)S(1)}, bf16[96,1536]{1,0:T(8,128)(2,1)}, u32[]{:S(2)}, u32[]{:S(2)}) collective-permute-start(bf16[96,1536]{1,0:T(8,128)(2,1)S(1)} %collective-permute-done.10.refs_11_), channel_id=1, source_target_pairs={{0,28},{4,0},{8,4},{12,8},{16,12},{20,16},{24,20},{28,24},{1,29},{... | collective-permute-start | bytes 884744 | tf_op jit(solution)/shard_map/ppermute | solution.py:38
  86.7 3.4 %collective-permute-start.14 = (bf16[96,1536]{1,0:T(8,128)(2,1)S(1)}, bf16[96,1536]{1,0:T(8,128)(2,1)}, u32[]{:S(2)}, u32[]{:S(2)}) collective-permute-start(bf16[96,1536]{1,0:T(8,128)(2,1)S(1)} %collective-permute-done.11.refs_12_), channel_id=1, source_target_pairs={{0,4},{4,8},{8,12},{12,16},{16,20},{20,24},{24,28},{28,0},{1,5},{5... | collective-permute-start | bytes 884744 | tf_op jit(solution)/shard_map/ppermute | solution.py:38
  90.5 5.2 %collective-permute-done.13.refs_14_ = bf16[96,1536]{1,0:T(8,128)(2,1)} collective-permute-done((bf16[96,1536]{1,0:T(8,128)(2,1)S(1)}, bf16[96,1536]{1,0:T(8,128)(2,1)}, u32[]{:S(2)}, u32[]{:S(2)}) %collective-permute-start.13) | collective-permute-done | bytes 294944 | tf_op jit(solution)/shard_map/ppermute | solution.py:38
  96.1 9.2 %all-gather.2.cloned.1.call-done.refs_16_ = bf16[8,768,384]{2,1,0:T(8,128)(2,1)} async-done(((bf16[1,768,384]{2,1,0:T(8,128)(2,1)}), bf16[8,768,384]{2,1,0:T(8,128)(2,1)}) %all-gather.2.cloned.1.call-update) | async-done | bytes 4718608 | tf_op jit(solution)/shard_map/all_gather | solution.py:199
  105.4 12.5 %shard_map.39 = (bf16[384,1536]{1,0:T(8,128)(2,1)}, bf16[384,1536]{1,0:T(8,128)(2,1)}, bf16[384,1536]{1,0:T(8,128)(2,1)}, bf16[384,1536]{1,0:T(8,128)(2,1)}) custom-call(s32[2]{0:T(128)S(1)} %pad_add_fusion.place, bf16[96,1536]{1,0:T(8,128)(2,1)S(1)} %get-tuple-element.32.refs_0_, bf16[96,1536]{1,0:T(8,128)(2,1)S(1)} %bitcast.14, ...), custom_call_target="tpu_custom_call" | custom-call | flops 7247757312 | bytes 14155784 | tf_op jit(solution)/shard_map/pallas_call | solution.py:26
  117.9 2.6 %collective-permute-start.19 = (bf16[384,1536]{1,0:T(8,128)(2,1)}, bf16[384,1536]{1,0:T(8,128)(2,1)S(1)}, u32[]{:S(2)}, u32[]{:S(2)}) collective-permute-start(bf16[384,1536]{1,0:T(8,128)(2,1)} %get-tuple-element.46), channel_id=1, source_target_pairs={{0,1},{1,0},{2,3},{3,2},{4,5},{5,4},{6,7},{7,6},{8,9},{9,8},{10,11... | collective-permute-start | bytes 3538952 | tf_op jit(solution)/shard_map/ppermute | solution.py:46
  124.7 3.2 %collective-permute-start.20 = (bf16[384,384]{1,0:T(8,128)(2,1)S(1)}, bf16[384,384]{1,0:T(8,128)(2,1)S(1)}, u32[]{:S(2)}, u32[]{:S(2)}) collective-permute-start(bf16[384,384]{1,0:T(8,128)(2,1)S(1)} %get-tuple-element.48), channel_id=1, source_target_pairs={{0,32},{32,64},{64,96},{96,0},{1,33},{33,65},{65,97},{97,1},{2,34}... | collective-permute-start | bytes 884744 | tf_op jit(solution)/shard_map/ppermute | solution.py:42
  127.9 4.3 %collective-permute-start.21 = (bf16[384,384]{1,0:T(8,128)(2,1)S(1)}, bf16[384,384]{1,0:T(8,128)(2,1)S(1)}, u32[]{:S(2)}, u32[]{:S(2)}) collective-permute-start(bf16[384,384]{1,0:T(8,128)(2,1)S(1)} %get-tuple-element.49), channel_id=1, source_target_pairs={{0,64},{32,96},{64,0},{96,32},{1,65},{33,97},{65,1},{97,33},{2,66}... | collective-permute-start | bytes 884744 | tf_op jit(solution)/shard_map/ppermute | solution.py:42
  132.3 3.1 %collective-permute-start.22 = (bf16[384,384]{1,0:T(8,128)(2,1)S(1)}, bf16[384,384]{1,0:T(8,128)(2,1)S(1)}, u32[]{:S(2)}, u32[]{:S(2)}) collective-permute-start(bf16[384,384]{1,0:T(8,128)(2,1)S(1)} %get-tuple-element.50), channel_id=1, source_target_pairs={{0,96},{32,0},{64,32},{96,64},{1,97},{33,1},{65,33},{97,65},{2,98}... | collective-permute-start | bytes 884744 | tf_op jit(solution)/shard_map/ppermute | solution.py:42
  135.7 2.2 %collective-permute-start.16 = (bf16[384,384]{1,0:T(8,128)(2,1)S(1)}, bf16[384,384]{1,0:T(8,128)(2,1)S(1)}, u32[]{:S(2)}, u32[]{:S(2)}) collective-permute-start(bf16[384,384]{1,0:T(8,128)(2,1)S(1)} %get-tuple-element.42), channel_id=1, source_target_pairs={{0,32},{32,64},{64,96},{96,0},{1,33},{33,65},{65,97},{97,1},{2,34}... | collective-permute-start | bytes 884744 | tf_op jit(solution)/shard_map/ppermute | solution.py:42
  137.9 2.8 %collective-permute-start.17 = (bf16[384,384]{1,0:T(8,128)(2,1)S(1)}, bf16[384,384]{1,0:T(8,128)(2,1)S(1)}, u32[]{:S(2)}, u32[]{:S(2)}) collective-permute-start(bf16[384,384]{1,0:T(8,128)(2,1)S(1)} %get-tuple-element.43), channel_id=1, source_target_pairs={{0,64},{32,96},{64,0},{96,32},{1,65},{33,97},{65,1},{97,33},{2,66}... | collective-permute-start | bytes 884744 | tf_op jit(solution)/shard_map/ppermute | solution.py:42
  140.7 3.4 %collective-permute-start.18 = (bf16[384,384]{1,0:T(8,128)(2,1)S(1)}, bf16[384,384]{1,0:T(8,128)(2,1)S(1)}, u32[]{:S(2)}, u32[]{:S(2)}) collective-permute-start(bf16[384,384]{1,0:T(8,128)(2,1)S(1)} %get-tuple-element.44), channel_id=1, source_target_pairs={{0,96},{32,0},{64,32},{96,64},{1,97},{33,1},{65,33},{97,65},{2,98}... | collective-permute-start | bytes 884744 | tf_op jit(solution)/shard_map/ppermute | solution.py:42
  145.5 5.8 %collective-permute-start.23 = (f32[1,384]{1,0:T(1,128)S(1)}, f32[1,384]{1,0:T(1,128)S(1)}, u32[]{:S(2)}, u32[]{:S(2)}) collective-permute-start(f32[1,384]{1,0:T(1,128)S(1)} %get-tuple-element.51), channel_id=1, source_target_pairs={{0,2},{2,0},{1,3},{3,1},{4,6},{6,4},{5,7},{7,5},{8,10},{10,8},{9,1... | collective-permute-start | bytes 4616 | tf_op jit(solution)/shard_map/ppermute | solution.py:46
  151.3 2.4 %collective-permute-done.23.refs_4_ = f32[1,384]{1,0:T(1,128)S(1)} collective-permute-done((f32[1,384]{1,0:T(1,128)S(1)}, f32[1,384]{1,0:T(1,128)S(1)}, u32[]{:S(2)}, u32[]{:S(2)}) %collective-permute-start.23) | collective-permute-done | bytes 1568 | tf_op jit(solution)/shard_map/ppermute | solution.py:46
  153.7 5.8 %collective-permute-start.24 = (bf16[384,384]{1,0:T(8,128)(2,1)S(1)}, bf16[384,384]{1,0:T(8,128)(2,1)S(1)}, u32[]{:S(2)}, u32[]{:S(2)}) collective-permute-start(bf16[384,384]{1,0:T(8,128)(2,1)S(1)} %get-tuple-element.55), channel_id=1, source_target_pairs={{0,2},{2,0},{1,3},{3,1},{4,6},{6,4},{5,7},{7,5},{8,10},{10,8},{9,1... | collective-permute-start | bytes 884744 | tf_op jit(solution)/shard_map/ppermute | solution.py:46
  160.4 7.0 %all-to-all-start.2 = ((f32[16,1,384]{2,1,0:T(1,128)}), f32[16,1,384]{2,1,0:T(1,128)S(1)}, u32[]{:S(2)}, u32[]{:S(2)}) async-start(f32[16,1,384]{2,1,0:T(1,128)} %get-tuple-element.56), calls=%async_computation.2 | async-start | bytes 49152 | tf_op jit(solution)/shard_map/all_to_all | solution.py:240
  167.6 10.5 %all-to-all-done.2.sums = f32[16,1,384]{2,1,0:T(1,128)S(1)} async-done(((f32[16,1,384]{2,1,0:T(1,128)}), f32[16,1,384]{2,1,0:T(1,128)S(1)}, u32[]{:S(2)}, u32[]{:S(2)}) %all-to-all-start.2) | async-done | bytes 24608 | tf_op jit(solution)/shard_map/all_to_all | solution.py:240
  (48 shorter events, 22.3 us)
Async XLA Ops:
  7.4 1.3 copy-start.2
  10.5 23.8 %all-to-all-start = ((bf16[8,3,48,384]{3,2,1,0:T(8,128)(2,1)}), bf16[8,3,48,384]{3,2,1,0:T(8,128)(2,1)S(1)}, u32[]{:S(2)}, u32[]{:S(2)}) async-start(bf16[8,3,48,384]{3,2,1,0:T(8,128)(2,1)} %get-tuple-element.31), calls=%async_computation | async-start | bytes 1769472 | tf_op jit(solution)/shard_map/all_to_all | solution.py:50
  20.8 84.6 %all-gather.2.cloned.1.call-start = ((), (), s32[]{:S(2)}) async-start(), calls=%async_computation.3 | async-start | bytes 5308416 | tf_op jit(solution)/shard_map/all_gather | solution.py:199
  20.8 15.4 %collective-permute-start.1 = (bf16[384,384]{1,0:T(8,128)(2,1)S(1)}, bf16[384,384]{1,0:T(8,128)(2,1)}, u32[]{:S(2)}, u32[]{:S(2)}) collective-permute-start(bf16[384,384]{1,0:T(8,128)(2,1)S(1)} %get-tuple-element.34), channel_id=1, source_target_pairs={{0,2},{2,0},{1,3},{3,1},{4,6},{6,4},{5,7},{7,5},{8,10},{10,8},{9,1... | collective-permute-start | bytes 884744 | tf_op jit(solution)/shard_map/ppermute | solution.py:46
  36.3 14.3 %collective-permute-start = (bf16[96,1536]{1,0:T(8,128)(2,1)S(1)}, bf16[96,1536]{1,0:T(8,128)(2,1)S(1)}, u32[]{:S(2)}, u32[]{:S(2)}) collective-permute-start(bf16[96,1536]{1,0:T(8,128)(2,1)S(1)} %get-tuple-element.32.refs_0_), channel_id=1, source_target_pairs={{0,4},{4,8},{8,12},{12,16},{16,20},{20,24},{24,28},{28,0},{1,5},{5... | collective-permute-start | bytes 884744 | tf_op jit(solution)/shard_map/ppermute | solution.py:38
  38.2 12.3 %all-to-all-start.1 = ((bf16[8,48,384]{2,1,0:T(8,128)(2,1)}), bf16[8,48,384]{2,1,0:T(8,128)(2,1)S(1)}, u32[]{:S(2)}, u32[]{:S(2)}) async-start(bf16[8,48,384]{2,1,0:T(8,128)(2,1)} %bitcast.5), calls=%async_computation.1 | async-start | bytes 589824 | tf_op jit(solution)/shard_map/all_to_all | solution.py:50
  43.7 13.6 %collective-permute-start.2 = (bf16[96,1536]{1,0:T(8,128)(2,1)S(1)}, bf16[96,1536]{1,0:T(8,128)(2,1)S(1)}, u32[]{:S(2)}, u32[]{:S(2)}) collective-permute-start(bf16[96,1536]{1,0:T(8,128)(2,1)S(1)} %get-tuple-element.32.refs_0_), channel_id=1, source_target_pairs={{0,28},{4,0},{8,4},{12,8},{16,12},{20,16},{24,20},{28,24},{1,29},{... | collective-permute-start | bytes 884744 | tf_op jit(solution)/shard_map/ppermute | solution.py:38
  50.6 11.2 %collective-permute-start.3 = (bf16[96,1536]{1,0:T(8,128)(2,1)S(1)}, bf16[96,1536]{1,0:T(8,128)(2,1)S(1)}, u32[]{:S(2)}, u32[]{:S(2)}) collective-permute-start(bf16[96,1536]{1,0:T(8,128)(2,1)S(1)} %bitcast.12), channel_id=1, source_target_pairs={{0,4},{4,8},{8,12},{12,16},{16,20},{20,24},{24,28},{28,0},{1,5},{5... | collective-permute-start | bytes 884744 | tf_op jit(solution)/shard_map/ppermute | solution.py:38
  53.2 12.8 %collective-permute-start.4 = (bf16[96,1536]{1,0:T(8,128)(2,1)S(1)}, bf16[96,1536]{1,0:T(8,128)(2,1)S(1)}, u32[]{:S(2)}, u32[]{:S(2)}) collective-permute-start(bf16[96,1536]{1,0:T(8,128)(2,1)S(1)} %bitcast.13), channel_id=1, source_target_pairs={{0,28},{4,0},{8,4},{12,8},{16,12},{20,16},{24,20},{28,24},{1,29},{... | collective-permute-start | bytes 884744 | tf_op jit(solution)/shard_map/ppermute | solution.py:38
  57.4 12.9 %collective-permute-start.6 = (bf16[96,1536]{1,0:T(8,128)(2,1)S(1)}, bf16[96,1536]{1,0:T(8,128)(2,1)S(1)}, u32[]{:S(2)}, u32[]{:S(2)}) collective-permute-start(bf16[96,1536]{1,0:T(8,128)(2,1)S(1)} %collective-permute-done.2.refs_3_), channel_id=1, source_target_pairs={{0,28},{4,0},{8,4},{12,8},{16,12},{20,16},{24,20},{28,24},{1,29},{... | collective-permute-start | bytes 884744 | tf_op jit(solution)/shard_map/ppermute | solution.py:38
  61.8 12.5 %collective-permute-start.7 = (bf16[96,1536]{1,0:T(8,128)(2,1)S(1)}, bf16[96,1536]{1,0:T(8,128)(2,1)S(1)}, u32[]{:S(2)}, u32[]{:S(2)}) collective-permute-start(bf16[96,1536]{1,0:T(8,128)(2,1)S(1)} %collective-permute-done.3.refs_4_), channel_id=1, source_target_pairs={{0,4},{4,8},{8,12},{12,16},{16,20},{20,24},{24,28},{28,0},{1,5},{5... | collective-permute-start | bytes 884744 | tf_op jit(solution)/shard_map/ppermute | solution.py:38
  63.7 14.5 %collective-permute-start.5 = (bf16[96,1536]{1,0:T(8,128)(2,1)S(1)}, bf16[96,1536]{1,0:T(8,128)(2,1)S(1)}, u32[]{:S(2)}, u32[]{:S(2)}) collective-permute-start(bf16[96,1536]{1,0:T(8,128)(2,1)S(1)} %collective-permute-done.refs_2_), channel_id=1, source_target_pairs={{0,4},{4,8},{8,12},{12,16},{16,20},{20,24},{24,28},{28,0},{1,5},{5... | collective-permute-start | bytes 884744 | tf_op jit(solution)/shard_map/ppermute | solution.py:38
  66.0 14.1 %collective-permute-start.8 = (bf16[96,1536]{1,0:T(8,128)(2,1)S(1)}, bf16[96,1536]{1,0:T(8,128)(2,1)S(1)}, u32[]{:S(2)}, u32[]{:S(2)}) collective-permute-start(bf16[96,1536]{1,0:T(8,128)(2,1)S(1)} %collective-permute-done.4.refs_5_), channel_id=1, source_target_pairs={{0,28},{4,0},{8,4},{12,8},{16,12},{20,16},{24,20},{28,24},{1,29},{... | collective-permute-start | bytes 884744 | tf_op jit(solution)/shard_map/ppermute | solution.py:38
  70.2 14.5 %collective-permute-start.10 = (bf16[96,1536]{1,0:T(8,128)(2,1)S(1)}, bf16[96,1536]{1,0:T(8,128)(2,1)S(1)}, u32[]{:S(2)}, u32[]{:S(2)}) collective-permute-start(bf16[96,1536]{1,0:T(8,128)(2,1)S(1)} %collective-permute-done.6.refs_7_), channel_id=1, source_target_pairs={{0,28},{4,0},{8,4},{12,8},{16,12},{20,16},{24,20},{28,24},{1,29},{... | collective-permute-start | bytes 884744 | tf_op jit(solution)/shard_map/ppermute | solution.py:38
  74.3 12.4 %collective-permute-start.11 = (bf16[96,1536]{1,0:T(8,128)(2,1)S(1)}, bf16[96,1536]{1,0:T(8,128)(2,1)S(1)}, u32[]{:S(2)}, u32[]{:S(2)}) collective-permute-start(bf16[96,1536]{1,0:T(8,128)(2,1)S(1)} %collective-permute-done.7.refs_8_), channel_id=1, source_target_pairs={{0,4},{4,8},{8,12},{12,16},{16,20},{20,24},{24,28},{28,0},{1,5},{5... | collective-permute-start | bytes 884744 | tf_op jit(solution)/shard_map/ppermute | solution.py:38
  78.2 12.3 %collective-permute-start.9 = (bf16[96,1536]{1,0:T(8,128)(2,1)S(1)}, bf16[96,1536]{1,0:T(8,128)(2,1)}, u32[]{:S(2)}, u32[]{:S(2)}) collective-permute-start(bf16[96,1536]{1,0:T(8,128)(2,1)S(1)} %collective-permute-done.5.refs_6_), channel_id=1, source_target_pairs={{0,4},{4,8},{8,12},{12,16},{16,20},{20,24},{24,28},{28,0},{1,5},{5... | collective-permute-start | bytes 884744 | tf_op jit(solution)/shard_map/ppermute | solution.py:38
  80.1 10.3 %collective-permute-start.12 = (bf16[96,1536]{1,0:T(8,128)(2,1)S(1)}, bf16[96,1536]{1,0:T(8,128)(2,1)}, u32[]{:S(2)}, u32[]{:S(2)}) collective-permute-start(bf16[96,1536]{1,0:T(8,128)(2,1)S(1)} %collective-permute-done.8.refs_9_), channel_id=1, source_target_pairs={{0,28},{4,0},{8,4},{12,8},{16,12},{20,16},{24,20},{28,24},{1,29},{... | collective-permute-start | bytes 884744 | tf_op jit(solution)/shard_map/ppermute | solution.py:38
  84.7 10.9 %collective-permute-start.13 = (bf16[96,1536]{1,0:T(8,128)(2,1)S(1)}, bf16[96,1536]{1,0:T(8,128)(2,1)}, u32[]{:S(2)}, u32[]{:S(2)}) collective-permute-start(bf16[96,1536]{1,0:T(8,128)(2,1)S(1)} %collective-permute-done.10.refs_11_), channel_id=1, source_target_pairs={{0,28},{4,0},{8,4},{12,8},{16,12},{20,16},{24,20},{28,24},{1,29},{... | collective-permute-start | bytes 884744 | tf_op jit(solution)/shard_map/ppermute | solution.py:38
  86.7 9.5 %collective-permute-start.14 = (bf16[96,1536]{1,0:T(8,128)(2,1)S(1)}, bf16[96,1536]{1,0:T(8,128)(2,1)}, u32[]{:S(2)}, u32[]{:S(2)}) collective-permute-start(bf16[96,1536]{1,0:T(8,128)(2,1)S(1)} %collective-permute-done.11.refs_12_), channel_id=1, source_target_pairs={{0,4},{4,8},{8,12},{12,16},{16,20},{20,24},{24,28},{28,0},{1,5},{5... | collective-permute-start | bytes 884744 | tf_op jit(solution)/shard_map/ppermute | solution.py:38
  117.9 5.3 %collective-permute-start.19 = (bf16[384,1536]{1,0:T(8,128)(2,1)}, bf16[384,1536]{1,0:T(8,128)(2,1)S(1)}, u32[]{:S(2)}, u32[]{:S(2)}) collective-permute-start(bf16[384,1536]{1,0:T(8,128)(2,1)} %get-tuple-element.46), channel_id=1, source_target_pairs={{0,1},{1,0},{2,3},{3,2},{4,5},{5,4},{6,7},{7,6},{8,9},{9,8},{10,11... | collective-permute-start | bytes 3538952 | tf_op jit(solution)/shard_map/ppermute | solution.py:46
  120.5 14.9 %collective-permute-start.15 = (bf16[384,1536]{1,0:T(8,128)(2,1)}, bf16[384,1536]{1,0:T(8,128)(2,1)S(1)}, u32[]{:S(2)}, u32[]{:S(2)}) collective-permute-start(bf16[384,1536]{1,0:T(8,128)(2,1)} %get-tuple-element.40), channel_id=1, source_target_pairs={{0,1},{1,0},{2,3},{3,2},{4,5},{5,4},{6,7},{7,6},{8,9},{9,8},{10,11... | collective-permute-start | bytes 3538952 | tf_op jit(solution)/shard_map/ppermute | solution.py:46
  124.4 10.9 %copy-start = (bf16[384,1536]{1,0:T(8,128)(2,1)S(1)}, bf16[384,1536]{1,0:T(8,128)(2,1)}, u32[]{:S(2)}) copy-start(bf16[384,1536]{1,0:T(8,128)(2,1)} %get-tuple-element.39.ours) | copy-start | bytes 3538948
  124.7 16.0 %collective-permute-start.20 = (bf16[384,384]{1,0:T(8,128)(2,1)S(1)}, bf16[384,384]{1,0:T(8,128)(2,1)S(1)}, u32[]{:S(2)}, u32[]{:S(2)}) collective-permute-start(bf16[384,384]{1,0:T(8,128)(2,1)S(1)} %get-tuple-element.48), channel_id=1, source_target_pairs={{0,32},{32,64},{64,96},{96,0},{1,33},{33,65},{65,97},{97,1},{2,34}... | collective-permute-start | bytes 884744 | tf_op jit(solution)/shard_map/ppermute | solution.py:42
  127.9 16.2 %collective-permute-start.21 = (bf16[384,384]{1,0:T(8,128)(2,1)S(1)}, bf16[384,384]{1,0:T(8,128)(2,1)S(1)}, u32[]{:S(2)}, u32[]{:S(2)}) collective-permute-start(bf16[384,384]{1,0:T(8,128)(2,1)S(1)} %get-tuple-element.49), channel_id=1, source_target_pairs={{0,64},{32,96},{64,0},{96,32},{1,65},{33,97},{65,1},{97,33},{2,66}... | collective-permute-start | bytes 884744 | tf_op jit(solution)/shard_map/ppermute | solution.py:42
  132.3 12.9 %collective-permute-start.22 = (bf16[384,384]{1,0:T(8,128)(2,1)S(1)}, bf16[384,384]{1,0:T(8,128)(2,1)S(1)}, u32[]{:S(2)}, u32[]{:S(2)}) collective-permute-start(bf16[384,384]{1,0:T(8,128)(2,1)S(1)} %get-tuple-element.50), channel_id=1, source_target_pairs={{0,96},{32,0},{64,32},{96,64},{1,97},{33,1},{65,33},{97,65},{2,98}... | collective-permute-start | bytes 884744 | tf_op jit(solution)/shard_map/ppermute | solution.py:42
  135.7 23.8 %collective-permute-start.16 = (bf16[384,384]{1,0:T(8,128)(2,1)S(1)}, bf16[384,384]{1,0:T(8,128)(2,1)S(1)}, u32[]{:S(2)}, u32[]{:S(2)}) collective-permute-start(bf16[384,384]{1,0:T(8,128)(2,1)S(1)} %get-tuple-element.42), channel_id=1, source_target_pairs={{0,32},{32,64},{64,96},{96,0},{1,33},{33,65},{65,97},{97,1},{2,34}... | collective-permute-start | bytes 884744 | tf_op jit(solution)/shard_map/ppermute | solution.py:42
  137.9 21.7 %collective-permute-start.17 = (bf16[384,384]{1,0:T(8,128)(2,1)S(1)}, bf16[384,384]{1,0:T(8,128)(2,1)S(1)}, u32[]{:S(2)}, u32[]{:S(2)}) collective-permute-start(bf16[384,384]{1,0:T(8,128)(2,1)S(1)} %get-tuple-element.43), channel_id=1, source_target_pairs={{0,64},{32,96},{64,0},{96,32},{1,65},{33,97},{65,1},{97,33},{2,66}... | collective-permute-start | bytes 884744 | tf_op jit(solution)/shard_map/ppermute | solution.py:42
  140.7 18.8 %collective-permute-start.18 = (bf16[384,384]{1,0:T(8,128)(2,1)S(1)}, bf16[384,384]{1,0:T(8,128)(2,1)S(1)}, u32[]{:S(2)}, u32[]{:S(2)}) collective-permute-start(bf16[384,384]{1,0:T(8,128)(2,1)S(1)} %get-tuple-element.44), channel_id=1, source_target_pairs={{0,96},{32,0},{64,32},{96,64},{1,97},{33,1},{65,33},{97,65},{2,98}... | collective-permute-start | bytes 884744 | tf_op jit(solution)/shard_map/ppermute | solution.py:42
  145.2 22.3 %copy-start.3 = (s32[6,3]{0,1:T(4,128)S(1)}, s32[6,3]{0,1:T(4,128)}, u32[]{:S(2)}) copy-start(s32[6,3]{0,1:T(4,128)} %param.5) | copy-start | bytes 220
  145.5 8.2 %collective-permute-start.23 = (f32[1,384]{1,0:T(1,128)S(1)}, f32[1,384]{1,0:T(1,128)S(1)}, u32[]{:S(2)}, u32[]{:S(2)}) collective-permute-start(f32[1,384]{1,0:T(1,128)S(1)} %get-tuple-element.51), channel_id=1, source_target_pairs={{0,2},{2,0},{1,3},{3,1},{4,6},{6,4},{5,7},{7,5},{8,10},{10,8},{9,1... | collective-permute-start | bytes 4616 | tf_op jit(solution)/shard_map/ppermute | solution.py:46
  153.7 24.4 %collective-permute-start.24 = (bf16[384,384]{1,0:T(8,128)(2,1)S(1)}, bf16[384,384]{1,0:T(8,128)(2,1)S(1)}, u32[]{:S(2)}, u32[]{:S(2)}) collective-permute-start(bf16[384,384]{1,0:T(8,128)(2,1)S(1)} %get-tuple-element.55), channel_id=1, source_target_pairs={{0,2},{2,0},{1,3},{3,1},{4,6},{6,4},{5,7},{7,5},{8,10},{10,8},{9,1... | collective-permute-start | bytes 884744 | tf_op jit(solution)/shard_map/ppermute | solution.py:46
  160.4 17.7 %all-to-all-start.2 = ((f32[16,1,384]{2,1,0:T(1,128)}), f32[16,1,384]{2,1,0:T(1,128)S(1)}, u32[]{:S(2)}, u32[]{:S(2)}) async-start(f32[16,1,384]{2,1,0:T(1,128)} %get-tuple-element.56), calls=%async_computation.2 | async-start | bytes 49152 | tf_op jit(solution)/shard_map/all_to_all | solution.py:240
  (1 other events, 1.3 us)
Sparse Core Ops, SparseCore 0:
  36.4 68.9 all-gather.1
